TPU v7x, 32 devices: a whole 2x2x4 slice. The times are simulated.
32 devices in a mesh: rows: 4 (over y, x), tm: 8 (over z, core).
Axes of the slice: x: 2, y: 2, z: 4, core: 2. Of those that a mesh axis runs over, the one named last changes fastest.
Arguments:
- snapshots: float32 [4096, 2048], P('rows', 'tm'), may hold values from -16 to 16
- right_basis: float32 [2048, 256], P('tm'), may hold values from -0.125 to 0.125
- threshold: float32 [2048], P('tm'), may hold values from 0.3 to 3
Outputs:
- low_rank: float32 [4096, 2048], P('rows', 'tm')
- sparse: float32 [4096, 2048], P('rows', 'tm')
All inputs are finite; a program needn't handle non-finite values.
Results may differ from a plain program's by a relative error of at most 0.0003.
Values sent between devices are 32-bit elements; how exact they have to be, the bound alone decides.
No kernel may reach another device: no remote copies, remote signals or barrier semaphores. Data moves between devices by JAX's collectives and lax.ppermute only.
A program may use at most 64 MiB of HBM per device.

v0:
```python
import jax
import jax.numpy as jnp
from jax import lax
from jax.sharding import PartitionSpec as P

ITERS = 2


highest = lax.Precision.HIGHEST


def gram_of(matrix):
    return lax.dot_general(
        matrix,
        matrix,
        (((0,), (0,)), ((), ())),
        precision=highest,
        preferred_element_type=jnp.float32,
    )


def inverse_factor(gram):
    lower = jnp.linalg.cholesky(gram)
    identity_rows = jnp.eye(gram.shape[0], dtype=gram.dtype)
    return lax.linalg.triangular_solve(lower, identity_rows, left_side=True, lower=True)


def times_inverse(matrix, inverse):
    return lax.dot_general(
        matrix,
        inverse,
        (((1,), (1,)), ((), ())),
        precision=highest,
        preferred_element_type=jnp.float32,
    )


def per_device(snapshots, right_basis, threshold):
    sparse = jnp.zeros_like(snapshots)
    basis = right_basis
    low_rank = jnp.zeros_like(snapshots)
    for iteration in range(ITERS):
        residual = snapshots - sparse
        partial_value = jnp.dot(
            residual, basis, precision=highest, preferred_element_type=jnp.float32
        )
        left = lax.psum(partial_value, "tm")
        ortho = times_inverse(left, inverse_factor(lax.psum(gram_of(left), "rows")))
        right_partial = lax.dot_general(
            residual,
            ortho,
            (((0,), (0,)), ((), ())),
            precision=highest,
            preferred_element_type=jnp.float32,
        )
        basis = lax.psum(right_partial, "rows")
        low_rank = times_inverse(ortho, basis)
        difference = snapshots - low_rank
        sparse = jnp.sign(difference) * jnp.maximum(jnp.abs(difference) - threshold[None, :], 0.0)
    return (low_rank, sparse)


def solution(mesh):
    return jax.shard_map(
        per_device,
        mesh=mesh,
        in_specs=(P("rows", "tm"), P("tm", None), P("tm")),
        out_specs=(P("rows", "tm"), P("rows", "tm")),
        check_vma=False,
    )
```

profile of v0, /device:TPU:0, one launch (start us, length us, event | category | flops | bytes accessed | tf_op | source)
XLA Modules:
  0.0 458.3 jit_solution(3017564738995210687)
XLA Ops:
  7.2 0.9 copy-done
  8.1 3.2 fusion.29
  11.4 61.6 %all-reduce.8.cloned.1.call-done = f32[1024,256]{1,0:T(8,128)} async-done(((f32[1024,256]{1,0:T(8,128)}), f32[1024,256]{1,0:T(8,128)}) %all-reduce.8.cloned.1.call-update) | async-done | bytes 1048592 | tf_op jit(solution)/shard_map/psum | solution.py:47
  73.0 4.1 fusion.30
  77.1 0.6 all-reduce.12.cloned.1.call-start
  77.7 41.4 %all-reduce.10.cloned.1.call-done = f32[256,256]{0,1:T(8,128)} async-done(((f32[256,256]{0,1:T(8,128)}), f32[256,256]{0,1:T(8,128)}) %all-reduce.10.cloned.1.call-update) | async-done | bytes 262160 | tf_op jit(solution)/shard_map/psum | solution.py:48
  119.1 1.1 copy.6
  120.3 11.7 %cholesky.130 = f32[128,128]{1,0:T(8,128)S(1)} custom-call(f32[128,128]{1,0:T(8,128)S(1)} %cholesky.194), custom_call_target="Cholesky" | custom-call | tf_op jit(solution)/shard_map/jit(cholesky)/cholesky | solution.py:23
  132.1 9.8 %custom-call.13 = f32[1,128,128]{1,2,0:T(8,128)S(1)} custom-call(f32[1,128,128]{2,1,0:T(8,128)S(1)} %get-tuple-element.47), custom_call_target="InvertDiagBlocksLowerTriangular" | custom-call | tf_op jit(solution)/shard_map/jit(cholesky)/cholesky | solution.py:23
  142.1 0.3 convolution_subtract_fusion.4
  142.4 11.7 %cholesky.147 = f32[128,128]{1,0:T(8,128)S(1)} custom-call(f32[128,128]{1,0:T(8,128)S(1)} %convolution_subtract_fusion.4), custom_call_target="Cholesky" | custom-call | tf_op jit(solution)/shard_map/jit(cholesky)/cholesky | solution.py:23
  154.1 0.7 compare_reduce_fusion.2
  156.2 4.1 while.4
  156.4 0.6 fusion.62
  157.0 1.4 bitcast_dynamic-update-slice_fusion.4
  158.4 0.6 fusion.62
  159.0 1.4 bitcast_dynamic-update-slice_fusion.4
  160.3 19.7 %custom-call.14 = f32[2,128,128]{1,2,0:T(8,128)S(1)} custom-call(f32[2,128,128]{2,1,0:T(8,128)S(1)} %get-tuple-element.18), custom_call_target="InvertDiagBlocksLowerTriangular" | custom-call | tf_op jit(solution)/shard_map/triangular_solve/custom-call.0 | solution.py:25
  180.0 0.3 fusion.13
  180.6 0.3 fusion.20
  181.0 1.0 fusion
  182.2 2.5 convolution_bitcast_fusion
  184.8 43.0 %all-reduce.12.cloned.1.call-done = f32[256,256]{0,1:T(8,128)} async-done(((f32[256,256]{0,1:T(8,128)}), f32[256,256]{0,1:T(8,128)}) %all-reduce.12.cloned.1.call-update) | async-done | bytes 262160 | tf_op jit(solution)/shard_map/psum | solution.py:56
  227.8 2.3 multiply_subtract_fusion
  230.1 1.0 copy-done.4
  231.1 2.0 fusion.31
  233.2 59.0 %all-reduce.14.cloned.1.call-done = f32[1024,256]{1,0:T(8,128)} async-done(((f32[1024,256]{1,0:T(8,128)}), f32[1024,256]{1,0:T(8,128)}) %all-reduce.14.cloned.1.call-update) | async-done | bytes 1048592 | tf_op jit(solution)/shard_map/psum | solution.py:47
  292.1 4.1 fusion.32
  296.5 41.8 %all-reduce.16.cloned.1.call-done = f32[256,256]{0,1:T(8,128)} async-done(((f32[256,256]{0,1:T(8,128)}), f32[256,256]{0,1:T(8,128)}) %all-reduce.16.cloned.1.call-update) | async-done | bytes 262160 | tf_op jit(solution)/shard_map/psum | solution.py:48
  338.3 1.1 copy.8
  339.5 11.7 %cholesky.164 = f32[128,128]{1,0:T(8,128)S(1)} custom-call(f32[128,128]{1,0:T(8,128)S(1)} %cholesky.197), custom_call_target="Cholesky" | custom-call | tf_op jit(solution)/shard_map/jit(cholesky)/cholesky | solution.py:23
  351.3 9.8 %custom-call.15 = f32[1,128,128]{1,2,0:T(8,128)S(1)} custom-call(f32[1,128,128]{2,1,0:T(8,128)S(1)} %get-tuple-element.43), custom_call_target="InvertDiagBlocksLowerTriangular" | custom-call | tf_op jit(solution)/shard_map/jit(cholesky)/cholesky | solution.py:23
  361.3 0.3 convolution_subtract_fusion.3
  361.6 11.7 %cholesky.181 = f32[128,128]{1,0:T(8,128)S(1)} custom-call(f32[128,128]{1,0:T(8,128)S(1)} %convolution_subtract_fusion.3), custom_call_target="Cholesky" | custom-call | tf_op jit(solution)/shard_map/jit(cholesky)/cholesky | solution.py:23
  373.3 0.7 compare_reduce_fusion
  374.0 0.6 compare_reduce_fusion.1
  376.0 4.2 while.5
  376.2 0.6 fusion.63
  376.8 1.4 bitcast_dynamic-update-slice_fusion.5
  378.2 0.6 fusion.63
  378.8 1.4 bitcast_dynamic-update-slice_fusion.5
  380.2 19.7 %custom-call.16 = f32[2,128,128]{1,2,0:T(8,128)S(1)} custom-call(f32[2,128,128]{2,1,0:T(8,128)S(1)} %get-tuple-element.19), custom_call_target="InvertDiagBlocksLowerTriangular" | custom-call | tf_op jit(solution)/shard_map/triangular_solve/custom-call.0 | solution.py:25
  399.9 0.3 fusion.11
  400.5 0.3 fusion.16
  400.8 1.0 fusion.4
  402.0 2.5 fusion.33
  404.6 43.1 %all-reduce.18.cloned.1.call-done = f32[256,256]{1,0:T(8,128)} async-done(((f32[256,256]{1,0:T(8,128)}), f32[256,256]{1,0:T(8,128)}) %all-reduce.18.cloned.1.call-update) | async-done | bytes 262160 | tf_op jit(solution)/shard_map/psum | solution.py:56
  447.6 3.6 maximum_multiply_fusion
  (58 shorter events, 2.3 us)
Async XLA Ops:
  7.2 1.0 copy-start
  7.2 65.8 %all-reduce.8.cloned.1.call-start = ((), (), s32[]{:S(2)}) async-start(), calls=%async_computation | async-start | bytes 2097152 | tf_op jit(solution)/shard_map/psum | solution.py:47
  11.3 107.8 %all-reduce.10.cloned.1.call-start = ((), (), s32[]{:S(2)}) async-start(), calls=%async_computation.1 | async-start | bytes 524288 | tf_op jit(solution)/shard_map/psum | solution.py:48
  77.1 150.8 %all-reduce.12.cloned.1.call-start = ((), (), s32[]{:S(2)}) async-start(), calls=%async_computation.2 | async-start | bytes 524288 | tf_op jit(solution)/shard_map/psum | solution.py:56
  77.7 102.7 %copy-start.6 = (f32[256,256]{1,0:T(8,128)}, f32[256,256]{1,0:T(8,128)S(1)}, u32[]{:S(2)}) copy-start(f32[256,256]{1,0:T(8,128)S(1)} %fusion.10) | copy-start | bytes 786436
  119.1 1.2 copy-start.9
  156.1 24.8 %copy-start.2 = (f32[1024,256]{1,0:T(8,128)S(1)}, f32[1024,256]{1,0:T(8,128)}, u32[]{:S(2)}) copy-start(f32[1024,256]{1,0:T(8,128)} %all-reduce.8.cloned.1.call-done) | copy-start | bytes 3145732
  181.0 1.2 copy-start.1
  184.7 43.1 %copy-start.11 = (f32[256]{0:T(256)S(1)}, f32[256]{0:T(256)}, u32[]{:S(2)}) copy-start(f32[256]{0:T(256)} %param.8) | copy-start | bytes 3076
  184.7 107.4 %all-reduce.14.cloned.1.call-start = ((), (), s32[]{:S(2)}) async-start(), calls=%async_computation.3 | async-start | bytes 2097152 | tf_op jit(solution)/shard_map/psum | solution.py:47
  227.8 3.3 copy-start.8
  230.1 1.0 copy-start.4
  233.1 105.1 %all-reduce.16.cloned.1.call-start = ((), (), s32[]{:S(2)}) async-start(), calls=%async_computation.4 | async-start | bytes 524288 | tf_op jit(solution)/shard_map/psum | solution.py:48
  296.2 151.4 %all-reduce.18.cloned.1.call-start = ((), (), s32[]{:S(2)}) async-start(), calls=%async_computation.5 | async-start | bytes 524288 | tf_op jit(solution)/shard_map/psum | solution.py:56
  338.3 1.2 copy-start.10
  375.9 24.0 %copy-start.7 = (f32[256,256]{1,0:T(8,128)S(1)}, f32[256,256]{1,0:T(8,128)}, u32[]{:S(2)}) copy-start(f32[256,256]{1,0:T(8,128)} %copy-done.6) | copy-start | bytes 786436
  375.9 24.8 %copy-start.3 = (f32[1024,256]{1,0:T(8,128)S(1)}, f32[1024,256]{1,0:T(8,128)}, u32[]{:S(2)}) copy-start(f32[1024,256]{1,0:T(8,128)} %all-reduce.14.cloned.1.call-done) | copy-start | bytes 3145732
  400.8 1.2 copy-start.5
Sparse Core Ops, SparseCore 0:
  11.4 61.4 all-reduce.7
  77.2 41.8 all-reduce.9
  184.9 42.9 all-reduce.11
  233.3 58.8 all-reduce.13
  296.4 41.8 all-reduce.15
  404.7 42.8 all-reduce.17
where the time goes:
time: 462 us; the launch traced here: 458 us
  waiting for transfers between devices  290 us (63%)
  other arithmetic  108 us (23%)
  matrix products  29 us (6%)
  between operations  17.3 us (4%)
  local copies, waits for them, and re-layouts  12.5 us (3%)
    psum x2, waiting for transfers between devices, per_device(): left = lax.psum(partial_value, 'tm')  121 us
    psum x2, waiting for transfers between devices, per_device(): basis = lax.psum(right_partial, 'rows')  86.1 us
    psum x2, waiting for transfers between devices, per_device(): ortho = times_inverse(left, inverse_factor(lax.psum(gram_of(left), 'rows')))  83.2 us
    another operation x13, other arithmetic, inverse_factor(): lower = jnp.linalg.cholesky(gram)  68.6 us
    another operation x5, other arithmetic, inverse_factor(): lax.linalg.triangular_solve(lower, identity_rows, left_side=True, lower=T...  39.4 us
  transfers between devices with their start and end apart: 6, of which 6 were waited for; matrix products, arithmetic and copies ran while one was open for 0% of the time, Pallas kernels for 0%

commit v1 on v0

v1 whole, which is shorter than its diff:
```python
import functools
import jax
import jax.numpy as jnp
from jax import lax
from jax.experimental import pallas as pl
from jax.experimental.pallas import tpu as pltpu
from jax.sharding import PartitionSpec as P

ITERS = 2
CHUNKS = 2

high = lax.Precision.HIGH
highest = lax.Precision.HIGHEST
NN = (((1,), (0,)), ((), ()))
NT = (((1,), (1,)), ((), ()))
TN = (((0,), (0,)), ((), ()))


def mm(a, b, dims, precision=high):
    return lax.dot_general(a, b, dims, precision=precision, preferred_element_type=jnp.float32)


def swap(x, axis, size, bit):
    return lax.ppermute(x, axis, [(i, i ^ bit) for i in range(size)])


def reorder(x, me, blocks):
    rows, cols = x.shape
    cut = x.reshape(CHUNKS, blocks, rows // (CHUNKS * blocks), cols)
    parts = [lax.dynamic_slice_in_dim(cut, p ^ me, 1, 1) for p in range(blocks)]
    return jnp.concatenate(parts, 1).reshape(rows, cols)


def sum_tm(chunks, size):
    bits = [1 << b for b in range(size.bit_length() - 1)]
    chunks = list(chunks)
    for bit in bits[:-1]:
        for i, x in enumerate(chunks):
            half = x.shape[0] // 2
            kept, sent = x[:half], x[half:]
            chunks[i] = kept + swap(sent, "tm", size, bit)
    for i, x in enumerate(chunks):
        chunks[i] = x + swap(x, "tm", size, bits[-1])
    for bit in reversed(bits[:-1]):
        for i, x in enumerate(chunks):
            chunks[i] = jnp.concatenate([x, swap(x, "tm", size, bit)], 0)
    return chunks


def sum_rows(x, size):
    bits = [1 << b for b in range(size.bit_length() - 1)]
    half = x.shape[0] // 2
    a, b = x[:half], x[half:]
    turn = len(bits) // 2
    for bit_a, bit_b in zip(bits, bits[turn:] + bits[:turn]):
        a, b = a + swap(a, "rows", size, bit_a), b + swap(b, "rows", size, bit_b)
    return jnp.concatenate([a, b], 0)


def halves(x):
    top = x.astype(jnp.bfloat16)
    return top, (x - top.astype(jnp.float32)).astype(jnp.bfloat16)


def dot3(a, b):
    a1, a2 = halves(a)
    b1, b2 = halves(b)
    dot = functools.partial(jnp.dot, preferred_element_type=jnp.float32)
    return dot(a1, b1) + (dot(a1, b2) + dot(a2, b1))


def dot6(a, b):
    return jnp.dot(a, b, precision=highest, preferred_element_type=jnp.float32)


def solve_kernel(gram_ref, right_ref, out_ref):
    gram = gram_ref[...]
    n = gram.shape[0]
    eye = (
        lax.broadcasted_iota(jnp.int32, (n, n), 0) == lax.broadcasted_iota(jnp.int32, (n, n), 1)
    ).astype(jnp.float32)
    on_diag = gram * eye
    down = lax.rsqrt(jnp.sum(on_diag, 1, keepdims=True))
    across = lax.rsqrt(jnp.sum(on_diag, 0, keepdims=True))
    scaled = gram * down * across
    bound = jnp.minimum(
        jnp.max(jnp.sum(jnp.abs(scaled), 0, keepdims=True)),
        jnp.sqrt(jnp.sum(scaled * scaled)),
    )
    step = 1.9 / bound
    error = eye - step * scaled
    inverse = step * eye

    def more(state):
        count, size, _, _ = state
        return jnp.logical_and(count < 40, size > 1e-4)

    def double(state):
        count, _, inverse, error = state
        size = jnp.sum(error * error)
        return count + 1, size, inverse + dot3(inverse, error), dot3(error, error)

    _, _, inverse, _ = lax.while_loop(more, double, (0, jnp.float32(1.0), inverse, error))

    def again(state):
        count, size, _ = state
        return jnp.logical_and(count < 20, size > 1e-6)

    def refine(state):
        count, _, inverse = state
        rest = eye - dot6(scaled, inverse)
        return count + 1, jnp.sum(rest * rest), inverse + dot3(inverse, rest)

    _, _, inverse = lax.while_loop(again, refine, (0, jnp.float32(1.0), inverse))
    out_ref[...] = down * dot6(inverse, down * right_ref[...])


def solve(gram, right):
    return pl.pallas_call(
        solve_kernel,
        out_shape=jax.ShapeDtypeStruct(right.shape, jnp.float32),
        compiler_params=pltpu.CompilerParams(vmem_limit_bytes=32 << 20),
    )(gram, right)


def per_device(n_tm, n_rows, snapshots, right_basis, threshold):
    rows, rank = snapshots.shape[0], right_basis.shape[1]
    me = lax.axis_index("tm")
    blocks = n_tm // 2
    low = 0
    for b in range(blocks.bit_length() - 1):
        low = low * 2 + (me >> b) % 2
    data = reorder(snapshots, low, blocks)
    residual = data
    part = rows // CHUNKS
    weights = right_basis.T
    for iteration in range(ITERS):
        chunks = [mm(residual[i * part : (i + 1) * part], weights, NT) for i in range(CHUNKS)]
        chunks = sum_tm(chunks, n_tm)
        products = 0.0
        for i, left in enumerate(chunks):
            products += jnp.concatenate(
                [mm(left, left, TN, highest), mm(left, residual[i * part : (i + 1) * part], TN)], 1
            )
        products = sum_rows(products, n_rows)
        weights = solve(products[:, :rank], products[:, rank:])
        low_rank = jnp.concatenate([mm(left, weights, NN) for left in chunks], 0)
        difference = data - low_rank
        sparse = jnp.sign(difference) * jnp.maximum(jnp.abs(difference) - threshold[None, :], 0.0)
        residual = data - sparse
    return reorder(low_rank, low, blocks), reorder(sparse, low, blocks)


def solution(mesh):
    return jax.shard_map(
        functools.partial(per_device, mesh.shape["tm"], mesh.shape["rows"]),
        mesh=mesh,
        in_specs=(P("rows", "tm"), P("tm", None), P("tm")),
        out_specs=(P("rows", "tm"), P("rows", "tm")),
        check_vma=False,
    )
```

time: 462 us -> 130 us (0.28)
  waiting for transfers between devices: 290 us -> 69.7 us
  other arithmetic: 108 us -> 3.96 us
  starting transfers between devices: 0.98 us -> 27.6 us
  matrix products: 29 us -> 9.56 us
  between operations: 17.3 us -> 1.18 us
  Pallas kernels: 0 us -> 15.7 us
  local copies, waits for them, and re-layouts: 12.5 us -> 2.06 us
    psum x6 -> x0, waiting for transfers between devices: 290 us -> none  [the longest x2 121 us: per_device(): left = lax.psum(partial_value, 'tm')]
    another operation x18 -> x0, other arithmetic: 108 us -> none  [the longest x13 68.6 us: inverse_factor(): lower = jnp.linalg.cholesky(gram)]
    ppermute x0 -> x28, waiting for transfers between devices: none -> 69.7 us  [swap(): return lax.ppermute(x, axis, [(i, i ^ bit) for i in range(size)])]
    ppermute x0 -> x28, starting transfers between devices: none -> 27.6 us  [swap(): return lax.ppermute(x, axis, [(i, i ^ bit) for i in range(size)])]
    dot_general x10 -> x16, matrix products: 26.3 us -> 9.56 us  [mm(): lax.dot_general(a, b, dims, precision=precision, preferred_element_type=j...]
    pallas_call x0 -> x2, Pallas kernels: none -> 15.7 us  [solve(): pl.pallas_call(solve_kernel, out_shape=jax.ShapeDtypeStruct(right.shape,...]
    another operation x19 -> x0, local copies, waits for them, and re-layouts: 7.96 us -> none  [the longest x15 7.91 us: inverse_factor(): lax.linalg.triangular_solve(lower, identity_rows, left_side=True, lower=T...]
  transfers between devices with their start and end apart: 6 -> 28, of which waited for: 6 -> 21; matrix products, arithmetic and copies ran while one was open for 0% -> 3% of each run, Pallas kernels for 0% -> 0%
where the time goes in v1:
time: 130 us
  waiting for transfers between devices  69.7 us (54%)
  starting transfers between devices  27.6 us (21%)
  Pallas kernels  15.7 us (12%)
  matrix products  9.56 us (7%)
  other arithmetic  3.96 us (3%)
  local copies, waits for them, and re-layouts  2.06 us (2%)
    ppermute x28, waiting for transfers between devices, swap(): return lax.ppermute(x, axis, [(i, i ^ bit) for i in range(size)])  69.7 us
    ppermute x28, starting transfers between devices, swap(): return lax.ppermute(x, axis, [(i, i ^ bit) for i in range(size)])  27.6 us
    pallas_call x2, Pallas kernels, solve(): pl.pallas_call(solve_kernel, out_shape=jax.ShapeDtypeStruct(right.shape,...  15.7 us
    dot_general x16, matrix products, mm(): lax.dot_general(a, b, dims, precision=precision, preferred_element_type=j...  9.56 us
  transfers between devices with their start and end apart: 28, of which 21 were waited for; matrix products, arithmetic and copies ran while one was open for 3% of the time, Pallas kernels for 0%

profile of v1, /device:TPU:0, one launch (start us, length us, event | category | flops | bytes accessed | tf_op | source)
XLA Modules:
  0.0 129.8 jit_solution(17680102441123082573)
XLA Ops:
  0.7 1.3 %constant_dynamic-slice_fusion.11 = (f32[2,1,128,256]{3,2,1,0:T(8,128)S(1)}, f32[2,1,128,256]{3,2,1,0:T(8,128)S(1)}, f32[2,1,128,256]{3,2,1,0:T(8,128)S(1)}, f32[2,1,128,256]{3,2,1,0:T(8,128)S(1)}) fusion(f32[2,4,128,256]{3,2,1,0:T(8,128)} %bitcast.29, s32[]{:T(128)S(6)} %select_n.33, s32[]{:T(128)S(6)} %select_n.36, s32[]{:T(128)S(6)} %select_n.35, ...), kind=kLoop, calls=%fused_computation.62 | loop fusion | bytes 2097168 | tf_op jit(solution)/shard_map/dynamic_slice | solution.py:30
  2.6 0.5 collective-permute-start
  3.1 1.2 collective-permute-done
  4.3 3.0 %collective-permute-start.1 = (f32[128,256]{1,0:T(8,128)S(1)}, f32[128,256]{1,0:T(8,128)S(1)}, u32[]{:S(2)}, u32[]{:S(2)}) collective-permute-start(f32[128,256]{1,0:T(8,128)S(1)} %slice.128), channel_id=1, source_target_pairs={{0,2},{1,3},{2,0},{3,1},{4,6},{5,7},{6,4},{7,5},{8,10},{9,11},{10,... | collective-permute-start | bytes 393224 | tf_op jit(solution)/shard_map/ppermute | solution.py:24
  7.8 3.3 %collective-permute-done.1 = f32[128,256]{1,0:T(8,128)S(1)} collective-permute-done((f32[128,256]{1,0:T(8,128)S(1)}, f32[128,256]{1,0:T(8,128)S(1)}, u32[]{:S(2)}, u32[]{:S(2)}) %collective-permute-start.1) | collective-permute-done | bytes 131104 | tf_op jit(solution)/shard_map/ppermute | solution.py:24
  11.1 2.8 %collective-permute-start.2 = (f32[128,256]{1,0:T(8,128)S(1)}, f32[128,256]{1,0:T(8,128)S(1)}, u32[]{:S(2)}, u32[]{:S(2)}) collective-permute-start(f32[128,256]{1,0:T(8,128)S(1)} %slice_add_fusion.7), channel_id=1, source_target_pairs={{0,4},{1,5},{2,6},{3,7},{4,0},{5,1},{6,2},{7,3},{8,12},{9,13},{10,... | collective-permute-start | bytes 393224 | tf_op jit(solution)/shard_map/ppermute | solution.py:24
  14.0 1.6 %collective-permute-start.6 = (f32[128,256]{1,0:T(8,128)S(1)}, f32[128,256]{1,0:T(8,128)S(1)}, u32[]{:S(2)}, u32[]{:S(2)}) collective-permute-start(f32[128,256]{1,0:T(8,128)S(1)} %slice.133), channel_id=1, source_target_pairs={{0,2},{1,3},{2,0},{3,1},{4,6},{5,7},{6,4},{7,5},{8,10},{9,11},{10,... | collective-permute-start | bytes 393224 | tf_op jit(solution)/shard_map/ppermute | solution.py:24
  15.7 4.3 %collective-permute-done.2 = f32[128,256]{1,0:T(8,128)S(1)} collective-permute-done((f32[128,256]{1,0:T(8,128)S(1)}, f32[128,256]{1,0:T(8,128)S(1)}, u32[]{:S(2)}, u32[]{:S(2)}) %collective-permute-start.2) | collective-permute-done | bytes 131104 | tf_op jit(solution)/shard_map/ppermute | solution.py:24
  20.0 0.5 collective-permute-start.3
  20.6 3.4 %collective-permute-start.7 = (f32[128,256]{1,0:T(8,128)S(1)}, f32[128,256]{1,0:T(8,128)S(1)}, u32[]{:S(2)}, u32[]{:S(2)}) collective-permute-start(f32[128,256]{1,0:T(8,128)S(1)} %slice_add_fusion.6), channel_id=1, source_target_pairs={{0,4},{1,5},{2,6},{3,7},{4,0},{5,1},{6,2},{7,3},{8,12},{9,13},{10,... | collective-permute-start | bytes 393224 | tf_op jit(solution)/shard_map/ppermute | solution.py:24
  24.0 3.2 %collective-permute-done.3 = f32[128,256]{1,0:T(8,128)S(1)} collective-permute-done((f32[128,256]{1,0:T(8,128)S(1)}, f32[128,256]{1,0:T(8,128)S(1)}, u32[]{:S(2)}, u32[]{:S(2)}) %collective-permute-start.3) | collective-permute-done | bytes 131104 | tf_op jit(solution)/shard_map/ppermute | solution.py:24
  27.3 2.8 %collective-permute-done.7 = f32[128,256]{1,0:T(8,128)S(1)} collective-permute-done((f32[128,256]{1,0:T(8,128)S(1)}, f32[128,256]{1,0:T(8,128)S(1)}, u32[]{:S(2)}, u32[]{:S(2)}) %collective-permute-start.7) | collective-permute-done | bytes 131104 | tf_op jit(solution)/shard_map/ppermute | solution.py:24
  30.4 4.7 %collective-permute-done.8 = f32[128,256]{1,0:T(8,128)S(1)} collective-permute-done((f32[128,256]{1,0:T(8,128)S(1)}, f32[128,256]{1,0:T(8,128)S(1)}, u32[]{:S(2)}, u32[]{:S(2)}) %collective-permute-start.8) | collective-permute-done | bytes 131104 | tf_op jit(solution)/shard_map/ppermute | solution.py:24
  35.2 1.0 fusion.19
  36.2 0.6 fusion.18
  36.9 0.6 fusion.15
  37.5 1.0 fusion.16
  38.6 1.6 %collective-permute-start.12 = (f32[128,512]{1,0:T(8,128)S(1)}, f32[128,512]{1,0:T(8,128)S(1)}, u32[]{:S(2)}, u32[]{:S(2)}) collective-permute-start(f32[128,512]{1,0:T(8,128)S(1)} %get-tuple-element.26), channel_id=1, source_target_pairs={{0,16},{8,24},{16,0},{24,8},{1,17},{9,25},{17,1},{25,9},{2,18},{10... | collective-permute-start | bytes 786440 | tf_op jit(solution)/shard_map/ppermute | solution.py:24
  40.2 1.5 %collective-permute-start.10 = (f32[128,512]{1,0:T(8,128)S(1)}, f32[128,512]{1,0:T(8,128)S(1)}, u32[]{:S(2)}, u32[]{:S(2)}) collective-permute-start(f32[128,512]{1,0:T(8,128)S(1)} %get-tuple-element.27), channel_id=1, source_target_pairs={{0,8},{8,0},{16,24},{24,16},{1,9},{9,1},{17,25},{25,17},{2,10},{10... | collective-permute-start | bytes 786440 | tf_op jit(solution)/shard_map/ppermute | solution.py:24
  41.7 5.7 %collective-permute-done.12 = f32[128,512]{1,0:T(8,128)S(1)} collective-permute-done((f32[128,512]{1,0:T(8,128)S(1)}, f32[128,512]{1,0:T(8,128)S(1)}, u32[]{:S(2)}, u32[]{:S(2)}) %collective-permute-start.12) | collective-permute-done | bytes 262176 | tf_op jit(solution)/shard_map/ppermute | solution.py:24
  47.4 1.3 collective-permute-done.10
  48.7 1.6 %collective-permute-start.13 = (f32[128,512]{1,0:T(8,128)S(1)}, f32[128,512]{1,0:T(8,128)S(1)}, u32[]{:S(2)}, u32[]{:S(2)}) collective-permute-start(f32[128,512]{1,0:T(8,128)S(1)} %get-tuple-element.24), channel_id=1, source_target_pairs={{0,8},{8,0},{16,24},{24,16},{1,9},{9,1},{17,25},{25,17},{2,10},{10... | collective-permute-start | bytes 786440 | tf_op jit(solution)/shard_map/ppermute | solution.py:24
  50.3 0.5 collective-permute-start.11
  50.8 5.6 %collective-permute-done.13 = f32[128,512]{1,0:T(8,128)S(1)} collective-permute-done((f32[128,512]{1,0:T(8,128)S(1)}, f32[128,512]{1,0:T(8,128)S(1)}, u32[]{:S(2)}, u32[]{:S(2)}) %collective-permute-start.13) | collective-permute-done | bytes 262176 | tf_op jit(solution)/shard_map/ppermute | solution.py:24
  56.4 1.2 collective-permute-done.11
  57.7 7.7 %shard_map.50 = f32[256,256]{1,0:T(8,128)S(1)} custom-call(f32[256,256]{1,0:T(8,128)S(1)} %get-tuple-element.23.gram_ref, f32[256,256]{1,0:T(8,128)S(1)} %get-tuple-element.22.right_ref), custom_call_target="tpu_custom_call" | custom-call | tf_op jit(solution)/shard_map/pallas_call | solution.py:119
  67.5 1.5 %collective-permute-done.19 = f32[256,256]{1,0:T(8,128)S(1)} collective-permute-done((f32[256,256]{1,0:T(8,128)S(1)}, f32[256,256]{1,0:T(8,128)S(1)}, u32[]{:S(2)}, u32[]{:S(2)}) %collective-permute-start.19) | collective-permute-done | bytes 262176 | tf_op jit(solution)/shard_map/ppermute | solution.py:24
  69.9 4.8 %collective-permute-done.20 = f32[128,256]{1,0:T(8,128)S(1)} collective-permute-done((f32[128,256]{1,0:T(8,128)S(1)}, f32[128,256]{1,0:T(8,128)S(1)}, u32[]{:S(2)}, u32[]{:S(2)}) %collective-permute-start.20) | collective-permute-done | bytes 131104 | tf_op jit(solution)/shard_map/ppermute | solution.py:24
  74.7 1.3 collective-permute-start.21
  76.0 1.8 %collective-permute-start.15 = (f32[128,256]{1,0:T(8,128)S(1)}, f32[128,256]{1,0:T(8,128)S(1)}, u32[]{:S(2)}, u32[]{:S(2)}) collective-permute-start(f32[128,256]{1,0:T(8,128)S(1)} %slice.142), channel_id=1, source_target_pairs={{0,2},{1,3},{2,0},{3,1},{4,6},{5,7},{6,4},{7,5},{8,10},{9,11},{10,... | collective-permute-start | bytes 393224 | tf_op jit(solution)/shard_map/ppermute | solution.py:24
  77.8 5.2 %collective-permute-done.21 = f32[128,256]{1,0:T(8,128)S(1)} collective-permute-done((f32[128,256]{1,0:T(8,128)S(1)}, f32[128,256]{1,0:T(8,128)S(1)}, u32[]{:S(2)}, u32[]{:S(2)}) %collective-permute-start.21) | collective-permute-done | bytes 131104 | tf_op jit(solution)/shard_map/ppermute | solution.py:24
  83.6 2.7 %collective-permute-start.16 = (f32[128,256]{1,0:T(8,128)S(1)}, f32[128,256]{1,0:T(8,128)S(1)}, u32[]{:S(2)}, u32[]{:S(2)}) collective-permute-start(f32[128,256]{1,0:T(8,128)S(1)} %slice_add_fusion.5), channel_id=1, source_target_pairs={{0,4},{1,5},{2,6},{3,7},{4,0},{5,1},{6,2},{7,3},{8,12},{9,13},{10,... | collective-permute-start | bytes 393224 | tf_op jit(solution)/shard_map/ppermute | solution.py:24
  86.3 4.3 %collective-permute-done.22 = f32[128,256]{1,0:T(8,128)S(1)} collective-permute-done((f32[128,256]{1,0:T(8,128)S(1)}, f32[128,256]{1,0:T(8,128)S(1)}, u32[]{:S(2)}, u32[]{:S(2)}) %collective-permute-start.22) | collective-permute-done | bytes 131104 | tf_op jit(solution)/shard_map/ppermute | solution.py:24
  90.7 1.8 %collective-permute-done.16 = f32[128,256]{1,0:T(8,128)S(1)} collective-permute-done((f32[128,256]{1,0:T(8,128)S(1)}, f32[128,256]{1,0:T(8,128)S(1)}, u32[]{:S(2)}, u32[]{:S(2)}) %collective-permute-start.16) | collective-permute-done | bytes 131104 | tf_op jit(solution)/shard_map/ppermute | solution.py:24
  92.8 4.7 %collective-permute-done.17 = f32[128,256]{1,0:T(8,128)S(1)} collective-permute-done((f32[128,256]{1,0:T(8,128)S(1)}, f32[128,256]{1,0:T(8,128)S(1)}, u32[]{:S(2)}, u32[]{:S(2)}) %collective-permute-start.17) | collective-permute-done | bytes 131104 | tf_op jit(solution)/shard_map/ppermute | solution.py:24
  97.6 1.0 fusion.11
  98.7 0.6 fusion
  99.3 0.6 fusion.4
  99.9 1.0 fusion.13
  101.0 0.7 collective-permute-start.26
  101.7 0.5 collective-permute-start.24
  102.2 7.6 %collective-permute-done.26 = f32[128,512]{1,0:T(8,128)S(1)} collective-permute-done((f32[128,512]{1,0:T(8,128)S(1)}, f32[128,512]{1,0:T(8,128)S(1)}, u32[]{:S(2)}, u32[]{:S(2)}) %collective-permute-start.26) | collective-permute-done | bytes 262176 | tf_op jit(solution)/shard_map/ppermute | solution.py:24
  110.2 0.6 collective-permute-start.27
  110.8 1.4 %collective-permute-start.25 = (f32[128,512]{1,0:T(8,128)S(1)}, f32[128,512]{1,0:T(8,128)S(1)}, u32[]{:S(2)}, u32[]{:S(2)}) collective-permute-start(f32[128,512]{1,0:T(8,128)S(1)} %get-tuple-element.19), channel_id=1, source_target_pairs={{0,16},{8,24},{16,0},{24,8},{1,17},{9,25},{17,1},{25,9},{2,18},{10... | collective-permute-start | bytes 786440 | tf_op jit(solution)/shard_map/ppermute | solution.py:24
  112.2 5.6 %collective-permute-done.27 = f32[128,512]{1,0:T(8,128)S(1)} collective-permute-done((f32[128,512]{1,0:T(8,128)S(1)}, f32[128,512]{1,0:T(8,128)S(1)}, u32[]{:S(2)}, u32[]{:S(2)}) %collective-permute-start.27) | collective-permute-done | bytes 262176 | tf_op jit(solution)/shard_map/ppermute | solution.py:24
  118.2 8.0 %shard_map.51 = f32[256,256]{1,0:T(8,128)S(1)} custom-call(f32[256,256]{1,0:T(8,128)S(1)} %get-tuple-element.17.gram_ref, f32[256,256]{1,0:T(8,128)S(1)} %get-tuple-element.16.right_ref), custom_call_target="tpu_custom_call" | custom-call | tf_op jit(solution)/shard_map/pallas_call | solution.py:119
  127.7 1.0 pad_maximum_fusion.3
  128.7 1.0 pad_maximum_fusion.2
  (75 shorter events, 8.3 us)
Async XLA Ops:
  0.6 1.5 %copy-start = (f32[256,256]{1,0:T(8,128)S(1)}, f32[256,256]{1,0:T(8,128)}, u32[]{:S(2)}) copy-start(f32[256,256]{1,0:T(8,128)} %param.4) | copy-start | bytes 786436
  2.6 1.7 %collective-permute-start = (f32[256,256]{1,0:T(8,128)S(1)}, f32[256,256]{1,0:T(8,128)S(1)}, u32[]{:S(2)}, u32[]{:S(2)}) collective-permute-start(f32[256,256]{1,0:T(8,128)S(1)} %slice.126), channel_id=1, source_target_pairs={{0,1},{1,0},{2,3},{3,2},{4,5},{5,4},{6,7},{7,6},{8,9},{9,8},{10,11... | collective-permute-start | bytes 786440 | tf_op jit(solution)/shard_map/ppermute | solution.py:24
  4.3 6.8 %collective-permute-start.1 = (f32[128,256]{1,0:T(8,128)S(1)}, f32[128,256]{1,0:T(8,128)S(1)}, u32[]{:S(2)}, u32[]{:S(2)}) collective-permute-start(f32[128,256]{1,0:T(8,128)S(1)} %slice.128), channel_id=1, source_target_pairs={{0,2},{1,3},{2,0},{3,1},{4,6},{5,7},{6,4},{7,5},{8,10},{9,11},{10,... | collective-permute-start | bytes 393224 | tf_op jit(solution)/shard_map/ppermute | solution.py:24
  7.7 6.2 %collective-permute-start.5 = (f32[256,256]{1,0:T(8,128)S(1)}, f32[256,256]{1,0:T(8,128)S(1)}, u32[]{:S(2)}, u32[]{:S(2)}) collective-permute-start(f32[256,256]{1,0:T(8,128)S(1)} %slice.131), channel_id=1, source_target_pairs={{0,1},{1,0},{2,3},{3,2},{4,5},{5,4},{6,7},{7,6},{8,9},{9,8},{10,11... | collective-permute-start | bytes 786440 | tf_op jit(solution)/shard_map/ppermute | solution.py:24
  11.1 8.9 %collective-permute-start.2 = (f32[128,256]{1,0:T(8,128)S(1)}, f32[128,256]{1,0:T(8,128)S(1)}, u32[]{:S(2)}, u32[]{:S(2)}) collective-permute-start(f32[128,256]{1,0:T(8,128)S(1)} %slice_add_fusion.7), channel_id=1, source_target_pairs={{0,4},{1,5},{2,6},{3,7},{4,0},{5,1},{6,2},{7,3},{8,12},{9,13},{10,... | collective-permute-start | bytes 393224 | tf_op jit(solution)/shard_map/ppermute | solution.py:24
  14.0 6.5 %collective-permute-start.6 = (f32[128,256]{1,0:T(8,128)S(1)}, f32[128,256]{1,0:T(8,128)S(1)}, u32[]{:S(2)}, u32[]{:S(2)}) collective-permute-start(f32[128,256]{1,0:T(8,128)S(1)} %slice.133), channel_id=1, source_target_pairs={{0,2},{1,3},{2,0},{3,1},{4,6},{5,7},{6,4},{7,5},{8,10},{9,11},{10,... | collective-permute-start | bytes 393224 | tf_op jit(solution)/shard_map/ppermute | solution.py:24
  20.0 7.2 %collective-permute-start.3 = (f32[128,256]{1,0:T(8,128)S(1)}, f32[128,256]{1,0:T(8,128)S(1)}, u32[]{:S(2)}, u32[]{:S(2)}) collective-permute-start(f32[128,256]{1,0:T(8,128)S(1)} %add.105), channel_id=1, source_target_pairs={{0,2},{1,3},{2,0},{3,1},{4,6},{5,7},{6,4},{7,5},{8,10},{9,11},{10,... | collective-permute-start | bytes 393224 | tf_op jit(solution)/shard_map/ppermute | solution.py:24
  20.6 9.5 %collective-permute-start.7 = (f32[128,256]{1,0:T(8,128)S(1)}, f32[128,256]{1,0:T(8,128)S(1)}, u32[]{:S(2)}, u32[]{:S(2)}) collective-permute-start(f32[128,256]{1,0:T(8,128)S(1)} %slice_add_fusion.6), channel_id=1, source_target_pairs={{0,4},{1,5},{2,6},{3,7},{4,0},{5,1},{6,2},{7,3},{8,12},{9,13},{10,... | collective-permute-start | bytes 393224 | tf_op jit(solution)/shard_map/ppermute | solution.py:24
  27.2 8.0 %collective-permute-start.4 = (f32[256,256]{1,0:T(8,128)S(1)}, f32[256,256]{1,0:T(8,128)S(1)}, u32[]{:S(2)}, u32[]{:S(2)}) collective-permute-start(f32[256,256]{1,0:T(8,128)S(1)} %pad_maximum_fusion.10), channel_id=1, source_target_pairs={{0,1},{1,0},{2,3},{3,2},{4,5},{5,4},{6,7},{7,6},{8,9},{9,8},{10,11... | collective-permute-start | bytes 786440 | tf_op jit(solution)/shard_map/ppermute | solution.py:24
  30.1 5.0 %collective-permute-start.8 = (f32[128,256]{1,0:T(8,128)S(1)}, f32[128,256]{1,0:T(8,128)S(1)}, u32[]{:S(2)}, u32[]{:S(2)}) collective-permute-start(f32[128,256]{1,0:T(8,128)S(1)} %add.108), channel_id=1, source_target_pairs={{0,2},{1,3},{2,0},{3,1},{4,6},{5,7},{6,4},{7,5},{8,10},{9,11},{10,... | collective-permute-start | bytes 393224 | tf_op jit(solution)/shard_map/ppermute | solution.py:24
  35.1 1.7 %collective-permute-start.9 = (f32[256,256]{1,0:T(8,128)S(1)}, f32[256,256]{1,0:T(8,128)S(1)}, u32[]{:S(2)}, u32[]{:S(2)}) collective-permute-start(f32[256,256]{1,0:T(8,128)S(1)} %pad_maximum_fusion.11), channel_id=1, source_target_pairs={{0,1},{1,0},{2,3},{3,2},{4,5},{5,4},{6,7},{7,6},{8,9},{9,8},{10,11... | collective-permute-start | bytes 786440 | tf_op jit(solution)/shard_map/ppermute | solution.py:24
  38.6 8.8 %collective-permute-start.12 = (f32[128,512]{1,0:T(8,128)S(1)}, f32[128,512]{1,0:T(8,128)S(1)}, u32[]{:S(2)}, u32[]{:S(2)}) collective-permute-start(f32[128,512]{1,0:T(8,128)S(1)} %get-tuple-element.26), channel_id=1, source_target_pairs={{0,16},{8,24},{16,0},{24,8},{1,17},{9,25},{17,1},{25,9},{2,18},{10... | collective-permute-start | bytes 786440 | tf_op jit(solution)/shard_map/ppermute | solution.py:24
  40.2 8.4 %collective-permute-start.10 = (f32[128,512]{1,0:T(8,128)S(1)}, f32[128,512]{1,0:T(8,128)S(1)}, u32[]{:S(2)}, u32[]{:S(2)}) collective-permute-start(f32[128,512]{1,0:T(8,128)S(1)} %get-tuple-element.27), channel_id=1, source_target_pairs={{0,8},{8,0},{16,24},{24,16},{1,9},{9,1},{17,25},{25,17},{2,10},{10... | collective-permute-start | bytes 786440 | tf_op jit(solution)/shard_map/ppermute | solution.py:24
  48.7 7.7 %collective-permute-start.13 = (f32[128,512]{1,0:T(8,128)S(1)}, f32[128,512]{1,0:T(8,128)S(1)}, u32[]{:S(2)}, u32[]{:S(2)}) collective-permute-start(f32[128,512]{1,0:T(8,128)S(1)} %get-tuple-element.24), channel_id=1, source_target_pairs={{0,8},{8,0},{16,24},{24,16},{1,9},{9,1},{17,25},{25,17},{2,10},{10... | collective-permute-start | bytes 786440 | tf_op jit(solution)/shard_map/ppermute | solution.py:24
  50.3 7.3 %collective-permute-start.11 = (f32[128,512]{1,0:T(8,128)S(1)}, f32[128,512]{1,0:T(8,128)S(1)}, u32[]{:S(2)}, u32[]{:S(2)}) collective-permute-start(f32[128,512]{1,0:T(8,128)S(1)} %get-tuple-element.25), channel_id=1, source_target_pairs={{0,16},{8,24},{16,0},{24,8},{1,17},{9,25},{17,1},{25,9},{2,18},{10... | collective-permute-start | bytes 786440 | tf_op jit(solution)/shard_map/ppermute | solution.py:24
  65.8 0.7 copy-start.1
  67.4 1.6 %collective-permute-start.19 = (f32[256,256]{1,0:T(8,128)S(1)}, f32[256,256]{1,0:T(8,128)S(1)}, u32[]{:S(2)}, u32[]{:S(2)}) collective-permute-start(f32[256,256]{1,0:T(8,128)S(1)} %slice.145), channel_id=1, source_target_pairs={{0,1},{1,0},{2,3},{3,2},{4,5},{5,4},{6,7},{7,6},{8,9},{9,8},{10,11... | collective-permute-start | bytes 786440 | tf_op jit(solution)/shard_map/ppermute | solution.py:24
  69.0 5.6 %collective-permute-start.20 = (f32[128,256]{1,0:T(8,128)S(1)}, f32[128,256]{1,0:T(8,128)S(1)}, u32[]{:S(2)}, u32[]{:S(2)}) collective-permute-start(f32[128,256]{1,0:T(8,128)S(1)} %slice.147), channel_id=1, source_target_pairs={{0,2},{1,3},{2,0},{3,1},{4,6},{5,7},{6,4},{7,5},{8,10},{9,11},{10,... | collective-permute-start | bytes 393224 | tf_op jit(solution)/shard_map/ppermute | solution.py:24
  69.8 6.1 %collective-permute-start.14 = (f32[256,256]{1,0:T(8,128)S(1)}, f32[256,256]{1,0:T(8,128)S(1)}, u32[]{:S(2)}, u32[]{:S(2)}) collective-permute-start(f32[256,256]{1,0:T(8,128)S(1)} %slice.140), channel_id=1, source_target_pairs={{0,1},{1,0},{2,3},{3,2},{4,5},{5,4},{6,7},{7,6},{8,9},{9,8},{10,11... | collective-permute-start | bytes 786440 | tf_op jit(solution)/shard_map/ppermute | solution.py:24
  74.7 8.3 %collective-permute-start.21 = (f32[128,256]{1,0:T(8,128)S(1)}, f32[128,256]{1,0:T(8,128)S(1)}, u32[]{:S(2)}, u32[]{:S(2)}) collective-permute-start(f32[128,256]{1,0:T(8,128)S(1)} %slice_add_fusion.4), channel_id=1, source_target_pairs={{0,4},{1,5},{2,6},{3,7},{4,0},{5,1},{6,2},{7,3},{8,12},{9,13},{10,... | collective-permute-start | bytes 393224 | tf_op jit(solution)/shard_map/ppermute | solution.py:24
  76.0 7.6 %collective-permute-start.15 = (f32[128,256]{1,0:T(8,128)S(1)}, f32[128,256]{1,0:T(8,128)S(1)}, u32[]{:S(2)}, u32[]{:S(2)}) collective-permute-start(f32[128,256]{1,0:T(8,128)S(1)} %slice.142), channel_id=1, source_target_pairs={{0,2},{1,3},{2,0},{3,1},{4,6},{5,7},{6,4},{7,5},{8,10},{9,11},{10,... | collective-permute-start | bytes 393224 | tf_op jit(solution)/shard_map/ppermute | solution.py:24
  83.0 7.6 %collective-permute-start.22 = (f32[128,256]{1,0:T(8,128)S(1)}, f32[128,256]{1,0:T(8,128)S(1)}, u32[]{:S(2)}, u32[]{:S(2)}) collective-permute-start(f32[128,256]{1,0:T(8,128)S(1)} %add.119), channel_id=1, source_target_pairs={{0,2},{1,3},{2,0},{3,1},{4,6},{5,7},{6,4},{7,5},{8,10},{9,11},{10,... | collective-permute-start | bytes 393224 | tf_op jit(solution)/shard_map/ppermute | solution.py:24
  83.6 8.9 %collective-permute-start.16 = (f32[128,256]{1,0:T(8,128)S(1)}, f32[128,256]{1,0:T(8,128)S(1)}, u32[]{:S(2)}, u32[]{:S(2)}) collective-permute-start(f32[128,256]{1,0:T(8,128)S(1)} %slice_add_fusion.5), channel_id=1, source_target_pairs={{0,4},{1,5},{2,6},{3,7},{4,0},{5,1},{6,2},{7,3},{8,12},{9,13},{10,... | collective-permute-start | bytes 393224 | tf_op jit(solution)/shard_map/ppermute | solution.py:24
  90.6 7.0 %collective-permute-start.23 = (f32[256,256]{1,0:T(8,128)S(1)}, f32[256,256]{1,0:T(8,128)S(1)}, u32[]{:S(2)}, u32[]{:S(2)}) collective-permute-start(f32[256,256]{1,0:T(8,128)S(1)} %pad_maximum_fusion.13), channel_id=1, source_target_pairs={{0,1},{1,0},{2,3},{3,2},{4,5},{5,4},{6,7},{7,6},{8,9},{9,8},{10,11... | collective-permute-start | bytes 786440 | tf_op jit(solution)/shard_map/ppermute | solution.py:24
  92.5 5.0 %collective-permute-start.17 = (f32[128,256]{1,0:T(8,128)S(1)}, f32[128,256]{1,0:T(8,128)S(1)}, u32[]{:S(2)}, u32[]{:S(2)}) collective-permute-start(f32[128,256]{1,0:T(8,128)S(1)} %add.116), channel_id=1, source_target_pairs={{0,2},{1,3},{2,0},{3,1},{4,6},{5,7},{6,4},{7,5},{8,10},{9,11},{10,... | collective-permute-start | bytes 393224 | tf_op jit(solution)/shard_map/ppermute | solution.py:24
  97.5 1.7 %collective-permute-start.18 = (f32[256,256]{1,0:T(8,128)S(1)}, f32[256,256]{1,0:T(8,128)S(1)}, u32[]{:S(2)}, u32[]{:S(2)}) collective-permute-start(f32[256,256]{1,0:T(8,128)S(1)} %pad_maximum_fusion.12), channel_id=1, source_target_pairs={{0,1},{1,0},{2,3},{3,2},{4,5},{5,4},{6,7},{7,6},{8,9},{9,8},{10,11... | collective-permute-start | bytes 786440 | tf_op jit(solution)/shard_map/ppermute | solution.py:24
  101.0 8.8 %collective-permute-start.26 = (f32[128,512]{1,0:T(8,128)S(1)}, f32[128,512]{1,0:T(8,128)S(1)}, u32[]{:S(2)}, u32[]{:S(2)}) collective-permute-start(f32[128,512]{1,0:T(8,128)S(1)} %get-tuple-element.20), channel_id=1, source_target_pairs={{0,16},{8,24},{16,0},{24,8},{1,17},{9,25},{17,1},{25,9},{2,18},{10... | collective-permute-start | bytes 786440 | tf_op jit(solution)/shard_map/ppermute | solution.py:24
  101.7 8.4 %collective-permute-start.24 = (f32[128,512]{1,0:T(8,128)S(1)}, f32[128,512]{1,0:T(8,128)S(1)}, u32[]{:S(2)}, u32[]{:S(2)}) collective-permute-start(f32[128,512]{1,0:T(8,128)S(1)} %get-tuple-element.21), channel_id=1, source_target_pairs={{0,8},{8,0},{16,24},{24,16},{1,9},{9,1},{17,25},{25,17},{2,10},{10... | collective-permute-start | bytes 786440 | tf_op jit(solution)/shard_map/ppermute | solution.py:24
  110.2 7.7 %collective-permute-start.27 = (f32[128,512]{1,0:T(8,128)S(1)}, f32[128,512]{1,0:T(8,128)S(1)}, u32[]{:S(2)}, u32[]{:S(2)}) collective-permute-start(f32[128,512]{1,0:T(8,128)S(1)} %get-tuple-element.18), channel_id=1, source_target_pairs={{0,8},{8,0},{16,24},{24,16},{1,9},{9,1},{17,25},{25,17},{2,10},{10... | collective-permute-start | bytes 786440 | tf_op jit(solution)/shard_map/ppermute | solution.py:24
  110.8 7.3 %collective-permute-start.25 = (f32[128,512]{1,0:T(8,128)S(1)}, f32[128,512]{1,0:T(8,128)S(1)}, u32[]{:S(2)}, u32[]{:S(2)}) collective-permute-start(f32[128,512]{1,0:T(8,128)S(1)} %get-tuple-element.19), channel_id=1, source_target_pairs={{0,16},{8,24},{16,0},{24,8},{1,17},{9,25},{17,1},{25,9},{2,18},{10... | collective-permute-start | bytes 786440 | tf_op jit(solution)/shard_map/ppermute | solution.py:24

commit v2 on v1

v2 whole, which is shorter than its diff:
```python
import functools
import jax
import jax.numpy as jnp
from jax import lax
from jax.experimental import pallas as pl
from jax.experimental.pallas import tpu as pltpu
from jax.sharding import PartitionSpec as P

ITERS = 2
CHUNKS = 4
VMEM_BYTES = 28 << 20

NN = (((1,), (0,)), ((), ()))
NT = (((1,), (1,)), ((), ()))
TN = (((0,), (0,)), ((), ()))
f32, bf16 = jnp.float32, jnp.bfloat16


def split(x, terms):
    out = []
    for _ in range(terms):
        out.append(x.astype(bf16))
        x = x - out[-1].astype(f32)
    return out


def dot(a, b, dims=NN):
    return lax.dot_general(a, b, dims, preferred_element_type=f32)


def dot3(a, b, dims=NN):
    return dot(a[0], b[0], dims) + (dot(a[0], b[1], dims) + dot(a[1], b[0], dims))


def dot6(a, b):
    small = dot(a[0], b[2]) + dot(a[1], b[1]) + dot(a[2], b[0])
    return dot(a[0], b[0]) + (dot(a[0], b[1]) + dot(a[1], b[0]) + small)


def swap(x, axis, size, bit):
    return lax.ppermute(x, axis, [(i, i ^ bit) for i in range(size)])


def bits_of(size):
    return [1 << b for b in range(size.bit_length() - 1)]


def sum_tm(chunks, size):
    first, *middle, last = bits_of(size)
    chunks = [kept + swap(sent, "tm", size, first) for kept, sent in chunks]
    for bit in middle:
        for i, x in enumerate(chunks):
            half = x.shape[0] // 2
            chunks[i] = x[:half] + swap(x[half:], "tm", size, bit)
    pieces = []
    for x in chunks:
        x = x + swap(x, "tm", size, last)
        parts = [x]
        for bit in reversed(middle):
            x = parts[0] if len(parts) == 1 else jnp.concatenate(parts, 0)
            parts.append(swap(x, "tm", size, bit))
        pieces.append(parts + [swap(x, "tm", size, first) for x in parts])
    return pieces


def sum_rows(a, b, size):
    bits = bits_of(size)
    turn = len(bits) // 2
    pair_a, pair_b = None, None
    for bit_a, bit_b in zip(bits, bits[turn:] + bits[:turn]):
        a = a if pair_a is None else pair_a[0] + pair_a[1]
        b = b if pair_b is None else pair_b[0] + pair_b[1]
        pair_a, pair_b = (a, swap(a, "rows", size, bit_a)), (b, swap(b, "rows", size, bit_b))
    return pair_a + pair_b


def lowest(blocks):
    me = lax.axis_index("tm")
    low = 0
    for b in range(blocks.bit_length() - 1):
        low = low * 2 + lax.rem(me >> b, 2)
    return low


def write_left(left, out_refs, blocks):
    tall = left[0].shape[0]
    share = tall // CHUNKS
    for p in range(blocks):
        for c in range(CHUNKS):
            at = p % (blocks // 2) * share
            out_refs[2 * c + p // (blocks // 2)][pl.ds(at, share), :] = left[p][c * share : (c + 1) * share]


def head_kernel(blocks, snap_ref, basis_ref, data_ref, top_ref, rest_ref, *more):
    *left_refs, sems = more
    tall = data_ref.shape[0] // blocks
    low = lowest(blocks)
    copies = []
    for p in range(blocks):
        copies.append(
            pltpu.make_async_copy(
                snap_ref.at[pl.ds(pl.multiple_of((p ^ low) * tall, tall), tall), :],
                data_ref.at[pl.ds(p * tall, tall), :],
                sems.at[p],
            )
        )
        copies[-1].start()
    basis = split(basis_ref[...], 2)
    left = []
    for p in range(blocks):
        copies[p].wait()
        block = split(data_ref[pl.ds(p * tall, tall), :], 2)
        top_ref[pl.ds(p * tall, tall), :], rest_ref[pl.ds(p * tall, tall), :] = block
        left.append(dot3(block, basis))
    write_left(left, left_refs, blocks)


def product_kernel(blocks, counts, top_ref, rest_ref, *more):
    left_refs, (a_ref, b_ref, left_top_ref, left_rest_ref) = more[:-4], more[-4:]
    rows, rank = left_top_ref.shape
    tall = rows // blocks
    share = tall // CHUNKS
    at = 0
    for c in range(CHUNKS):
        p = 0
        for ref in left_refs[at : at + counts[c]]:
            terms = split(ref[...], 2)
            for k in range(ref.shape[0] // share):
                for out_ref, term in zip((left_top_ref, left_rest_ref), terms):
                    out_ref[pl.ds(p * tall + c * share, share), :] = term[k * share : (k + 1) * share]
                p += 1
        at += counts[c]
    left = left_top_ref[...], left_rest_ref[...]
    right = dot3(left, (top_ref[...], rest_ref[...]), TN)
    cross = dot(left[0], left[1], TN)
    gram = dot(left[0], left[0], TN) + (cross + cross.T)
    half = rank // 2
    a_ref[:, : right.shape[1]] = right[:half]
    b_ref[:, : right.shape[1]] = right[half:]
    a_ref[:, right.shape[1] :] = gram[:half]
    b_ref[:, right.shape[1] :] = gram[half:]


def solve(gram, right):
    n = gram.shape[0]
    eye = (
        lax.broadcasted_iota(jnp.int32, (n, n), 0) == lax.broadcasted_iota(jnp.int32, (n, n), 1)
    ).astype(f32)
    on_diag = gram * eye
    down = lax.rsqrt(jnp.sum(on_diag, 1, keepdims=True))
    across = lax.rsqrt(jnp.sum(on_diag, 0, keepdims=True))
    scaled = gram * down * across
    bound = jnp.minimum(
        jnp.max(jnp.sum(jnp.abs(scaled), 0, keepdims=True)),
        jnp.sqrt(jnp.sum(scaled * scaled)),
    )
    step = 1.9 / bound
    error = eye - step * scaled
    inverse = step * eye

    def more(state):
        count, size, _, _ = state
        return jnp.logical_and(count < 40, size > 1e-4)

    def double(state):
        count, _, inverse, error = state
        size = jnp.sum(error * error)
        terms = split(error, 2)
        return count + 1, size, inverse + dot3(split(inverse, 2), terms), dot3(terms, terms)

    _, _, inverse, _ = lax.while_loop(more, double, (0, jnp.float32(1.0), inverse, error))
    exact = split(scaled, 3)

    def again(state):
        count, size, _ = state
        return jnp.logical_and(count < 20, size > 1e-6)

    def refine(state):
        count, _, inverse = state
        rest = eye - dot6(exact, split(inverse, 3))
        return count + 1, jnp.sum(rest * rest), inverse + dot3(split(inverse, 2), split(rest, 2))

    _, _, inverse = lax.while_loop(again, refine, (0, jnp.float32(1.0), inverse))
    return down * dot6(split(inverse, 3), split(down * right, 3))


def weights_of(sum_refs, cols):
    a = sum_refs[0][...] + sum_refs[1][...]
    b = sum_refs[2][...] + sum_refs[3][...]
    both = jnp.concatenate([a, b], 0)
    return solve(both[:, cols:], both[:, :cols])


def shrink(data, low_rank, level):
    difference = data - low_rank
    size = jnp.maximum(jnp.abs(difference) - level, 0.0)
    return jnp.where(difference < 0, -size, size)


def middle_kernel(blocks, *refs):
    sum_refs, refs = refs[:4], refs[4:]
    left_top_ref, left_rest_ref, data_ref, level_ref, top_ref, rest_ref, *left_refs = refs
    tall = data_ref.shape[0] // blocks
    weights = split(weights_of(sum_refs, data_ref.shape[1]), 2)
    left = []
    for p in range(blocks):
        at = pl.ds(p * tall, tall)
        low_rank = dot3((left_top_ref[at, :], left_rest_ref[at, :]), weights)
        data = data_ref[at, :]
        residual = split(data - shrink(data, low_rank, level_ref[...]), 2)
        top_ref[at, :], rest_ref[at, :] = residual
        left.append(dot3(residual, weights, NT))
    write_left(left, left_refs, blocks)


def last_kernel(blocks, *refs):
    sum_refs, refs = refs[:4], refs[4:]
    left_top_ref, left_rest_ref, data_ref, level_ref, low_rank_ref, sparse_ref, low_rank, sparse, sems = refs
    tall = data_ref.shape[0] // blocks
    low = lowest(blocks)
    weights = split(weights_of(sum_refs, data_ref.shape[1]), 2)
    copies = []
    for p in range(blocks):
        at = pl.ds(p * tall, tall)
        low_rank[at, :] = dot3((left_top_ref[at, :], left_rest_ref[at, :]), weights)
        sparse[at, :] = shrink(data_ref[at, :], low_rank[at, :], level_ref[...])
        to = pl.ds(pl.multiple_of((p ^ low) * tall, tall), tall)
        for k, (source, target) in enumerate(((low_rank, low_rank_ref), (sparse, sparse_ref))):
            copies.append(pltpu.make_async_copy(source.at[at, :], target.at[to, :], sems.at[2 * p + k]))
            copies[-1].start()
    for copy in copies:
        copy.wait()


VMEM = pl.BlockSpec(memory_space=pltpu.VMEM)
ANY = pl.BlockSpec(memory_space=pl.ANY)


def call(body, args, outs, in_specs=None, out_specs=None, scratch=(), name=None):
    return pl.pallas_call(
        body,
        out_shape=[jax.ShapeDtypeStruct(shape, dtype) for shape, dtype in outs],
        in_specs=in_specs or [VMEM] * len(args),
        out_specs=out_specs or [VMEM] * len(outs),
        scratch_shapes=list(scratch),
        compiler_params=pltpu.CompilerParams(vmem_limit_bytes=VMEM_BYTES),
        name=name,
    )(*args)


def per_device(n_tm, n_rows, snapshots, right_basis, threshold):
    rows, cols = snapshots.shape
    rank = right_basis.shape[1]
    blocks = n_tm // 2
    level = threshold[None, :]
    whole = [((rows, cols), bf16)] * 2
    lefts = [((rows // CHUNKS // 2, rank), f32)] * (2 * CHUNKS)
    data, top, rest, *left = call(
        functools.partial(head_kernel, blocks),
        (snapshots, right_basis),
        [((rows, cols), f32)] + whole + lefts,
        in_specs=[ANY, VMEM],
        scratch=[pltpu.SemaphoreType.DMA((blocks,))],
        name="head",
    )
    for iteration in range(ITERS):
        pieces = sum_tm(list(zip(left[::2], left[1::2])), n_tm)
        a, b, left_top, left_rest = call(
            functools.partial(product_kernel, blocks, [len(x) for x in pieces]),
            (top, rest, *[x for parts in pieces for x in parts]),
            [((rank // 2, cols + rank), f32)] * 2 + [((rows, rank), bf16)] * 2,
            name="products",
        )
        args = (*sum_rows(a, b, n_rows), left_top, left_rest, data, level)
        if iteration < ITERS - 1:
            top, rest, *left = call(
                functools.partial(middle_kernel, blocks), args, whole + lefts, name="middle"
            )
    return call(
        functools.partial(last_kernel, blocks),
        args,
        [((rows, cols), f32)] * 2,
        out_specs=[ANY] * 2,
        scratch=[pltpu.VMEM((rows, cols), f32)] * 2 + [pltpu.SemaphoreType.DMA((2 * blocks,))],
        name="last",
    )


def solution(mesh):
    return jax.shard_map(
        functools.partial(per_device, mesh.shape["tm"], mesh.shape["rows"]),
        mesh=mesh,
        in_specs=(P("rows", "tm"), P("tm", None), P("tm")),
        out_specs=(P("rows", "tm"), P("rows", "tm")),
        check_vma=False,
    )
```

time: 130 us -> 120 us (0.923)
  waiting for transfers between devices: 69.7 us -> 46.3 us
  starting transfers between devices: 27.6 us -> 45.9 us
  matrix products: 9.56 us -> 0 us
  Pallas kernels: 15.7 us -> 23.1 us
  other arithmetic: 3.96 us -> 0.45 us
    ppermute x28 -> x56, waiting for transfers between devices: 69.7 us -> 46.3 us  [swap(): return lax.ppermute(x, axis, [(i, i ^ bit) for i in range(size)])]
    ppermute x28 -> x56, starting transfers between devices: 27.6 us -> 45.9 us  [swap(): return lax.ppermute(x, axis, [(i, i ^ bit) for i in range(size)])]
    dot_general x16 -> x0, matrix products: 9.56 us -> none  [mm(): lax.dot_general(a, b, dims, precision=precision, preferred_element_type=j...]
    pallas_call x2 -> x5, Pallas kernels: 15.7 us -> 23.1 us  [call(): pl.pallas_call(body, out_shape=[jax.ShapeDtypeStruct(shape, dtype) for sh...]
    unnamed x4 -> x6, local copies, waits for them, and re-layouts: 0.3 us -> 2.85 us
    concatenate x10 -> x0, other arithmetic: 2.36 us -> none  [the longest x3 2.15 us: reorder(): return jnp.concatenate(parts, 1).reshape(rows, cols)]
    dynamic_slice x2 -> x0, local copies, waits for them, and re-layouts: 1.5 us -> none  [reorder(): parts = [lax.dynamic_slice_in_dim(cut, p ^ me, 1, 1) for p in range(blocks)]]
  transfers between devices with their start and end apart: 28 -> 56, of which waited for: 21 -> 26; matrix products, arithmetic and copies ran while one was open for 3% -> 0% of each run, Pallas kernels for 0% -> 0%
where the time goes in v2:
time: 120 us
  waiting for transfers between devices  46.3 us (39%)
  starting transfers between devices  45.9 us (38%)
  Pallas kernels  23.1 us (19%)
  local copies, waits for them, and re-layouts  2.9 us (2%)
    ppermute x56, waiting for transfers between devices, swap(): return lax.ppermute(x, axis, [(i, i ^ bit) for i in range(size)])  46.3 us
    ppermute x56, starting transfers between devices, swap(): return lax.ppermute(x, axis, [(i, i ^ bit) for i in range(size)])  45.9 us
    pallas_call x5, Pallas kernels, call(): pl.pallas_call(body, out_shape=[jax.ShapeDtypeStruct(shape, dtype) for sh...  23.1 us
    unnamed x6, local copies, waits for them, and re-layouts  2.85 us
  transfers between devices with their start and end apart: 56, of which 26 were waited for; matrix products, arithmetic and copies ran while one was open for 0% of the time, Pallas kernels for 0%

profile of v2, /device:TPU:0, one launch (start us, length us, event | category | flops | bytes accessed | tf_op | source)
XLA Modules:
  0.0 119.6 jit_solution(1858397181336579302)
XLA Ops:
  0.6 1.2 %copy-done = f32[1024,256]{1,0:T(8,128)S(1)} copy-done((f32[1024,256]{1,0:T(8,128)S(1)}, f32[1024,256]{1,0:T(8,128)}, u32[]{:S(2)}) %copy-start) | copy-done | bytes 1048600
  1.9 0.9 copy-done.1
  2.8 1.6 %head.1 = (f32[1024,256]{1,0:T(8,128)S(1)}, bf16[1024,256]{1,0:T(8,128)(2,1)S(1)}, bf16[1024,256]{1,0:T(8,128)(2,1)S(1)}, f32[128,256]{1,0:T(8,128)S(1)}, f32[12...) custom-call(f32[1024,256]{1,0:T(8,128)S(1)} %copy-done, ...), custom_call_target="tpu_custom_call" | custom-call | tf_op jit(solution)/shard_map/head/pallas_call | solution.py:240
  6.0 3.0 %collective-permute-start.1 = (f32[64,256]{1,0:T(8,128)S(1)}, f32[64,256]{1,0:T(8,128)S(1)}, u32[]{:S(2)}, u32[]{:S(2)}) collective-permute-start(f32[64,256]{1,0:T(8,128)S(1)} %slice.65), channel_id=1, source_target_pairs={{0,2},{1,3},{2,0},{3,1},{4,6},{5,7},{6,4},{7,5},{8,10},{9,11},{10,... | collective-permute-start | bytes 196616 | tf_op jit(solution)/shard_map/ppermute | solution.py:41
  9.2 2.0 %collective-permute-start.13 = (f32[64,256]{1,0:T(8,128)S(1)}, f32[64,256]{1,0:T(8,128)S(1)}, u32[]{:S(2)}, u32[]{:S(2)}) collective-permute-start(f32[64,256]{1,0:T(8,128)S(1)} %slice.69), channel_id=1, source_target_pairs={{0,2},{1,3},{2,0},{3,1},{4,6},{5,7},{6,4},{7,5},{8,10},{9,11},{10,... | collective-permute-start | bytes 196616 | tf_op jit(solution)/shard_map/ppermute | solution.py:41
  11.4 3.1 %collective-permute-start.2 = (f32[64,256]{1,0:T(8,128)S(1)}, f32[64,256]{1,0:T(8,128)S(1)}, u32[]{:S(2)}, u32[]{:S(2)}) collective-permute-start(f32[64,256]{1,0:T(8,128)S(1)} %slice_add_fusion.7), channel_id=1, source_target_pairs={{0,4},{1,5},{2,6},{3,7},{4,0},{5,1},{6,2},{7,3},{8,12},{9,13},{10,... | collective-permute-start | bytes 196616 | tf_op jit(solution)/shard_map/ppermute | solution.py:41
  14.5 2.2 %collective-permute-start.8 = (f32[64,256]{1,0:T(8,128)S(1)}, f32[64,256]{1,0:T(8,128)S(1)}, u32[]{:S(2)}, u32[]{:S(2)}) collective-permute-start(f32[64,256]{1,0:T(8,128)S(1)} %slice_add_fusion.6), channel_id=1, source_target_pairs={{0,4},{1,5},{2,6},{3,7},{4,0},{5,1},{6,2},{7,3},{8,12},{9,13},{10,... | collective-permute-start | bytes 196616 | tf_op jit(solution)/shard_map/ppermute | solution.py:41
  16.7 1.4 %collective-permute-start.14 = (f32[64,256]{1,0:T(8,128)S(1)}, f32[64,256]{1,0:T(8,128)S(1)}, u32[]{:S(2)}, u32[]{:S(2)}) collective-permute-start(f32[64,256]{1,0:T(8,128)S(1)} %slice_add_fusion.5), channel_id=1, source_target_pairs={{0,4},{1,5},{2,6},{3,7},{4,0},{5,1},{6,2},{7,3},{8,12},{9,13},{10,... | collective-permute-start | bytes 196616 | tf_op jit(solution)/shard_map/ppermute | solution.py:41
  18.1 1.7 %collective-permute-start.20 = (f32[64,256]{1,0:T(8,128)S(1)}, f32[64,256]{1,0:T(8,128)S(1)}, u32[]{:S(2)}, u32[]{:S(2)}) collective-permute-start(f32[64,256]{1,0:T(8,128)S(1)} %slice_add_fusion.4), channel_id=1, source_target_pairs={{0,4},{1,5},{2,6},{3,7},{4,0},{5,1},{6,2},{7,3},{8,12},{9,13},{10,... | collective-permute-start | bytes 196616 | tf_op jit(solution)/shard_map/ppermute | solution.py:41
  19.9 2.8 %collective-permute-start.3 = (f32[64,256]{1,0:T(8,128)S(1)}, f32[64,256]{1,0:T(8,128)S(1)}, u32[]{:S(2)}, u32[]{:S(2)}) collective-permute-start(f32[64,256]{1,0:T(8,128)S(1)} %add.86.more_0_), channel_id=1, source_target_pairs={{0,2},{1,3},{2,0},{3,1},{4,6},{5,7},{6,4},{7,5},{8,10},{9,11},{10,... | collective-permute-start | bytes 196616 | tf_op jit(solution)/shard_map/ppermute | solution.py:41
  22.7 2.4 %collective-permute-done.8 = f32[64,256]{1,0:T(8,128)S(1)} collective-permute-done((f32[64,256]{1,0:T(8,128)S(1)}, f32[64,256]{1,0:T(8,128)S(1)}, u32[]{:S(2)}, u32[]{:S(2)}) %collective-permute-start.8) | collective-permute-done | bytes 65568 | tf_op jit(solution)/shard_map/ppermute | solution.py:41
  26.8 1.5 %collective-permute-start.15 = (f32[64,256]{1,0:T(8,128)S(1)}, f32[64,256]{1,0:T(8,128)S(1)}, u32[]{:S(2)}, u32[]{:S(2)}) collective-permute-start(f32[64,256]{1,0:T(8,128)S(1)} %add.92.more_8_), channel_id=1, source_target_pairs={{0,2},{1,3},{2,0},{3,1},{4,6},{5,7},{6,4},{7,5},{8,10},{9,11},{10,... | collective-permute-start | bytes 196616 | tf_op jit(solution)/shard_map/ppermute | solution.py:41
  28.9 1.8 %collective-permute-done.9.more_5_ = f32[64,256]{1,0:T(8,128)S(1)} collective-permute-done((f32[64,256]{1,0:T(8,128)S(1)}, f32[64,256]{1,0:T(8,128)S(1)}, u32[]{:S(2)}, u32[]{:S(2)}) %collective-permute-start.9) | collective-permute-done | bytes 65568 | tf_op jit(solution)/shard_map/ppermute | solution.py:41
  32.1 1.0 collective-permute-done.21.more_13_
  33.4 1.0 collective-permute-done.23.more_15_
  34.4 0.9 products.2
  35.4 1.8 %collective-permute-start.24 = (f32[128,512]{1,0:T(8,128)S(1)}, f32[128,512]{1,0:T(8,128)S(1)}, u32[]{:S(2)}, u32[]{:S(2)}) collective-permute-start(f32[128,512]{1,0:T(8,128)S(1)} %get-tuple-element.41), channel_id=1, source_target_pairs={{0,8},{8,0},{16,24},{24,16},{1,9},{9,1},{17,25},{25,17},{2,10},{10... | collective-permute-start | bytes 786440 | tf_op jit(solution)/shard_map/ppermute | solution.py:41
  37.2 1.5 %collective-permute-start.26 = (f32[128,512]{1,0:T(8,128)S(1)}, f32[128,512]{1,0:T(8,128)S(1)}, u32[]{:S(2)}, u32[]{:S(2)}) collective-permute-start(f32[128,512]{1,0:T(8,128)S(1)} %get-tuple-element.42), channel_id=1, source_target_pairs={{0,16},{8,24},{16,0},{24,8},{1,17},{9,25},{17,1},{25,9},{2,18},{10... | collective-permute-start | bytes 786440 | tf_op jit(solution)/shard_map/ppermute | solution.py:41
  38.7 5.1 %collective-permute-done.24 = f32[128,512]{1,0:T(8,128)S(1)} collective-permute-done((f32[128,512]{1,0:T(8,128)S(1)}, f32[128,512]{1,0:T(8,128)S(1)}, u32[]{:S(2)}, u32[]{:S(2)}) %collective-permute-start.24) | collective-permute-done | bytes 262176 | tf_op jit(solution)/shard_map/ppermute | solution.py:41
  43.8 1.8 %collective-permute-start.25 = (f32[128,512]{1,0:T(8,128)S(1)}, f32[128,512]{1,0:T(8,128)S(1)}, u32[]{:S(2)}, u32[]{:S(2)}) collective-permute-start(f32[128,512]{1,0:T(8,128)S(1)} %add.96.refs_0_), channel_id=1, source_target_pairs={{0,16},{8,24},{16,0},{24,8},{1,17},{9,25},{17,1},{25,9},{2,18},{10... | collective-permute-start | bytes 786440 | tf_op jit(solution)/shard_map/ppermute | solution.py:41
  45.7 1.6 %collective-permute-start.27 = (f32[128,512]{1,0:T(8,128)S(1)}, f32[128,512]{1,0:T(8,128)S(1)}, u32[]{:S(2)}, u32[]{:S(2)}) collective-permute-start(f32[128,512]{1,0:T(8,128)S(1)} %add.97.refs_2_), channel_id=1, source_target_pairs={{0,8},{8,0},{16,24},{24,16},{1,9},{9,1},{17,25},{25,17},{2,10},{10... | collective-permute-start | bytes 786440 | tf_op jit(solution)/shard_map/ppermute | solution.py:41
  47.3 4.2 %collective-permute-done.25.refs_1_ = f32[128,512]{1,0:T(8,128)S(1)} collective-permute-done((f32[128,512]{1,0:T(8,128)S(1)}, f32[128,512]{1,0:T(8,128)S(1)}, u32[]{:S(2)}, u32[]{:S(2)}) %collective-permute-start.25) | collective-permute-done | bytes 262176 | tf_op jit(solution)/shard_map/ppermute | solution.py:41
  51.5 1.6 %collective-permute-done.27.refs_3_ = f32[128,512]{1,0:T(8,128)S(1)} collective-permute-done((f32[128,512]{1,0:T(8,128)S(1)}, f32[128,512]{1,0:T(8,128)S(1)}, u32[]{:S(2)}, u32[]{:S(2)}) %collective-permute-start.27) | collective-permute-done | bytes 262176 | tf_op jit(solution)/shard_map/ppermute | solution.py:41
  53.7 9.1 %middle.1 = (bf16[1024,256]{1,0:T(8,128)(2,1)S(1)}, bf16[1024,256]{1,0:T(8,128)(2,1)S(1)}, f32[128,256]{1,0:T(8,128)S(1)}, f32[128,256]{1,0:T(8,128)S(1)}, f32[1...) custom-call(f32[128,512]{1,0:T(8,128)S(1)} %add.96.refs_0_, ...), custom_call_target="tpu_custom_call" | custom-call | tf_op jit(solution)/shard_map/middle/pallas_call | solution.py:240
  64.3 1.1 collective-permute-start.29
  65.4 1.1 collective-permute-start.35
  66.5 1.1 collective-permute-start.41
  67.7 1.1 collective-permute-start.47
  69.3 2.1 %collective-permute-start.30 = (f32[64,256]{1,0:T(8,128)S(1)}, f32[64,256]{1,0:T(8,128)S(1)}, u32[]{:S(2)}, u32[]{:S(2)}) collective-permute-start(f32[64,256]{1,0:T(8,128)S(1)} %slice_add_fusion.3), channel_id=1, source_target_pairs={{0,4},{1,5},{2,6},{3,7},{4,0},{5,1},{6,2},{7,3},{8,12},{9,13},{10,... | collective-permute-start | bytes 196616 | tf_op jit(solution)/shard_map/ppermute | solution.py:41
  71.4 1.4 %collective-permute-start.36 = (f32[64,256]{1,0:T(8,128)S(1)}, f32[64,256]{1,0:T(8,128)S(1)}, u32[]{:S(2)}, u32[]{:S(2)}) collective-permute-start(f32[64,256]{1,0:T(8,128)S(1)} %slice_add_fusion.2), channel_id=1, source_target_pairs={{0,4},{1,5},{2,6},{3,7},{4,0},{5,1},{6,2},{7,3},{8,12},{9,13},{10,... | collective-permute-start | bytes 196616 | tf_op jit(solution)/shard_map/ppermute | solution.py:41
  72.8 1.7 %collective-permute-start.42 = (f32[64,256]{1,0:T(8,128)S(1)}, f32[64,256]{1,0:T(8,128)S(1)}, u32[]{:S(2)}, u32[]{:S(2)}) collective-permute-start(f32[64,256]{1,0:T(8,128)S(1)} %slice_add_fusion.1), channel_id=1, source_target_pairs={{0,4},{1,5},{2,6},{3,7},{4,0},{5,1},{6,2},{7,3},{8,12},{9,13},{10,... | collective-permute-start | bytes 196616 | tf_op jit(solution)/shard_map/ppermute | solution.py:41
  74.5 1.4 %collective-permute-start.48 = (f32[64,256]{1,0:T(8,128)S(1)}, f32[64,256]{1,0:T(8,128)S(1)}, u32[]{:S(2)}, u32[]{:S(2)}) collective-permute-start(f32[64,256]{1,0:T(8,128)S(1)} %slice_add_fusion), channel_id=1, source_target_pairs={{0,4},{1,5},{2,6},{3,7},{4,0},{5,1},{6,2},{7,3},{8,12},{9,13},{10,... | collective-permute-start | bytes 196616 | tf_op jit(solution)/shard_map/ppermute | solution.py:41
  75.9 3.9 %collective-permute-done.30 = f32[64,256]{1,0:T(8,128)S(1)} collective-permute-done((f32[64,256]{1,0:T(8,128)S(1)}, f32[64,256]{1,0:T(8,128)S(1)}, u32[]{:S(2)}, u32[]{:S(2)}) %collective-permute-start.30) | collective-permute-done | bytes 65568 | tf_op jit(solution)/shard_map/ppermute | solution.py:41
  80.0 1.9 %collective-permute-done.36 = f32[64,256]{1,0:T(8,128)S(1)} collective-permute-done((f32[64,256]{1,0:T(8,128)S(1)}, f32[64,256]{1,0:T(8,128)S(1)}, u32[]{:S(2)}, u32[]{:S(2)}) %collective-permute-start.36) | collective-permute-done | bytes 65568 | tf_op jit(solution)/shard_map/ppermute | solution.py:41
  82.0 0.9 collective-permute-done.42
  83.7 1.4 %collective-permute-start.43 = (f32[64,256]{1,0:T(8,128)S(1)}, f32[64,256]{1,0:T(8,128)S(1)}, u32[]{:S(2)}, u32[]{:S(2)}) collective-permute-start(f32[64,256]{1,0:T(8,128)S(1)} %add.106.more_8_), channel_id=1, source_target_pairs={{0,2},{1,3},{2,0},{3,1},{4,6},{5,7},{6,4},{7,5},{8,10},{9,11},{10,... | collective-permute-start | bytes 196616 | tf_op jit(solution)/shard_map/ppermute | solution.py:41
  85.8 1.7 %collective-permute-done.37.more_5_ = f32[64,256]{1,0:T(8,128)S(1)} collective-permute-done((f32[64,256]{1,0:T(8,128)S(1)}, f32[64,256]{1,0:T(8,128)S(1)}, u32[]{:S(2)}, u32[]{:S(2)}) %collective-permute-start.37) | collective-permute-done | bytes 65568 | tf_op jit(solution)/shard_map/ppermute | solution.py:41
  88.1 0.9 collective-permute-done.43.more_9_
  89.0 1.0 collective-permute-done.49.more_13_
  90.3 1.0 collective-permute-done.51.more_15_
  91.3 1.0 products.3
  92.2 1.6 %collective-permute-start.52 = (f32[128,512]{1,0:T(8,128)S(1)}, f32[128,512]{1,0:T(8,128)S(1)}, u32[]{:S(2)}, u32[]{:S(2)}) collective-permute-start(f32[128,512]{1,0:T(8,128)S(1)} %get-tuple-element.56), channel_id=1, source_target_pairs={{0,8},{8,0},{16,24},{24,16},{1,9},{9,1},{17,25},{25,17},{2,10},{10... | collective-permute-start | bytes 786440 | tf_op jit(solution)/shard_map/ppermute | solution.py:41
  94.3 6.4 %collective-permute-done.52 = f32[128,512]{1,0:T(8,128)S(1)} collective-permute-done((f32[128,512]{1,0:T(8,128)S(1)}, f32[128,512]{1,0:T(8,128)S(1)}, u32[]{:S(2)}, u32[]{:S(2)}) %collective-permute-start.52) | collective-permute-done | bytes 262176 | tf_op jit(solution)/shard_map/ppermute | solution.py:41
  100.7 1.1 collective-permute-start.53
  101.9 1.0 collective-permute-start.55
  102.9 5.4 %collective-permute-done.53.refs_1_ = f32[128,512]{1,0:T(8,128)S(1)} collective-permute-done((f32[128,512]{1,0:T(8,128)S(1)}, f32[128,512]{1,0:T(8,128)S(1)}, u32[]{:S(2)}, u32[]{:S(2)}) %collective-permute-start.53) | collective-permute-done | bytes 262176 | tf_op jit(solution)/shard_map/ppermute | solution.py:41
  108.3 0.9 collective-permute-done.55.refs_3_
  109.2 10.4 %last.1 = (f32[1024,256]{1,0:T(8,128)}, f32[1024,256]{1,0:T(8,128)}) custom-call(f32[128,512]{1,0:T(8,128)S(1)} %add.110.refs_0_, f32[128,512]{1,0:T(8,128)S(1)} %collective-permute-done.53.refs_1_, f32[128,512]{1,0:T(8,128)S(1)} %add.111.refs_2_, f32[128,512]{1,0:T(8,128)S(1)} %collective-permute-done.55.refs_3_, ...), custom_call_target="tpu_custom_call" | custom-call | tf_op jit(solution)/shard_map/last/pallas_call | solution.py:240
  (111 shorter events, 11.8 us)
Async XLA Ops:
  5.0 4.0 %collective-permute-start.6 = (f32[128,256]{1,0:T(8,128)S(1)}, f32[128,256]{1,0:T(8,128)S(1)}, u32[]{:S(2)}, u32[]{:S(2)}) collective-permute-start(f32[128,256]{1,0:T(8,128)S(1)} %get-tuple-element.36), channel_id=1, source_target_pairs={{0,1},{1,0},{2,3},{3,2},{4,5},{5,4},{6,7},{7,6},{8,9},{9,8},{10,11... | collective-permute-start | bytes 393224 | tf_op jit(solution)/shard_map/ppermute | solution.py:41
  5.0 4.1 %collective-permute-start.12 = (f32[128,256]{1,0:T(8,128)S(1)}, f32[128,256]{1,0:T(8,128)S(1)}, u32[]{:S(2)}, u32[]{:S(2)}) collective-permute-start(f32[128,256]{1,0:T(8,128)S(1)} %get-tuple-element.38), channel_id=1, source_target_pairs={{0,1},{1,0},{2,3},{3,2},{4,5},{5,4},{6,7},{7,6},{8,9},{9,8},{10,11... | collective-permute-start | bytes 393224 | tf_op jit(solution)/shard_map/ppermute | solution.py:41
  5.5 5.7 %collective-permute-start.18 = (f32[128,256]{1,0:T(8,128)S(1)}, f32[128,256]{1,0:T(8,128)S(1)}, u32[]{:S(2)}, u32[]{:S(2)}) collective-permute-start(f32[128,256]{1,0:T(8,128)S(1)} %get-tuple-element.40), channel_id=1, source_target_pairs={{0,1},{1,0},{2,3},{3,2},{4,5},{5,4},{6,7},{7,6},{8,9},{9,8},{10,11... | collective-permute-start | bytes 393224 | tf_op jit(solution)/shard_map/ppermute | solution.py:41
  6.0 5.5 %collective-permute-start.1 = (f32[64,256]{1,0:T(8,128)S(1)}, f32[64,256]{1,0:T(8,128)S(1)}, u32[]{:S(2)}, u32[]{:S(2)}) collective-permute-start(f32[64,256]{1,0:T(8,128)S(1)} %slice.65), channel_id=1, source_target_pairs={{0,2},{1,3},{2,0},{3,1},{4,6},{5,7},{6,4},{7,5},{8,10},{9,11},{10,... | collective-permute-start | bytes 196616 | tf_op jit(solution)/shard_map/ppermute | solution.py:41
  9.0 5.5 %collective-permute-start.7 = (f32[64,256]{1,0:T(8,128)S(1)}, f32[64,256]{1,0:T(8,128)S(1)}, u32[]{:S(2)}, u32[]{:S(2)}) collective-permute-start(f32[64,256]{1,0:T(8,128)S(1)} %slice.67), channel_id=1, source_target_pairs={{0,2},{1,3},{2,0},{3,1},{4,6},{5,7},{6,4},{7,5},{8,10},{9,11},{10,... | collective-permute-start | bytes 196616 | tf_op jit(solution)/shard_map/ppermute | solution.py:41
  9.2 7.5 %collective-permute-start.13 = (f32[64,256]{1,0:T(8,128)S(1)}, f32[64,256]{1,0:T(8,128)S(1)}, u32[]{:S(2)}, u32[]{:S(2)}) collective-permute-start(f32[64,256]{1,0:T(8,128)S(1)} %slice.69), channel_id=1, source_target_pairs={{0,2},{1,3},{2,0},{3,1},{4,6},{5,7},{6,4},{7,5},{8,10},{9,11},{10,... | collective-permute-start | bytes 196616 | tf_op jit(solution)/shard_map/ppermute | solution.py:41
  11.2 6.9 %collective-permute-start.19 = (f32[64,256]{1,0:T(8,128)S(1)}, f32[64,256]{1,0:T(8,128)S(1)}, u32[]{:S(2)}, u32[]{:S(2)}) collective-permute-start(f32[64,256]{1,0:T(8,128)S(1)} %slice.71), channel_id=1, source_target_pairs={{0,2},{1,3},{2,0},{3,1},{4,6},{5,7},{6,4},{7,5},{8,10},{9,11},{10,... | collective-permute-start | bytes 196616 | tf_op jit(solution)/shard_map/ppermute | solution.py:41
  11.4 8.4 %collective-permute-start.2 = (f32[64,256]{1,0:T(8,128)S(1)}, f32[64,256]{1,0:T(8,128)S(1)}, u32[]{:S(2)}, u32[]{:S(2)}) collective-permute-start(f32[64,256]{1,0:T(8,128)S(1)} %slice_add_fusion.7), channel_id=1, source_target_pairs={{0,4},{1,5},{2,6},{3,7},{4,0},{5,1},{6,2},{7,3},{8,12},{9,13},{10,... | collective-permute-start | bytes 196616 | tf_op jit(solution)/shard_map/ppermute | solution.py:41
  14.5 10.7 %collective-permute-start.8 = (f32[64,256]{1,0:T(8,128)S(1)}, f32[64,256]{1,0:T(8,128)S(1)}, u32[]{:S(2)}, u32[]{:S(2)}) collective-permute-start(f32[64,256]{1,0:T(8,128)S(1)} %slice_add_fusion.6), channel_id=1, source_target_pairs={{0,4},{1,5},{2,6},{3,7},{4,0},{5,1},{6,2},{7,3},{8,12},{9,13},{10,... | collective-permute-start | bytes 196616 | tf_op jit(solution)/shard_map/ppermute | solution.py:41
  16.7 9.3 %collective-permute-start.14 = (f32[64,256]{1,0:T(8,128)S(1)}, f32[64,256]{1,0:T(8,128)S(1)}, u32[]{:S(2)}, u32[]{:S(2)}) collective-permute-start(f32[64,256]{1,0:T(8,128)S(1)} %slice_add_fusion.5), channel_id=1, source_target_pairs={{0,4},{1,5},{2,6},{3,7},{4,0},{5,1},{6,2},{7,3},{8,12},{9,13},{10,... | collective-permute-start | bytes 196616 | tf_op jit(solution)/shard_map/ppermute | solution.py:41
  18.1 8.6 %collective-permute-start.20 = (f32[64,256]{1,0:T(8,128)S(1)}, f32[64,256]{1,0:T(8,128)S(1)}, u32[]{:S(2)}, u32[]{:S(2)}) collective-permute-start(f32[64,256]{1,0:T(8,128)S(1)} %slice_add_fusion.4), channel_id=1, source_target_pairs={{0,4},{1,5},{2,6},{3,7},{4,0},{5,1},{6,2},{7,3},{8,12},{9,13},{10,... | collective-permute-start | bytes 196616 | tf_op jit(solution)/shard_map/ppermute | solution.py:41
  19.8 7.0 %collective-permute-start.4 = (f32[64,256]{1,0:T(8,128)S(1)}, f32[64,256]{1,0:T(8,128)S(1)}, u32[]{:S(2)}, u32[]{:S(2)}) collective-permute-start(f32[64,256]{1,0:T(8,128)S(1)} %add.86.more_0_), channel_id=1, source_target_pairs={{0,1},{1,0},{2,3},{3,2},{4,5},{5,4},{6,7},{7,6},{8,9},{9,8},{10,11... | collective-permute-start | bytes 196616 | tf_op jit(solution)/shard_map/ppermute | solution.py:41
  19.9 8.4 %collective-permute-start.3 = (f32[64,256]{1,0:T(8,128)S(1)}, f32[64,256]{1,0:T(8,128)S(1)}, u32[]{:S(2)}, u32[]{:S(2)}) collective-permute-start(f32[64,256]{1,0:T(8,128)S(1)} %add.86.more_0_), channel_id=1, source_target_pairs={{0,2},{1,3},{2,0},{3,1},{4,6},{5,7},{6,4},{7,5},{8,10},{9,11},{10,... | collective-permute-start | bytes 196616 | tf_op jit(solution)/shard_map/ppermute | solution.py:41
  25.2 3.7 %collective-permute-start.10 = (f32[64,256]{1,0:T(8,128)S(1)}, f32[64,256]{1,0:T(8,128)S(1)}, u32[]{:S(2)}, u32[]{:S(2)}) collective-permute-start(f32[64,256]{1,0:T(8,128)S(1)} %add.89.more_4_), channel_id=1, source_target_pairs={{0,1},{1,0},{2,3},{3,2},{4,5},{5,4},{6,7},{7,6},{8,9},{9,8},{10,11... | collective-permute-start | bytes 196616 | tf_op jit(solution)/shard_map/ppermute | solution.py:41
  26.1 4.6 %collective-permute-start.9 = (f32[64,256]{1,0:T(8,128)S(1)}, f32[64,256]{1,0:T(8,128)S(1)}, u32[]{:S(2)}, u32[]{:S(2)}) collective-permute-start(f32[64,256]{1,0:T(8,128)S(1)} %add.89.more_4_), channel_id=1, source_target_pairs={{0,2},{1,3},{2,0},{3,1},{4,6},{5,7},{6,4},{7,5},{8,10},{9,11},{10,... | collective-permute-start | bytes 196616 | tf_op jit(solution)/shard_map/ppermute | solution.py:41
  26.8 3.9 %collective-permute-start.16 = (f32[64,256]{1,0:T(8,128)S(1)}, f32[64,256]{1,0:T(8,128)S(1)}, u32[]{:S(2)}, u32[]{:S(2)}) collective-permute-start(f32[64,256]{1,0:T(8,128)S(1)} %add.92.more_8_), channel_id=1, source_target_pairs={{0,1},{1,0},{2,3},{3,2},{4,5},{5,4},{6,7},{7,6},{8,9},{9,8},{10,11... | collective-permute-start | bytes 196616 | tf_op jit(solution)/shard_map/ppermute | solution.py:41
  26.8 5.3 %collective-permute-start.15 = (f32[64,256]{1,0:T(8,128)S(1)}, f32[64,256]{1,0:T(8,128)S(1)}, u32[]{:S(2)}, u32[]{:S(2)}) collective-permute-start(f32[64,256]{1,0:T(8,128)S(1)} %add.92.more_8_), channel_id=1, source_target_pairs={{0,2},{1,3},{2,0},{3,1},{4,6},{5,7},{6,4},{7,5},{8,10},{9,11},{10,... | collective-permute-start | bytes 196616 | tf_op jit(solution)/shard_map/ppermute | solution.py:41
  28.3 4.8 %collective-permute-start.21 = (f32[64,256]{1,0:T(8,128)S(1)}, f32[64,256]{1,0:T(8,128)S(1)}, u32[]{:S(2)}, u32[]{:S(2)}) collective-permute-start(f32[64,256]{1,0:T(8,128)S(1)} %add.95.more_12_), channel_id=1, source_target_pairs={{0,2},{1,3},{2,0},{3,1},{4,6},{5,7},{6,4},{7,5},{8,10},{9,11},{10,... | collective-permute-start | bytes 196616 | tf_op jit(solution)/shard_map/ppermute | solution.py:41
  28.9 4.2 %collective-permute-start.22 = (f32[64,256]{1,0:T(8,128)S(1)}, f32[64,256]{1,0:T(8,128)S(1)}, u32[]{:S(2)}, u32[]{:S(2)}) collective-permute-start(f32[64,256]{1,0:T(8,128)S(1)} %add.95.more_12_), channel_id=1, source_target_pairs={{0,1},{1,0},{2,3},{3,2},{4,5},{5,4},{6,7},{7,6},{8,9},{9,8},{10,11... | collective-permute-start | bytes 196616 | tf_op jit(solution)/shard_map/ppermute | solution.py:41
  30.7 2.5 %collective-permute-start.5 = (f32[64,256]{1,0:T(8,128)S(1)}, f32[64,256]{1,0:T(8,128)S(1)}, u32[]{:S(2)}, u32[]{:S(2)}) collective-permute-start(f32[64,256]{1,0:T(8,128)S(1)} %collective-permute-done.3.more_1_), channel_id=1, source_target_pairs={{0,1},{1,0},{2,3},{3,2},{4,5},{5,4},{6,7},{7,6},{8,9},{9,8},{10,11... | collective-permute-start | bytes 196616 | tf_op jit(solution)/shard_map/ppermute | solution.py:41
  30.7 2.5 %collective-permute-start.11 = (f32[64,256]{1,0:T(8,128)S(1)}, f32[64,256]{1,0:T(8,128)S(1)}, u32[]{:S(2)}, u32[]{:S(2)}) collective-permute-start(f32[64,256]{1,0:T(8,128)S(1)} %collective-permute-done.9.more_5_), channel_id=1, source_target_pairs={{0,1},{1,0},{2,3},{3,2},{4,5},{5,4},{6,7},{7,6},{8,9},{9,8},{10,11... | collective-permute-start | bytes 196616 | tf_op jit(solution)/shard_map/ppermute | solution.py:41
  35.4 8.4 %collective-permute-start.24 = (f32[128,512]{1,0:T(8,128)S(1)}, f32[128,512]{1,0:T(8,128)S(1)}, u32[]{:S(2)}, u32[]{:S(2)}) collective-permute-start(f32[128,512]{1,0:T(8,128)S(1)} %get-tuple-element.41), channel_id=1, source_target_pairs={{0,8},{8,0},{16,24},{24,16},{1,9},{9,1},{17,25},{25,17},{2,10},{10... | collective-permute-start | bytes 786440 | tf_op jit(solution)/shard_map/ppermute | solution.py:41
  37.2 8.5 %collective-permute-start.26 = (f32[128,512]{1,0:T(8,128)S(1)}, f32[128,512]{1,0:T(8,128)S(1)}, u32[]{:S(2)}, u32[]{:S(2)}) collective-permute-start(f32[128,512]{1,0:T(8,128)S(1)} %get-tuple-element.42), channel_id=1, source_target_pairs={{0,16},{8,24},{16,0},{24,8},{1,17},{9,25},{17,1},{25,9},{2,18},{10... | collective-permute-start | bytes 786440 | tf_op jit(solution)/shard_map/ppermute | solution.py:41
  43.8 7.6 %collective-permute-start.25 = (f32[128,512]{1,0:T(8,128)S(1)}, f32[128,512]{1,0:T(8,128)S(1)}, u32[]{:S(2)}, u32[]{:S(2)}) collective-permute-start(f32[128,512]{1,0:T(8,128)S(1)} %add.96.refs_0_), channel_id=1, source_target_pairs={{0,16},{8,24},{16,0},{24,8},{1,17},{9,25},{17,1},{25,9},{2,18},{10... | collective-permute-start | bytes 786440 | tf_op jit(solution)/shard_map/ppermute | solution.py:41
  45.7 7.3 %collective-permute-start.27 = (f32[128,512]{1,0:T(8,128)S(1)}, f32[128,512]{1,0:T(8,128)S(1)}, u32[]{:S(2)}, u32[]{:S(2)}) collective-permute-start(f32[128,512]{1,0:T(8,128)S(1)} %add.97.refs_2_), channel_id=1, source_target_pairs={{0,8},{8,0},{16,24},{24,16},{1,9},{9,1},{17,25},{25,17},{2,10},{10... | collective-permute-start | bytes 786440 | tf_op jit(solution)/shard_map/ppermute | solution.py:41
  62.9 2.5 %collective-permute-start.34 = (f32[128,256]{1,0:T(8,128)S(1)}, f32[128,256]{1,0:T(8,128)S(1)}, u32[]{:S(2)}, u32[]{:S(2)}) collective-permute-start(f32[128,256]{1,0:T(8,128)S(1)} %get-tuple-element.51), channel_id=1, source_target_pairs={{0,1},{1,0},{2,3},{3,2},{4,5},{5,4},{6,7},{7,6},{8,9},{9,8},{10,11... | collective-permute-start | bytes 393224 | tf_op jit(solution)/shard_map/ppermute | solution.py:41
  63.4 3.1 %collective-permute-start.40 = (f32[128,256]{1,0:T(8,128)S(1)}, f32[128,256]{1,0:T(8,128)S(1)}, u32[]{:S(2)}, u32[]{:S(2)}) collective-permute-start(f32[128,256]{1,0:T(8,128)S(1)} %get-tuple-element.53), channel_id=1, source_target_pairs={{0,1},{1,0},{2,3},{3,2},{4,5},{5,4},{6,7},{7,6},{8,9},{9,8},{10,11... | collective-permute-start | bytes 393224 | tf_op jit(solution)/shard_map/ppermute | solution.py:41
  63.5 4.1 %collective-permute-start.46 = (f32[128,256]{1,0:T(8,128)S(1)}, f32[128,256]{1,0:T(8,128)S(1)}, u32[]{:S(2)}, u32[]{:S(2)}) collective-permute-start(f32[128,256]{1,0:T(8,128)S(1)} %get-tuple-element.55), channel_id=1, source_target_pairs={{0,1},{1,0},{2,3},{3,2},{4,5},{5,4},{6,7},{7,6},{8,9},{9,8},{10,11... | collective-permute-start | bytes 393224 | tf_op jit(solution)/shard_map/ppermute | solution.py:41
  64.3 5.0 %collective-permute-start.29 = (f32[64,256]{1,0:T(8,128)S(1)}, f32[64,256]{1,0:T(8,128)S(1)}, u32[]{:S(2)}, u32[]{:S(2)}) collective-permute-start(f32[64,256]{1,0:T(8,128)S(1)} %slice.73), channel_id=1, source_target_pairs={{0,2},{1,3},{2,0},{3,1},{4,6},{5,7},{6,4},{7,5},{8,10},{9,11},{10,... | collective-permute-start | bytes 196616 | tf_op jit(solution)/shard_map/ppermute | solution.py:41
  65.4 6.0 %collective-permute-start.35 = (f32[64,256]{1,0:T(8,128)S(1)}, f32[64,256]{1,0:T(8,128)S(1)}, u32[]{:S(2)}, u32[]{:S(2)}) collective-permute-start(f32[64,256]{1,0:T(8,128)S(1)} %slice.75), channel_id=1, source_target_pairs={{0,2},{1,3},{2,0},{3,1},{4,6},{5,7},{6,4},{7,5},{8,10},{9,11},{10,... | collective-permute-start | bytes 196616 | tf_op jit(solution)/shard_map/ppermute | solution.py:41
  66.5 6.3 %collective-permute-start.41 = (f32[64,256]{1,0:T(8,128)S(1)}, f32[64,256]{1,0:T(8,128)S(1)}, u32[]{:S(2)}, u32[]{:S(2)}) collective-permute-start(f32[64,256]{1,0:T(8,128)S(1)} %slice.77), channel_id=1, source_target_pairs={{0,2},{1,3},{2,0},{3,1},{4,6},{5,7},{6,4},{7,5},{8,10},{9,11},{10,... | collective-permute-start | bytes 196616 | tf_op jit(solution)/shard_map/ppermute | solution.py:41
  67.7 6.8 %collective-permute-start.47 = (f32[64,256]{1,0:T(8,128)S(1)}, f32[64,256]{1,0:T(8,128)S(1)}, u32[]{:S(2)}, u32[]{:S(2)}) collective-permute-start(f32[64,256]{1,0:T(8,128)S(1)} %slice.79), channel_id=1, source_target_pairs={{0,2},{1,3},{2,0},{3,1},{4,6},{5,7},{6,4},{7,5},{8,10},{9,11},{10,... | collective-permute-start | bytes 196616 | tf_op jit(solution)/shard_map/ppermute | solution.py:41
  69.3 10.5 %collective-permute-start.30 = (f32[64,256]{1,0:T(8,128)S(1)}, f32[64,256]{1,0:T(8,128)S(1)}, u32[]{:S(2)}, u32[]{:S(2)}) collective-permute-start(f32[64,256]{1,0:T(8,128)S(1)} %slice_add_fusion.3), channel_id=1, source_target_pairs={{0,4},{1,5},{2,6},{3,7},{4,0},{5,1},{6,2},{7,3},{8,12},{9,13},{10,... | collective-permute-start | bytes 196616 | tf_op jit(solution)/shard_map/ppermute | solution.py:41
  71.4 10.5 %collective-permute-start.36 = (f32[64,256]{1,0:T(8,128)S(1)}, f32[64,256]{1,0:T(8,128)S(1)}, u32[]{:S(2)}, u32[]{:S(2)}) collective-permute-start(f32[64,256]{1,0:T(8,128)S(1)} %slice_add_fusion.2), channel_id=1, source_target_pairs={{0,4},{1,5},{2,6},{3,7},{4,0},{5,1},{6,2},{7,3},{8,12},{9,13},{10,... | collective-permute-start | bytes 196616 | tf_op jit(solution)/shard_map/ppermute | solution.py:41
  72.8 10.1 %collective-permute-start.42 = (f32[64,256]{1,0:T(8,128)S(1)}, f32[64,256]{1,0:T(8,128)S(1)}, u32[]{:S(2)}, u32[]{:S(2)}) collective-permute-start(f32[64,256]{1,0:T(8,128)S(1)} %slice_add_fusion.1), channel_id=1, source_target_pairs={{0,4},{1,5},{2,6},{3,7},{4,0},{5,1},{6,2},{7,3},{8,12},{9,13},{10,... | collective-permute-start | bytes 196616 | tf_op jit(solution)/shard_map/ppermute | solution.py:41
  74.5 9.2 %collective-permute-start.48 = (f32[64,256]{1,0:T(8,128)S(1)}, f32[64,256]{1,0:T(8,128)S(1)}, u32[]{:S(2)}, u32[]{:S(2)}) collective-permute-start(f32[64,256]{1,0:T(8,128)S(1)} %slice_add_fusion), channel_id=1, source_target_pairs={{0,4},{1,5},{2,6},{3,7},{4,0},{5,1},{6,2},{7,3},{8,12},{9,13},{10,... | collective-permute-start | bytes 196616 | tf_op jit(solution)/shard_map/ppermute | solution.py:41
  79.8 3.9 %collective-permute-start.32 = (f32[64,256]{1,0:T(8,128)S(1)}, f32[64,256]{1,0:T(8,128)S(1)}, u32[]{:S(2)}, u32[]{:S(2)}) collective-permute-start(f32[64,256]{1,0:T(8,128)S(1)} %add.100.more_0_), channel_id=1, source_target_pairs={{0,1},{1,0},{2,3},{3,2},{4,5},{5,4},{6,7},{7,6},{8,9},{9,8},{10,11... | collective-permute-start | bytes 196616 | tf_op jit(solution)/shard_map/ppermute | solution.py:41
  79.9 5.3 %collective-permute-start.31 = (f32[64,256]{1,0:T(8,128)S(1)}, f32[64,256]{1,0:T(8,128)S(1)}, u32[]{:S(2)}, u32[]{:S(2)}) collective-permute-start(f32[64,256]{1,0:T(8,128)S(1)} %add.100.more_0_), channel_id=1, source_target_pairs={{0,2},{1,3},{2,0},{3,1},{4,6},{5,7},{6,4},{7,5},{8,10},{9,11},{10,... | collective-permute-start | bytes 196616 | tf_op jit(solution)/shard_map/ppermute | solution.py:41
  81.9 3.9 %collective-permute-start.38 = (f32[64,256]{1,0:T(8,128)S(1)}, f32[64,256]{1,0:T(8,128)S(1)}, u32[]{:S(2)}, u32[]{:S(2)}) collective-permute-start(f32[64,256]{1,0:T(8,128)S(1)} %add.103.more_4_), channel_id=1, source_target_pairs={{0,1},{1,0},{2,3},{3,2},{4,5},{5,4},{6,7},{7,6},{8,9},{9,8},{10,11... | collective-permute-start | bytes 196616 | tf_op jit(solution)/shard_map/ppermute | solution.py:41
  82.9 4.6 %collective-permute-start.37 = (f32[64,256]{1,0:T(8,128)S(1)}, f32[64,256]{1,0:T(8,128)S(1)}, u32[]{:S(2)}, u32[]{:S(2)}) collective-permute-start(f32[64,256]{1,0:T(8,128)S(1)} %add.103.more_4_), channel_id=1, source_target_pairs={{0,2},{1,3},{2,0},{3,1},{4,6},{5,7},{6,4},{7,5},{8,10},{9,11},{10,... | collective-permute-start | bytes 196616 | tf_op jit(solution)/shard_map/ppermute | solution.py:41
  83.7 3.9 %collective-permute-start.44 = (f32[64,256]{1,0:T(8,128)S(1)}, f32[64,256]{1,0:T(8,128)S(1)}, u32[]{:S(2)}, u32[]{:S(2)}) collective-permute-start(f32[64,256]{1,0:T(8,128)S(1)} %add.106.more_8_), channel_id=1, source_target_pairs={{0,1},{1,0},{2,3},{3,2},{4,5},{5,4},{6,7},{7,6},{8,9},{9,8},{10,11... | collective-permute-start | bytes 196616 | tf_op jit(solution)/shard_map/ppermute | solution.py:41
  83.7 5.3 %collective-permute-start.43 = (f32[64,256]{1,0:T(8,128)S(1)}, f32[64,256]{1,0:T(8,128)S(1)}, u32[]{:S(2)}, u32[]{:S(2)}) collective-permute-start(f32[64,256]{1,0:T(8,128)S(1)} %add.106.more_8_), channel_id=1, source_target_pairs={{0,2},{1,3},{2,0},{3,1},{4,6},{5,7},{6,4},{7,5},{8,10},{9,11},{10,... | collective-permute-start | bytes 196616 | tf_op jit(solution)/shard_map/ppermute | solution.py:41
  85.2 4.8 %collective-permute-start.49 = (f32[64,256]{1,0:T(8,128)S(1)}, f32[64,256]{1,0:T(8,128)S(1)}, u32[]{:S(2)}, u32[]{:S(2)}) collective-permute-start(f32[64,256]{1,0:T(8,128)S(1)} %add.109.more_12_), channel_id=1, source_target_pairs={{0,2},{1,3},{2,0},{3,1},{4,6},{5,7},{6,4},{7,5},{8,10},{9,11},{10,... | collective-permute-start | bytes 196616 | tf_op jit(solution)/shard_map/ppermute | solution.py:41
  85.8 4.2 %collective-permute-start.50 = (f32[64,256]{1,0:T(8,128)S(1)}, f32[64,256]{1,0:T(8,128)S(1)}, u32[]{:S(2)}, u32[]{:S(2)}) collective-permute-start(f32[64,256]{1,0:T(8,128)S(1)} %add.109.more_12_), channel_id=1, source_target_pairs={{0,1},{1,0},{2,3},{3,2},{4,5},{5,4},{6,7},{7,6},{8,9},{9,8},{10,11... | collective-permute-start | bytes 196616 | tf_op jit(solution)/shard_map/ppermute | solution.py:41
  92.2 8.4 %collective-permute-start.52 = (f32[128,512]{1,0:T(8,128)S(1)}, f32[128,512]{1,0:T(8,128)S(1)}, u32[]{:S(2)}, u32[]{:S(2)}) collective-permute-start(f32[128,512]{1,0:T(8,128)S(1)} %get-tuple-element.56), channel_id=1, source_target_pairs={{0,8},{8,0},{16,24},{24,16},{1,9},{9,1},{17,25},{25,17},{2,10},{10... | collective-permute-start | bytes 786440 | tf_op jit(solution)/shard_map/ppermute | solution.py:41
  93.8 8.1 %collective-permute-start.54 = (f32[128,512]{1,0:T(8,128)S(1)}, f32[128,512]{1,0:T(8,128)S(1)}, u32[]{:S(2)}, u32[]{:S(2)}) collective-permute-start(f32[128,512]{1,0:T(8,128)S(1)} %get-tuple-element.57), channel_id=1, source_target_pairs={{0,16},{8,24},{16,0},{24,8},{1,17},{9,25},{17,1},{25,9},{2,18},{10... | collective-permute-start | bytes 786440 | tf_op jit(solution)/shard_map/ppermute | solution.py:41
  100.7 7.6 %collective-permute-start.53 = (f32[128,512]{1,0:T(8,128)S(1)}, f32[128,512]{1,0:T(8,128)S(1)}, u32[]{:S(2)}, u32[]{:S(2)}) collective-permute-start(f32[128,512]{1,0:T(8,128)S(1)} %add.110.refs_0_), channel_id=1, source_target_pairs={{0,16},{8,24},{16,0},{24,8},{1,17},{9,25},{17,1},{25,9},{2,18},{10... | collective-permute-start | bytes 786440 | tf_op jit(solution)/shard_map/ppermute | solution.py:41
  101.9 7.3 %collective-permute-start.55 = (f32[128,512]{1,0:T(8,128)S(1)}, f32[128,512]{1,0:T(8,128)S(1)}, u32[]{:S(2)}, u32[]{:S(2)}) collective-permute-start(f32[128,512]{1,0:T(8,128)S(1)} %add.111.refs_2_), channel_id=1, source_target_pairs={{0,8},{8,0},{16,24},{24,16},{1,9},{9,1},{17,25},{25,17},{2,10},{10... | collective-permute-start | bytes 786440 | tf_op jit(solution)/shard_map/ppermute | solution.py:41
  (11 other events, 15.7 us)

commit v3 on v2

--- a/solution.py
+++ b/solution.py
@@ -8,7 +8,8 @@
 
 ITERS = 2
 CHUNKS = 4
-VMEM_BYTES = 28 << 20
+SUBLANES = 8
+VMEM_BYTES = 16 << 20
 
 NN = (((1,), (0,)), ((), ()))
 NT = (((1,), (1,)), ((), ()))
@@ -134,33 +135,54 @@
     right = dot3(left, (top_ref[...], rest_ref[...]), TN)
     cross = dot(left[0], left[1], TN)
     gram = dot(left[0], left[0], TN) + (cross + cross.T)
-    half = rank // 2
-    a_ref[:, : right.shape[1]] = right[:half]
-    b_ref[:, : right.shape[1]] = right[half:]
-    a_ref[:, right.shape[1] :] = gram[:half]
-    b_ref[:, right.shape[1] :] = gram[half:]
-
-
-def solve(gram, right):
-    n = gram.shape[0]
-    eye = (
-        lax.broadcasted_iota(jnp.int32, (n, n), 0) == lax.broadcasted_iota(jnp.int32, (n, n), 1)
-    ).astype(f32)
-    on_diag = gram * eye
-    down = lax.rsqrt(jnp.sum(on_diag, 1, keepdims=True))
-    across = lax.rsqrt(jnp.sum(on_diag, 0, keepdims=True))
-    scaled = gram * down * across
-    bound = jnp.minimum(
-        jnp.max(jnp.sum(jnp.abs(scaled), 0, keepdims=True)),
-        jnp.sqrt(jnp.sum(scaled * scaled)),
+    pack(gram, right, a_ref, b_ref)
+
+
+def pack(gram, right, a_ref, b_ref):
+    half = gram.shape[0] // 2
+    lower = below(half)
+    a_ref[:half, :half] = jnp.where(lower, gram[:half, :half], gram[half:, half:])
+    a_ref[:half, half:] = gram[half:, :half]
+    diagonal = jnp.sum(jnp.where(identity(half), gram[half:, half:], 0.0), 0, keepdims=True)
+    a_ref[half : half + SUBLANES, :] = jnp.broadcast_to(
+        jnp.concatenate([diagonal, diagonal], 1), (SUBLANES, 2 * half)
     )
-    step = 1.9 / bound
-    error = eye - step * scaled
-    inverse = step * eye
-
+    taken = a_ref.shape[0] - half - SUBLANES
+    a_ref[half + SUBLANES :, :] = right[:taken]
+    b_ref[...] = right[taken:]
+
+
+def unpack_gram(a):
+    half = a.shape[1] // 2
+    lower = below(half)
+    both, off = a[:half, :half], a[:half, half:]
+    turned = both.T
+    first = jnp.where(lower, both, turned)
+    second = jnp.where(identity(half), a[half : half + 1, :half], jnp.where(lower, turned, both))
+    return jnp.concatenate([jnp.concatenate([first, off.T], 1), jnp.concatenate([off, second], 1)], 0)
+
+
+def unpack_right(a, b):
+    return jnp.concatenate([a[a.shape[1] // 2 + SUBLANES :], b], 0)
+
+
+def identity(n):
+    return lax.broadcasted_iota(jnp.int32, (n, n), 0) == lax.broadcasted_iota(jnp.int32, (n, n), 1)
+
+
+def below(n):
+    return lax.broadcasted_iota(jnp.int32, (n, n), 0) >= lax.broadcasted_iota(jnp.int32, (n, n), 1)
+
+
+def norm_bound(x):
+    size = jnp.abs(x)
+    return jnp.minimum(jnp.max(jnp.sum(size, 0, keepdims=True)), jnp.max(jnp.sum(size, 1, keepdims=True)))
+
+
+def converge(inverse, error, enough):
     def more(state):
         count, size, _, _ = state
-        return jnp.logical_and(count < 40, size > 1e-4)
+        return jnp.logical_and(count < 40, size > enough)
 
     def double(state):
         count, _, inverse, error = state
@@ -168,27 +190,72 @@
         terms = split(error, 2)
         return count + 1, size, inverse + dot3(split(inverse, 2), terms), dot3(terms, terms)
 
-    _, _, inverse, _ = lax.while_loop(more, double, (0, jnp.float32(1.0), inverse, error))
+    _, size, inverse, _ = lax.while_loop(more, double, (0, jnp.float32(1e9), inverse, error))
+    return inverse, size
+
+
+def diagonals(gram):
+    on_diag = jnp.where(identity(gram.shape[0]), gram, 0.0)
+    return jnp.sum(on_diag, 1, keepdims=True), jnp.sum(on_diag, 0, keepdims=True)
+
+
+def plain_start(scaled):
+    eye = identity(scaled.shape[0]).astype(f32)
+    step = 1.9 / norm_bound(scaled)
+    return step * eye, eye - step * scaled
+
+
+def inverse_kernel(a_ref, out_ref, size_ref):
+    gram = unpack_gram(a_ref[...])
+    down, across = diagonals(gram)
+    down, across = lax.rsqrt(down), lax.rsqrt(across)
+    inverse, size = converge(*plain_start(gram * down * across), 1e-2)
+    out_ref[...] = inverse * down * across
+    size_ref[...] = jnp.full(size_ref.shape, size)
+
+
+def solve(gram, right, start, start_size):
+    down, across = diagonals(gram)
+    start = start * jnp.sqrt(down) * jnp.sqrt(across)
+    down, across = lax.rsqrt(down), lax.rsqrt(across)
+    scaled = gram * down * across
+    right = right * down
     exact = split(scaled, 3)
+    eye = identity(gram.shape[0]).astype(f32)
+    product = dot6(exact, split(start, 3))
+    terms = split(product, 2)
+    square = dot3(terms, terms)
+    bound = jnp.minimum(norm_bound(product), jnp.sqrt(norm_bound(square)))
+    good = jnp.logical_and(start_size <= 1e-2, bound < 1e3)
+    step = 2.0 / (1.0 + bound)
+
+    def from_start():
+        error = eye - (2.0 * step) * product + (step * step) * square
+        return (2.0 * step) * start - (step * step) * dot3(split(start, 2), terms), error
+
+    inverse, error = lax.cond(good, from_start, lambda: plain_start(scaled))
+    inverse, _ = converge(inverse, error, 1e-4)
+    factors = split(inverse, 2)
+    out = dot3(factors, split(right, 2))
+    scale = jnp.sum(right * right)
 
     def again(state):
         count, size, _ = state
-        return jnp.logical_and(count < 20, size > 1e-6)
+        return jnp.logical_and(count < 20, size > 1e-6 * scale)
 
     def refine(state):
-        count, _, inverse = state
-        rest = eye - dot6(exact, split(inverse, 3))
-        return count + 1, jnp.sum(rest * rest), inverse + dot3(split(inverse, 2), split(rest, 2))
-
-    _, _, inverse = lax.while_loop(again, refine, (0, jnp.float32(1.0), inverse))
-    return down * dot6(split(inverse, 3), split(down * right, 3))
-
-
-def weights_of(sum_refs, cols):
-    a = sum_refs[0][...] + sum_refs[1][...]
-    b = sum_refs[2][...] + sum_refs[3][...]
-    both = jnp.concatenate([a, b], 0)
-    return solve(both[:, cols:], both[:, :cols])
+        count, _, out = state
+        rest = right - dot6(exact, split(out, 3))
+        return count + 1, jnp.sum(rest * rest), out + dot3(factors, split(rest, 2))
+
+    _, _, out = lax.while_loop(again, refine, (0, 2.0 * scale, out))
+    return out * down
+
+
+def weights_of(refs):
+    a1_ref, a2_ref, b1_ref, b2_ref, start_ref, size_ref = refs
+    a, b = a1_ref[...] + a2_ref[...], b1_ref[...] + b2_ref[...]
+    return solve(unpack_gram(a), unpack_right(a, b), start_ref[...], jnp.max(size_ref[...]))
 
 
 def shrink(data, low_rank, level):
@@ -198,10 +265,10 @@
 
 
 def middle_kernel(blocks, *refs):
-    sum_refs, refs = refs[:4], refs[4:]
+    sum_refs, refs = refs[:6], refs[6:]
     left_top_ref, left_rest_ref, data_ref, level_ref, top_ref, rest_ref, *left_refs = refs
     tall = data_ref.shape[0] // blocks
-    weights = split(weights_of(sum_refs, data_ref.shape[1]), 2)
+    weights = split(weights_of(sum_refs), 2)
     left = []
     for p in range(blocks):
         at = pl.ds(p * tall, tall)
@@ -214,11 +281,11 @@
 
 
 def last_kernel(blocks, *refs):
-    sum_refs, refs = refs[:4], refs[4:]
+    sum_refs, refs = refs[:6], refs[6:]
     left_top_ref, left_rest_ref, data_ref, level_ref, low_rank_ref, sparse_ref, low_rank, sparse, sems = refs
     tall = data_ref.shape[0] // blocks
     low = lowest(blocks)
-    weights = split(weights_of(sum_refs, data_ref.shape[1]), 2)
+    weights = split(weights_of(sum_refs), 2)
     copies = []
     for p in range(blocks):
         at = pl.ds(p * tall, tall)
@@ -236,7 +303,7 @@
 ANY = pl.BlockSpec(memory_space=pl.ANY)
 
 
-def call(body, args, outs, in_specs=None, out_specs=None, scratch=(), name=None):
+def call(body, args, outs, in_specs=None, out_specs=None, scratch=(), cost=None, name=None):
     return pl.pallas_call(
         body,
         out_shape=[jax.ShapeDtypeStruct(shape, dtype) for shape, dtype in outs],
@@ -244,6 +311,7 @@
         out_specs=out_specs or [VMEM] * len(outs),
         scratch_shapes=list(scratch),
         compiler_params=pltpu.CompilerParams(vmem_limit_bytes=VMEM_BYTES),
+        cost_estimate=cost,
         name=name,
     )(*args)
 
@@ -254,6 +322,7 @@
     blocks = n_tm // 2
     level = threshold[None, :]
     whole = [((rows, cols), bf16)] * 2
+    a_rows = (rank + rank // 2 + SUBLANES) // 16 * 8 + SUBLANES
     lefts = [((rows // CHUNKS // 2, rank), f32)] * (2 * CHUNKS)
     data, top, rest, *left = call(
         functools.partial(head_kernel, blocks),
@@ -268,10 +337,18 @@
         a, b, left_top, left_rest = call(
             functools.partial(product_kernel, blocks, [len(x) for x in pieces]),
             (top, rest, *[x for parts in pieces for x in parts]),
-            [((rank // 2, cols + rank), f32)] * 2 + [((rows, rank), bf16)] * 2,
+            [((a_rows, cols), f32), ((rank + rank // 2 + SUBLANES - a_rows, cols), f32)] + [((rows, rank), bf16)] * 2,
             name="products",
         )
-        args = (*sum_rows(a, b, n_rows), left_top, left_rest, data, level)
+        sums = sum_rows(a, b, n_rows)
+        start = call(
+            inverse_kernel,
+            sums[:1],
+            [((rank, rank), f32), ((SUBLANES, 128), f32)],
+            cost=pl.CostEstimate(flops=80 * rank**3, bytes_accessed=rank * rank * 8, transcendentals=0),
+            name="inverse",
+        )
+        args = (*sums, *start, left_top, left_rest, data, level)
         if iteration < ITERS - 1:
             top, rest, *left = call(
                 functools.partial(middle_kernel, blocks), args, whole + lefts, name="middle"

time: 120 us -> 110 us (0.917)
  waiting for transfers between devices: 46.3 us -> 32.3 us
  Pallas kernels: 23.1 us -> 28.3 us
    ppermute x56, waiting for transfers between devices: 46.3 us -> 32.3 us  [swap(): return lax.ppermute(x, axis, [(i, i ^ bit) for i in range(size)])]
    pallas_call x5 -> x7, Pallas kernels: 23.1 us -> 28.3 us  [call(): pl.pallas_call(body, out_shape=[jax.ShapeDtypeStruct(shape, dtype) for sh...]
  transfers between devices with their start and end apart: 56 -> 56, of which waited for: 26 -> 22; matrix products, arithmetic and copies ran while one was open for 0% -> 0% of each run, Pallas kernels for 0% -> 11%
where the time goes in v3:
time: 110 us
  starting transfers between devices  44.9 us (41%)
  waiting for transfers between devices  32.3 us (29%)
  Pallas kernels  28.3 us (26%)
  local copies, waits for them, and re-layouts  2.89 us (3%)
  between operations  1.17 us (1%)
    ppermute x56, starting transfers between devices, swap(): return lax.ppermute(x, axis, [(i, i ^ bit) for i in range(size)])  44.9 us
    ppermute x56, waiting for transfers between devices, swap(): return lax.ppermute(x, axis, [(i, i ^ bit) for i in range(size)])  32.3 us
    pallas_call x7, Pallas kernels, call(): pl.pallas_call(body, out_shape=[jax.ShapeDtypeStruct(shape, dtype) for sh...  28.3 us
    unnamed x6, local copies, waits for them, and re-layouts  2.84 us
  transfers between devices with their start and end apart: 56, of which 22 were waited for; matrix products, arithmetic and copies ran while one was open for 0% of the time, Pallas kernels for 11%

profile of v3, /device:TPU:0, one launch (start us, length us, event | category | flops | bytes accessed | tf_op | source)
XLA Modules:
  0.0 109.9 jit_solution(15723006021750110321)
XLA Ops:
  0.6 1.2 %copy-done = f32[1024,256]{1,0:T(8,128)S(1)} copy-done((f32[1024,256]{1,0:T(8,128)S(1)}, f32[1024,256]{1,0:T(8,128)}, u32[]{:S(2)}) %copy-start) | copy-done | bytes 1048600
  1.9 0.9 copy-done.1
  2.8 1.6 %head.1 = (f32[1024,256]{1,0:T(8,128)S(1)}, bf16[1024,256]{1,0:T(8,128)(2,1)S(1)}, bf16[1024,256]{1,0:T(8,128)(2,1)S(1)}, f32[128,256]{1,0:T(8,128)S(1)}, f32[12...) custom-call(f32[1024,256]{1,0:T(8,128)S(1)} %copy-done, ...), custom_call_target="tpu_custom_call" | custom-call | tf_op jit(solution)/shard_map/head/pallas_call | solution.py:307
  6.0 3.0 %collective-permute-start.1 = (f32[64,256]{1,0:T(8,128)S(1)}, f32[64,256]{1,0:T(8,128)S(1)}, u32[]{:S(2)}, u32[]{:S(2)}) collective-permute-start(f32[64,256]{1,0:T(8,128)S(1)} %slice.65), channel_id=1, source_target_pairs={{0,2},{1,3},{2,0},{3,1},{4,6},{5,7},{6,4},{7,5},{8,10},{9,11},{10,... | collective-permute-start | bytes 196616 | tf_op jit(solution)/shard_map/ppermute | solution.py:42
  9.2 2.0 %collective-permute-start.13 = (f32[64,256]{1,0:T(8,128)S(1)}, f32[64,256]{1,0:T(8,128)S(1)}, u32[]{:S(2)}, u32[]{:S(2)}) collective-permute-start(f32[64,256]{1,0:T(8,128)S(1)} %slice.69), channel_id=1, source_target_pairs={{0,2},{1,3},{2,0},{3,1},{4,6},{5,7},{6,4},{7,5},{8,10},{9,11},{10,... | collective-permute-start | bytes 196616 | tf_op jit(solution)/shard_map/ppermute | solution.py:42
  11.4 3.1 %collective-permute-start.2 = (f32[64,256]{1,0:T(8,128)S(1)}, f32[64,256]{1,0:T(8,128)S(1)}, u32[]{:S(2)}, u32[]{:S(2)}) collective-permute-start(f32[64,256]{1,0:T(8,128)S(1)} %slice_add_fusion.7), channel_id=1, source_target_pairs={{0,4},{1,5},{2,6},{3,7},{4,0},{5,1},{6,2},{7,3},{8,12},{9,13},{10,... | collective-permute-start | bytes 196616 | tf_op jit(solution)/shard_map/ppermute | solution.py:42
  14.5 2.2 %collective-permute-start.8 = (f32[64,256]{1,0:T(8,128)S(1)}, f32[64,256]{1,0:T(8,128)S(1)}, u32[]{:S(2)}, u32[]{:S(2)}) collective-permute-start(f32[64,256]{1,0:T(8,128)S(1)} %slice_add_fusion.6), channel_id=1, source_target_pairs={{0,4},{1,5},{2,6},{3,7},{4,0},{5,1},{6,2},{7,3},{8,12},{9,13},{10,... | collective-permute-start | bytes 196616 | tf_op jit(solution)/shard_map/ppermute | solution.py:42
  16.7 1.4 %collective-permute-start.14 = (f32[64,256]{1,0:T(8,128)S(1)}, f32[64,256]{1,0:T(8,128)S(1)}, u32[]{:S(2)}, u32[]{:S(2)}) collective-permute-start(f32[64,256]{1,0:T(8,128)S(1)} %slice_add_fusion.5), channel_id=1, source_target_pairs={{0,4},{1,5},{2,6},{3,7},{4,0},{5,1},{6,2},{7,3},{8,12},{9,13},{10,... | collective-permute-start | bytes 196616 | tf_op jit(solution)/shard_map/ppermute | solution.py:42
  18.1 1.7 %collective-permute-start.20 = (f32[64,256]{1,0:T(8,128)S(1)}, f32[64,256]{1,0:T(8,128)S(1)}, u32[]{:S(2)}, u32[]{:S(2)}) collective-permute-start(f32[64,256]{1,0:T(8,128)S(1)} %slice_add_fusion.4), channel_id=1, source_target_pairs={{0,4},{1,5},{2,6},{3,7},{4,0},{5,1},{6,2},{7,3},{8,12},{9,13},{10,... | collective-permute-start | bytes 196616 | tf_op jit(solution)/shard_map/ppermute | solution.py:42
  19.9 2.8 %collective-permute-start.3 = (f32[64,256]{1,0:T(8,128)S(1)}, f32[64,256]{1,0:T(8,128)S(1)}, u32[]{:S(2)}, u32[]{:S(2)}) collective-permute-start(f32[64,256]{1,0:T(8,128)S(1)} %add.86.more_0_), channel_id=1, source_target_pairs={{0,2},{1,3},{2,0},{3,1},{4,6},{5,7},{6,4},{7,5},{8,10},{9,11},{10,... | collective-permute-start | bytes 196616 | tf_op jit(solution)/shard_map/ppermute | solution.py:42
  22.7 2.4 %collective-permute-done.8 = f32[64,256]{1,0:T(8,128)S(1)} collective-permute-done((f32[64,256]{1,0:T(8,128)S(1)}, f32[64,256]{1,0:T(8,128)S(1)}, u32[]{:S(2)}, u32[]{:S(2)}) %collective-permute-start.8) | collective-permute-done | bytes 65568 | tf_op jit(solution)/shard_map/ppermute | solution.py:42
  25.3 0.8 collective-permute-done.14
  26.8 1.5 %collective-permute-start.15 = (f32[64,256]{1,0:T(8,128)S(1)}, f32[64,256]{1,0:T(8,128)S(1)}, u32[]{:S(2)}, u32[]{:S(2)}) collective-permute-start(f32[64,256]{1,0:T(8,128)S(1)} %add.92.more_8_), channel_id=1, source_target_pairs={{0,2},{1,3},{2,0},{3,1},{4,6},{5,7},{6,4},{7,5},{8,10},{9,11},{10,... | collective-permute-start | bytes 196616 | tf_op jit(solution)/shard_map/ppermute | solution.py:42
  28.9 1.8 %collective-permute-done.9.more_5_ = f32[64,256]{1,0:T(8,128)S(1)} collective-permute-done((f32[64,256]{1,0:T(8,128)S(1)}, f32[64,256]{1,0:T(8,128)S(1)}, u32[]{:S(2)}, u32[]{:S(2)}) %collective-permute-start.9) | collective-permute-done | bytes 65568 | tf_op jit(solution)/shard_map/ppermute | solution.py:42
  31.2 0.9 collective-permute-done.15.more_9_
  32.1 1.0 collective-permute-done.21.more_13_
  33.4 1.0 collective-permute-done.23.more_15_
  34.4 0.9 products.2
  35.3 1.8 %collective-permute-start.24 = (f32[200,256]{1,0:T(8,128)S(1)}, f32[200,256]{1,0:T(8,128)S(1)}, u32[]{:S(2)}, u32[]{:S(2)}) collective-permute-start(f32[200,256]{1,0:T(8,128)S(1)} %get-tuple-element.45), channel_id=1, source_target_pairs={{0,8},{8,0},{16,24},{24,16},{1,9},{9,1},{17,25},{25,17},{2,10},{10... | collective-permute-start | bytes 614408 | tf_op jit(solution)/shard_map/ppermute | solution.py:42
  37.1 1.5 %collective-permute-start.26 = (f32[192,256]{1,0:T(8,128)S(1)}, f32[192,256]{1,0:T(8,128)S(1)}, u32[]{:S(2)}, u32[]{:S(2)}) collective-permute-start(f32[192,256]{1,0:T(8,128)S(1)} %get-tuple-element.46), channel_id=1, source_target_pairs={{0,16},{8,24},{16,0},{24,8},{1,17},{9,25},{17,1},{25,9},{2,18},{10... | collective-permute-start | bytes 589832 | tf_op jit(solution)/shard_map/ppermute | solution.py:42
  38.6 3.9 %collective-permute-done.24 = f32[200,256]{1,0:T(8,128)S(1)} collective-permute-done((f32[200,256]{1,0:T(8,128)S(1)}, f32[200,256]{1,0:T(8,128)S(1)}, u32[]{:S(2)}, u32[]{:S(2)}) %collective-permute-start.24) | collective-permute-done | bytes 204832 | tf_op jit(solution)/shard_map/ppermute | solution.py:42
  42.6 1.8 %collective-permute-start.25 = (f32[200,256]{1,0:T(8,128)S(1)}, f32[200,256]{1,0:T(8,128)S(1)}, u32[]{:S(2)}, u32[]{:S(2)}) collective-permute-start(f32[200,256]{1,0:T(8,128)S(1)} %add.96.a_ref.refs_0_), channel_id=1, source_target_pairs={{0,16},{8,24},{16,0},{24,8},{1,17},{9,25},{17,1},{25,9},{2,18},{10... | collective-permute-start | bytes 614408 | tf_op jit(solution)/shard_map/ppermute | solution.py:42
  44.4 1.6 %collective-permute-start.27 = (f32[192,256]{1,0:T(8,128)S(1)}, f32[192,256]{1,0:T(8,128)S(1)}, u32[]{:S(2)}, u32[]{:S(2)}) collective-permute-start(f32[192,256]{1,0:T(8,128)S(1)} %add.97.refs_2_), channel_id=1, source_target_pairs={{0,8},{8,0},{16,24},{24,16},{1,9},{9,1},{17,25},{25,17},{2,10},{10... | collective-permute-start | bytes 589832 | tf_op jit(solution)/shard_map/ppermute | solution.py:42
  46.0 5.6 %inverse.2 = (f32[256,256]{1,0:T(8,128)S(1)}, f32[8,128]{1,0:T(8,128)S(1)}) custom-call(f32[200,256]{1,0:T(8,128)S(1)} %add.96.a_ref.refs_0_), custom_call_target="tpu_custom_call" | custom-call | flops 1342177280 | bytes 524288 | tf_op jit(solution)/shard_map/inverse/pallas_call | solution.py:307
  52.3 6.4 %middle.1 = (bf16[1024,256]{1,0:T(8,128)(2,1)S(1)}, bf16[1024,256]{1,0:T(8,128)(2,1)S(1)}, f32[128,256]{1,0:T(8,128)S(1)}, f32[128,256]{1,0:T(8,128)S(1)}, f32[1...) custom-call(f32[200,256]{1,0:T(8,128)S(1)} %add.96.a_ref.refs_0_, ...), custom_call_target="tpu_custom_call" | custom-call | tf_op jit(solution)/shard_map/middle/pallas_call | solution.py:307
  60.2 1.1 %collective-permute-start.29 = (f32[64,256]{1,0:T(8,128)S(1)}, f32[64,256]{1,0:T(8,128)S(1)}, u32[]{:S(2)}, u32[]{:S(2)}) collective-permute-start(f32[64,256]{1,0:T(8,128)S(1)} %slice.73), channel_id=1, source_target_pairs={{0,2},{1,3},{2,0},{3,1},{4,6},{5,7},{6,4},{7,5},{8,10},{9,11},{10,... | collective-permute-start | bytes 196616 | tf_op jit(solution)/shard_map/ppermute | solution.py:42
  61.3 1.1 collective-permute-start.35
  62.4 1.1 %collective-permute-start.41 = (f32[64,256]{1,0:T(8,128)S(1)}, f32[64,256]{1,0:T(8,128)S(1)}, u32[]{:S(2)}, u32[]{:S(2)}) collective-permute-start(f32[64,256]{1,0:T(8,128)S(1)} %slice.77), channel_id=1, source_target_pairs={{0,2},{1,3},{2,0},{3,1},{4,6},{5,7},{6,4},{7,5},{8,10},{9,11},{10,... | collective-permute-start | bytes 196616 | tf_op jit(solution)/shard_map/ppermute | solution.py:42
  63.6 1.1 collective-permute-start.47
  65.2 2.1 %collective-permute-start.30 = (f32[64,256]{1,0:T(8,128)S(1)}, f32[64,256]{1,0:T(8,128)S(1)}, u32[]{:S(2)}, u32[]{:S(2)}) collective-permute-start(f32[64,256]{1,0:T(8,128)S(1)} %slice_add_fusion.3), channel_id=1, source_target_pairs={{0,4},{1,5},{2,6},{3,7},{4,0},{5,1},{6,2},{7,3},{8,12},{9,13},{10,... | collective-permute-start | bytes 196616 | tf_op jit(solution)/shard_map/ppermute | solution.py:42
  67.3 1.4 %collective-permute-start.36 = (f32[64,256]{1,0:T(8,128)S(1)}, f32[64,256]{1,0:T(8,128)S(1)}, u32[]{:S(2)}, u32[]{:S(2)}) collective-permute-start(f32[64,256]{1,0:T(8,128)S(1)} %slice_add_fusion.2), channel_id=1, source_target_pairs={{0,4},{1,5},{2,6},{3,7},{4,0},{5,1},{6,2},{7,3},{8,12},{9,13},{10,... | collective-permute-start | bytes 196616 | tf_op jit(solution)/shard_map/ppermute | solution.py:42
  68.7 1.7 %collective-permute-start.42 = (f32[64,256]{1,0:T(8,128)S(1)}, f32[64,256]{1,0:T(8,128)S(1)}, u32[]{:S(2)}, u32[]{:S(2)}) collective-permute-start(f32[64,256]{1,0:T(8,128)S(1)} %slice_add_fusion.1), channel_id=1, source_target_pairs={{0,4},{1,5},{2,6},{3,7},{4,0},{5,1},{6,2},{7,3},{8,12},{9,13},{10,... | collective-permute-start | bytes 196616 | tf_op jit(solution)/shard_map/ppermute | solution.py:42
  70.4 1.4 %collective-permute-start.48 = (f32[64,256]{1,0:T(8,128)S(1)}, f32[64,256]{1,0:T(8,128)S(1)}, u32[]{:S(2)}, u32[]{:S(2)}) collective-permute-start(f32[64,256]{1,0:T(8,128)S(1)} %slice_add_fusion), channel_id=1, source_target_pairs={{0,4},{1,5},{2,6},{3,7},{4,0},{5,1},{6,2},{7,3},{8,12},{9,13},{10,... | collective-permute-start | bytes 196616 | tf_op jit(solution)/shard_map/ppermute | solution.py:42
  71.8 3.9 %collective-permute-done.30 = f32[64,256]{1,0:T(8,128)S(1)} collective-permute-done((f32[64,256]{1,0:T(8,128)S(1)}, f32[64,256]{1,0:T(8,128)S(1)}, u32[]{:S(2)}, u32[]{:S(2)}) %collective-permute-start.30) | collective-permute-done | bytes 65568 | tf_op jit(solution)/shard_map/ppermute | solution.py:42
  75.8 1.9 %collective-permute-done.36 = f32[64,256]{1,0:T(8,128)S(1)} collective-permute-done((f32[64,256]{1,0:T(8,128)S(1)}, f32[64,256]{1,0:T(8,128)S(1)}, u32[]{:S(2)}, u32[]{:S(2)}) %collective-permute-start.36) | collective-permute-done | bytes 65568 | tf_op jit(solution)/shard_map/ppermute | solution.py:42
  77.9 1.0 collective-permute-done.42
  78.8 0.8 collective-permute-done.48
  79.6 1.4 %collective-permute-start.43 = (f32[64,256]{1,0:T(8,128)S(1)}, f32[64,256]{1,0:T(8,128)S(1)}, u32[]{:S(2)}, u32[]{:S(2)}) collective-permute-start(f32[64,256]{1,0:T(8,128)S(1)} %add.106.more_8_), channel_id=1, source_target_pairs={{0,2},{1,3},{2,0},{3,1},{4,6},{5,7},{6,4},{7,5},{8,10},{9,11},{10,... | collective-permute-start | bytes 196616 | tf_op jit(solution)/shard_map/ppermute | solution.py:42
  81.7 1.7 %collective-permute-done.37.more_5_ = f32[64,256]{1,0:T(8,128)S(1)} collective-permute-done((f32[64,256]{1,0:T(8,128)S(1)}, f32[64,256]{1,0:T(8,128)S(1)}, u32[]{:S(2)}, u32[]{:S(2)}) %collective-permute-start.37) | collective-permute-done | bytes 65568 | tf_op jit(solution)/shard_map/ppermute | solution.py:42
  84.0 0.9 collective-permute-done.43.more_9_
  84.9 1.0 collective-permute-done.49.more_13_
  86.1 1.0 collective-permute-done.51.more_15_
  87.2 1.0 products.3
  88.7 0.9 collective-permute-start.54
  89.7 5.7 %collective-permute-done.52 = f32[200,256]{1,0:T(8,128)S(1)} collective-permute-done((f32[200,256]{1,0:T(8,128)S(1)}, f32[200,256]{1,0:T(8,128)S(1)}, u32[]{:S(2)}, u32[]{:S(2)}) %collective-permute-start.52) | collective-permute-done | bytes 204832 | tf_op jit(solution)/shard_map/ppermute | solution.py:42
  96.0 1.0 collective-permute-start.55
  97.0 6.1 %inverse.3 = (f32[256,256]{1,0:T(8,128)S(1)}, f32[8,128]{1,0:T(8,128)S(1)}) custom-call(f32[200,256]{1,0:T(8,128)S(1)} %add.110.a_ref.refs_0_), custom_call_target="tpu_custom_call" | custom-call | flops 1342177280 | bytes 524288 | tf_op jit(solution)/shard_map/inverse/pallas_call | solution.py:307
  103.1 6.7 %last.1 = (f32[1024,256]{1,0:T(8,128)}, f32[1024,256]{1,0:T(8,128)}) custom-call(f32[200,256]{1,0:T(8,128)S(1)} %add.110.a_ref.refs_0_, f32[200,256]{1,0:T(8,128)S(1)} %collective-permute-done.53.refs_1_, f32[192,256]{1,0:T(8,128)S(1)} %add.111.refs_2_, f32[192,256]{1,0:T(8,128)S(1)} %collective-permute-done.55.refs_3_, ...), custom_call_target="tpu_custom_call" | custom-call | tf_op jit(solution)/shard_map/last/pallas_call | solution.py:307
  (113 shorter events, 10.0 us)
Async XLA Ops:
  4.9 4.0 %collective-permute-start.6 = (f32[128,256]{1,0:T(8,128)S(1)}, f32[128,256]{1,0:T(8,128)S(1)}, u32[]{:S(2)}, u32[]{:S(2)}) collective-permute-start(f32[128,256]{1,0:T(8,128)S(1)} %get-tuple-element.40), channel_id=1, source_target_pairs={{0,1},{1,0},{2,3},{3,2},{4,5},{5,4},{6,7},{7,6},{8,9},{9,8},{10,11... | collective-permute-start | bytes 393224 | tf_op jit(solution)/shard_map/ppermute | solution.py:42
  5.0 4.1 %collective-permute-start.12 = (f32[128,256]{1,0:T(8,128)S(1)}, f32[128,256]{1,0:T(8,128)S(1)}, u32[]{:S(2)}, u32[]{:S(2)}) collective-permute-start(f32[128,256]{1,0:T(8,128)S(1)} %get-tuple-element.42), channel_id=1, source_target_pairs={{0,1},{1,0},{2,3},{3,2},{4,5},{5,4},{6,7},{7,6},{8,9},{9,8},{10,11... | collective-permute-start | bytes 393224 | tf_op jit(solution)/shard_map/ppermute | solution.py:42
  5.5 5.7 %collective-permute-start.18 = (f32[128,256]{1,0:T(8,128)S(1)}, f32[128,256]{1,0:T(8,128)S(1)}, u32[]{:S(2)}, u32[]{:S(2)}) collective-permute-start(f32[128,256]{1,0:T(8,128)S(1)} %get-tuple-element.44), channel_id=1, source_target_pairs={{0,1},{1,0},{2,3},{3,2},{4,5},{5,4},{6,7},{7,6},{8,9},{9,8},{10,11... | collective-permute-start | bytes 393224 | tf_op jit(solution)/shard_map/ppermute | solution.py:42
  6.0 5.5 %collective-permute-start.1 = (f32[64,256]{1,0:T(8,128)S(1)}, f32[64,256]{1,0:T(8,128)S(1)}, u32[]{:S(2)}, u32[]{:S(2)}) collective-permute-start(f32[64,256]{1,0:T(8,128)S(1)} %slice.65), channel_id=1, source_target_pairs={{0,2},{1,3},{2,0},{3,1},{4,6},{5,7},{6,4},{7,5},{8,10},{9,11},{10,... | collective-permute-start | bytes 196616 | tf_op jit(solution)/shard_map/ppermute | solution.py:42
  9.0 5.5 %collective-permute-start.7 = (f32[64,256]{1,0:T(8,128)S(1)}, f32[64,256]{1,0:T(8,128)S(1)}, u32[]{:S(2)}, u32[]{:S(2)}) collective-permute-start(f32[64,256]{1,0:T(8,128)S(1)} %slice.67), channel_id=1, source_target_pairs={{0,2},{1,3},{2,0},{3,1},{4,6},{5,7},{6,4},{7,5},{8,10},{9,11},{10,... | collective-permute-start | bytes 196616 | tf_op jit(solution)/shard_map/ppermute | solution.py:42
  9.2 7.5 %collective-permute-start.13 = (f32[64,256]{1,0:T(8,128)S(1)}, f32[64,256]{1,0:T(8,128)S(1)}, u32[]{:S(2)}, u32[]{:S(2)}) collective-permute-start(f32[64,256]{1,0:T(8,128)S(1)} %slice.69), channel_id=1, source_target_pairs={{0,2},{1,3},{2,0},{3,1},{4,6},{5,7},{6,4},{7,5},{8,10},{9,11},{10,... | collective-permute-start | bytes 196616 | tf_op jit(solution)/shard_map/ppermute | solution.py:42
  11.2 6.9 %collective-permute-start.19 = (f32[64,256]{1,0:T(8,128)S(1)}, f32[64,256]{1,0:T(8,128)S(1)}, u32[]{:S(2)}, u32[]{:S(2)}) collective-permute-start(f32[64,256]{1,0:T(8,128)S(1)} %slice.71), channel_id=1, source_target_pairs={{0,2},{1,3},{2,0},{3,1},{4,6},{5,7},{6,4},{7,5},{8,10},{9,11},{10,... | collective-permute-start | bytes 196616 | tf_op jit(solution)/shard_map/ppermute | solution.py:42
  11.4 8.4 %collective-permute-start.2 = (f32[64,256]{1,0:T(8,128)S(1)}, f32[64,256]{1,0:T(8,128)S(1)}, u32[]{:S(2)}, u32[]{:S(2)}) collective-permute-start(f32[64,256]{1,0:T(8,128)S(1)} %slice_add_fusion.7), channel_id=1, source_target_pairs={{0,4},{1,5},{2,6},{3,7},{4,0},{5,1},{6,2},{7,3},{8,12},{9,13},{10,... | collective-permute-start | bytes 196616 | tf_op jit(solution)/shard_map/ppermute | solution.py:42
  14.5 10.7 %collective-permute-start.8 = (f32[64,256]{1,0:T(8,128)S(1)}, f32[64,256]{1,0:T(8,128)S(1)}, u32[]{:S(2)}, u32[]{:S(2)}) collective-permute-start(f32[64,256]{1,0:T(8,128)S(1)} %slice_add_fusion.6), channel_id=1, source_target_pairs={{0,4},{1,5},{2,6},{3,7},{4,0},{5,1},{6,2},{7,3},{8,12},{9,13},{10,... | collective-permute-start | bytes 196616 | tf_op jit(solution)/shard_map/ppermute | solution.py:42
  16.7 9.3 %collective-permute-start.14 = (f32[64,256]{1,0:T(8,128)S(1)}, f32[64,256]{1,0:T(8,128)S(1)}, u32[]{:S(2)}, u32[]{:S(2)}) collective-permute-start(f32[64,256]{1,0:T(8,128)S(1)} %slice_add_fusion.5), channel_id=1, source_target_pairs={{0,4},{1,5},{2,6},{3,7},{4,0},{5,1},{6,2},{7,3},{8,12},{9,13},{10,... | collective-permute-start | bytes 196616 | tf_op jit(solution)/shard_map/ppermute | solution.py:42
  18.1 8.6 %collective-permute-start.20 = (f32[64,256]{1,0:T(8,128)S(1)}, f32[64,256]{1,0:T(8,128)S(1)}, u32[]{:S(2)}, u32[]{:S(2)}) collective-permute-start(f32[64,256]{1,0:T(8,128)S(1)} %slice_add_fusion.4), channel_id=1, source_target_pairs={{0,4},{1,5},{2,6},{3,7},{4,0},{5,1},{6,2},{7,3},{8,12},{9,13},{10,... | collective-permute-start | bytes 196616 | tf_op jit(solution)/shard_map/ppermute | solution.py:42
  19.8 7.0 %collective-permute-start.4 = (f32[64,256]{1,0:T(8,128)S(1)}, f32[64,256]{1,0:T(8,128)S(1)}, u32[]{:S(2)}, u32[]{:S(2)}) collective-permute-start(f32[64,256]{1,0:T(8,128)S(1)} %add.86.more_0_), channel_id=1, source_target_pairs={{0,1},{1,0},{2,3},{3,2},{4,5},{5,4},{6,7},{7,6},{8,9},{9,8},{10,11... | collective-permute-start | bytes 196616 | tf_op jit(solution)/shard_map/ppermute | solution.py:42
  19.9 8.4 %collective-permute-start.3 = (f32[64,256]{1,0:T(8,128)S(1)}, f32[64,256]{1,0:T(8,128)S(1)}, u32[]{:S(2)}, u32[]{:S(2)}) collective-permute-start(f32[64,256]{1,0:T(8,128)S(1)} %add.86.more_0_), channel_id=1, source_target_pairs={{0,2},{1,3},{2,0},{3,1},{4,6},{5,7},{6,4},{7,5},{8,10},{9,11},{10,... | collective-permute-start | bytes 196616 | tf_op jit(solution)/shard_map/ppermute | solution.py:42
  25.2 3.7 %collective-permute-start.10 = (f32[64,256]{1,0:T(8,128)S(1)}, f32[64,256]{1,0:T(8,128)S(1)}, u32[]{:S(2)}, u32[]{:S(2)}) collective-permute-start(f32[64,256]{1,0:T(8,128)S(1)} %add.89.more_4_), channel_id=1, source_target_pairs={{0,1},{1,0},{2,3},{3,2},{4,5},{5,4},{6,7},{7,6},{8,9},{9,8},{10,11... | collective-permute-start | bytes 196616 | tf_op jit(solution)/shard_map/ppermute | solution.py:42
  26.1 4.6 %collective-permute-start.9 = (f32[64,256]{1,0:T(8,128)S(1)}, f32[64,256]{1,0:T(8,128)S(1)}, u32[]{:S(2)}, u32[]{:S(2)}) collective-permute-start(f32[64,256]{1,0:T(8,128)S(1)} %add.89.more_4_), channel_id=1, source_target_pairs={{0,2},{1,3},{2,0},{3,1},{4,6},{5,7},{6,4},{7,5},{8,10},{9,11},{10,... | collective-permute-start | bytes 196616 | tf_op jit(solution)/shard_map/ppermute | solution.py:42
  26.8 3.9 %collective-permute-start.16 = (f32[64,256]{1,0:T(8,128)S(1)}, f32[64,256]{1,0:T(8,128)S(1)}, u32[]{:S(2)}, u32[]{:S(2)}) collective-permute-start(f32[64,256]{1,0:T(8,128)S(1)} %add.92.more_8_), channel_id=1, source_target_pairs={{0,1},{1,0},{2,3},{3,2},{4,5},{5,4},{6,7},{7,6},{8,9},{9,8},{10,11... | collective-permute-start | bytes 196616 | tf_op jit(solution)/shard_map/ppermute | solution.py:42
  26.8 5.3 %collective-permute-start.15 = (f32[64,256]{1,0:T(8,128)S(1)}, f32[64,256]{1,0:T(8,128)S(1)}, u32[]{:S(2)}, u32[]{:S(2)}) collective-permute-start(f32[64,256]{1,0:T(8,128)S(1)} %add.92.more_8_), channel_id=1, source_target_pairs={{0,2},{1,3},{2,0},{3,1},{4,6},{5,7},{6,4},{7,5},{8,10},{9,11},{10,... | collective-permute-start | bytes 196616 | tf_op jit(solution)/shard_map/ppermute | solution.py:42
  28.3 4.8 %collective-permute-start.21 = (f32[64,256]{1,0:T(8,128)S(1)}, f32[64,256]{1,0:T(8,128)S(1)}, u32[]{:S(2)}, u32[]{:S(2)}) collective-permute-start(f32[64,256]{1,0:T(8,128)S(1)} %add.95.more_12_), channel_id=1, source_target_pairs={{0,2},{1,3},{2,0},{3,1},{4,6},{5,7},{6,4},{7,5},{8,10},{9,11},{10,... | collective-permute-start | bytes 196616 | tf_op jit(solution)/shard_map/ppermute | solution.py:42
  28.9 4.2 %collective-permute-start.22 = (f32[64,256]{1,0:T(8,128)S(1)}, f32[64,256]{1,0:T(8,128)S(1)}, u32[]{:S(2)}, u32[]{:S(2)}) collective-permute-start(f32[64,256]{1,0:T(8,128)S(1)} %add.95.more_12_), channel_id=1, source_target_pairs={{0,1},{1,0},{2,3},{3,2},{4,5},{5,4},{6,7},{7,6},{8,9},{9,8},{10,11... | collective-permute-start | bytes 196616 | tf_op jit(solution)/shard_map/ppermute | solution.py:42
  30.7 2.5 %collective-permute-start.5 = (f32[64,256]{1,0:T(8,128)S(1)}, f32[64,256]{1,0:T(8,128)S(1)}, u32[]{:S(2)}, u32[]{:S(2)}) collective-permute-start(f32[64,256]{1,0:T(8,128)S(1)} %collective-permute-done.3.more_1_), channel_id=1, source_target_pairs={{0,1},{1,0},{2,3},{3,2},{4,5},{5,4},{6,7},{7,6},{8,9},{9,8},{10,11... | collective-permute-start | bytes 196616 | tf_op jit(solution)/shard_map/ppermute | solution.py:42
  30.7 2.5 %collective-permute-start.11 = (f32[64,256]{1,0:T(8,128)S(1)}, f32[64,256]{1,0:T(8,128)S(1)}, u32[]{:S(2)}, u32[]{:S(2)}) collective-permute-start(f32[64,256]{1,0:T(8,128)S(1)} %collective-permute-done.9.more_5_), channel_id=1, source_target_pairs={{0,1},{1,0},{2,3},{3,2},{4,5},{5,4},{6,7},{7,6},{8,9},{9,8},{10,11... | collective-permute-start | bytes 196616 | tf_op jit(solution)/shard_map/ppermute | solution.py:42
  35.3 7.2 %collective-permute-start.24 = (f32[200,256]{1,0:T(8,128)S(1)}, f32[200,256]{1,0:T(8,128)S(1)}, u32[]{:S(2)}, u32[]{:S(2)}) collective-permute-start(f32[200,256]{1,0:T(8,128)S(1)} %get-tuple-element.45), channel_id=1, source_target_pairs={{0,8},{8,0},{16,24},{24,16},{1,9},{9,1},{17,25},{25,17},{2,10},{10... | collective-permute-start | bytes 614408 | tf_op jit(solution)/shard_map/ppermute | solution.py:42
  37.1 7.3 %collective-permute-start.26 = (f32[192,256]{1,0:T(8,128)S(1)}, f32[192,256]{1,0:T(8,128)S(1)}, u32[]{:S(2)}, u32[]{:S(2)}) collective-permute-start(f32[192,256]{1,0:T(8,128)S(1)} %get-tuple-element.46), channel_id=1, source_target_pairs={{0,16},{8,24},{16,0},{24,8},{1,17},{9,25},{17,1},{25,9},{2,18},{10... | collective-permute-start | bytes 589832 | tf_op jit(solution)/shard_map/ppermute | solution.py:42
  42.6 9.1 %collective-permute-start.25 = (f32[200,256]{1,0:T(8,128)S(1)}, f32[200,256]{1,0:T(8,128)S(1)}, u32[]{:S(2)}, u32[]{:S(2)}) collective-permute-start(f32[200,256]{1,0:T(8,128)S(1)} %add.96.a_ref.refs_0_), channel_id=1, source_target_pairs={{0,16},{8,24},{16,0},{24,8},{1,17},{9,25},{17,1},{25,9},{2,18},{10... | collective-permute-start | bytes 614408 | tf_op jit(solution)/shard_map/ppermute | solution.py:42
  44.4 7.2 %collective-permute-start.27 = (f32[192,256]{1,0:T(8,128)S(1)}, f32[192,256]{1,0:T(8,128)S(1)}, u32[]{:S(2)}, u32[]{:S(2)}) collective-permute-start(f32[192,256]{1,0:T(8,128)S(1)} %add.97.refs_2_), channel_id=1, source_target_pairs={{0,8},{8,0},{16,24},{24,16},{1,9},{9,1},{17,25},{25,17},{2,10},{10... | collective-permute-start | bytes 589832 | tf_op jit(solution)/shard_map/ppermute | solution.py:42
  58.8 2.5 %collective-permute-start.34 = (f32[128,256]{1,0:T(8,128)S(1)}, f32[128,256]{1,0:T(8,128)S(1)}, u32[]{:S(2)}, u32[]{:S(2)}) collective-permute-start(f32[128,256]{1,0:T(8,128)S(1)} %get-tuple-element.57), channel_id=1, source_target_pairs={{0,1},{1,0},{2,3},{3,2},{4,5},{5,4},{6,7},{7,6},{8,9},{9,8},{10,11... | collective-permute-start | bytes 393224 | tf_op jit(solution)/shard_map/ppermute | solution.py:42
  59.3 3.1 %collective-permute-start.40 = (f32[128,256]{1,0:T(8,128)S(1)}, f32[128,256]{1,0:T(8,128)S(1)}, u32[]{:S(2)}, u32[]{:S(2)}) collective-permute-start(f32[128,256]{1,0:T(8,128)S(1)} %get-tuple-element.59), channel_id=1, source_target_pairs={{0,1},{1,0},{2,3},{3,2},{4,5},{5,4},{6,7},{7,6},{8,9},{9,8},{10,11... | collective-permute-start | bytes 393224 | tf_op jit(solution)/shard_map/ppermute | solution.py:42
  59.4 4.1 %collective-permute-start.46 = (f32[128,256]{1,0:T(8,128)S(1)}, f32[128,256]{1,0:T(8,128)S(1)}, u32[]{:S(2)}, u32[]{:S(2)}) collective-permute-start(f32[128,256]{1,0:T(8,128)S(1)} %get-tuple-element.61), channel_id=1, source_target_pairs={{0,1},{1,0},{2,3},{3,2},{4,5},{5,4},{6,7},{7,6},{8,9},{9,8},{10,11... | collective-permute-start | bytes 393224 | tf_op jit(solution)/shard_map/ppermute | solution.py:42
  60.2 5.0 %collective-permute-start.29 = (f32[64,256]{1,0:T(8,128)S(1)}, f32[64,256]{1,0:T(8,128)S(1)}, u32[]{:S(2)}, u32[]{:S(2)}) collective-permute-start(f32[64,256]{1,0:T(8,128)S(1)} %slice.73), channel_id=1, source_target_pairs={{0,2},{1,3},{2,0},{3,1},{4,6},{5,7},{6,4},{7,5},{8,10},{9,11},{10,... | collective-permute-start | bytes 196616 | tf_op jit(solution)/shard_map/ppermute | solution.py:42
  61.3 6.0 %collective-permute-start.35 = (f32[64,256]{1,0:T(8,128)S(1)}, f32[64,256]{1,0:T(8,128)S(1)}, u32[]{:S(2)}, u32[]{:S(2)}) collective-permute-start(f32[64,256]{1,0:T(8,128)S(1)} %slice.75), channel_id=1, source_target_pairs={{0,2},{1,3},{2,0},{3,1},{4,6},{5,7},{6,4},{7,5},{8,10},{9,11},{10,... | collective-permute-start | bytes 196616 | tf_op jit(solution)/shard_map/ppermute | solution.py:42
  62.4 6.3 %collective-permute-start.41 = (f32[64,256]{1,0:T(8,128)S(1)}, f32[64,256]{1,0:T(8,128)S(1)}, u32[]{:S(2)}, u32[]{:S(2)}) collective-permute-start(f32[64,256]{1,0:T(8,128)S(1)} %slice.77), channel_id=1, source_target_pairs={{0,2},{1,3},{2,0},{3,1},{4,6},{5,7},{6,4},{7,5},{8,10},{9,11},{10,... | collective-permute-start | bytes 196616 | tf_op jit(solution)/shard_map/ppermute | solution.py:42
  63.6 6.8 %collective-permute-start.47 = (f32[64,256]{1,0:T(8,128)S(1)}, f32[64,256]{1,0:T(8,128)S(1)}, u32[]{:S(2)}, u32[]{:S(2)}) collective-permute-start(f32[64,256]{1,0:T(8,128)S(1)} %slice.79), channel_id=1, source_target_pairs={{0,2},{1,3},{2,0},{3,1},{4,6},{5,7},{6,4},{7,5},{8,10},{9,11},{10,... | collective-permute-start | bytes 196616 | tf_op jit(solution)/shard_map/ppermute | solution.py:42
  65.2 10.5 %collective-permute-start.30 = (f32[64,256]{1,0:T(8,128)S(1)}, f32[64,256]{1,0:T(8,128)S(1)}, u32[]{:S(2)}, u32[]{:S(2)}) collective-permute-start(f32[64,256]{1,0:T(8,128)S(1)} %slice_add_fusion.3), channel_id=1, source_target_pairs={{0,4},{1,5},{2,6},{3,7},{4,0},{5,1},{6,2},{7,3},{8,12},{9,13},{10,... | collective-permute-start | bytes 196616 | tf_op jit(solution)/shard_map/ppermute | solution.py:42
  67.3 10.5 %collective-permute-start.36 = (f32[64,256]{1,0:T(8,128)S(1)}, f32[64,256]{1,0:T(8,128)S(1)}, u32[]{:S(2)}, u32[]{:S(2)}) collective-permute-start(f32[64,256]{1,0:T(8,128)S(1)} %slice_add_fusion.2), channel_id=1, source_target_pairs={{0,4},{1,5},{2,6},{3,7},{4,0},{5,1},{6,2},{7,3},{8,12},{9,13},{10,... | collective-permute-start | bytes 196616 | tf_op jit(solution)/shard_map/ppermute | solution.py:42
  68.7 10.1 %collective-permute-start.42 = (f32[64,256]{1,0:T(8,128)S(1)}, f32[64,256]{1,0:T(8,128)S(1)}, u32[]{:S(2)}, u32[]{:S(2)}) collective-permute-start(f32[64,256]{1,0:T(8,128)S(1)} %slice_add_fusion.1), channel_id=1, source_target_pairs={{0,4},{1,5},{2,6},{3,7},{4,0},{5,1},{6,2},{7,3},{8,12},{9,13},{10,... | collective-permute-start | bytes 196616 | tf_op jit(solution)/shard_map/ppermute | solution.py:42
  70.4 9.2 %collective-permute-start.48 = (f32[64,256]{1,0:T(8,128)S(1)}, f32[64,256]{1,0:T(8,128)S(1)}, u32[]{:S(2)}, u32[]{:S(2)}) collective-permute-start(f32[64,256]{1,0:T(8,128)S(1)} %slice_add_fusion), channel_id=1, source_target_pairs={{0,4},{1,5},{2,6},{3,7},{4,0},{5,1},{6,2},{7,3},{8,12},{9,13},{10,... | collective-permute-start | bytes 196616 | tf_op jit(solution)/shard_map/ppermute | solution.py:42
  75.7 3.9 %collective-permute-start.32 = (f32[64,256]{1,0:T(8,128)S(1)}, f32[64,256]{1,0:T(8,128)S(1)}, u32[]{:S(2)}, u32[]{:S(2)}) collective-permute-start(f32[64,256]{1,0:T(8,128)S(1)} %add.100.more_0_), channel_id=1, source_target_pairs={{0,1},{1,0},{2,3},{3,2},{4,5},{5,4},{6,7},{7,6},{8,9},{9,8},{10,11... | collective-permute-start | bytes 196616 | tf_op jit(solution)/shard_map/ppermute | solution.py:42
  75.8 5.3 %collective-permute-start.31 = (f32[64,256]{1,0:T(8,128)S(1)}, f32[64,256]{1,0:T(8,128)S(1)}, u32[]{:S(2)}, u32[]{:S(2)}) collective-permute-start(f32[64,256]{1,0:T(8,128)S(1)} %add.100.more_0_), channel_id=1, source_target_pairs={{0,2},{1,3},{2,0},{3,1},{4,6},{5,7},{6,4},{7,5},{8,10},{9,11},{10,... | collective-permute-start | bytes 196616 | tf_op jit(solution)/shard_map/ppermute | solution.py:42
  77.8 3.9 %collective-permute-start.38 = (f32[64,256]{1,0:T(8,128)S(1)}, f32[64,256]{1,0:T(8,128)S(1)}, u32[]{:S(2)}, u32[]{:S(2)}) collective-permute-start(f32[64,256]{1,0:T(8,128)S(1)} %add.103.more_4_), channel_id=1, source_target_pairs={{0,1},{1,0},{2,3},{3,2},{4,5},{5,4},{6,7},{7,6},{8,9},{9,8},{10,11... | collective-permute-start | bytes 196616 | tf_op jit(solution)/shard_map/ppermute | solution.py:42
  78.8 4.6 %collective-permute-start.37 = (f32[64,256]{1,0:T(8,128)S(1)}, f32[64,256]{1,0:T(8,128)S(1)}, u32[]{:S(2)}, u32[]{:S(2)}) collective-permute-start(f32[64,256]{1,0:T(8,128)S(1)} %add.103.more_4_), channel_id=1, source_target_pairs={{0,2},{1,3},{2,0},{3,1},{4,6},{5,7},{6,4},{7,5},{8,10},{9,11},{10,... | collective-permute-start | bytes 196616 | tf_op jit(solution)/shard_map/ppermute | solution.py:42
  79.6 3.9 %collective-permute-start.44 = (f32[64,256]{1,0:T(8,128)S(1)}, f32[64,256]{1,0:T(8,128)S(1)}, u32[]{:S(2)}, u32[]{:S(2)}) collective-permute-start(f32[64,256]{1,0:T(8,128)S(1)} %add.106.more_8_), channel_id=1, source_target_pairs={{0,1},{1,0},{2,3},{3,2},{4,5},{5,4},{6,7},{7,6},{8,9},{9,8},{10,11... | collective-permute-start | bytes 196616 | tf_op jit(solution)/shard_map/ppermute | solution.py:42
  79.6 5.3 %collective-permute-start.43 = (f32[64,256]{1,0:T(8,128)S(1)}, f32[64,256]{1,0:T(8,128)S(1)}, u32[]{:S(2)}, u32[]{:S(2)}) collective-permute-start(f32[64,256]{1,0:T(8,128)S(1)} %add.106.more_8_), channel_id=1, source_target_pairs={{0,2},{1,3},{2,0},{3,1},{4,6},{5,7},{6,4},{7,5},{8,10},{9,11},{10,... | collective-permute-start | bytes 196616 | tf_op jit(solution)/shard_map/ppermute | solution.py:42
  81.0 4.8 %collective-permute-start.49 = (f32[64,256]{1,0:T(8,128)S(1)}, f32[64,256]{1,0:T(8,128)S(1)}, u32[]{:S(2)}, u32[]{:S(2)}) collective-permute-start(f32[64,256]{1,0:T(8,128)S(1)} %add.109.more_12_), channel_id=1, source_target_pairs={{0,2},{1,3},{2,0},{3,1},{4,6},{5,7},{6,4},{7,5},{8,10},{9,11},{10,... | collective-permute-start | bytes 196616 | tf_op jit(solution)/shard_map/ppermute | solution.py:42
  81.7 4.2 %collective-permute-start.50 = (f32[64,256]{1,0:T(8,128)S(1)}, f32[64,256]{1,0:T(8,128)S(1)}, u32[]{:S(2)}, u32[]{:S(2)}) collective-permute-start(f32[64,256]{1,0:T(8,128)S(1)} %add.109.more_12_), channel_id=1, source_target_pairs={{0,1},{1,0},{2,3},{3,2},{4,5},{5,4},{6,7},{7,6},{8,9},{9,8},{10,11... | collective-permute-start | bytes 196616 | tf_op jit(solution)/shard_map/ppermute | solution.py:42
  88.1 7.2 %collective-permute-start.52 = (f32[200,256]{1,0:T(8,128)S(1)}, f32[200,256]{1,0:T(8,128)S(1)}, u32[]{:S(2)}, u32[]{:S(2)}) collective-permute-start(f32[200,256]{1,0:T(8,128)S(1)} %get-tuple-element.62), channel_id=1, source_target_pairs={{0,8},{8,0},{16,24},{24,16},{1,9},{9,1},{17,25},{25,17},{2,10},{10... | collective-permute-start | bytes 614408 | tf_op jit(solution)/shard_map/ppermute | solution.py:42
  88.7 7.2 %collective-permute-start.54 = (f32[192,256]{1,0:T(8,128)S(1)}, f32[192,256]{1,0:T(8,128)S(1)}, u32[]{:S(2)}, u32[]{:S(2)}) collective-permute-start(f32[192,256]{1,0:T(8,128)S(1)} %get-tuple-element.63), channel_id=1, source_target_pairs={{0,16},{8,24},{16,0},{24,8},{1,17},{9,25},{17,1},{25,9},{2,18},{10... | collective-permute-start | bytes 589832 | tf_op jit(solution)/shard_map/ppermute | solution.py:42
  95.4 7.7 %collective-permute-start.53 = (f32[200,256]{1,0:T(8,128)S(1)}, f32[200,256]{1,0:T(8,128)S(1)}, u32[]{:S(2)}, u32[]{:S(2)}) collective-permute-start(f32[200,256]{1,0:T(8,128)S(1)} %add.110.a_ref.refs_0_), channel_id=1, source_target_pairs={{0,16},{8,24},{16,0},{24,8},{1,17},{9,25},{17,1},{25,9},{2,18},{10... | collective-permute-start | bytes 614408 | tf_op jit(solution)/shard_map/ppermute | solution.py:42
  96.0 7.1 %collective-permute-start.55 = (f32[192,256]{1,0:T(8,128)S(1)}, f32[192,256]{1,0:T(8,128)S(1)}, u32[]{:S(2)}, u32[]{:S(2)}) collective-permute-start(f32[192,256]{1,0:T(8,128)S(1)} %add.111.refs_2_), channel_id=1, source_target_pairs={{0,8},{8,0},{16,24},{24,16},{1,9},{9,1},{17,25},{25,17},{2,10},{10... | collective-permute-start | bytes 589832 | tf_op jit(solution)/shard_map/ppermute | solution.py:42
  (11 other events, 15.7 us)

commit v4 on v3

--- a/solution.py
+++ b/solution.py
@@ -9,6 +9,8 @@
 ITERS = 2
 CHUNKS = 4
 SUBLANES = 8
+LOW = 1e-3
+NEAR, FAR = 1.25, 4.2
 VMEM_BYTES = 16 << 20
 
 NN = (((1,), (0,)), ((), ()))
@@ -92,26 +94,34 @@
             out_refs[2 * c + p // (blocks // 2)][pl.ds(at, share), :] = left[p][c * share : (c + 1) * share]
 
 
-def head_kernel(blocks, snap_ref, basis_ref, data_ref, top_ref, rest_ref, *more):
-    *left_refs, sems = more
-    tall = data_ref.shape[0] // blocks
+def fetches(snap_ref, data, sems, blocks):
+    tall = data.shape[0] // blocks
     low = lowest(blocks)
-    copies = []
-    for p in range(blocks):
-        copies.append(
-            pltpu.make_async_copy(
-                snap_ref.at[pl.ds(pl.multiple_of((p ^ low) * tall, tall), tall), :],
-                data_ref.at[pl.ds(p * tall, tall), :],
-                sems.at[p],
-            )
+    return [
+        pltpu.make_async_copy(
+            snap_ref.at[pl.ds(pl.multiple_of((p ^ low) * tall, tall), tall), :],
+            data.at[pl.ds(p * tall, tall), :],
+            sems.at[p],
         )
-        copies[-1].start()
-    basis = split(basis_ref[...], 2)
+        for p in range(blocks)
+    ]
+
+
+def head_kernel(blocks, snap_ref, basis_ref, data, top_ref, rest_ref, *more):
+    *left_refs, basis, sems, basis_sem = more
+    tall = data.shape[0] // blocks
+    copies = fetches(snap_ref, data, sems, blocks)
+    first = pltpu.make_async_copy(basis_ref, basis, basis_sem)
+    first.start()
+    for copy in copies:
+        copy.start()
+    first.wait()
+    basis = split(basis[...], 2)
     left = []
     for p in range(blocks):
+        at = pl.ds(p * tall, tall)
         copies[p].wait()
-        block = split(data_ref[pl.ds(p * tall, tall), :], 2)
-        top_ref[pl.ds(p * tall, tall), :], rest_ref[pl.ds(p * tall, tall), :] = block
+        top_ref[at, :], rest_ref[at, :] = block = split(data[at, :], 2)
         left.append(dot3(block, basis))
     write_left(left, left_refs, blocks)
 
@@ -134,7 +144,7 @@
     left = left_top_ref[...], left_rest_ref[...]
     right = dot3(left, (top_ref[...], rest_ref[...]), TN)
     cross = dot(left[0], left[1], TN)
-    gram = dot(left[0], left[0], TN) + (cross + cross.T)
+    gram = dot(left[0], left[0], TN) + (cross + cross.T + dot(left[1], left[1], TN))
     pack(gram, right, a_ref, b_ref)
 
 
@@ -175,22 +185,36 @@
 
 
 def norm_bound(x):
-    size = jnp.abs(x)
-    return jnp.minimum(jnp.max(jnp.sum(size, 0, keepdims=True)), jnp.max(jnp.sum(size, 1, keepdims=True)))
-
-
-def converge(inverse, error, enough):
+    return jnp.max(jnp.sum(jnp.abs(x), 0, keepdims=True))
+
+
+def chebyshev(matrix, square, low, high):
+    at_zero, slope = (high + low) / (high - low), 2.0 / (high - low)
+    growth = 2.0 * at_zero * at_zero - 1.0
+    a, b = 4.0 * at_zero * slope / growth, 2.0 * slope * slope / growth
+    return a, b, identity(matrix.shape[0]).astype(f32) - a * matrix + b * square, growth
+
+
+def double(inverse, error, growth):
+    growth = 2.0 * growth * growth - 1.0
+    eye = identity(error.shape[0]).astype(f32)
+    terms = split(error, 2)
+    inverse = (1.0 + 1.0 / growth) * (inverse + dot3(split(inverse, 2), terms))
+    error = (1.0 + 1.0 / growth) * dot3(terms, terms) - (1.0 / growth) * eye
+    return inverse, error, growth
+
+
+def converge(inverse, error, growth, enough):
     def more(state):
-        count, size, _, _ = state
+        count, size, *_ = state
         return jnp.logical_and(count < 40, size > enough)
 
-    def double(state):
-        count, _, inverse, error = state
-        size = jnp.sum(error * error)
-        terms = split(error, 2)
-        return count + 1, size, inverse + dot3(split(inverse, 2), terms), dot3(terms, terms)
-
-    _, size, inverse, _ = lax.while_loop(more, double, (0, jnp.float32(1e9), inverse, error))
+    def body(state):
+        count, _, *state = state
+        inverse, error, growth = double(*state)
+        return count + 1, jnp.sum(state[1] * state[1]), inverse, error, jnp.minimum(growth, 1e4)
+
+    _, size, inverse, *_ = lax.while_loop(more, body, (0, jnp.float32(1e9), inverse, error, growth))
     return inverse, size
 
 
@@ -199,63 +223,67 @@
     return jnp.sum(on_diag, 1, keepdims=True), jnp.sum(on_diag, 0, keepdims=True)
 
 
-def plain_start(scaled):
+def invert(scaled, enough):
+    terms = split(scaled, 2)
     eye = identity(scaled.shape[0]).astype(f32)
-    step = 1.9 / norm_bound(scaled)
-    return step * eye, eye - step * scaled
-
-
-def inverse_kernel(a_ref, out_ref, size_ref):
+    high = norm_bound(scaled)
+    a, b, error, growth = chebyshev(scaled, dot3(terms, terms), LOW * high, high)
+    return converge(a * eye - b * scaled, error, growth, enough)
+
+
+def inverse_kernel(a_ref, level_ref, out_ref, level_out_ref):
+    level_out_ref[...] = level_ref[...]
     gram = unpack_gram(a_ref[...])
     down, across = diagonals(gram)
     down, across = lax.rsqrt(down), lax.rsqrt(across)
-    inverse, size = converge(*plain_start(gram * down * across), 1e-2)
-    out_ref[...] = inverse * down * across
-    size_ref[...] = jnp.full(size_ref.shape, size)
-
-
-def solve(gram, right, start, start_size):
+    out_ref[...] = invert(gram * down * across, 0.5)[0] * down * across
+
+
+def refine(exact, factors, right, scale, out):
+    def again(state):
+        count, size, _ = state
+        return jnp.logical_and(count < 60, size > 2e-5 * scale)
+
+    def body(state):
+        count, _, out = state
+        rest = right - dot6(exact, split(out, 3))
+        return count + 1, jnp.sum(rest * rest), out + dot3(factors, split(rest, 2))
+
+    return lax.while_loop(again, body, (0, 2.0 * scale, out))[1:]
+
+
+def solve(gram, right, start):
     down, across = diagonals(gram)
     start = start * jnp.sqrt(down) * jnp.sqrt(across)
     down, across = lax.rsqrt(down), lax.rsqrt(across)
     scaled = gram * down * across
     right = right * down
+    scale = jnp.sum(right * right)
     exact = split(scaled, 3)
-    eye = identity(gram.shape[0]).astype(f32)
     product = dot6(exact, split(start, 3))
     terms = split(product, 2)
-    square = dot3(terms, terms)
-    bound = jnp.minimum(norm_bound(product), jnp.sqrt(norm_bound(square)))
-    good = jnp.logical_and(start_size <= 1e-2, bound < 1e3)
-    step = 2.0 / (1.0 + bound)
-
-    def from_start():
-        error = eye - (2.0 * step) * product + (step * step) * square
-        return (2.0 * step) * start - (step * step) * dot3(split(start, 2), terms), error
-
-    inverse, error = lax.cond(good, from_start, lambda: plain_start(scaled))
-    inverse, _ = converge(inverse, error, 1e-4)
-    factors = split(inverse, 2)
-    out = dot3(factors, split(right, 2))
-    scale = jnp.sum(right * right)
-
-    def again(state):
-        count, size, _ = state
-        return jnp.logical_and(count < 20, size > 1e-6 * scale)
-
-    def refine(state):
-        count, _, out = state
-        rest = right - dot6(exact, split(out, 3))
-        return count + 1, jnp.sum(rest * rest), out + dot3(factors, split(rest, 2))
-
-    _, _, out = lax.while_loop(again, refine, (0, 2.0 * scale, out))
-    return out * down
+    follow = dot3(split(start, 2), terms)
+    a, b, error, growth = chebyshev(product, dot3(terms, terms), NEAR, FAR)
+    inverse = a * start - b * follow
+    while growth < 1e3:
+        inverse, error, growth = double(inverse, error, growth)
+    factors, sides = split(inverse, 2), split(right, 2)
+    out = dot3(factors, sides)
+    rest = right - dot6(exact, split(out, 3))
+    size = jnp.sum(rest * rest)
+    out = out + dot3(factors, split(rest, 2))
+
+    def slow():
+        factors = split(invert(scaled, 0.1)[0], 2)
+        return refine(exact, factors, right, scale, dot3(factors, sides))[1]
+
+    return lax.cond(size <= 2e-5 * scale, lambda: out, slow) * down
 
 
 def weights_of(refs):
-    a1_ref, a2_ref, b1_ref, b2_ref, start_ref, size_ref = refs
+    a1_ref, a2_ref, b1_ref, b2_ref, start_ref = refs
     a, b = a1_ref[...] + a2_ref[...], b1_ref[...] + b2_ref[...]
-    return solve(unpack_gram(a), unpack_right(a, b), start_ref[...], jnp.max(size_ref[...]))
+    return solve(unpack_gram(a), unpack_right(a, b), start_ref[...])
 
 
 def shrink(data, low_rank, level):
@@ -265,7 +293,7 @@
 
 
 def middle_kernel(blocks, *refs):
-    sum_refs, refs = refs[:6], refs[6:]
+    sum_refs, refs = refs[:5], refs[5:]
     left_top_ref, left_rest_ref, data_ref, level_ref, top_ref, rest_ref, *left_refs = refs
     tall = data_ref.shape[0] // blocks
     weights = split(weights_of(sum_refs), 2)
@@ -281,7 +309,7 @@
 
 
 def last_kernel(blocks, *refs):
-    sum_refs, refs = refs[:6], refs[6:]
+    sum_refs, refs = refs[:5], refs[5:]
     left_top_ref, left_rest_ref, data_ref, level_ref, low_rank_ref, sparse_ref, low_rank, sparse, sems = refs
     tall = data_ref.shape[0] // blocks
     low = lowest(blocks)
@@ -300,7 +328,7 @@
 
 
 VMEM = pl.BlockSpec(memory_space=pltpu.VMEM)
-ANY = pl.BlockSpec(memory_space=pl.ANY)
+HBM = pl.BlockSpec(memory_space=pltpu.HBM)
 
 
 def call(body, args, outs, in_specs=None, out_specs=None, scratch=(), cost=None, name=None):
@@ -320,7 +348,6 @@
     rows, cols = snapshots.shape
     rank = right_basis.shape[1]
     blocks = n_tm // 2
-    level = threshold[None, :]
     whole = [((rows, cols), bf16)] * 2
     a_rows = (rank + rank // 2 + SUBLANES) // 16 * 8 + SUBLANES
     lefts = [((rows // CHUNKS // 2, rank), f32)] * (2 * CHUNKS)
@@ -328,10 +355,15 @@
         functools.partial(head_kernel, blocks),
         (snapshots, right_basis),
         [((rows, cols), f32)] + whole + lefts,
-        in_specs=[ANY, VMEM],
-        scratch=[pltpu.SemaphoreType.DMA((blocks,))],
+        in_specs=[HBM] * 2,
+        scratch=[
+            pltpu.VMEM(right_basis.shape, f32),
+            pltpu.SemaphoreType.DMA((blocks,)),
+            pltpu.SemaphoreType.DMA,
+        ],
         name="head",
     )
+    level = threshold[None, :]
     for iteration in range(ITERS):
         pieces = sum_tm(list(zip(left[::2], left[1::2])), n_tm)
         a, b, left_top, left_rest = call(
@@ -341,23 +373,26 @@
             name="products",
         )
         sums = sum_rows(a, b, n_rows)
-        start = call(
+        start, level = call(
             inverse_kernel,
-            sums[:1],
-            [((rank, rank), f32), ((SUBLANES, 128), f32)],
+            (sums[0], level),
+            [((rank, rank), f32), (level.shape, f32)],
             cost=pl.CostEstimate(flops=80 * rank**3, bytes_accessed=rank * rank * 8, transcendentals=0),
             name="inverse",
         )
-        args = (*sums, *start, left_top, left_rest, data, level)
+        args = (*sums, start, left_top, left_rest, data, level)
         if iteration < ITERS - 1:
             top, rest, *left = call(
-                functools.partial(middle_kernel, blocks), args, whole + lefts, name="middle"
+                functools.partial(middle_kernel, blocks),
+                args,
+                whole + lefts,
+                name="middle",
             )
     return call(
         functools.partial(last_kernel, blocks),
         args,
         [((rows, cols), f32)] * 2,
-        out_specs=[ANY] * 2,
+        out_specs=[HBM] * 2,
         scratch=[pltpu.VMEM((rows, cols), f32)] * 2 + [pltpu.SemaphoreType.DMA((2 * blocks,))],
         name="last",
     )

time: 110 us -> 104 us (0.945)
  Pallas kernels: 28.3 us -> 19.7 us
  waiting for transfers between devices: 32.3 us -> 34.3 us
  starting transfers between devices: 44.9 us -> 46 us
    pallas_call x7, Pallas kernels: 28.3 us -> 19.7 us  [call(): pl.pallas_call(body, out_shape=[jax.ShapeDtypeStruct(shape, dtype) for sh...]
    ppermute x56, waiting for transfers between devices: 32.3 us -> 34.3 us  [swap(): return lax.ppermute(x, axis, [(i, i ^ bit) for i in range(size)])]
  transfers between devices with their start and end apart: 56 -> 56, of which waited for: 22 -> 24; matrix products, arithmetic and copies ran while one was open for 0% -> 0% of each run, Pallas kernels for 11% -> 6%
where the time goes in v4:
time: 104 us
  starting transfers between devices  46 us (44%)
  waiting for transfers between devices  34.3 us (33%)
  Pallas kernels  19.7 us (19%)
  local copies, waits for them, and re-layouts  2.22 us (2%)
  between operations  1.13 us (1%)
    ppermute x56, starting transfers between devices, swap(): return lax.ppermute(x, axis, [(i, i ^ bit) for i in range(size)])  46 us
    ppermute x56, waiting for transfers between devices, swap(): return lax.ppermute(x, axis, [(i, i ^ bit) for i in range(size)])  34.3 us
    pallas_call x7, Pallas kernels, call(): pl.pallas_call(body, out_shape=[jax.ShapeDtypeStruct(shape, dtype) for sh...  19.7 us
    unnamed x6, local copies, waits for them, and re-layouts  2.17 us
  transfers between devices with their start and end apart: 56, of which 24 were waited for; matrix products, arithmetic and copies ran while one was open for 0% of the time, Pallas kernels for 6%

profile of v4, /device:TPU:0, one launch (start us, length us, event | category | flops | bytes accessed | tf_op | source)
XLA Modules:
  0.0 103.7 jit_solution(16658454909446919951)
XLA Ops:
  0.6 1.2 %copy-done = f32[1024,256]{1,0:T(8,128)S(1)} copy-done((f32[1024,256]{1,0:T(8,128)S(1)}, f32[1024,256]{1,0:T(8,128)}, u32[]{:S(2)}) %copy-start) | copy-done | bytes 1048600
  1.9 0.9 copy-done.1
  2.8 1.6 %head.1 = (f32[1024,256]{1,0:T(8,128)S(1)}, bf16[1024,256]{1,0:T(8,128)(2,1)S(1)}, bf16[1024,256]{1,0:T(8,128)(2,1)S(1)}, f32[128,256]{1,0:T(8,128)S(1)}, f32[12...) custom-call(f32[1024,256]{1,0:T(8,128)S(1)} %copy-done, ...), custom_call_target="tpu_custom_call" | custom-call | tf_op jit(solution)/shard_map/head/pallas_call | solution.py:335
  6.0 3.0 %collective-permute-start.1 = (f32[64,256]{1,0:T(8,128)S(1)}, f32[64,256]{1,0:T(8,128)S(1)}, u32[]{:S(2)}, u32[]{:S(2)}) collective-permute-start(f32[64,256]{1,0:T(8,128)S(1)} %slice.65), channel_id=1, source_target_pairs={{0,2},{1,3},{2,0},{3,1},{4,6},{5,7},{6,4},{7,5},{8,10},{9,11},{10,... | collective-permute-start | bytes 196616 | tf_op jit(solution)/shard_map/ppermute | solution.py:44
  9.2 2.0 %collective-permute-start.13 = (f32[64,256]{1,0:T(8,128)S(1)}, f32[64,256]{1,0:T(8,128)S(1)}, u32[]{:S(2)}, u32[]{:S(2)}) collective-permute-start(f32[64,256]{1,0:T(8,128)S(1)} %slice.69), channel_id=1, source_target_pairs={{0,2},{1,3},{2,0},{3,1},{4,6},{5,7},{6,4},{7,5},{8,10},{9,11},{10,... | collective-permute-start | bytes 196616 | tf_op jit(solution)/shard_map/ppermute | solution.py:44
  11.5 3.1 %collective-permute-start.2 = (f32[64,256]{1,0:T(8,128)S(1)}, f32[64,256]{1,0:T(8,128)S(1)}, u32[]{:S(2)}, u32[]{:S(2)}) collective-permute-start(f32[64,256]{1,0:T(8,128)S(1)} %slice_add_fusion.7), channel_id=1, source_target_pairs={{0,4},{1,5},{2,6},{3,7},{4,0},{5,1},{6,2},{7,3},{8,12},{9,13},{10,... | collective-permute-start | bytes 196616 | tf_op jit(solution)/shard_map/ppermute | solution.py:44
  14.5 2.2 %collective-permute-start.8 = (f32[64,256]{1,0:T(8,128)S(1)}, f32[64,256]{1,0:T(8,128)S(1)}, u32[]{:S(2)}, u32[]{:S(2)}) collective-permute-start(f32[64,256]{1,0:T(8,128)S(1)} %slice_add_fusion.6), channel_id=1, source_target_pairs={{0,4},{1,5},{2,6},{3,7},{4,0},{5,1},{6,2},{7,3},{8,12},{9,13},{10,... | collective-permute-start | bytes 196616 | tf_op jit(solution)/shard_map/ppermute | solution.py:44
  16.8 1.4 %collective-permute-start.14 = (f32[64,256]{1,0:T(8,128)S(1)}, f32[64,256]{1,0:T(8,128)S(1)}, u32[]{:S(2)}, u32[]{:S(2)}) collective-permute-start(f32[64,256]{1,0:T(8,128)S(1)} %slice_add_fusion.5), channel_id=1, source_target_pairs={{0,4},{1,5},{2,6},{3,7},{4,0},{5,1},{6,2},{7,3},{8,12},{9,13},{10,... | collective-permute-start | bytes 196616 | tf_op jit(solution)/shard_map/ppermute | solution.py:44
  18.2 1.7 %collective-permute-start.20 = (f32[64,256]{1,0:T(8,128)S(1)}, f32[64,256]{1,0:T(8,128)S(1)}, u32[]{:S(2)}, u32[]{:S(2)}) collective-permute-start(f32[64,256]{1,0:T(8,128)S(1)} %slice_add_fusion.4), channel_id=1, source_target_pairs={{0,4},{1,5},{2,6},{3,7},{4,0},{5,1},{6,2},{7,3},{8,12},{9,13},{10,... | collective-permute-start | bytes 196616 | tf_op jit(solution)/shard_map/ppermute | solution.py:44
  19.9 2.8 %collective-permute-start.3 = (f32[64,256]{1,0:T(8,128)S(1)}, f32[64,256]{1,0:T(8,128)S(1)}, u32[]{:S(2)}, u32[]{:S(2)}) collective-permute-start(f32[64,256]{1,0:T(8,128)S(1)} %add.86.more_0_), channel_id=1, source_target_pairs={{0,2},{1,3},{2,0},{3,1},{4,6},{5,7},{6,4},{7,5},{8,10},{9,11},{10,... | collective-permute-start | bytes 196616 | tf_op jit(solution)/shard_map/ppermute | solution.py:44
  22.8 2.4 %collective-permute-done.8 = f32[64,256]{1,0:T(8,128)S(1)} collective-permute-done((f32[64,256]{1,0:T(8,128)S(1)}, f32[64,256]{1,0:T(8,128)S(1)}, u32[]{:S(2)}, u32[]{:S(2)}) %collective-permute-start.8) | collective-permute-done | bytes 65568 | tf_op jit(solution)/shard_map/ppermute | solution.py:44
  26.8 1.5 %collective-permute-start.15 = (f32[64,256]{1,0:T(8,128)S(1)}, f32[64,256]{1,0:T(8,128)S(1)}, u32[]{:S(2)}, u32[]{:S(2)}) collective-permute-start(f32[64,256]{1,0:T(8,128)S(1)} %add.92.more_8_), channel_id=1, source_target_pairs={{0,2},{1,3},{2,0},{3,1},{4,6},{5,7},{6,4},{7,5},{8,10},{9,11},{10,... | collective-permute-start | bytes 196616 | tf_op jit(solution)/shard_map/ppermute | solution.py:44
  28.9 1.8 %collective-permute-done.9.more_5_ = f32[64,256]{1,0:T(8,128)S(1)} collective-permute-done((f32[64,256]{1,0:T(8,128)S(1)}, f32[64,256]{1,0:T(8,128)S(1)}, u32[]{:S(2)}, u32[]{:S(2)}) %collective-permute-start.9) | collective-permute-done | bytes 65568 | tf_op jit(solution)/shard_map/ppermute | solution.py:44
  32.1 1.0 %collective-permute-done.21.more_13_ = f32[64,256]{1,0:T(8,128)S(1)} collective-permute-done((f32[64,256]{1,0:T(8,128)S(1)}, f32[64,256]{1,0:T(8,128)S(1)}, u32[]{:S(2)}, u32[]{:S(2)}) %collective-permute-start.21) | collective-permute-done | bytes 65568 | tf_op jit(solution)/shard_map/ppermute | solution.py:44
  33.4 1.0 %collective-permute-done.23.more_15_ = f32[64,256]{1,0:T(8,128)S(1)} collective-permute-done((f32[64,256]{1,0:T(8,128)S(1)}, f32[64,256]{1,0:T(8,128)S(1)}, u32[]{:S(2)}, u32[]{:S(2)}) %collective-permute-start.23) | collective-permute-done | bytes 65568 | tf_op jit(solution)/shard_map/ppermute | solution.py:44
  34.4 1.1 %products.2 = (f32[200,256]{1,0:T(8,128)S(1)}, f32[192,256]{1,0:T(8,128)S(1)}, bf16[1024,256]{1,0:T(8,128)(2,1)S(1)}, bf16[1024,256]{1,0:T(8,128)(2,1)S(1)}) custom-call(bf16[1024,256]{1,0:T(8,128)(2,1)S(1)} %get-tuple-element.35.top_ref, bf16[1024,256]{1,0:T(8,128)(2,1)S(1)} %get-tuple-element.36.rest_ref, f32[64,256]{1,0:T(8,128)S(1)} %add.86.more_0_, ...), custom_call_target="tpu_custom_call" | custom-call | tf_op jit(solution)/shard_map/products/pallas_call | solution.py:335
  35.5 1.8 %collective-permute-start.24 = (f32[200,256]{1,0:T(8,128)S(1)}, f32[200,256]{1,0:T(8,128)S(1)}, u32[]{:S(2)}, u32[]{:S(2)}) collective-permute-start(f32[200,256]{1,0:T(8,128)S(1)} %get-tuple-element.45), channel_id=1, source_target_pairs={{0,8},{8,0},{16,24},{24,16},{1,9},{9,1},{17,25},{25,17},{2,10},{10... | collective-permute-start | bytes 614408 | tf_op jit(solution)/shard_map/ppermute | solution.py:44
  37.3 1.5 %collective-permute-start.26 = (f32[192,256]{1,0:T(8,128)S(1)}, f32[192,256]{1,0:T(8,128)S(1)}, u32[]{:S(2)}, u32[]{:S(2)}) collective-permute-start(f32[192,256]{1,0:T(8,128)S(1)} %get-tuple-element.46), channel_id=1, source_target_pairs={{0,16},{8,24},{16,0},{24,8},{1,17},{9,25},{17,1},{25,9},{2,18},{10... | collective-permute-start | bytes 589832 | tf_op jit(solution)/shard_map/ppermute | solution.py:44
  38.8 3.9 %collective-permute-done.24 = f32[200,256]{1,0:T(8,128)S(1)} collective-permute-done((f32[200,256]{1,0:T(8,128)S(1)}, f32[200,256]{1,0:T(8,128)S(1)}, u32[]{:S(2)}, u32[]{:S(2)}) %collective-permute-start.24) | collective-permute-done | bytes 204832 | tf_op jit(solution)/shard_map/ppermute | solution.py:44
  42.7 1.8 %collective-permute-start.25 = (f32[200,256]{1,0:T(8,128)S(1)}, f32[200,256]{1,0:T(8,128)S(1)}, u32[]{:S(2)}, u32[]{:S(2)}) collective-permute-start(f32[200,256]{1,0:T(8,128)S(1)} %add.96.a_ref.refs_0_), channel_id=1, source_target_pairs={{0,16},{8,24},{16,0},{24,8},{1,17},{9,25},{17,1},{25,9},{2,18},{10... | collective-permute-start | bytes 614408 | tf_op jit(solution)/shard_map/ppermute | solution.py:44
  44.6 1.6 %collective-permute-start.27 = (f32[192,256]{1,0:T(8,128)S(1)}, f32[192,256]{1,0:T(8,128)S(1)}, u32[]{:S(2)}, u32[]{:S(2)}) collective-permute-start(f32[192,256]{1,0:T(8,128)S(1)} %add.97.refs_2_), channel_id=1, source_target_pairs={{0,8},{8,0},{16,24},{24,16},{1,9},{9,1},{17,25},{25,17},{2,10},{10... | collective-permute-start | bytes 589832 | tf_op jit(solution)/shard_map/ppermute | solution.py:44
  46.2 3.3 %inverse.2 = (f32[256,256]{1,0:T(8,128)S(1)}, f32[1,256]{1,0:T(1,128)S(1)}) custom-call(f32[200,256]{1,0:T(8,128)S(1)} %add.96.a_ref.refs_0_, f32[1,256]{1,0:T(1,128)S(1)} %bitcast.1), custom_call_target="tpu_custom_call" | custom-call | flops 1342177280 | bytes 524288 | tf_op jit(solution)/shard_map/inverse/pallas_call | solution.py:335
  49.4 1.1 %collective-permute-done.27.refs_3_ = f32[192,256]{1,0:T(8,128)S(1)} collective-permute-done((f32[192,256]{1,0:T(8,128)S(1)}, f32[192,256]{1,0:T(8,128)S(1)}, u32[]{:S(2)}, u32[]{:S(2)}) %collective-permute-start.27) | collective-permute-done | bytes 196640 | tf_op jit(solution)/shard_map/ppermute | solution.py:44
  50.5 4.5 %middle.1 = (bf16[1024,256]{1,0:T(8,128)(2,1)S(1)}, bf16[1024,256]{1,0:T(8,128)(2,1)S(1)}, f32[128,256]{1,0:T(8,128)S(1)}, f32[128,256]{1,0:T(8,128)S(1)}, f32[1...) custom-call(f32[200,256]{1,0:T(8,128)S(1)} %add.96.a_ref.refs_0_, ...), custom_call_target="tpu_custom_call" | custom-call | tf_op jit(solution)/shard_map/middle/pallas_call | solution.py:335
  56.5 1.1 %collective-permute-start.29 = (f32[64,256]{1,0:T(8,128)S(1)}, f32[64,256]{1,0:T(8,128)S(1)}, u32[]{:S(2)}, u32[]{:S(2)}) collective-permute-start(f32[64,256]{1,0:T(8,128)S(1)} %slice.73), channel_id=1, source_target_pairs={{0,2},{1,3},{2,0},{3,1},{4,6},{5,7},{6,4},{7,5},{8,10},{9,11},{10,... | collective-permute-start | bytes 196616 | tf_op jit(solution)/shard_map/ppermute | solution.py:44
  57.6 1.0 %collective-permute-start.35 = (f32[64,256]{1,0:T(8,128)S(1)}, f32[64,256]{1,0:T(8,128)S(1)}, u32[]{:S(2)}, u32[]{:S(2)}) collective-permute-start(f32[64,256]{1,0:T(8,128)S(1)} %slice.75), channel_id=1, source_target_pairs={{0,2},{1,3},{2,0},{3,1},{4,6},{5,7},{6,4},{7,5},{8,10},{9,11},{10,... | collective-permute-start | bytes 196616 | tf_op jit(solution)/shard_map/ppermute | solution.py:44
  58.7 1.1 %collective-permute-start.41 = (f32[64,256]{1,0:T(8,128)S(1)}, f32[64,256]{1,0:T(8,128)S(1)}, u32[]{:S(2)}, u32[]{:S(2)}) collective-permute-start(f32[64,256]{1,0:T(8,128)S(1)} %slice.77), channel_id=1, source_target_pairs={{0,2},{1,3},{2,0},{3,1},{4,6},{5,7},{6,4},{7,5},{8,10},{9,11},{10,... | collective-permute-start | bytes 196616 | tf_op jit(solution)/shard_map/ppermute | solution.py:44
  59.9 1.0 collective-permute-start.47
  61.5 2.1 %collective-permute-start.30 = (f32[64,256]{1,0:T(8,128)S(1)}, f32[64,256]{1,0:T(8,128)S(1)}, u32[]{:S(2)}, u32[]{:S(2)}) collective-permute-start(f32[64,256]{1,0:T(8,128)S(1)} %slice_add_fusion.3), channel_id=1, source_target_pairs={{0,4},{1,5},{2,6},{3,7},{4,0},{5,1},{6,2},{7,3},{8,12},{9,13},{10,... | collective-permute-start | bytes 196616 | tf_op jit(solution)/shard_map/ppermute | solution.py:44
  63.6 1.4 %collective-permute-start.36 = (f32[64,256]{1,0:T(8,128)S(1)}, f32[64,256]{1,0:T(8,128)S(1)}, u32[]{:S(2)}, u32[]{:S(2)}) collective-permute-start(f32[64,256]{1,0:T(8,128)S(1)} %slice_add_fusion.2), channel_id=1, source_target_pairs={{0,4},{1,5},{2,6},{3,7},{4,0},{5,1},{6,2},{7,3},{8,12},{9,13},{10,... | collective-permute-start | bytes 196616 | tf_op jit(solution)/shard_map/ppermute | solution.py:44
  65.0 1.7 %collective-permute-start.42 = (f32[64,256]{1,0:T(8,128)S(1)}, f32[64,256]{1,0:T(8,128)S(1)}, u32[]{:S(2)}, u32[]{:S(2)}) collective-permute-start(f32[64,256]{1,0:T(8,128)S(1)} %slice_add_fusion.1), channel_id=1, source_target_pairs={{0,4},{1,5},{2,6},{3,7},{4,0},{5,1},{6,2},{7,3},{8,12},{9,13},{10,... | collective-permute-start | bytes 196616 | tf_op jit(solution)/shard_map/ppermute | solution.py:44
  66.7 1.4 %collective-permute-start.48 = (f32[64,256]{1,0:T(8,128)S(1)}, f32[64,256]{1,0:T(8,128)S(1)}, u32[]{:S(2)}, u32[]{:S(2)}) collective-permute-start(f32[64,256]{1,0:T(8,128)S(1)} %slice_add_fusion), channel_id=1, source_target_pairs={{0,4},{1,5},{2,6},{3,7},{4,0},{5,1},{6,2},{7,3},{8,12},{9,13},{10,... | collective-permute-start | bytes 196616 | tf_op jit(solution)/shard_map/ppermute | solution.py:44
  68.1 3.9 %collective-permute-done.30 = f32[64,256]{1,0:T(8,128)S(1)} collective-permute-done((f32[64,256]{1,0:T(8,128)S(1)}, f32[64,256]{1,0:T(8,128)S(1)}, u32[]{:S(2)}, u32[]{:S(2)}) %collective-permute-start.30) | collective-permute-done | bytes 65568 | tf_op jit(solution)/shard_map/ppermute | solution.py:44
  72.2 1.9 %collective-permute-done.36 = f32[64,256]{1,0:T(8,128)S(1)} collective-permute-done((f32[64,256]{1,0:T(8,128)S(1)}, f32[64,256]{1,0:T(8,128)S(1)}, u32[]{:S(2)}, u32[]{:S(2)}) %collective-permute-start.36) | collective-permute-done | bytes 65568 | tf_op jit(solution)/shard_map/ppermute | solution.py:44
  74.2 0.9 collective-permute-done.42
  75.9 1.4 %collective-permute-start.43 = (f32[64,256]{1,0:T(8,128)S(1)}, f32[64,256]{1,0:T(8,128)S(1)}, u32[]{:S(2)}, u32[]{:S(2)}) collective-permute-start(f32[64,256]{1,0:T(8,128)S(1)} %add.106.more_8_), channel_id=1, source_target_pairs={{0,2},{1,3},{2,0},{3,1},{4,6},{5,7},{6,4},{7,5},{8,10},{9,11},{10,... | collective-permute-start | bytes 196616 | tf_op jit(solution)/shard_map/ppermute | solution.py:44
  78.0 1.7 %collective-permute-done.37.more_5_ = f32[64,256]{1,0:T(8,128)S(1)} collective-permute-done((f32[64,256]{1,0:T(8,128)S(1)}, f32[64,256]{1,0:T(8,128)S(1)}, u32[]{:S(2)}, u32[]{:S(2)}) %collective-permute-start.37) | collective-permute-done | bytes 65568 | tf_op jit(solution)/shard_map/ppermute | solution.py:44
  80.3 0.9 collective-permute-done.43.more_9_
  81.2 1.0 collective-permute-done.49.more_13_
  82.4 1.0 collective-permute-done.51.more_15_
  83.5 1.1 %products.3 = (f32[200,256]{1,0:T(8,128)S(1)}, f32[192,256]{1,0:T(8,128)S(1)}, bf16[1024,256]{1,0:T(8,128)(2,1)S(1)}, bf16[1024,256]{1,0:T(8,128)(2,1)S(1)}) custom-call(bf16[1024,256]{1,0:T(8,128)(2,1)S(1)} %get-tuple-element.52.top_ref, bf16[1024,256]{1,0:T(8,128)(2,1)S(1)} %get-tuple-element.53.rest_ref, f32[64,256]{1,0:T(8,128)S(1)} %add.100.more_0_, ...), custom_call_target="tpu_custom_call" | custom-call | tf_op jit(solution)/shard_map/products/pallas_call | solution.py:335
  84.6 1.6 %collective-permute-start.52 = (f32[200,256]{1,0:T(8,128)S(1)}, f32[200,256]{1,0:T(8,128)S(1)}, u32[]{:S(2)}, u32[]{:S(2)}) collective-permute-start(f32[200,256]{1,0:T(8,128)S(1)} %get-tuple-element.62), channel_id=1, source_target_pairs={{0,8},{8,0},{16,24},{24,16},{1,9},{9,1},{17,25},{25,17},{2,10},{10... | collective-permute-start | bytes 614408 | tf_op jit(solution)/shard_map/ppermute | solution.py:44
  86.6 5.1 %collective-permute-done.52 = f32[200,256]{1,0:T(8,128)S(1)} collective-permute-done((f32[200,256]{1,0:T(8,128)S(1)}, f32[200,256]{1,0:T(8,128)S(1)}, u32[]{:S(2)}, u32[]{:S(2)}) %collective-permute-start.52) | collective-permute-done | bytes 204832 | tf_op jit(solution)/shard_map/ppermute | solution.py:44
  91.8 1.0 collective-permute-start.53
  92.8 1.1 %collective-permute-start.55 = (f32[192,256]{1,0:T(8,128)S(1)}, f32[192,256]{1,0:T(8,128)S(1)}, u32[]{:S(2)}, u32[]{:S(2)}) collective-permute-start(f32[192,256]{1,0:T(8,128)S(1)} %add.111.refs_2_), channel_id=1, source_target_pairs={{0,8},{8,0},{16,24},{24,16},{1,9},{9,1},{17,25},{25,17},{2,10},{10... | collective-permute-start | bytes 589832 | tf_op jit(solution)/shard_map/ppermute | solution.py:44
  94.0 3.3 %inverse.3 = (f32[256,256]{1,0:T(8,128)S(1)}, f32[1,256]{1,0:T(1,128)S(1)}) custom-call(f32[200,256]{1,0:T(8,128)S(1)} %add.110.a_ref.refs_0_, f32[1,256]{1,0:T(1,128)S(1)} %get-tuple-element.51.refs_8_.level_ref), custom_call_target="tpu_custom_call" | custom-call | flops 1342177280 | bytes 524288 | tf_op jit(solution)/shard_map/inverse/pallas_call | solution.py:335
  97.3 1.5 %collective-permute-done.55.refs_3_ = f32[192,256]{1,0:T(8,128)S(1)} collective-permute-done((f32[192,256]{1,0:T(8,128)S(1)}, f32[192,256]{1,0:T(8,128)S(1)}, u32[]{:S(2)}, u32[]{:S(2)}) %collective-permute-start.55) | collective-permute-done | bytes 196640 | tf_op jit(solution)/shard_map/ppermute | solution.py:44
  98.7 4.8 %last.1 = (f32[1024,256]{1,0:T(8,128)}, f32[1024,256]{1,0:T(8,128)}) custom-call(f32[200,256]{1,0:T(8,128)S(1)} %add.110.a_ref.refs_0_, f32[200,256]{1,0:T(8,128)S(1)} %collective-permute-done.53.refs_1_, f32[192,256]{1,0:T(8,128)S(1)} %add.111.refs_2_, f32[192,256]{1,0:T(8,128)S(1)} %collective-permute-done.55.refs_3_, ...), custom_call_target="tpu_custom_call" | custom-call | tf_op jit(solution)/shard_map/last/pallas_call | solution.py:335
  (113 shorter events, 11.1 us)
Async XLA Ops:
  5.0 4.0 %collective-permute-start.6 = (f32[128,256]{1,0:T(8,128)S(1)}, f32[128,256]{1,0:T(8,128)S(1)}, u32[]{:S(2)}, u32[]{:S(2)}) collective-permute-start(f32[128,256]{1,0:T(8,128)S(1)} %get-tuple-element.40), channel_id=1, source_target_pairs={{0,1},{1,0},{2,3},{3,2},{4,5},{5,4},{6,7},{7,6},{8,9},{9,8},{10,11... | collective-permute-start | bytes 393224 | tf_op jit(solution)/shard_map/ppermute | solution.py:44
  5.0 4.1 %collective-permute-start.12 = (f32[128,256]{1,0:T(8,128)S(1)}, f32[128,256]{1,0:T(8,128)S(1)}, u32[]{:S(2)}, u32[]{:S(2)}) collective-permute-start(f32[128,256]{1,0:T(8,128)S(1)} %get-tuple-element.42), channel_id=1, source_target_pairs={{0,1},{1,0},{2,3},{3,2},{4,5},{5,4},{6,7},{7,6},{8,9},{9,8},{10,11... | collective-permute-start | bytes 393224 | tf_op jit(solution)/shard_map/ppermute | solution.py:44
  5.5 5.7 %collective-permute-start.18 = (f32[128,256]{1,0:T(8,128)S(1)}, f32[128,256]{1,0:T(8,128)S(1)}, u32[]{:S(2)}, u32[]{:S(2)}) collective-permute-start(f32[128,256]{1,0:T(8,128)S(1)} %get-tuple-element.44), channel_id=1, source_target_pairs={{0,1},{1,0},{2,3},{3,2},{4,5},{5,4},{6,7},{7,6},{8,9},{9,8},{10,11... | collective-permute-start | bytes 393224 | tf_op jit(solution)/shard_map/ppermute | solution.py:44
  6.0 5.5 %collective-permute-start.1 = (f32[64,256]{1,0:T(8,128)S(1)}, f32[64,256]{1,0:T(8,128)S(1)}, u32[]{:S(2)}, u32[]{:S(2)}) collective-permute-start(f32[64,256]{1,0:T(8,128)S(1)} %slice.65), channel_id=1, source_target_pairs={{0,2},{1,3},{2,0},{3,1},{4,6},{5,7},{6,4},{7,5},{8,10},{9,11},{10,... | collective-permute-start | bytes 196616 | tf_op jit(solution)/shard_map/ppermute | solution.py:44
  9.0 5.5 %collective-permute-start.7 = (f32[64,256]{1,0:T(8,128)S(1)}, f32[64,256]{1,0:T(8,128)S(1)}, u32[]{:S(2)}, u32[]{:S(2)}) collective-permute-start(f32[64,256]{1,0:T(8,128)S(1)} %slice.67), channel_id=1, source_target_pairs={{0,2},{1,3},{2,0},{3,1},{4,6},{5,7},{6,4},{7,5},{8,10},{9,11},{10,... | collective-permute-start | bytes 196616 | tf_op jit(solution)/shard_map/ppermute | solution.py:44
  9.2 7.5 %collective-permute-start.13 = (f32[64,256]{1,0:T(8,128)S(1)}, f32[64,256]{1,0:T(8,128)S(1)}, u32[]{:S(2)}, u32[]{:S(2)}) collective-permute-start(f32[64,256]{1,0:T(8,128)S(1)} %slice.69), channel_id=1, source_target_pairs={{0,2},{1,3},{2,0},{3,1},{4,6},{5,7},{6,4},{7,5},{8,10},{9,11},{10,... | collective-permute-start | bytes 196616 | tf_op jit(solution)/shard_map/ppermute | solution.py:44
  11.3 6.9 %collective-permute-start.19 = (f32[64,256]{1,0:T(8,128)S(1)}, f32[64,256]{1,0:T(8,128)S(1)}, u32[]{:S(2)}, u32[]{:S(2)}) collective-permute-start(f32[64,256]{1,0:T(8,128)S(1)} %slice.71), channel_id=1, source_target_pairs={{0,2},{1,3},{2,0},{3,1},{4,6},{5,7},{6,4},{7,5},{8,10},{9,11},{10,... | collective-permute-start | bytes 196616 | tf_op jit(solution)/shard_map/ppermute | solution.py:44
  11.5 8.4 %collective-permute-start.2 = (f32[64,256]{1,0:T(8,128)S(1)}, f32[64,256]{1,0:T(8,128)S(1)}, u32[]{:S(2)}, u32[]{:S(2)}) collective-permute-start(f32[64,256]{1,0:T(8,128)S(1)} %slice_add_fusion.7), channel_id=1, source_target_pairs={{0,4},{1,5},{2,6},{3,7},{4,0},{5,1},{6,2},{7,3},{8,12},{9,13},{10,... | collective-permute-start | bytes 196616 | tf_op jit(solution)/shard_map/ppermute | solution.py:44
  14.5 10.7 %collective-permute-start.8 = (f32[64,256]{1,0:T(8,128)S(1)}, f32[64,256]{1,0:T(8,128)S(1)}, u32[]{:S(2)}, u32[]{:S(2)}) collective-permute-start(f32[64,256]{1,0:T(8,128)S(1)} %slice_add_fusion.6), channel_id=1, source_target_pairs={{0,4},{1,5},{2,6},{3,7},{4,0},{5,1},{6,2},{7,3},{8,12},{9,13},{10,... | collective-permute-start | bytes 196616 | tf_op jit(solution)/shard_map/ppermute | solution.py:44
  16.8 9.3 %collective-permute-start.14 = (f32[64,256]{1,0:T(8,128)S(1)}, f32[64,256]{1,0:T(8,128)S(1)}, u32[]{:S(2)}, u32[]{:S(2)}) collective-permute-start(f32[64,256]{1,0:T(8,128)S(1)} %slice_add_fusion.5), channel_id=1, source_target_pairs={{0,4},{1,5},{2,6},{3,7},{4,0},{5,1},{6,2},{7,3},{8,12},{9,13},{10,... | collective-permute-start | bytes 196616 | tf_op jit(solution)/shard_map/ppermute | solution.py:44
  18.2 8.6 %collective-permute-start.20 = (f32[64,256]{1,0:T(8,128)S(1)}, f32[64,256]{1,0:T(8,128)S(1)}, u32[]{:S(2)}, u32[]{:S(2)}) collective-permute-start(f32[64,256]{1,0:T(8,128)S(1)} %slice_add_fusion.4), channel_id=1, source_target_pairs={{0,4},{1,5},{2,6},{3,7},{4,0},{5,1},{6,2},{7,3},{8,12},{9,13},{10,... | collective-permute-start | bytes 196616 | tf_op jit(solution)/shard_map/ppermute | solution.py:44
  19.8 7.0 %collective-permute-start.4 = (f32[64,256]{1,0:T(8,128)S(1)}, f32[64,256]{1,0:T(8,128)S(1)}, u32[]{:S(2)}, u32[]{:S(2)}) collective-permute-start(f32[64,256]{1,0:T(8,128)S(1)} %add.86.more_0_), channel_id=1, source_target_pairs={{0,1},{1,0},{2,3},{3,2},{4,5},{5,4},{6,7},{7,6},{8,9},{9,8},{10,11... | collective-permute-start | bytes 196616 | tf_op jit(solution)/shard_map/ppermute | solution.py:44
  19.9 8.4 %collective-permute-start.3 = (f32[64,256]{1,0:T(8,128)S(1)}, f32[64,256]{1,0:T(8,128)S(1)}, u32[]{:S(2)}, u32[]{:S(2)}) collective-permute-start(f32[64,256]{1,0:T(8,128)S(1)} %add.86.more_0_), channel_id=1, source_target_pairs={{0,2},{1,3},{2,0},{3,1},{4,6},{5,7},{6,4},{7,5},{8,10},{9,11},{10,... | collective-permute-start | bytes 196616 | tf_op jit(solution)/shard_map/ppermute | solution.py:44
  25.2 3.7 %collective-permute-start.10 = (f32[64,256]{1,0:T(8,128)S(1)}, f32[64,256]{1,0:T(8,128)S(1)}, u32[]{:S(2)}, u32[]{:S(2)}) collective-permute-start(f32[64,256]{1,0:T(8,128)S(1)} %add.89.more_4_), channel_id=1, source_target_pairs={{0,1},{1,0},{2,3},{3,2},{4,5},{5,4},{6,7},{7,6},{8,9},{9,8},{10,11... | collective-permute-start | bytes 196616 | tf_op jit(solution)/shard_map/ppermute | solution.py:44
  26.1 4.6 %collective-permute-start.9 = (f32[64,256]{1,0:T(8,128)S(1)}, f32[64,256]{1,0:T(8,128)S(1)}, u32[]{:S(2)}, u32[]{:S(2)}) collective-permute-start(f32[64,256]{1,0:T(8,128)S(1)} %add.89.more_4_), channel_id=1, source_target_pairs={{0,2},{1,3},{2,0},{3,1},{4,6},{5,7},{6,4},{7,5},{8,10},{9,11},{10,... | collective-permute-start | bytes 196616 | tf_op jit(solution)/shard_map/ppermute | solution.py:44
  26.8 3.9 %collective-permute-start.16 = (f32[64,256]{1,0:T(8,128)S(1)}, f32[64,256]{1,0:T(8,128)S(1)}, u32[]{:S(2)}, u32[]{:S(2)}) collective-permute-start(f32[64,256]{1,0:T(8,128)S(1)} %add.92.more_8_), channel_id=1, source_target_pairs={{0,1},{1,0},{2,3},{3,2},{4,5},{5,4},{6,7},{7,6},{8,9},{9,8},{10,11... | collective-permute-start | bytes 196616 | tf_op jit(solution)/shard_map/ppermute | solution.py:44
  26.8 5.3 %collective-permute-start.15 = (f32[64,256]{1,0:T(8,128)S(1)}, f32[64,256]{1,0:T(8,128)S(1)}, u32[]{:S(2)}, u32[]{:S(2)}) collective-permute-start(f32[64,256]{1,0:T(8,128)S(1)} %add.92.more_8_), channel_id=1, source_target_pairs={{0,2},{1,3},{2,0},{3,1},{4,6},{5,7},{6,4},{7,5},{8,10},{9,11},{10,... | collective-permute-start | bytes 196616 | tf_op jit(solution)/shard_map/ppermute | solution.py:44
  28.3 4.8 %collective-permute-start.21 = (f32[64,256]{1,0:T(8,128)S(1)}, f32[64,256]{1,0:T(8,128)S(1)}, u32[]{:S(2)}, u32[]{:S(2)}) collective-permute-start(f32[64,256]{1,0:T(8,128)S(1)} %add.95.more_12_), channel_id=1, source_target_pairs={{0,2},{1,3},{2,0},{3,1},{4,6},{5,7},{6,4},{7,5},{8,10},{9,11},{10,... | collective-permute-start | bytes 196616 | tf_op jit(solution)/shard_map/ppermute | solution.py:44
  28.9 4.2 %collective-permute-start.22 = (f32[64,256]{1,0:T(8,128)S(1)}, f32[64,256]{1,0:T(8,128)S(1)}, u32[]{:S(2)}, u32[]{:S(2)}) collective-permute-start(f32[64,256]{1,0:T(8,128)S(1)} %add.95.more_12_), channel_id=1, source_target_pairs={{0,1},{1,0},{2,3},{3,2},{4,5},{5,4},{6,7},{7,6},{8,9},{9,8},{10,11... | collective-permute-start | bytes 196616 | tf_op jit(solution)/shard_map/ppermute | solution.py:44
  30.7 2.5 %collective-permute-start.5 = (f32[64,256]{1,0:T(8,128)S(1)}, f32[64,256]{1,0:T(8,128)S(1)}, u32[]{:S(2)}, u32[]{:S(2)}) collective-permute-start(f32[64,256]{1,0:T(8,128)S(1)} %collective-permute-done.3.more_1_), channel_id=1, source_target_pairs={{0,1},{1,0},{2,3},{3,2},{4,5},{5,4},{6,7},{7,6},{8,9},{9,8},{10,11... | collective-permute-start | bytes 196616 | tf_op jit(solution)/shard_map/ppermute | solution.py:44
  30.7 2.5 %collective-permute-start.11 = (f32[64,256]{1,0:T(8,128)S(1)}, f32[64,256]{1,0:T(8,128)S(1)}, u32[]{:S(2)}, u32[]{:S(2)}) collective-permute-start(f32[64,256]{1,0:T(8,128)S(1)} %collective-permute-done.9.more_5_), channel_id=1, source_target_pairs={{0,1},{1,0},{2,3},{3,2},{4,5},{5,4},{6,7},{7,6},{8,9},{9,8},{10,11... | collective-permute-start | bytes 196616 | tf_op jit(solution)/shard_map/ppermute | solution.py:44
  35.5 7.2 %collective-permute-start.24 = (f32[200,256]{1,0:T(8,128)S(1)}, f32[200,256]{1,0:T(8,128)S(1)}, u32[]{:S(2)}, u32[]{:S(2)}) collective-permute-start(f32[200,256]{1,0:T(8,128)S(1)} %get-tuple-element.45), channel_id=1, source_target_pairs={{0,8},{8,0},{16,24},{24,16},{1,9},{9,1},{17,25},{25,17},{2,10},{10... | collective-permute-start | bytes 614408 | tf_op jit(solution)/shard_map/ppermute | solution.py:44
  37.3 7.3 %collective-permute-start.26 = (f32[192,256]{1,0:T(8,128)S(1)}, f32[192,256]{1,0:T(8,128)S(1)}, u32[]{:S(2)}, u32[]{:S(2)}) collective-permute-start(f32[192,256]{1,0:T(8,128)S(1)} %get-tuple-element.46), channel_id=1, source_target_pairs={{0,16},{8,24},{16,0},{24,8},{1,17},{9,25},{17,1},{25,9},{2,18},{10... | collective-permute-start | bytes 589832 | tf_op jit(solution)/shard_map/ppermute | solution.py:44
  42.7 7.8 %collective-permute-start.25 = (f32[200,256]{1,0:T(8,128)S(1)}, f32[200,256]{1,0:T(8,128)S(1)}, u32[]{:S(2)}, u32[]{:S(2)}) collective-permute-start(f32[200,256]{1,0:T(8,128)S(1)} %add.96.a_ref.refs_0_), channel_id=1, source_target_pairs={{0,16},{8,24},{16,0},{24,8},{1,17},{9,25},{17,1},{25,9},{2,18},{10... | collective-permute-start | bytes 614408 | tf_op jit(solution)/shard_map/ppermute | solution.py:44
  44.6 5.9 %collective-permute-start.27 = (f32[192,256]{1,0:T(8,128)S(1)}, f32[192,256]{1,0:T(8,128)S(1)}, u32[]{:S(2)}, u32[]{:S(2)}) collective-permute-start(f32[192,256]{1,0:T(8,128)S(1)} %add.97.refs_2_), channel_id=1, source_target_pairs={{0,8},{8,0},{16,24},{24,16},{1,9},{9,1},{17,25},{25,17},{2,10},{10... | collective-permute-start | bytes 589832 | tf_op jit(solution)/shard_map/ppermute | solution.py:44
  55.1 2.5 %collective-permute-start.34 = (f32[128,256]{1,0:T(8,128)S(1)}, f32[128,256]{1,0:T(8,128)S(1)}, u32[]{:S(2)}, u32[]{:S(2)}) collective-permute-start(f32[128,256]{1,0:T(8,128)S(1)} %get-tuple-element.57), channel_id=1, source_target_pairs={{0,1},{1,0},{2,3},{3,2},{4,5},{5,4},{6,7},{7,6},{8,9},{9,8},{10,11... | collective-permute-start | bytes 393224 | tf_op jit(solution)/shard_map/ppermute | solution.py:44
  55.6 3.1 %collective-permute-start.40 = (f32[128,256]{1,0:T(8,128)S(1)}, f32[128,256]{1,0:T(8,128)S(1)}, u32[]{:S(2)}, u32[]{:S(2)}) collective-permute-start(f32[128,256]{1,0:T(8,128)S(1)} %get-tuple-element.59), channel_id=1, source_target_pairs={{0,1},{1,0},{2,3},{3,2},{4,5},{5,4},{6,7},{7,6},{8,9},{9,8},{10,11... | collective-permute-start | bytes 393224 | tf_op jit(solution)/shard_map/ppermute | solution.py:44
  55.7 4.2 %collective-permute-start.46 = (f32[128,256]{1,0:T(8,128)S(1)}, f32[128,256]{1,0:T(8,128)S(1)}, u32[]{:S(2)}, u32[]{:S(2)}) collective-permute-start(f32[128,256]{1,0:T(8,128)S(1)} %get-tuple-element.61), channel_id=1, source_target_pairs={{0,1},{1,0},{2,3},{3,2},{4,5},{5,4},{6,7},{7,6},{8,9},{9,8},{10,11... | collective-permute-start | bytes 393224 | tf_op jit(solution)/shard_map/ppermute | solution.py:44
  56.5 5.0 %collective-permute-start.29 = (f32[64,256]{1,0:T(8,128)S(1)}, f32[64,256]{1,0:T(8,128)S(1)}, u32[]{:S(2)}, u32[]{:S(2)}) collective-permute-start(f32[64,256]{1,0:T(8,128)S(1)} %slice.73), channel_id=1, source_target_pairs={{0,2},{1,3},{2,0},{3,1},{4,6},{5,7},{6,4},{7,5},{8,10},{9,11},{10,... | collective-permute-start | bytes 196616 | tf_op jit(solution)/shard_map/ppermute | solution.py:44
  57.6 5.9 %collective-permute-start.35 = (f32[64,256]{1,0:T(8,128)S(1)}, f32[64,256]{1,0:T(8,128)S(1)}, u32[]{:S(2)}, u32[]{:S(2)}) collective-permute-start(f32[64,256]{1,0:T(8,128)S(1)} %slice.75), channel_id=1, source_target_pairs={{0,2},{1,3},{2,0},{3,1},{4,6},{5,7},{6,4},{7,5},{8,10},{9,11},{10,... | collective-permute-start | bytes 196616 | tf_op jit(solution)/shard_map/ppermute | solution.py:44
  58.7 6.3 %collective-permute-start.41 = (f32[64,256]{1,0:T(8,128)S(1)}, f32[64,256]{1,0:T(8,128)S(1)}, u32[]{:S(2)}, u32[]{:S(2)}) collective-permute-start(f32[64,256]{1,0:T(8,128)S(1)} %slice.77), channel_id=1, source_target_pairs={{0,2},{1,3},{2,0},{3,1},{4,6},{5,7},{6,4},{7,5},{8,10},{9,11},{10,... | collective-permute-start | bytes 196616 | tf_op jit(solution)/shard_map/ppermute | solution.py:44
  59.9 6.8 %collective-permute-start.47 = (f32[64,256]{1,0:T(8,128)S(1)}, f32[64,256]{1,0:T(8,128)S(1)}, u32[]{:S(2)}, u32[]{:S(2)}) collective-permute-start(f32[64,256]{1,0:T(8,128)S(1)} %slice.79), channel_id=1, source_target_pairs={{0,2},{1,3},{2,0},{3,1},{4,6},{5,7},{6,4},{7,5},{8,10},{9,11},{10,... | collective-permute-start | bytes 196616 | tf_op jit(solution)/shard_map/ppermute | solution.py:44
  61.5 10.5 %collective-permute-start.30 = (f32[64,256]{1,0:T(8,128)S(1)}, f32[64,256]{1,0:T(8,128)S(1)}, u32[]{:S(2)}, u32[]{:S(2)}) collective-permute-start(f32[64,256]{1,0:T(8,128)S(1)} %slice_add_fusion.3), channel_id=1, source_target_pairs={{0,4},{1,5},{2,6},{3,7},{4,0},{5,1},{6,2},{7,3},{8,12},{9,13},{10,... | collective-permute-start | bytes 196616 | tf_op jit(solution)/shard_map/ppermute | solution.py:44
  63.6 10.5 %collective-permute-start.36 = (f32[64,256]{1,0:T(8,128)S(1)}, f32[64,256]{1,0:T(8,128)S(1)}, u32[]{:S(2)}, u32[]{:S(2)}) collective-permute-start(f32[64,256]{1,0:T(8,128)S(1)} %slice_add_fusion.2), channel_id=1, source_target_pairs={{0,4},{1,5},{2,6},{3,7},{4,0},{5,1},{6,2},{7,3},{8,12},{9,13},{10,... | collective-permute-start | bytes 196616 | tf_op jit(solution)/shard_map/ppermute | solution.py:44
  65.0 10.1 %collective-permute-start.42 = (f32[64,256]{1,0:T(8,128)S(1)}, f32[64,256]{1,0:T(8,128)S(1)}, u32[]{:S(2)}, u32[]{:S(2)}) collective-permute-start(f32[64,256]{1,0:T(8,128)S(1)} %slice_add_fusion.1), channel_id=1, source_target_pairs={{0,4},{1,5},{2,6},{3,7},{4,0},{5,1},{6,2},{7,3},{8,12},{9,13},{10,... | collective-permute-start | bytes 196616 | tf_op jit(solution)/shard_map/ppermute | solution.py:44
  66.7 9.2 %collective-permute-start.48 = (f32[64,256]{1,0:T(8,128)S(1)}, f32[64,256]{1,0:T(8,128)S(1)}, u32[]{:S(2)}, u32[]{:S(2)}) collective-permute-start(f32[64,256]{1,0:T(8,128)S(1)} %slice_add_fusion), channel_id=1, source_target_pairs={{0,4},{1,5},{2,6},{3,7},{4,0},{5,1},{6,2},{7,3},{8,12},{9,13},{10,... | collective-permute-start | bytes 196616 | tf_op jit(solution)/shard_map/ppermute | solution.py:44
  72.0 3.9 %collective-permute-start.32 = (f32[64,256]{1,0:T(8,128)S(1)}, f32[64,256]{1,0:T(8,128)S(1)}, u32[]{:S(2)}, u32[]{:S(2)}) collective-permute-start(f32[64,256]{1,0:T(8,128)S(1)} %add.100.more_0_), channel_id=1, source_target_pairs={{0,1},{1,0},{2,3},{3,2},{4,5},{5,4},{6,7},{7,6},{8,9},{9,8},{10,11... | collective-permute-start | bytes 196616 | tf_op jit(solution)/shard_map/ppermute | solution.py:44
  72.1 5.3 %collective-permute-start.31 = (f32[64,256]{1,0:T(8,128)S(1)}, f32[64,256]{1,0:T(8,128)S(1)}, u32[]{:S(2)}, u32[]{:S(2)}) collective-permute-start(f32[64,256]{1,0:T(8,128)S(1)} %add.100.more_0_), channel_id=1, source_target_pairs={{0,2},{1,3},{2,0},{3,1},{4,6},{5,7},{6,4},{7,5},{8,10},{9,11},{10,... | collective-permute-start | bytes 196616 | tf_op jit(solution)/shard_map/ppermute | solution.py:44
  74.1 3.9 %collective-permute-start.38 = (f32[64,256]{1,0:T(8,128)S(1)}, f32[64,256]{1,0:T(8,128)S(1)}, u32[]{:S(2)}, u32[]{:S(2)}) collective-permute-start(f32[64,256]{1,0:T(8,128)S(1)} %add.103.more_4_), channel_id=1, source_target_pairs={{0,1},{1,0},{2,3},{3,2},{4,5},{5,4},{6,7},{7,6},{8,9},{9,8},{10,11... | collective-permute-start | bytes 196616 | tf_op jit(solution)/shard_map/ppermute | solution.py:44
  75.1 4.6 %collective-permute-start.37 = (f32[64,256]{1,0:T(8,128)S(1)}, f32[64,256]{1,0:T(8,128)S(1)}, u32[]{:S(2)}, u32[]{:S(2)}) collective-permute-start(f32[64,256]{1,0:T(8,128)S(1)} %add.103.more_4_), channel_id=1, source_target_pairs={{0,2},{1,3},{2,0},{3,1},{4,6},{5,7},{6,4},{7,5},{8,10},{9,11},{10,... | collective-permute-start | bytes 196616 | tf_op jit(solution)/shard_map/ppermute | solution.py:44
  75.9 3.9 %collective-permute-start.44 = (f32[64,256]{1,0:T(8,128)S(1)}, f32[64,256]{1,0:T(8,128)S(1)}, u32[]{:S(2)}, u32[]{:S(2)}) collective-permute-start(f32[64,256]{1,0:T(8,128)S(1)} %add.106.more_8_), channel_id=1, source_target_pairs={{0,1},{1,0},{2,3},{3,2},{4,5},{5,4},{6,7},{7,6},{8,9},{9,8},{10,11... | collective-permute-start | bytes 196616 | tf_op jit(solution)/shard_map/ppermute | solution.py:44
  75.9 5.3 %collective-permute-start.43 = (f32[64,256]{1,0:T(8,128)S(1)}, f32[64,256]{1,0:T(8,128)S(1)}, u32[]{:S(2)}, u32[]{:S(2)}) collective-permute-start(f32[64,256]{1,0:T(8,128)S(1)} %add.106.more_8_), channel_id=1, source_target_pairs={{0,2},{1,3},{2,0},{3,1},{4,6},{5,7},{6,4},{7,5},{8,10},{9,11},{10,... | collective-permute-start | bytes 196616 | tf_op jit(solution)/shard_map/ppermute | solution.py:44
  77.4 4.8 %collective-permute-start.49 = (f32[64,256]{1,0:T(8,128)S(1)}, f32[64,256]{1,0:T(8,128)S(1)}, u32[]{:S(2)}, u32[]{:S(2)}) collective-permute-start(f32[64,256]{1,0:T(8,128)S(1)} %add.109.more_12_), channel_id=1, source_target_pairs={{0,2},{1,3},{2,0},{3,1},{4,6},{5,7},{6,4},{7,5},{8,10},{9,11},{10,... | collective-permute-start | bytes 196616 | tf_op jit(solution)/shard_map/ppermute | solution.py:44
  78.0 4.2 %collective-permute-start.50 = (f32[64,256]{1,0:T(8,128)S(1)}, f32[64,256]{1,0:T(8,128)S(1)}, u32[]{:S(2)}, u32[]{:S(2)}) collective-permute-start(f32[64,256]{1,0:T(8,128)S(1)} %add.109.more_12_), channel_id=1, source_target_pairs={{0,1},{1,0},{2,3},{3,2},{4,5},{5,4},{6,7},{7,6},{8,9},{9,8},{10,11... | collective-permute-start | bytes 196616 | tf_op jit(solution)/shard_map/ppermute | solution.py:44
  84.6 7.2 %collective-permute-start.52 = (f32[200,256]{1,0:T(8,128)S(1)}, f32[200,256]{1,0:T(8,128)S(1)}, u32[]{:S(2)}, u32[]{:S(2)}) collective-permute-start(f32[200,256]{1,0:T(8,128)S(1)} %get-tuple-element.62), channel_id=1, source_target_pairs={{0,8},{8,0},{16,24},{24,16},{1,9},{9,1},{17,25},{25,17},{2,10},{10... | collective-permute-start | bytes 614408 | tf_op jit(solution)/shard_map/ppermute | solution.py:44
  86.1 6.7 %collective-permute-start.54 = (f32[192,256]{1,0:T(8,128)S(1)}, f32[192,256]{1,0:T(8,128)S(1)}, u32[]{:S(2)}, u32[]{:S(2)}) collective-permute-start(f32[192,256]{1,0:T(8,128)S(1)} %get-tuple-element.63), channel_id=1, source_target_pairs={{0,16},{8,24},{16,0},{24,8},{1,17},{9,25},{17,1},{25,9},{2,18},{10... | collective-permute-start | bytes 589832 | tf_op jit(solution)/shard_map/ppermute | solution.py:44
  91.8 6.9 %collective-permute-start.53 = (f32[200,256]{1,0:T(8,128)S(1)}, f32[200,256]{1,0:T(8,128)S(1)}, u32[]{:S(2)}, u32[]{:S(2)}) collective-permute-start(f32[200,256]{1,0:T(8,128)S(1)} %add.110.a_ref.refs_0_), channel_id=1, source_target_pairs={{0,16},{8,24},{16,0},{24,8},{1,17},{9,25},{17,1},{25,9},{2,18},{10... | collective-permute-start | bytes 614408 | tf_op jit(solution)/shard_map/ppermute | solution.py:44
  92.8 5.9 %collective-permute-start.55 = (f32[192,256]{1,0:T(8,128)S(1)}, f32[192,256]{1,0:T(8,128)S(1)}, u32[]{:S(2)}, u32[]{:S(2)}) collective-permute-start(f32[192,256]{1,0:T(8,128)S(1)} %add.111.refs_2_), channel_id=1, source_target_pairs={{0,8},{8,0},{16,24},{24,16},{1,9},{9,1},{17,25},{25,17},{2,10},{10... | collective-permute-start | bytes 589832 | tf_op jit(solution)/shard_map/ppermute | solution.py:44
  (11 other events, 16.6 us)

commit v5 on v4

--- a/solution.py
+++ b/solution.py
@@ -7,7 +7,7 @@
 from jax.sharding import PartitionSpec as P
 
 ITERS = 2
-CHUNKS = 4
+SHARES = 6, 6, 4
 SUBLANES = 8
 LOW = 1e-3
 NEAR, FAR = 1.25, 4.2
@@ -85,13 +85,16 @@
     return low
 
 
+def chunks_of(tall):
+    ends = [sum(SHARES[:i]) * tall // sum(SHARES) for i in range(len(SHARES) + 1)]
+    return [(at, end - at) for at, end in zip(ends, ends[1:])]
+
+
 def write_left(left, out_refs, blocks):
-    tall = left[0].shape[0]
-    share = tall // CHUNKS
     for p in range(blocks):
-        for c in range(CHUNKS):
-            at = p % (blocks // 2) * share
-            out_refs[2 * c + p // (blocks // 2)][pl.ds(at, share), :] = left[p][c * share : (c + 1) * share]
+        for c, (at, share) in enumerate(chunks_of(left[0].shape[0])):
+            to = pl.ds(p % (blocks // 2) * share, share)
+            out_refs[2 * c + p // (blocks // 2)][to, :] = left[p][at : at + share]
 
 
 def fetches(snap_ref, data, sems, blocks):
@@ -130,17 +133,16 @@
     left_refs, (a_ref, b_ref, left_top_ref, left_rest_ref) = more[:-4], more[-4:]
     rows, rank = left_top_ref.shape
     tall = rows // blocks
-    share = tall // CHUNKS
-    at = 0
-    for c in range(CHUNKS):
+    taken = 0
+    for c, (at, share) in enumerate(chunks_of(tall)):
         p = 0
-        for ref in left_refs[at : at + counts[c]]:
+        for ref in left_refs[taken : taken + counts[c]]:
             terms = split(ref[...], 2)
             for k in range(ref.shape[0] // share):
                 for out_ref, term in zip((left_top_ref, left_rest_ref), terms):
-                    out_ref[pl.ds(p * tall + c * share, share), :] = term[k * share : (k + 1) * share]
+                    out_ref[pl.ds(p * tall + at, share), :] = term[k * share : (k + 1) * share]
                 p += 1
-        at += counts[c]
+        taken += counts[c]
     left = left_top_ref[...], left_rest_ref[...]
     right = dot3(left, (top_ref[...], rest_ref[...]), TN)
     cross = dot(left[0], left[1], TN)
@@ -350,10 +352,10 @@
     blocks = n_tm // 2
     whole = [((rows, cols), bf16)] * 2
     a_rows = (rank + rank // 2 + SUBLANES) // 16 * 8 + SUBLANES
-    lefts = [((rows // CHUNKS // 2, rank), f32)] * (2 * CHUNKS)
+    lefts = [((share * blocks // 2, rank), f32) for _, share in chunks_of(rows // blocks) for _ in range(2)]
     data, top, rest, *left = call(
         functools.partial(head_kernel, blocks),
-        (snapshots, right_basis),
+        [pltpu.with_memory_space_constraint(x, pltpu.HBM) for x in (snapshots, right_basis)],
         [((rows, cols), f32)] + whole + lefts,
         in_specs=[HBM] * 2,
         scratch=[

time: 104 us -> 102 us (0.981)
  starting transfers between devices: 46 us -> 39.5 us
  waiting for transfers between devices: 34.3 us -> 39.8 us
  local copies, waits for them, and re-layouts: 2.22 us -> 0.05 us
    ppermute x56 -> x44, starting transfers between devices: 46 us -> 39.5 us  [swap(): return lax.ppermute(x, axis, [(i, i ^ bit) for i in range(size)])]
    ppermute x56 -> x44, waiting for transfers between devices: 34.3 us -> 39.8 us  [swap(): return lax.ppermute(x, axis, [(i, i ^ bit) for i in range(size)])]
    unnamed x6 -> x2, local copies, waits for them, and re-layouts: 2.17 us -> 0.01 us
  transfers between devices with their start and end apart: 56 -> 44, of which waited for: 24 -> 24; matrix products, arithmetic and copies ran while one was open for 0% -> 0% of each run, Pallas kernels for 6% -> 6%
where the time goes in v5:
time: 102 us; the launch traced here: 101 us
  waiting for transfers between devices  39.8 us (39%)
  starting transfers between devices  39.5 us (39%)
  Pallas kernels  20.6 us (20%)
  between operations  1.04 us (1%)
    ppermute x44, waiting for transfers between devices, swap(): return lax.ppermute(x, axis, [(i, i ^ bit) for i in range(size)])  39.8 us
    ppermute x44, starting transfers between devices, swap(): return lax.ppermute(x, axis, [(i, i ^ bit) for i in range(size)])  39.5 us
    pallas_call x7, Pallas kernels, call(): pl.pallas_call(body, out_shape=[jax.ShapeDtypeStruct(shape, dtype) for sh...  20.6 us
  transfers between devices with their start and end apart: 44, of which 24 were waited for; matrix products, arithmetic and copies ran while one was open for 0% of the time, Pallas kernels for 6%

profile of v5, /device:TPU:0, one launch (start us, length us, event | category | flops | bytes accessed | tf_op | source)
XLA Modules:
  0.0 101.4 jit_solution(15153506057042078210)
XLA Ops:
  0.6 2.5 %head.1 = (f32[1024,256]{1,0:T(8,128)S(1)}, bf16[1024,256]{1,0:T(8,128)(2,1)S(1)}, bf16[1024,256]{1,0:T(8,128)(2,1)S(1)}, f32[192,256]{1,0:T(8,128)S(1)}, f32[19...) custom-call(f32[1024,256]{1,0:T(8,128)} %snap_ref.1, ...), custom_call_target="tpu_custom_call" | custom-call | tf_op jit(solution)/shard_map/head/pallas_call | solution.py:337
  4.8 3.0 %collective-permute-start.1 = (f32[96,256]{1,0:T(8,128)S(1)}, f32[96,256]{1,0:T(8,128)S(1)}, u32[]{:S(2)}, u32[]{:S(2)}) collective-permute-start(f32[96,256]{1,0:T(8,128)S(1)} %slice.49), channel_id=1, source_target_pairs={{0,2},{1,3},{2,0},{3,1},{4,6},{5,7},{6,4},{7,5},{8,10},{9,11},{10,... | collective-permute-start | bytes 294920 | tf_op jit(solution)/shard_map/ppermute | solution.py:44
  8.3 1.7 %collective-permute-start.7 = (f32[96,256]{1,0:T(8,128)S(1)}, f32[96,256]{1,0:T(8,128)S(1)}, u32[]{:S(2)}, u32[]{:S(2)}) collective-permute-start(f32[96,256]{1,0:T(8,128)S(1)} %slice.51), channel_id=1, source_target_pairs={{0,2},{1,3},{2,0},{3,1},{4,6},{5,7},{6,4},{7,5},{8,10},{9,11},{10,... | collective-permute-start | bytes 294920 | tf_op jit(solution)/shard_map/ppermute | solution.py:44
  10.1 1.3 %collective-permute-done.1 = f32[96,256]{1,0:T(8,128)S(1)} collective-permute-done((f32[96,256]{1,0:T(8,128)S(1)}, f32[96,256]{1,0:T(8,128)S(1)}, u32[]{:S(2)}, u32[]{:S(2)}) %collective-permute-start.1) | collective-permute-done | bytes 98336 | tf_op jit(solution)/shard_map/ppermute | solution.py:44
  11.4 3.1 %collective-permute-start.2 = (f32[96,256]{1,0:T(8,128)S(1)}, f32[96,256]{1,0:T(8,128)S(1)}, u32[]{:S(2)}, u32[]{:S(2)}) collective-permute-start(f32[96,256]{1,0:T(8,128)S(1)} %slice_add_fusion.3), channel_id=1, source_target_pairs={{0,4},{1,5},{2,6},{3,7},{4,0},{5,1},{6,2},{7,3},{8,12},{9,13},{10,... | collective-permute-start | bytes 294920 | tf_op jit(solution)/shard_map/ppermute | solution.py:44
  14.5 1.0 collective-permute-done.7
  15.5 2.5 %collective-permute-start.8 = (f32[96,256]{1,0:T(8,128)S(1)}, f32[96,256]{1,0:T(8,128)S(1)}, u32[]{:S(2)}, u32[]{:S(2)}) collective-permute-start(f32[96,256]{1,0:T(8,128)S(1)} %slice_add_fusion.2), channel_id=1, source_target_pairs={{0,4},{1,5},{2,6},{3,7},{4,0},{5,1},{6,2},{7,3},{8,12},{9,13},{10,... | collective-permute-start | bytes 294920 | tf_op jit(solution)/shard_map/ppermute | solution.py:44
  18.6 1.9 %collective-permute-done.2 = f32[96,256]{1,0:T(8,128)S(1)} collective-permute-done((f32[96,256]{1,0:T(8,128)S(1)}, f32[96,256]{1,0:T(8,128)S(1)}, u32[]{:S(2)}, u32[]{:S(2)}) %collective-permute-start.2) | collective-permute-done | bytes 98336 | tf_op jit(solution)/shard_map/ppermute | solution.py:44
  20.5 3.0 %collective-permute-start.3 = (f32[96,256]{1,0:T(8,128)S(1)}, f32[96,256]{1,0:T(8,128)S(1)}, u32[]{:S(2)}, u32[]{:S(2)}) collective-permute-start(f32[96,256]{1,0:T(8,128)S(1)} %add.68.more_0_), channel_id=1, source_target_pairs={{0,2},{1,3},{2,0},{3,1},{4,6},{5,7},{6,4},{7,5},{8,10},{9,11},{10,... | collective-permute-start | bytes 294920 | tf_op jit(solution)/shard_map/ppermute | solution.py:44
  23.6 1.4 %collective-permute-done.8 = f32[96,256]{1,0:T(8,128)S(1)} collective-permute-done((f32[96,256]{1,0:T(8,128)S(1)}, f32[96,256]{1,0:T(8,128)S(1)}, u32[]{:S(2)}, u32[]{:S(2)}) %collective-permute-start.8) | collective-permute-done | bytes 98336 | tf_op jit(solution)/shard_map/ppermute | solution.py:44
  25.6 0.7 collective-permute-done.14
  26.3 0.9 collective-permute-start.15
  28.1 1.8 %collective-permute-done.9.more_5_ = f32[96,256]{1,0:T(8,128)S(1)} collective-permute-done((f32[96,256]{1,0:T(8,128)S(1)}, f32[96,256]{1,0:T(8,128)S(1)}, u32[]{:S(2)}, u32[]{:S(2)}) %collective-permute-start.9) | collective-permute-done | bytes 98336 | tf_op jit(solution)/shard_map/ppermute | solution.py:44
  29.9 1.1 %collective-permute-done.15.more_9_ = f32[64,256]{1,0:T(8,128)S(1)} collective-permute-done((f32[64,256]{1,0:T(8,128)S(1)}, f32[64,256]{1,0:T(8,128)S(1)}, u32[]{:S(2)}, u32[]{:S(2)}) %collective-permute-start.15) | collective-permute-done | bytes 65568 | tf_op jit(solution)/shard_map/ppermute | solution.py:44
  31.1 1.3 %collective-permute-done.17.more_11_ = f32[64,256]{1,0:T(8,128)S(1)} collective-permute-done((f32[64,256]{1,0:T(8,128)S(1)}, f32[64,256]{1,0:T(8,128)S(1)}, u32[]{:S(2)}, u32[]{:S(2)}) %collective-permute-start.17) | collective-permute-done | bytes 65568 | tf_op jit(solution)/shard_map/ppermute | solution.py:44
  32.3 1.1 %products.2 = (f32[200,256]{1,0:T(8,128)S(1)}, f32[192,256]{1,0:T(8,128)S(1)}, bf16[1024,256]{1,0:T(8,128)(2,1)S(1)}, bf16[1024,256]{1,0:T(8,128)(2,1)S(1)}) custom-call(bf16[1024,256]{1,0:T(8,128)(2,1)S(1)} %get-tuple-element.31.top_ref, bf16[1024,256]{1,0:T(8,128)(2,1)S(1)} %get-tuple-element.32.rest_ref, f32[96,256]{1,0:T(8,128)S(1)} %add.68.more_0_, ...), custom_call_target="tpu_custom_call" | custom-call | tf_op jit(solution)/shard_map/products/pallas_call | solution.py:337
  33.4 1.9 %collective-permute-start.18 = (f32[200,256]{1,0:T(8,128)S(1)}, f32[200,256]{1,0:T(8,128)S(1)}, u32[]{:S(2)}, u32[]{:S(2)}) collective-permute-start(f32[200,256]{1,0:T(8,128)S(1)} %get-tuple-element.39), channel_id=1, source_target_pairs={{0,8},{8,0},{16,24},{24,16},{1,9},{9,1},{17,25},{25,17},{2,10},{10... | collective-permute-start | bytes 614408 | tf_op jit(solution)/shard_map/ppermute | solution.py:44
  35.3 1.5 %collective-permute-start.20 = (f32[192,256]{1,0:T(8,128)S(1)}, f32[192,256]{1,0:T(8,128)S(1)}, u32[]{:S(2)}, u32[]{:S(2)}) collective-permute-start(f32[192,256]{1,0:T(8,128)S(1)} %get-tuple-element.40), channel_id=1, source_target_pairs={{0,16},{8,24},{16,0},{24,8},{1,17},{9,25},{17,1},{25,9},{2,18},{10... | collective-permute-start | bytes 589832 | tf_op jit(solution)/shard_map/ppermute | solution.py:44
  36.9 3.9 %collective-permute-done.18 = f32[200,256]{1,0:T(8,128)S(1)} collective-permute-done((f32[200,256]{1,0:T(8,128)S(1)}, f32[200,256]{1,0:T(8,128)S(1)}, u32[]{:S(2)}, u32[]{:S(2)}) %collective-permute-start.18) | collective-permute-done | bytes 204832 | tf_op jit(solution)/shard_map/ppermute | solution.py:44
  40.8 1.8 %collective-permute-start.19 = (f32[200,256]{1,0:T(8,128)S(1)}, f32[200,256]{1,0:T(8,128)S(1)}, u32[]{:S(2)}, u32[]{:S(2)}) collective-permute-start(f32[200,256]{1,0:T(8,128)S(1)} %add.75.a_ref.refs_0_), channel_id=1, source_target_pairs={{0,16},{8,24},{16,0},{24,8},{1,17},{9,25},{17,1},{25,9},{2,18},{10... | collective-permute-start | bytes 614408 | tf_op jit(solution)/shard_map/ppermute | solution.py:44
  42.7 1.6 %collective-permute-start.21 = (f32[192,256]{1,0:T(8,128)S(1)}, f32[192,256]{1,0:T(8,128)S(1)}, u32[]{:S(2)}, u32[]{:S(2)}) collective-permute-start(f32[192,256]{1,0:T(8,128)S(1)} %add.76.refs_2_), channel_id=1, source_target_pairs={{0,8},{8,0},{16,24},{24,16},{1,9},{9,1},{17,25},{25,17},{2,10},{10... | collective-permute-start | bytes 589832 | tf_op jit(solution)/shard_map/ppermute | solution.py:44
  44.2 3.3 %inverse.2 = (f32[256,256]{1,0:T(8,128)S(1)}, f32[1,256]{1,0:T(1,128)S(1)}) custom-call(f32[200,256]{1,0:T(8,128)S(1)} %add.75.a_ref.refs_0_, f32[1,256]{1,0:T(1,128)S(1)} %bitcast.1), custom_call_target="tpu_custom_call" | custom-call | flops 1342177280 | bytes 524288 | tf_op jit(solution)/shard_map/inverse/pallas_call | solution.py:337
  47.5 1.1 %collective-permute-done.21.refs_3_ = f32[192,256]{1,0:T(8,128)S(1)} collective-permute-done((f32[192,256]{1,0:T(8,128)S(1)}, f32[192,256]{1,0:T(8,128)S(1)}, u32[]{:S(2)}, u32[]{:S(2)}) %collective-permute-start.21) | collective-permute-done | bytes 196640 | tf_op jit(solution)/shard_map/ppermute | solution.py:44
  48.6 4.5 %middle.1 = (bf16[1024,256]{1,0:T(8,128)(2,1)S(1)}, bf16[1024,256]{1,0:T(8,128)(2,1)S(1)}, f32[192,256]{1,0:T(8,128)S(1)}, f32[192,256]{1,0:T(8,128)S(1)}, f32[1...) custom-call(f32[200,256]{1,0:T(8,128)S(1)} %add.75.a_ref.refs_0_, ...), custom_call_target="tpu_custom_call" | custom-call | tf_op jit(solution)/shard_map/middle/pallas_call | solution.py:337
  53.8 0.9 collective-permute-done.22
  54.7 0.7 collective-permute-start.23
  55.4 1.5 %collective-permute-start.35 = (f32[64,256]{1,0:T(8,128)S(1)}, f32[64,256]{1,0:T(8,128)S(1)}, u32[]{:S(2)}, u32[]{:S(2)}) collective-permute-start(f32[64,256]{1,0:T(8,128)S(1)} %slice.59), channel_id=1, source_target_pairs={{0,2},{1,3},{2,0},{3,1},{4,6},{5,7},{6,4},{7,5},{8,10},{9,11},{10,... | collective-permute-start | bytes 196616 | tf_op jit(solution)/shard_map/ppermute | solution.py:44
  56.9 0.7 collective-permute-start.29
  57.6 2.8 %collective-permute-done.23 = f32[96,256]{1,0:T(8,128)S(1)} collective-permute-done((f32[96,256]{1,0:T(8,128)S(1)}, f32[96,256]{1,0:T(8,128)S(1)}, u32[]{:S(2)}, u32[]{:S(2)}) %collective-permute-start.23) | collective-permute-done | bytes 98336 | tf_op jit(solution)/shard_map/ppermute | solution.py:44
  60.4 2.2 %collective-permute-start.24 = (f32[96,256]{1,0:T(8,128)S(1)}, f32[96,256]{1,0:T(8,128)S(1)}, u32[]{:S(2)}, u32[]{:S(2)}) collective-permute-start(f32[96,256]{1,0:T(8,128)S(1)} %slice_add_fusion.1), channel_id=1, source_target_pairs={{0,4},{1,5},{2,6},{3,7},{4,0},{5,1},{6,2},{7,3},{8,12},{9,13},{10,... | collective-permute-start | bytes 294920 | tf_op jit(solution)/shard_map/ppermute | solution.py:44
  62.6 1.6 %collective-permute-done.29 = f32[96,256]{1,0:T(8,128)S(1)} collective-permute-done((f32[96,256]{1,0:T(8,128)S(1)}, f32[96,256]{1,0:T(8,128)S(1)}, u32[]{:S(2)}, u32[]{:S(2)}) %collective-permute-start.29) | collective-permute-done | bytes 98336 | tf_op jit(solution)/shard_map/ppermute | solution.py:44
  64.1 1.9 %collective-permute-start.30 = (f32[96,256]{1,0:T(8,128)S(1)}, f32[96,256]{1,0:T(8,128)S(1)}, u32[]{:S(2)}, u32[]{:S(2)}) collective-permute-start(f32[96,256]{1,0:T(8,128)S(1)} %slice_add_fusion), channel_id=1, source_target_pairs={{0,4},{1,5},{2,6},{3,7},{4,0},{5,1},{6,2},{7,3},{8,12},{9,13},{10,... | collective-permute-start | bytes 294920 | tf_op jit(solution)/shard_map/ppermute | solution.py:44
  66.1 1.1 %collective-permute-start.36 = (f32[64,256]{1,0:T(8,128)S(1)}, f32[64,256]{1,0:T(8,128)S(1)}, u32[]{:S(2)}, u32[]{:S(2)}) collective-permute-start(f32[64,256]{1,0:T(8,128)S(1)} %slice_add_fusion.4), channel_id=1, source_target_pairs={{0,4},{1,5},{2,6},{3,7},{4,0},{5,1},{6,2},{7,3},{8,12},{9,13},{10,... | collective-permute-start | bytes 196616 | tf_op jit(solution)/shard_map/ppermute | solution.py:44
  67.2 4.5 %collective-permute-done.24 = f32[96,256]{1,0:T(8,128)S(1)} collective-permute-done((f32[96,256]{1,0:T(8,128)S(1)}, f32[96,256]{1,0:T(8,128)S(1)}, u32[]{:S(2)}, u32[]{:S(2)}) %collective-permute-start.24) | collective-permute-done | bytes 98336 | tf_op jit(solution)/shard_map/ppermute | solution.py:44
  71.8 2.0 %collective-permute-done.30 = f32[96,256]{1,0:T(8,128)S(1)} collective-permute-done((f32[96,256]{1,0:T(8,128)S(1)}, f32[96,256]{1,0:T(8,128)S(1)}, u32[]{:S(2)}, u32[]{:S(2)}) %collective-permute-start.30) | collective-permute-done | bytes 98336 | tf_op jit(solution)/shard_map/ppermute | solution.py:44
  74.6 1.5 %collective-permute-start.37 = (f32[64,256]{1,0:T(8,128)S(1)}, f32[64,256]{1,0:T(8,128)S(1)}, u32[]{:S(2)}, u32[]{:S(2)}) collective-permute-start(f32[64,256]{1,0:T(8,128)S(1)} %add.85.more_8_), channel_id=1, source_target_pairs={{0,2},{1,3},{2,0},{3,1},{4,6},{5,7},{6,4},{7,5},{8,10},{9,11},{10,... | collective-permute-start | bytes 196616 | tf_op jit(solution)/shard_map/ppermute | solution.py:44
  76.6 0.7 collective-permute-done.25.more_1_
  77.3 1.9 %collective-permute-done.31.more_5_ = f32[96,256]{1,0:T(8,128)S(1)} collective-permute-done((f32[96,256]{1,0:T(8,128)S(1)}, f32[96,256]{1,0:T(8,128)S(1)}, u32[]{:S(2)}, u32[]{:S(2)}) %collective-permute-start.31) | collective-permute-done | bytes 98336 | tf_op jit(solution)/shard_map/ppermute | solution.py:44
  79.2 0.7 collective-permute-done.37.more_9_
  79.9 1.3 %collective-permute-done.39.more_11_ = f32[64,256]{1,0:T(8,128)S(1)} collective-permute-done((f32[64,256]{1,0:T(8,128)S(1)}, f32[64,256]{1,0:T(8,128)S(1)}, u32[]{:S(2)}, u32[]{:S(2)}) %collective-permute-start.39) | collective-permute-done | bytes 65568 | tf_op jit(solution)/shard_map/ppermute | solution.py:44
  81.2 1.1 %products.3 = (f32[200,256]{1,0:T(8,128)S(1)}, f32[192,256]{1,0:T(8,128)S(1)}, bf16[1024,256]{1,0:T(8,128)(2,1)S(1)}, bf16[1024,256]{1,0:T(8,128)(2,1)S(1)}) custom-call(bf16[1024,256]{1,0:T(8,128)(2,1)S(1)} %get-tuple-element.46.top_ref, bf16[1024,256]{1,0:T(8,128)(2,1)S(1)} %get-tuple-element.47.rest_ref, f32[96,256]{1,0:T(8,128)S(1)} %add.79.more_0_, ...), custom_call_target="tpu_custom_call" | custom-call | tf_op jit(solution)/shard_map/products/pallas_call | solution.py:337
  82.3 1.6 %collective-permute-start.40 = (f32[200,256]{1,0:T(8,128)S(1)}, f32[200,256]{1,0:T(8,128)S(1)}, u32[]{:S(2)}, u32[]{:S(2)}) collective-permute-start(f32[200,256]{1,0:T(8,128)S(1)} %get-tuple-element.54), channel_id=1, source_target_pairs={{0,8},{8,0},{16,24},{24,16},{1,9},{9,1},{17,25},{25,17},{2,10},{10... | collective-permute-start | bytes 614408 | tf_op jit(solution)/shard_map/ppermute | solution.py:44
  84.4 5.1 %collective-permute-done.40 = f32[200,256]{1,0:T(8,128)S(1)} collective-permute-done((f32[200,256]{1,0:T(8,128)S(1)}, f32[200,256]{1,0:T(8,128)S(1)}, u32[]{:S(2)}, u32[]{:S(2)}) %collective-permute-start.40) | collective-permute-done | bytes 204832 | tf_op jit(solution)/shard_map/ppermute | solution.py:44
  89.5 1.0 collective-permute-start.41
  90.6 1.1 %collective-permute-start.43 = (f32[192,256]{1,0:T(8,128)S(1)}, f32[192,256]{1,0:T(8,128)S(1)}, u32[]{:S(2)}, u32[]{:S(2)}) collective-permute-start(f32[192,256]{1,0:T(8,128)S(1)} %add.87.refs_2_), channel_id=1, source_target_pairs={{0,8},{8,0},{16,24},{24,16},{1,9},{9,1},{17,25},{25,17},{2,10},{10... | collective-permute-start | bytes 589832 | tf_op jit(solution)/shard_map/ppermute | solution.py:44
  91.7 3.3 %inverse.3 = (f32[256,256]{1,0:T(8,128)S(1)}, f32[1,256]{1,0:T(1,128)S(1)}) custom-call(f32[200,256]{1,0:T(8,128)S(1)} %add.86.a_ref.refs_0_, f32[1,256]{1,0:T(1,128)S(1)} %get-tuple-element.45.refs_8_.level_ref), custom_call_target="tpu_custom_call" | custom-call | flops 1342177280 | bytes 524288 | tf_op jit(solution)/shard_map/inverse/pallas_call | solution.py:337
  95.0 1.5 %collective-permute-done.43.refs_3_ = f32[192,256]{1,0:T(8,128)S(1)} collective-permute-done((f32[192,256]{1,0:T(8,128)S(1)}, f32[192,256]{1,0:T(8,128)S(1)}, u32[]{:S(2)}, u32[]{:S(2)}) %collective-permute-start.43) | collective-permute-done | bytes 196640 | tf_op jit(solution)/shard_map/ppermute | solution.py:44
  96.5 4.8 %last.1 = (f32[1024,256]{1,0:T(8,128)}, f32[1024,256]{1,0:T(8,128)}) custom-call(f32[200,256]{1,0:T(8,128)S(1)} %add.86.a_ref.refs_0_, f32[200,256]{1,0:T(8,128)S(1)} %collective-permute-done.41.refs_1_, f32[192,256]{1,0:T(8,128)S(1)} %add.87.refs_2_, f32[192,256]{1,0:T(8,128)S(1)} %collective-permute-done.43.refs_3_, ...), custom_call_target="tpu_custom_call" | custom-call | tf_op jit(solution)/shard_map/last/pallas_call | solution.py:337
  (77 shorter events, 7.1 us)
Async XLA Ops:
  3.2 1.6 %collective-permute-start = (f32[192,256]{1,0:T(8,128)S(1)}, f32[192,256]{1,0:T(8,128)S(1)}, u32[]{:S(2)}, u32[]{:S(2)}) collective-permute-start(f32[192,256]{1,0:T(8,128)S(1)} %get-tuple-element.34), channel_id=1, source_target_pairs={{0,1},{1,0},{2,3},{3,2},{4,5},{5,4},{6,7},{7,6},{8,9},{9,8},{10,11... | collective-permute-start | bytes 589832 | tf_op jit(solution)/shard_map/ppermute | solution.py:44
  3.7 4.6 %collective-permute-start.6 = (f32[192,256]{1,0:T(8,128)S(1)}, f32[192,256]{1,0:T(8,128)S(1)}, u32[]{:S(2)}, u32[]{:S(2)}) collective-permute-start(f32[192,256]{1,0:T(8,128)S(1)} %get-tuple-element.36), channel_id=1, source_target_pairs={{0,1},{1,0},{2,3},{3,2},{4,5},{5,4},{6,7},{7,6},{8,9},{9,8},{10,11... | collective-permute-start | bytes 589832 | tf_op jit(solution)/shard_map/ppermute | solution.py:44
  3.8 4.0 %collective-permute-start.12 = (f32[128,256]{1,0:T(8,128)S(1)}, f32[128,256]{1,0:T(8,128)S(1)}, u32[]{:S(2)}, u32[]{:S(2)}) collective-permute-start(f32[128,256]{1,0:T(8,128)S(1)} %get-tuple-element.38), channel_id=1, source_target_pairs={{0,1},{1,0},{2,3},{3,2},{4,5},{5,4},{6,7},{7,6},{8,9},{9,8},{10,11... | collective-permute-start | bytes 393224 | tf_op jit(solution)/shard_map/ppermute | solution.py:44
  4.8 6.6 %collective-permute-start.1 = (f32[96,256]{1,0:T(8,128)S(1)}, f32[96,256]{1,0:T(8,128)S(1)}, u32[]{:S(2)}, u32[]{:S(2)}) collective-permute-start(f32[96,256]{1,0:T(8,128)S(1)} %slice.49), channel_id=1, source_target_pairs={{0,2},{1,3},{2,0},{3,1},{4,6},{5,7},{6,4},{7,5},{8,10},{9,11},{10,... | collective-permute-start | bytes 294920 | tf_op jit(solution)/shard_map/ppermute | solution.py:44
  7.9 10.2 %collective-permute-start.13 = (f32[64,256]{1,0:T(8,128)S(1)}, f32[64,256]{1,0:T(8,128)S(1)}, u32[]{:S(2)}, u32[]{:S(2)}) collective-permute-start(f32[64,256]{1,0:T(8,128)S(1)} %slice.53), channel_id=1, source_target_pairs={{0,2},{1,3},{2,0},{3,1},{4,6},{5,7},{6,4},{7,5},{8,10},{9,11},{10,... | collective-permute-start | bytes 196616 | tf_op jit(solution)/shard_map/ppermute | solution.py:44
  8.3 7.2 %collective-permute-start.7 = (f32[96,256]{1,0:T(8,128)S(1)}, f32[96,256]{1,0:T(8,128)S(1)}, u32[]{:S(2)}, u32[]{:S(2)}) collective-permute-start(f32[96,256]{1,0:T(8,128)S(1)} %slice.51), channel_id=1, source_target_pairs={{0,2},{1,3},{2,0},{3,1},{4,6},{5,7},{6,4},{7,5},{8,10},{9,11},{10,... | collective-permute-start | bytes 294920 | tf_op jit(solution)/shard_map/ppermute | solution.py:44
  11.4 9.1 %collective-permute-start.2 = (f32[96,256]{1,0:T(8,128)S(1)}, f32[96,256]{1,0:T(8,128)S(1)}, u32[]{:S(2)}, u32[]{:S(2)}) collective-permute-start(f32[96,256]{1,0:T(8,128)S(1)} %slice_add_fusion.3), channel_id=1, source_target_pairs={{0,4},{1,5},{2,6},{3,7},{4,0},{5,1},{6,2},{7,3},{8,12},{9,13},{10,... | collective-permute-start | bytes 294920 | tf_op jit(solution)/shard_map/ppermute | solution.py:44
  15.5 9.5 %collective-permute-start.8 = (f32[96,256]{1,0:T(8,128)S(1)}, f32[96,256]{1,0:T(8,128)S(1)}, u32[]{:S(2)}, u32[]{:S(2)}) collective-permute-start(f32[96,256]{1,0:T(8,128)S(1)} %slice_add_fusion.2), channel_id=1, source_target_pairs={{0,4},{1,5},{2,6},{3,7},{4,0},{5,1},{6,2},{7,3},{8,12},{9,13},{10,... | collective-permute-start | bytes 294920 | tf_op jit(solution)/shard_map/ppermute | solution.py:44
  18.0 8.2 %collective-permute-start.14 = (f32[64,256]{1,0:T(8,128)S(1)}, f32[64,256]{1,0:T(8,128)S(1)}, u32[]{:S(2)}, u32[]{:S(2)}) collective-permute-start(f32[64,256]{1,0:T(8,128)S(1)} %slice_add_fusion.5), channel_id=1, source_target_pairs={{0,4},{1,5},{2,6},{3,7},{4,0},{5,1},{6,2},{7,3},{8,12},{9,13},{10,... | collective-permute-start | bytes 196616 | tf_op jit(solution)/shard_map/ppermute | solution.py:44
  20.5 7.2 %collective-permute-start.3 = (f32[96,256]{1,0:T(8,128)S(1)}, f32[96,256]{1,0:T(8,128)S(1)}, u32[]{:S(2)}, u32[]{:S(2)}) collective-permute-start(f32[96,256]{1,0:T(8,128)S(1)} %add.68.more_0_), channel_id=1, source_target_pairs={{0,2},{1,3},{2,0},{3,1},{4,6},{5,7},{6,4},{7,5},{8,10},{9,11},{10,... | collective-permute-start | bytes 294920 | tf_op jit(solution)/shard_map/ppermute | solution.py:44
  25.0 4.9 %collective-permute-start.9 = (f32[96,256]{1,0:T(8,128)S(1)}, f32[96,256]{1,0:T(8,128)S(1)}, u32[]{:S(2)}, u32[]{:S(2)}) collective-permute-start(f32[96,256]{1,0:T(8,128)S(1)} %add.71.more_4_), channel_id=1, source_target_pairs={{0,2},{1,3},{2,0},{3,1},{4,6},{5,7},{6,4},{7,5},{8,10},{9,11},{10,... | collective-permute-start | bytes 294920 | tf_op jit(solution)/shard_map/ppermute | solution.py:44
  26.2 1.3 %collective-permute-start.16 = (f32[64,256]{1,0:T(8,128)S(1)}, f32[64,256]{1,0:T(8,128)S(1)}, u32[]{:S(2)}, u32[]{:S(2)}) collective-permute-start(f32[64,256]{1,0:T(8,128)S(1)} %add.74.more_8_), channel_id=1, source_target_pairs={{0,1},{1,0},{2,3},{3,2},{4,5},{5,4},{6,7},{7,6},{8,9},{9,8},{10,11... | collective-permute-start | bytes 196616 | tf_op jit(solution)/shard_map/ppermute | solution.py:44
  26.3 4.7 %collective-permute-start.15 = (f32[64,256]{1,0:T(8,128)S(1)}, f32[64,256]{1,0:T(8,128)S(1)}, u32[]{:S(2)}, u32[]{:S(2)}) collective-permute-start(f32[64,256]{1,0:T(8,128)S(1)} %add.74.more_8_), channel_id=1, source_target_pairs={{0,2},{1,3},{2,0},{3,1},{4,6},{5,7},{6,4},{7,5},{8,10},{9,11},{10,... | collective-permute-start | bytes 196616 | tf_op jit(solution)/shard_map/ppermute | solution.py:44
  27.2 5.1 %collective-permute-start.4 = (f32[96,256]{1,0:T(8,128)S(1)}, f32[96,256]{1,0:T(8,128)S(1)}, u32[]{:S(2)}, u32[]{:S(2)}) collective-permute-start(f32[96,256]{1,0:T(8,128)S(1)} %add.68.more_0_), channel_id=1, source_target_pairs={{0,1},{1,0},{2,3},{3,2},{4,5},{5,4},{6,7},{7,6},{8,9},{9,8},{10,11... | collective-permute-start | bytes 294920 | tf_op jit(solution)/shard_map/ppermute | solution.py:44
  27.6 4.8 %collective-permute-start.10 = (f32[96,256]{1,0:T(8,128)S(1)}, f32[96,256]{1,0:T(8,128)S(1)}, u32[]{:S(2)}, u32[]{:S(2)}) collective-permute-start(f32[96,256]{1,0:T(8,128)S(1)} %add.71.more_4_), channel_id=1, source_target_pairs={{0,1},{1,0},{2,3},{3,2},{4,5},{5,4},{6,7},{7,6},{8,9},{9,8},{10,11... | collective-permute-start | bytes 294920 | tf_op jit(solution)/shard_map/ppermute | solution.py:44
  27.8 4.6 %collective-permute-start.5 = (f32[96,256]{1,0:T(8,128)S(1)}, f32[96,256]{1,0:T(8,128)S(1)}, u32[]{:S(2)}, u32[]{:S(2)}) collective-permute-start(f32[96,256]{1,0:T(8,128)S(1)} %collective-permute-done.3.more_1_), channel_id=1, source_target_pairs={{0,1},{1,0},{2,3},{3,2},{4,5},{5,4},{6,7},{7,6},{8,9},{9,8},{10,11... | collective-permute-start | bytes 294920 | tf_op jit(solution)/shard_map/ppermute | solution.py:44
  29.9 2.4 %collective-permute-start.11 = (f32[96,256]{1,0:T(8,128)S(1)}, f32[96,256]{1,0:T(8,128)S(1)}, u32[]{:S(2)}, u32[]{:S(2)}) collective-permute-start(f32[96,256]{1,0:T(8,128)S(1)} %collective-permute-done.9.more_5_), channel_id=1, source_target_pairs={{0,1},{1,0},{2,3},{3,2},{4,5},{5,4},{6,7},{7,6},{8,9},{9,8},{10,11... | collective-permute-start | bytes 294920 | tf_op jit(solution)/shard_map/ppermute | solution.py:44
  31.1 1.3 %collective-permute-start.17 = (f32[64,256]{1,0:T(8,128)S(1)}, f32[64,256]{1,0:T(8,128)S(1)}, u32[]{:S(2)}, u32[]{:S(2)}) collective-permute-start(f32[64,256]{1,0:T(8,128)S(1)} %collective-permute-done.15.more_9_), channel_id=1, source_target_pairs={{0,1},{1,0},{2,3},{3,2},{4,5},{5,4},{6,7},{7,6},{8,9},{9,8},{10,11... | collective-permute-start | bytes 196616 | tf_op jit(solution)/shard_map/ppermute | solution.py:44
  33.4 7.3 %collective-permute-start.18 = (f32[200,256]{1,0:T(8,128)S(1)}, f32[200,256]{1,0:T(8,128)S(1)}, u32[]{:S(2)}, u32[]{:S(2)}) collective-permute-start(f32[200,256]{1,0:T(8,128)S(1)} %get-tuple-element.39), channel_id=1, source_target_pairs={{0,8},{8,0},{16,24},{24,16},{1,9},{9,1},{17,25},{25,17},{2,10},{10... | collective-permute-start | bytes 614408 | tf_op jit(solution)/shard_map/ppermute | solution.py:44
  35.3 7.3 %collective-permute-start.20 = (f32[192,256]{1,0:T(8,128)S(1)}, f32[192,256]{1,0:T(8,128)S(1)}, u32[]{:S(2)}, u32[]{:S(2)}) collective-permute-start(f32[192,256]{1,0:T(8,128)S(1)} %get-tuple-element.40), channel_id=1, source_target_pairs={{0,16},{8,24},{16,0},{24,8},{1,17},{9,25},{17,1},{25,9},{2,18},{10... | collective-permute-start | bytes 589832 | tf_op jit(solution)/shard_map/ppermute | solution.py:44
  40.8 7.8 %collective-permute-start.19 = (f32[200,256]{1,0:T(8,128)S(1)}, f32[200,256]{1,0:T(8,128)S(1)}, u32[]{:S(2)}, u32[]{:S(2)}) collective-permute-start(f32[200,256]{1,0:T(8,128)S(1)} %add.75.a_ref.refs_0_), channel_id=1, source_target_pairs={{0,16},{8,24},{16,0},{24,8},{1,17},{9,25},{17,1},{25,9},{2,18},{10... | collective-permute-start | bytes 614408 | tf_op jit(solution)/shard_map/ppermute | solution.py:44
  42.6 1.6 %copy-start = (f32[256]{0:T(256)S(1)}, f32[256]{0:T(256)}, u32[]{:S(2)}) copy-start(f32[256]{0:T(256)} %param.5) | copy-start | bytes 3076
  42.7 5.9 %collective-permute-start.21 = (f32[192,256]{1,0:T(8,128)S(1)}, f32[192,256]{1,0:T(8,128)S(1)}, u32[]{:S(2)}, u32[]{:S(2)}) collective-permute-start(f32[192,256]{1,0:T(8,128)S(1)} %add.76.refs_2_), channel_id=1, source_target_pairs={{0,8},{8,0},{16,24},{24,16},{1,9},{9,1},{17,25},{25,17},{2,10},{10... | collective-permute-start | bytes 589832 | tf_op jit(solution)/shard_map/ppermute | solution.py:44
  53.1 1.5 %collective-permute-start.22 = (f32[192,256]{1,0:T(8,128)S(1)}, f32[192,256]{1,0:T(8,128)S(1)}, u32[]{:S(2)}, u32[]{:S(2)}) collective-permute-start(f32[192,256]{1,0:T(8,128)S(1)} %get-tuple-element.49), channel_id=1, source_target_pairs={{0,1},{1,0},{2,3},{3,2},{4,5},{5,4},{6,7},{7,6},{8,9},{9,8},{10,11... | collective-permute-start | bytes 589832 | tf_op jit(solution)/shard_map/ppermute | solution.py:44
  53.2 3.7 %collective-permute-start.28 = (f32[192,256]{1,0:T(8,128)S(1)}, f32[192,256]{1,0:T(8,128)S(1)}, u32[]{:S(2)}, u32[]{:S(2)}) collective-permute-start(f32[192,256]{1,0:T(8,128)S(1)} %get-tuple-element.51), channel_id=1, source_target_pairs={{0,1},{1,0},{2,3},{3,2},{4,5},{5,4},{6,7},{7,6},{8,9},{9,8},{10,11... | collective-permute-start | bytes 589832 | tf_op jit(solution)/shard_map/ppermute | solution.py:44
  53.7 1.7 %collective-permute-start.34 = (f32[128,256]{1,0:T(8,128)S(1)}, f32[128,256]{1,0:T(8,128)S(1)}, u32[]{:S(2)}, u32[]{:S(2)}) collective-permute-start(f32[128,256]{1,0:T(8,128)S(1)} %get-tuple-element.53), channel_id=1, source_target_pairs={{0,1},{1,0},{2,3},{3,2},{4,5},{5,4},{6,7},{7,6},{8,9},{9,8},{10,11... | collective-permute-start | bytes 393224 | tf_op jit(solution)/shard_map/ppermute | solution.py:44
  54.7 5.7 %collective-permute-start.23 = (f32[96,256]{1,0:T(8,128)S(1)}, f32[96,256]{1,0:T(8,128)S(1)}, u32[]{:S(2)}, u32[]{:S(2)}) collective-permute-start(f32[96,256]{1,0:T(8,128)S(1)} %slice.55), channel_id=1, source_target_pairs={{0,2},{1,3},{2,0},{3,1},{4,6},{5,7},{6,4},{7,5},{8,10},{9,11},{10,... | collective-permute-start | bytes 294920 | tf_op jit(solution)/shard_map/ppermute | solution.py:44
  55.4 10.7 %collective-permute-start.35 = (f32[64,256]{1,0:T(8,128)S(1)}, f32[64,256]{1,0:T(8,128)S(1)}, u32[]{:S(2)}, u32[]{:S(2)}) collective-permute-start(f32[64,256]{1,0:T(8,128)S(1)} %slice.59), channel_id=1, source_target_pairs={{0,2},{1,3},{2,0},{3,1},{4,6},{5,7},{6,4},{7,5},{8,10},{9,11},{10,... | collective-permute-start | bytes 196616 | tf_op jit(solution)/shard_map/ppermute | solution.py:44
  56.9 7.2 %collective-permute-start.29 = (f32[96,256]{1,0:T(8,128)S(1)}, f32[96,256]{1,0:T(8,128)S(1)}, u32[]{:S(2)}, u32[]{:S(2)}) collective-permute-start(f32[96,256]{1,0:T(8,128)S(1)} %slice.57), channel_id=1, source_target_pairs={{0,2},{1,3},{2,0},{3,1},{4,6},{5,7},{6,4},{7,5},{8,10},{9,11},{10,... | collective-permute-start | bytes 294920 | tf_op jit(solution)/shard_map/ppermute | solution.py:44
  60.4 11.3 %collective-permute-start.24 = (f32[96,256]{1,0:T(8,128)S(1)}, f32[96,256]{1,0:T(8,128)S(1)}, u32[]{:S(2)}, u32[]{:S(2)}) collective-permute-start(f32[96,256]{1,0:T(8,128)S(1)} %slice_add_fusion.1), channel_id=1, source_target_pairs={{0,4},{1,5},{2,6},{3,7},{4,0},{5,1},{6,2},{7,3},{8,12},{9,13},{10,... | collective-permute-start | bytes 294920 | tf_op jit(solution)/shard_map/ppermute | solution.py:44
  64.1 9.7 %collective-permute-start.30 = (f32[96,256]{1,0:T(8,128)S(1)}, f32[96,256]{1,0:T(8,128)S(1)}, u32[]{:S(2)}, u32[]{:S(2)}) collective-permute-start(f32[96,256]{1,0:T(8,128)S(1)} %slice_add_fusion), channel_id=1, source_target_pairs={{0,4},{1,5},{2,6},{3,7},{4,0},{5,1},{6,2},{7,3},{8,12},{9,13},{10,... | collective-permute-start | bytes 294920 | tf_op jit(solution)/shard_map/ppermute | solution.py:44
  66.1 8.5 %collective-permute-start.36 = (f32[64,256]{1,0:T(8,128)S(1)}, f32[64,256]{1,0:T(8,128)S(1)}, u32[]{:S(2)}, u32[]{:S(2)}) collective-permute-start(f32[64,256]{1,0:T(8,128)S(1)} %slice_add_fusion.4), channel_id=1, source_target_pairs={{0,4},{1,5},{2,6},{3,7},{4,0},{5,1},{6,2},{7,3},{8,12},{9,13},{10,... | collective-permute-start | bytes 196616 | tf_op jit(solution)/shard_map/ppermute | solution.py:44
  71.7 5.6 %collective-permute-start.25 = (f32[96,256]{1,0:T(8,128)S(1)}, f32[96,256]{1,0:T(8,128)S(1)}, u32[]{:S(2)}, u32[]{:S(2)}) collective-permute-start(f32[96,256]{1,0:T(8,128)S(1)} %add.79.more_0_), channel_id=1, source_target_pairs={{0,2},{1,3},{2,0},{3,1},{4,6},{5,7},{6,4},{7,5},{8,10},{9,11},{10,... | collective-permute-start | bytes 294920 | tf_op jit(solution)/shard_map/ppermute | solution.py:44
  73.8 5.4 %collective-permute-start.31 = (f32[96,256]{1,0:T(8,128)S(1)}, f32[96,256]{1,0:T(8,128)S(1)}, u32[]{:S(2)}, u32[]{:S(2)}) collective-permute-start(f32[96,256]{1,0:T(8,128)S(1)} %add.82.more_4_), channel_id=1, source_target_pairs={{0,2},{1,3},{2,0},{3,1},{4,6},{5,7},{6,4},{7,5},{8,10},{9,11},{10,... | collective-permute-start | bytes 294920 | tf_op jit(solution)/shard_map/ppermute | solution.py:44
  74.6 1.7 %collective-permute-start.38 = (f32[64,256]{1,0:T(8,128)S(1)}, f32[64,256]{1,0:T(8,128)S(1)}, u32[]{:S(2)}, u32[]{:S(2)}) collective-permute-start(f32[64,256]{1,0:T(8,128)S(1)} %add.85.more_8_), channel_id=1, source_target_pairs={{0,1},{1,0},{2,3},{3,2},{4,5},{5,4},{6,7},{7,6},{8,9},{9,8},{10,11... | collective-permute-start | bytes 196616 | tf_op jit(solution)/shard_map/ppermute | solution.py:44
  74.6 5.3 %collective-permute-start.37 = (f32[64,256]{1,0:T(8,128)S(1)}, f32[64,256]{1,0:T(8,128)S(1)}, u32[]{:S(2)}, u32[]{:S(2)}) collective-permute-start(f32[64,256]{1,0:T(8,128)S(1)} %add.85.more_8_), channel_id=1, source_target_pairs={{0,2},{1,3},{2,0},{3,1},{4,6},{5,7},{6,4},{7,5},{8,10},{9,11},{10,... | collective-permute-start | bytes 196616 | tf_op jit(solution)/shard_map/ppermute | solution.py:44
  76.1 5.1 %collective-permute-start.26 = (f32[96,256]{1,0:T(8,128)S(1)}, f32[96,256]{1,0:T(8,128)S(1)}, u32[]{:S(2)}, u32[]{:S(2)}) collective-permute-start(f32[96,256]{1,0:T(8,128)S(1)} %add.79.more_0_), channel_id=1, source_target_pairs={{0,1},{1,0},{2,3},{3,2},{4,5},{5,4},{6,7},{7,6},{8,9},{9,8},{10,11... | collective-permute-start | bytes 294920 | tf_op jit(solution)/shard_map/ppermute | solution.py:44
  76.3 4.9 %collective-permute-start.32 = (f32[96,256]{1,0:T(8,128)S(1)}, f32[96,256]{1,0:T(8,128)S(1)}, u32[]{:S(2)}, u32[]{:S(2)}) collective-permute-start(f32[96,256]{1,0:T(8,128)S(1)} %add.82.more_4_), channel_id=1, source_target_pairs={{0,1},{1,0},{2,3},{3,2},{4,5},{5,4},{6,7},{7,6},{8,9},{9,8},{10,11... | collective-permute-start | bytes 294920 | tf_op jit(solution)/shard_map/ppermute | solution.py:44
  77.3 3.8 %collective-permute-start.27 = (f32[96,256]{1,0:T(8,128)S(1)}, f32[96,256]{1,0:T(8,128)S(1)}, u32[]{:S(2)}, u32[]{:S(2)}) collective-permute-start(f32[96,256]{1,0:T(8,128)S(1)} %collective-permute-done.25.more_1_), channel_id=1, source_target_pairs={{0,1},{1,0},{2,3},{3,2},{4,5},{5,4},{6,7},{7,6},{8,9},{9,8},{10,11... | collective-permute-start | bytes 294920 | tf_op jit(solution)/shard_map/ppermute | solution.py:44
  79.2 2.0 %collective-permute-start.33 = (f32[96,256]{1,0:T(8,128)S(1)}, f32[96,256]{1,0:T(8,128)S(1)}, u32[]{:S(2)}, u32[]{:S(2)}) collective-permute-start(f32[96,256]{1,0:T(8,128)S(1)} %collective-permute-done.31.more_5_), channel_id=1, source_target_pairs={{0,1},{1,0},{2,3},{3,2},{4,5},{5,4},{6,7},{7,6},{8,9},{9,8},{10,11... | collective-permute-start | bytes 294920 | tf_op jit(solution)/shard_map/ppermute | solution.py:44
  79.9 1.3 %collective-permute-start.39 = (f32[64,256]{1,0:T(8,128)S(1)}, f32[64,256]{1,0:T(8,128)S(1)}, u32[]{:S(2)}, u32[]{:S(2)}) collective-permute-start(f32[64,256]{1,0:T(8,128)S(1)} %collective-permute-done.37.more_9_), channel_id=1, source_target_pairs={{0,1},{1,0},{2,3},{3,2},{4,5},{5,4},{6,7},{7,6},{8,9},{9,8},{10,11... | collective-permute-start | bytes 196616 | tf_op jit(solution)/shard_map/ppermute | solution.py:44
  82.3 7.2 %collective-permute-start.40 = (f32[200,256]{1,0:T(8,128)S(1)}, f32[200,256]{1,0:T(8,128)S(1)}, u32[]{:S(2)}, u32[]{:S(2)}) collective-permute-start(f32[200,256]{1,0:T(8,128)S(1)} %get-tuple-element.54), channel_id=1, source_target_pairs={{0,8},{8,0},{16,24},{24,16},{1,9},{9,1},{17,25},{25,17},{2,10},{10... | collective-permute-start | bytes 614408 | tf_op jit(solution)/shard_map/ppermute | solution.py:44
  83.9 6.7 %collective-permute-start.42 = (f32[192,256]{1,0:T(8,128)S(1)}, f32[192,256]{1,0:T(8,128)S(1)}, u32[]{:S(2)}, u32[]{:S(2)}) collective-permute-start(f32[192,256]{1,0:T(8,128)S(1)} %get-tuple-element.55), channel_id=1, source_target_pairs={{0,16},{8,24},{16,0},{24,8},{1,17},{9,25},{17,1},{25,9},{2,18},{10... | collective-permute-start | bytes 589832 | tf_op jit(solution)/shard_map/ppermute | solution.py:44
  89.5 6.9 %collective-permute-start.41 = (f32[200,256]{1,0:T(8,128)S(1)}, f32[200,256]{1,0:T(8,128)S(1)}, u32[]{:S(2)}, u32[]{:S(2)}) collective-permute-start(f32[200,256]{1,0:T(8,128)S(1)} %add.86.a_ref.refs_0_), channel_id=1, source_target_pairs={{0,16},{8,24},{16,0},{24,8},{1,17},{9,25},{17,1},{25,9},{2,18},{10... | collective-permute-start | bytes 614408 | tf_op jit(solution)/shard_map/ppermute | solution.py:44
  90.6 5.9 %collective-permute-start.43 = (f32[192,256]{1,0:T(8,128)S(1)}, f32[192,256]{1,0:T(8,128)S(1)}, u32[]{:S(2)}, u32[]{:S(2)}) collective-permute-start(f32[192,256]{1,0:T(8,128)S(1)} %add.87.refs_2_), channel_id=1, source_target_pairs={{0,8},{8,0},{16,24},{24,16},{1,9},{9,1},{17,25},{25,17},{2,10},{10... | collective-permute-start | bytes 589832 | tf_op jit(solution)/shard_map/ppermute | solution.py:44

commit v6 on v5

--- a/solution.py
+++ b/solution.py
@@ -9,7 +9,7 @@
 ITERS = 2
 SHARES = 6, 6, 4
 SUBLANES = 8
-LOW = 1e-3
+LOW = 7e-4
 NEAR, FAR = 1.25, 4.2
 VMEM_BYTES = 16 << 20
 
@@ -66,15 +66,15 @@
     return pieces
 
 
-def sum_rows(a, b, size):
+def sum_rows(parts, turns, size):
     bits = bits_of(size)
-    turn = len(bits) // 2
-    pair_a, pair_b = None, None
-    for bit_a, bit_b in zip(bits, bits[turn:] + bits[:turn]):
-        a = a if pair_a is None else pair_a[0] + pair_a[1]
-        b = b if pair_b is None else pair_b[0] + pair_b[1]
-        pair_a, pair_b = (a, swap(a, "rows", size, bit_a)), (b, swap(b, "rows", size, bit_b))
-    return pair_a + pair_b
+    out = []
+    for x, turn in zip(parts, turns):
+        order = bits[turn * (len(bits) // 2) :] + bits[: turn * (len(bits) // 2)]
+        for bit in order[:-1]:
+            x = x + swap(x, "rows", size, bit)
+        out += [x, swap(x, "rows", size, order[-1])]
+    return out
 
 
 def lowest(blocks):
@@ -86,7 +86,7 @@
 
 
 def chunks_of(tall):
-    ends = [sum(SHARES[:i]) * tall // sum(SHARES) for i in range(len(SHARES) + 1)]
+    ends = [(sum(SHARES[:i]) * tall // sum(SHARES) + 8) // 16 * 16 for i in range(len(SHARES) + 1)]
     return [(at, end - at) for at, end in zip(ends, ends[1:])]
 
 
@@ -129,8 +129,8 @@
     write_left(left, left_refs, blocks)
 
 
-def product_kernel(blocks, counts, top_ref, rest_ref, *more):
-    left_refs, (a_ref, b_ref, left_top_ref, left_rest_ref) = more[:-4], more[-4:]
+def gram_kernel(blocks, counts, *more):
+    left_refs, (gram_ref, left_top_ref, left_rest_ref) = more[:-3], more[-3:]
     rows, rank = left_top_ref.shape
     tall = rows // blocks
     taken = 0
@@ -144,24 +144,22 @@
                 p += 1
         taken += counts[c]
     left = left_top_ref[...], left_rest_ref[...]
-    right = dot3(left, (top_ref[...], rest_ref[...]), TN)
     cross = dot(left[0], left[1], TN)
     gram = dot(left[0], left[0], TN) + (cross + cross.T + dot(left[1], left[1], TN))
-    pack(gram, right, a_ref, b_ref)
-
-
-def pack(gram, right, a_ref, b_ref):
+    pack(gram, gram_ref)
+
+
+def right_kernel(left_top_ref, left_rest_ref, top_ref, rest_ref, a_ref, b_ref):
+    right = dot3((left_top_ref[...], left_rest_ref[...]), (top_ref[...], rest_ref[...]), TN)
+    a_ref[...], b_ref[...] = right[: a_ref.shape[0]], right[a_ref.shape[0] :]
+
+
+def pack(gram, out_ref):
     half = gram.shape[0] // 2
-    lower = below(half)
-    a_ref[:half, :half] = jnp.where(lower, gram[:half, :half], gram[half:, half:])
-    a_ref[:half, half:] = gram[half:, :half]
+    out_ref[:half, :half] = jnp.where(below(half), gram[:half, :half], gram[half:, half:])
+    out_ref[:half, half:] = gram[half:, :half]
     diagonal = jnp.sum(jnp.where(identity(half), gram[half:, half:], 0.0), 0, keepdims=True)
-    a_ref[half : half + SUBLANES, :] = jnp.broadcast_to(
-        jnp.concatenate([diagonal, diagonal], 1), (SUBLANES, 2 * half)
-    )
-    taken = a_ref.shape[0] - half - SUBLANES
-    a_ref[half + SUBLANES :, :] = right[:taken]
-    b_ref[...] = right[taken:]
+    out_ref[half:, :] = jnp.broadcast_to(jnp.concatenate([diagonal, diagonal], 1), (SUBLANES, 2 * half))
 
 
 def unpack_gram(a):
@@ -174,10 +172,6 @@
     return jnp.concatenate([jnp.concatenate([first, off.T], 1), jnp.concatenate([off, second], 1)], 0)
 
 
-def unpack_right(a, b):
-    return jnp.concatenate([a[a.shape[1] // 2 + SUBLANES :], b], 0)
-
-
 def identity(n):
     return lax.broadcasted_iota(jnp.int32, (n, n), 0) == lax.broadcasted_iota(jnp.int32, (n, n), 1)
 
@@ -225,12 +219,18 @@
     return jnp.sum(on_diag, 1, keepdims=True), jnp.sum(on_diag, 0, keepdims=True)
 
 
-def invert(scaled, enough):
+def begin(scaled):
     terms = split(scaled, 2)
     eye = identity(scaled.shape[0]).astype(f32)
     high = norm_bound(scaled)
-    a, b, error, growth = chebyshev(scaled, dot3(terms, terms), LOW * high, high)
-    return converge(a * eye - b * scaled, error, growth, enough)
+    step = 1.0 / high
+    a, b, error, growth = chebyshev(step * scaled, (step * step) * dot3(terms, terms), LOW, 1.0)
+    return step * (a * eye - (b * step) * scaled), error, growth
+
+
+def invert(scaled, enough):
+    inverse, error, growth = begin(scaled)
+    return converge(inverse, error, jnp.float32(growth), enough)
 
 
 def inverse_kernel(a_ref, level_ref, out_ref, level_out_ref):
@@ -238,7 +238,10 @@
     gram = unpack_gram(a_ref[...])
     down, across = diagonals(gram)
     down, across = lax.rsqrt(down), lax.rsqrt(across)
-    out_ref[...] = invert(gram * down * across, 0.5)[0] * down * across
+    inverse, error, growth = begin(gram * down * across)
+    while growth < 10.0:
+        inverse, error, growth = double(inverse, error, growth)
+    out_ref[...] = inverse * down * across
 
 
 def refine(exact, factors, right, scale, out):
@@ -254,14 +257,12 @@
     return lax.while_loop(again, body, (0, 2.0 * scale, out))[1:]
 
 
-def solve(gram, right, start):
+def prepare_kernel(half_ref, other_ref, start_ref, top_ref, rest_ref, *out_refs):
+    gram = unpack_gram(half_ref[...] + other_ref[...])
     down, across = diagonals(gram)
-    start = start * jnp.sqrt(down) * jnp.sqrt(across)
+    start = start_ref[...] * jnp.sqrt(down) * jnp.sqrt(across)
     down, across = lax.rsqrt(down), lax.rsqrt(across)
-    scaled = gram * down * across
-    right = right * down
-    scale = jnp.sum(right * right)
-    exact = split(scaled, 3)
+    exact = split(gram * down * across, 3)
     product = dot6(exact, split(start, 3))
     terms = split(product, 2)
     follow = dot3(split(start, 2), terms)
@@ -269,23 +270,31 @@
     inverse = a * start - b * follow
     while growth < 1e3:
         inverse, error, growth = double(inverse, error, growth)
-    factors, sides = split(inverse, 2), split(right, 2)
+    top_ref[...], rest_ref[...] = split(inverse, 2)
+    *exact_refs, down_ref = out_refs
+    for ref, term in zip(exact_refs, exact):
+        ref[...] = term
+    down_ref[...] = jnp.broadcast_to(down, down_ref.shape)
+
+
+def weights_of(refs):
+    a_ref, other_a_ref, b_ref, other_b_ref, top_ref, rest_ref, *exact_refs, down_ref = refs
+    down = down_ref[:, :1]
+    right = jnp.concatenate([a_ref[...] + other_a_ref[...], b_ref[...] + other_b_ref[...]], 0) * down
+    factors, exact = (top_ref[...], rest_ref[...]), [ref[...] for ref in exact_refs]
+    scale = jnp.sum(right * right)
+    sides = split(right, 2)
     out = dot3(factors, sides)
     rest = right - dot6(exact, split(out, 3))
     size = jnp.sum(rest * rest)
     out = out + dot3(factors, split(rest, 2))
 
     def slow():
+        scaled = exact[0].astype(f32) + (exact[1].astype(f32) + exact[2].astype(f32))
         factors = split(invert(scaled, 0.1)[0], 2)
         return refine(exact, factors, right, scale, dot3(factors, sides))[1]
 
     return lax.cond(size <= 2e-5 * scale, lambda: out, slow) * down
-
-
-def weights_of(refs):
-    a1_ref, a2_ref, b1_ref, b2_ref, start_ref = refs
-    a, b = a1_ref[...] + a2_ref[...], b1_ref[...] + b2_ref[...]
-    return solve(unpack_gram(a), unpack_right(a, b), start_ref[...])
 
 
 def shrink(data, low_rank, level):
@@ -295,7 +304,7 @@
 
 
 def middle_kernel(blocks, *refs):
-    sum_refs, refs = refs[:5], refs[5:]
+    sum_refs, refs = refs[:10], refs[10:]
     left_top_ref, left_rest_ref, data_ref, level_ref, top_ref, rest_ref, *left_refs = refs
     tall = data_ref.shape[0] // blocks
     weights = split(weights_of(sum_refs), 2)
@@ -311,7 +320,7 @@
 
 
 def last_kernel(blocks, *refs):
-    sum_refs, refs = refs[:5], refs[5:]
+    sum_refs, refs = refs[:10], refs[10:]
     left_top_ref, left_rest_ref, data_ref, level_ref, low_rank_ref, sparse_ref, low_rank, sparse, sems = refs
     tall = data_ref.shape[0] // blocks
     low = lowest(blocks)
@@ -351,7 +360,6 @@
     rank = right_basis.shape[1]
     blocks = n_tm // 2
     whole = [((rows, cols), bf16)] * 2
-    a_rows = (rank + rank // 2 + SUBLANES) // 16 * 8 + SUBLANES
     lefts = [((share * blocks // 2, rank), f32) for _, share in chunks_of(rows // blocks) for _ in range(2)]
     data, top, rest, *left = call(
         functools.partial(head_kernel, blocks),
@@ -368,21 +376,34 @@
     level = threshold[None, :]
     for iteration in range(ITERS):
         pieces = sum_tm(list(zip(left[::2], left[1::2])), n_tm)
-        a, b, left_top, left_rest = call(
-            functools.partial(product_kernel, blocks, [len(x) for x in pieces]),
-            (top, rest, *[x for parts in pieces for x in parts]),
-            [((a_rows, cols), f32), ((rank + rank // 2 + SUBLANES - a_rows, cols), f32)] + [((rows, rank), bf16)] * 2,
-            name="products",
+        gram, left_top, left_rest = call(
+            functools.partial(gram_kernel, blocks, [len(x) for x in pieces]),
+            [x for parts in pieces for x in parts],
+            [((rank // 2 + SUBLANES, rank), f32)] + [((rows, rank), bf16)] * 2,
+            name="gram",
         )
-        sums = sum_rows(a, b, n_rows)
+        a, b = call(
+            right_kernel,
+            (left_top, left_rest, top, rest),
+            [((rank // 4, cols), f32), ((rank - rank // 4, cols), f32)],
+            name="right",
+        )
+        gram, other_gram, *sums = sum_rows((gram, a, b), (0, 0, 1), n_rows)
         start, level = call(
             inverse_kernel,
-            (sums[0], level),
+            (gram, level),
             [((rank, rank), f32), (level.shape, f32)],
             cost=pl.CostEstimate(flops=80 * rank**3, bytes_accessed=rank * rank * 8, transcendentals=0),
             name="inverse",
         )
-        args = (*sums, start, left_top, left_rest, data, level)
+        prepared = call(
+            prepare_kernel,
+            (gram, other_gram, start),
+            [((rank, rank), bf16)] * 5 + [((rank, 128), f32)],
+            cost=pl.CostEstimate(flops=60 * rank**3, bytes_accessed=rank * rank * 8, transcendentals=0),
+            name="prepare",
+        )
+        args = (*sums, *prepared, left_top, left_rest, data, level)
         if iteration < ITERS - 1:
             top, rest, *left = call(
                 functools.partial(middle_kernel, blocks),

time: 102 us -> 100 us (0.980)
  waiting for transfers between devices: 39.8 us -> 36.8 us
  starting transfers between devices: 39.5 us -> 42.3 us
  Pallas kernels: 20.6 us -> 19.4 us
    ppermute x44 -> x48, waiting for transfers between devices: 39.8 us -> 36.8 us  [swap(): return lax.ppermute(x, axis, [(i, i ^ bit) for i in range(size)])]
    ppermute x44 -> x48, starting transfers between devices: 39.5 us -> 42.3 us  [swap(): return lax.ppermute(x, axis, [(i, i ^ bit) for i in range(size)])]
    pallas_call x7 -> x11, Pallas kernels: 20.6 us -> 19.4 us  [call(): pl.pallas_call(body, out_shape=[jax.ShapeDtypeStruct(shape, dtype) for sh...]
  transfers between devices with their start and end apart: 44 -> 48, of which waited for: 24 -> 23; matrix products, arithmetic and copies ran while one was open for 0% -> 0% of each run, Pallas kernels for 6% -> 8%
where the time goes in v6:
time: 100 us
  starting transfers between devices  42.3 us (42%)
  waiting for transfers between devices  36.8 us (37%)
  Pallas kernels  19.4 us (19%)
  between operations  1.13 us (1%)
    ppermute x48, starting transfers between devices, swap(): return lax.ppermute(x, axis, [(i, i ^ bit) for i in range(size)])  42.3 us
    ppermute x48, waiting for transfers between devices, swap(): return lax.ppermute(x, axis, [(i, i ^ bit) for i in range(size)])  36.8 us
    pallas_call x11, Pallas kernels, call(): pl.pallas_call(body, out_shape=[jax.ShapeDtypeStruct(shape, dtype) for sh...  19.4 us
  transfers between devices with their start and end apart: 48, of which 23 were waited for; matrix products, arithmetic and copies ran while one was open for 0% of the time, Pallas kernels for 8%

profile of v6, /device:TPU:0, one launch (start us, length us, event | category | flops | bytes accessed | tf_op | source)
XLA Modules:
  0.0 100.0 jit_solution(2935568662354768067)
XLA Ops:
  0.6 2.5 %head.1 = (f32[1024,256]{1,0:T(8,128)S(1)}, bf16[1024,256]{1,0:T(8,128)(2,1)S(1)}, bf16[1024,256]{1,0:T(8,128)(2,1)S(1)}, f32[192,256]{1,0:T(8,128)S(1)}, f32[19...) custom-call(f32[1024,256]{1,0:T(8,128)} %snap_ref.1, ...), custom_call_target="tpu_custom_call" | custom-call | tf_op jit(solution)/shard_map/head/pallas_call | solution.py:346
  4.8 3.0 %collective-permute-start.1 = (f32[96,256]{1,0:T(8,128)S(1)}, f32[96,256]{1,0:T(8,128)S(1)}, u32[]{:S(2)}, u32[]{:S(2)}) collective-permute-start(f32[96,256]{1,0:T(8,128)S(1)} %slice.49), channel_id=1, source_target_pairs={{0,2},{1,3},{2,0},{3,1},{4,6},{5,7},{6,4},{7,5},{8,10},{9,11},{10,... | collective-permute-start | bytes 294920 | tf_op jit(solution)/shard_map/ppermute | solution.py:44
  8.3 1.7 %collective-permute-start.7 = (f32[96,256]{1,0:T(8,128)S(1)}, f32[96,256]{1,0:T(8,128)S(1)}, u32[]{:S(2)}, u32[]{:S(2)}) collective-permute-start(f32[96,256]{1,0:T(8,128)S(1)} %slice.51), channel_id=1, source_target_pairs={{0,2},{1,3},{2,0},{3,1},{4,6},{5,7},{6,4},{7,5},{8,10},{9,11},{10,... | collective-permute-start | bytes 294920 | tf_op jit(solution)/shard_map/ppermute | solution.py:44
  10.1 1.3 %collective-permute-done.1 = f32[96,256]{1,0:T(8,128)S(1)} collective-permute-done((f32[96,256]{1,0:T(8,128)S(1)}, f32[96,256]{1,0:T(8,128)S(1)}, u32[]{:S(2)}, u32[]{:S(2)}) %collective-permute-start.1) | collective-permute-done | bytes 98336 | tf_op jit(solution)/shard_map/ppermute | solution.py:44
  11.4 3.1 %collective-permute-start.2 = (f32[96,256]{1,0:T(8,128)S(1)}, f32[96,256]{1,0:T(8,128)S(1)}, u32[]{:S(2)}, u32[]{:S(2)}) collective-permute-start(f32[96,256]{1,0:T(8,128)S(1)} %slice_add_fusion.3), channel_id=1, source_target_pairs={{0,4},{1,5},{2,6},{3,7},{4,0},{5,1},{6,2},{7,3},{8,12},{9,13},{10,... | collective-permute-start | bytes 294920 | tf_op jit(solution)/shard_map/ppermute | solution.py:44
  14.5 1.0 collective-permute-done.7
  15.5 2.5 %collective-permute-start.8 = (f32[96,256]{1,0:T(8,128)S(1)}, f32[96,256]{1,0:T(8,128)S(1)}, u32[]{:S(2)}, u32[]{:S(2)}) collective-permute-start(f32[96,256]{1,0:T(8,128)S(1)} %slice_add_fusion.2), channel_id=1, source_target_pairs={{0,4},{1,5},{2,6},{3,7},{4,0},{5,1},{6,2},{7,3},{8,12},{9,13},{10,... | collective-permute-start | bytes 294920 | tf_op jit(solution)/shard_map/ppermute | solution.py:44
  18.6 1.9 %collective-permute-done.2 = f32[96,256]{1,0:T(8,128)S(1)} collective-permute-done((f32[96,256]{1,0:T(8,128)S(1)}, f32[96,256]{1,0:T(8,128)S(1)}, u32[]{:S(2)}, u32[]{:S(2)}) %collective-permute-start.2) | collective-permute-done | bytes 98336 | tf_op jit(solution)/shard_map/ppermute | solution.py:44
  20.5 3.0 %collective-permute-start.3 = (f32[96,256]{1,0:T(8,128)S(1)}, f32[96,256]{1,0:T(8,128)S(1)}, u32[]{:S(2)}, u32[]{:S(2)}) collective-permute-start(f32[96,256]{1,0:T(8,128)S(1)} %add.74.more_0_), channel_id=1, source_target_pairs={{0,2},{1,3},{2,0},{3,1},{4,6},{5,7},{6,4},{7,5},{8,10},{9,11},{10,... | collective-permute-start | bytes 294920 | tf_op jit(solution)/shard_map/ppermute | solution.py:44
  23.6 1.4 %collective-permute-done.8 = f32[96,256]{1,0:T(8,128)S(1)} collective-permute-done((f32[96,256]{1,0:T(8,128)S(1)}, f32[96,256]{1,0:T(8,128)S(1)}, u32[]{:S(2)}, u32[]{:S(2)}) %collective-permute-start.8) | collective-permute-done | bytes 98336 | tf_op jit(solution)/shard_map/ppermute | solution.py:44
  26.3 0.9 collective-permute-start.15
  28.1 1.8 %collective-permute-done.9.more_5_ = f32[96,256]{1,0:T(8,128)S(1)} collective-permute-done((f32[96,256]{1,0:T(8,128)S(1)}, f32[96,256]{1,0:T(8,128)S(1)}, u32[]{:S(2)}, u32[]{:S(2)}) %collective-permute-start.9) | collective-permute-done | bytes 98336 | tf_op jit(solution)/shard_map/ppermute | solution.py:44
  29.9 1.1 %collective-permute-done.15.more_9_ = f32[64,256]{1,0:T(8,128)S(1)} collective-permute-done((f32[64,256]{1,0:T(8,128)S(1)}, f32[64,256]{1,0:T(8,128)S(1)}, u32[]{:S(2)}, u32[]{:S(2)}) %collective-permute-start.15) | collective-permute-done | bytes 65568 | tf_op jit(solution)/shard_map/ppermute | solution.py:44
  31.1 1.3 %collective-permute-done.17.more_11_ = f32[64,256]{1,0:T(8,128)S(1)} collective-permute-done((f32[64,256]{1,0:T(8,128)S(1)}, f32[64,256]{1,0:T(8,128)S(1)}, u32[]{:S(2)}, u32[]{:S(2)}) %collective-permute-start.17) | collective-permute-done | bytes 65568 | tf_op jit(solution)/shard_map/ppermute | solution.py:44
  33.7 1.9 %collective-permute-start.20 = (f32[192,256]{1,0:T(8,128)S(1)}, f32[192,256]{1,0:T(8,128)S(1)}, u32[]{:S(2)}, u32[]{:S(2)}) collective-permute-start(f32[192,256]{1,0:T(8,128)S(1)} %get-tuple-element.56), channel_id=1, source_target_pairs={{0,16},{8,24},{16,0},{24,8},{1,17},{9,25},{17,1},{25,9},{2,18},{10... | collective-permute-start | bytes 589832 | tf_op jit(solution)/shard_map/ppermute | solution.py:44
  35.6 1.5 %collective-permute-start.22 = (f32[136,256]{1,0:T(8,128)S(1)}, f32[136,256]{1,0:T(8,128)S(1)}, u32[]{:S(2)}, u32[]{:S(2)}) collective-permute-start(f32[136,256]{1,0:T(8,128)S(1)} %get-tuple-element.57), channel_id=1, source_target_pairs={{0,8},{8,0},{16,24},{24,16},{1,9},{9,1},{17,25},{25,17},{2,10},{10... | collective-permute-start | bytes 417800 | tf_op jit(solution)/shard_map/ppermute | solution.py:44
  37.6 4.1 %collective-permute-done.22 = f32[136,256]{1,0:T(8,128)S(1)} collective-permute-done((f32[136,256]{1,0:T(8,128)S(1)}, f32[136,256]{1,0:T(8,128)S(1)}, u32[]{:S(2)}, u32[]{:S(2)}) %collective-permute-start.22) | collective-permute-done | bytes 139296 | tf_op jit(solution)/shard_map/ppermute | solution.py:44
  42.5 1.5 %collective-permute-start.19 = (f32[64,256]{1,0:T(8,128)S(1)}, f32[64,256]{1,0:T(8,128)S(1)}, u32[]{:S(2)}, u32[]{:S(2)}) collective-permute-start(f32[64,256]{1,0:T(8,128)S(1)} %add.81.refs_0_), channel_id=1, source_target_pairs={{0,16},{8,24},{16,0},{24,8},{1,17},{9,25},{17,1},{25,9},{2,18},{10... | collective-permute-start | bytes 196616 | tf_op jit(solution)/shard_map/ppermute | solution.py:44
  44.0 1.6 %collective-permute-start.21 = (f32[192,256]{1,0:T(8,128)S(1)}, f32[192,256]{1,0:T(8,128)S(1)}, u32[]{:S(2)}, u32[]{:S(2)}) collective-permute-start(f32[192,256]{1,0:T(8,128)S(1)} %add.82.refs_2_), channel_id=1, source_target_pairs={{0,8},{8,0},{16,24},{24,16},{1,9},{9,1},{17,25},{25,17},{2,10},{10... | collective-permute-start | bytes 589832 | tf_op jit(solution)/shard_map/ppermute | solution.py:44
  45.6 2.3 %inverse.2 = (f32[256,256]{1,0:T(8,128)S(1)}, f32[1,256]{1,0:T(1,128)S(1)}) custom-call(f32[136,256]{1,0:T(8,128)S(1)} %add.83.a_ref.half_ref, f32[1,256]{1,0:T(1,128)S(1)} %bitcast.1), custom_call_target="tpu_custom_call" | custom-call | flops 1342177280 | bytes 524288 | tf_op jit(solution)/shard_map/inverse/pallas_call | solution.py:346
  47.9 1.9 %prepare.2 = (bf16[256,256]{1,0:T(8,128)(2,1)S(1)}, bf16[256,256]{1,0:T(8,128)(2,1)S(1)}, bf16[256,256]{1,0:T(8,128)(2,1)S(1)}, bf16[256,256]{1,0:T(8,128)(2,1)S...) custom-call(f32[136,256]{1,0:T(8,128)S(1)} %add.83.a_ref.half_ref, ...), custom_call_target="tpu_custom_call" | custom-call | flops 1006632960 | bytes 524288 | tf_op jit(solution)/shard_map/prepare/pallas_call | solution.py:346
  49.9 2.7 %middle.1 = (bf16[1024,256]{1,0:T(8,128)(2,1)S(1)}, bf16[1024,256]{1,0:T(8,128)(2,1)S(1)}, f32[192,256]{1,0:T(8,128)S(1)}, f32[192,256]{1,0:T(8,128)S(1)}, f32[1...) custom-call(f32[64,256]{1,0:T(8,128)S(1)} %add.81.refs_0_, ...), custom_call_target="tpu_custom_call" | custom-call | tf_op jit(solution)/shard_map/middle/pallas_call | solution.py:346
  53.3 0.9 collective-permute-done.24
  54.2 0.7 collective-permute-start.25
  54.9 1.5 %collective-permute-start.37 = (f32[64,256]{1,0:T(8,128)S(1)}, f32[64,256]{1,0:T(8,128)S(1)}, u32[]{:S(2)}, u32[]{:S(2)}) collective-permute-start(f32[64,256]{1,0:T(8,128)S(1)} %slice.59), channel_id=1, source_target_pairs={{0,2},{1,3},{2,0},{3,1},{4,6},{5,7},{6,4},{7,5},{8,10},{9,11},{10,... | collective-permute-start | bytes 196616 | tf_op jit(solution)/shard_map/ppermute | solution.py:44
  56.4 0.7 collective-permute-start.31
  57.1 2.8 %collective-permute-done.25 = f32[96,256]{1,0:T(8,128)S(1)} collective-permute-done((f32[96,256]{1,0:T(8,128)S(1)}, f32[96,256]{1,0:T(8,128)S(1)}, u32[]{:S(2)}, u32[]{:S(2)}) %collective-permute-start.25) | collective-permute-done | bytes 98336 | tf_op jit(solution)/shard_map/ppermute | solution.py:44
  59.9 2.2 %collective-permute-start.26 = (f32[96,256]{1,0:T(8,128)S(1)}, f32[96,256]{1,0:T(8,128)S(1)}, u32[]{:S(2)}, u32[]{:S(2)}) collective-permute-start(f32[96,256]{1,0:T(8,128)S(1)} %slice_add_fusion.1), channel_id=1, source_target_pairs={{0,4},{1,5},{2,6},{3,7},{4,0},{5,1},{6,2},{7,3},{8,12},{9,13},{10,... | collective-permute-start | bytes 294920 | tf_op jit(solution)/shard_map/ppermute | solution.py:44
  62.1 1.6 %collective-permute-done.31 = f32[96,256]{1,0:T(8,128)S(1)} collective-permute-done((f32[96,256]{1,0:T(8,128)S(1)}, f32[96,256]{1,0:T(8,128)S(1)}, u32[]{:S(2)}, u32[]{:S(2)}) %collective-permute-start.31) | collective-permute-done | bytes 98336 | tf_op jit(solution)/shard_map/ppermute | solution.py:44
  63.6 1.9 %collective-permute-start.32 = (f32[96,256]{1,0:T(8,128)S(1)}, f32[96,256]{1,0:T(8,128)S(1)}, u32[]{:S(2)}, u32[]{:S(2)}) collective-permute-start(f32[96,256]{1,0:T(8,128)S(1)} %slice_add_fusion), channel_id=1, source_target_pairs={{0,4},{1,5},{2,6},{3,7},{4,0},{5,1},{6,2},{7,3},{8,12},{9,13},{10,... | collective-permute-start | bytes 294920 | tf_op jit(solution)/shard_map/ppermute | solution.py:44
  65.6 1.1 %collective-permute-start.38 = (f32[64,256]{1,0:T(8,128)S(1)}, f32[64,256]{1,0:T(8,128)S(1)}, u32[]{:S(2)}, u32[]{:S(2)}) collective-permute-start(f32[64,256]{1,0:T(8,128)S(1)} %slice_add_fusion.4), channel_id=1, source_target_pairs={{0,4},{1,5},{2,6},{3,7},{4,0},{5,1},{6,2},{7,3},{8,12},{9,13},{10,... | collective-permute-start | bytes 196616 | tf_op jit(solution)/shard_map/ppermute | solution.py:44
  66.7 4.5 %collective-permute-done.26 = f32[96,256]{1,0:T(8,128)S(1)} collective-permute-done((f32[96,256]{1,0:T(8,128)S(1)}, f32[96,256]{1,0:T(8,128)S(1)}, u32[]{:S(2)}, u32[]{:S(2)}) %collective-permute-start.26) | collective-permute-done | bytes 98336 | tf_op jit(solution)/shard_map/ppermute | solution.py:44
  71.3 2.0 %collective-permute-done.32 = f32[96,256]{1,0:T(8,128)S(1)} collective-permute-done((f32[96,256]{1,0:T(8,128)S(1)}, f32[96,256]{1,0:T(8,128)S(1)}, u32[]{:S(2)}, u32[]{:S(2)}) %collective-permute-start.32) | collective-permute-done | bytes 98336 | tf_op jit(solution)/shard_map/ppermute | solution.py:44
  74.1 1.5 %collective-permute-start.39 = (f32[64,256]{1,0:T(8,128)S(1)}, f32[64,256]{1,0:T(8,128)S(1)}, u32[]{:S(2)}, u32[]{:S(2)}) collective-permute-start(f32[64,256]{1,0:T(8,128)S(1)} %add.92.more_8_), channel_id=1, source_target_pairs={{0,2},{1,3},{2,0},{3,1},{4,6},{5,7},{6,4},{7,5},{8,10},{9,11},{10,... | collective-permute-start | bytes 196616 | tf_op jit(solution)/shard_map/ppermute | solution.py:44
  76.1 0.7 collective-permute-done.27.more_1_
  76.9 1.9 %collective-permute-done.33.more_5_ = f32[96,256]{1,0:T(8,128)S(1)} collective-permute-done((f32[96,256]{1,0:T(8,128)S(1)}, f32[96,256]{1,0:T(8,128)S(1)}, u32[]{:S(2)}, u32[]{:S(2)}) %collective-permute-start.33) | collective-permute-done | bytes 98336 | tf_op jit(solution)/shard_map/ppermute | solution.py:44
  78.7 0.7 collective-permute-done.39.more_9_
  79.4 1.3 %collective-permute-done.41.more_11_ = f32[64,256]{1,0:T(8,128)S(1)} collective-permute-done((f32[64,256]{1,0:T(8,128)S(1)}, f32[64,256]{1,0:T(8,128)S(1)}, u32[]{:S(2)}, u32[]{:S(2)}) %collective-permute-start.41) | collective-permute-done | bytes 65568 | tf_op jit(solution)/shard_map/ppermute | solution.py:44
  80.7 0.7 gram.3
  82.0 0.7 collective-permute-start.44
  82.7 1.4 %collective-permute-start.46 = (f32[136,256]{1,0:T(8,128)S(1)}, f32[136,256]{1,0:T(8,128)S(1)}, u32[]{:S(2)}, u32[]{:S(2)}) collective-permute-start(f32[136,256]{1,0:T(8,128)S(1)} %get-tuple-element.79), channel_id=1, source_target_pairs={{0,8},{8,0},{16,24},{24,16},{1,9},{9,1},{17,25},{25,17},{2,10},{10... | collective-permute-start | bytes 417800 | tf_op jit(solution)/shard_map/ppermute | solution.py:44
  84.7 4.1 %collective-permute-done.46 = f32[136,256]{1,0:T(8,128)S(1)} collective-permute-done((f32[136,256]{1,0:T(8,128)S(1)}, f32[136,256]{1,0:T(8,128)S(1)}, u32[]{:S(2)}, u32[]{:S(2)}) %collective-permute-start.46) | collective-permute-done | bytes 139296 | tf_op jit(solution)/shard_map/ppermute | solution.py:44
  88.9 1.5 %collective-permute-start.47 = (f32[136,256]{1,0:T(8,128)S(1)}, f32[136,256]{1,0:T(8,128)S(1)}, u32[]{:S(2)}, u32[]{:S(2)}) collective-permute-start(f32[136,256]{1,0:T(8,128)S(1)} %add.95.a_ref.half_ref), channel_id=1, source_target_pairs={{0,16},{8,24},{16,0},{24,8},{1,17},{9,25},{17,1},{25,9},{2,18},{10... | collective-permute-start | bytes 417800 | tf_op jit(solution)/shard_map/ppermute | solution.py:44
  90.4 0.7 collective-permute-start.43
  91.1 1.4 %collective-permute-start.45 = (f32[192,256]{1,0:T(8,128)S(1)}, f32[192,256]{1,0:T(8,128)S(1)}, u32[]{:S(2)}, u32[]{:S(2)}) collective-permute-start(f32[192,256]{1,0:T(8,128)S(1)} %add.94.refs_2_), channel_id=1, source_target_pairs={{0,8},{8,0},{16,24},{24,16},{1,9},{9,1},{17,25},{25,17},{2,10},{10... | collective-permute-start | bytes 589832 | tf_op jit(solution)/shard_map/ppermute | solution.py:44
  92.5 2.3 %inverse.3 = (f32[256,256]{1,0:T(8,128)S(1)}, f32[1,256]{1,0:T(1,128)S(1)}) custom-call(f32[136,256]{1,0:T(8,128)S(1)} %add.95.a_ref.half_ref, f32[1,256]{1,0:T(1,128)S(1)} %get-tuple-element.66.refs_13_.level_ref), custom_call_target="tpu_custom_call" | custom-call | flops 1342177280 | bytes 524288 | tf_op jit(solution)/shard_map/inverse/pallas_call | solution.py:346
  94.9 1.9 %prepare.3 = (bf16[256,256]{1,0:T(8,128)(2,1)S(1)}, bf16[256,256]{1,0:T(8,128)(2,1)S(1)}, bf16[256,256]{1,0:T(8,128)(2,1)S(1)}, bf16[256,256]{1,0:T(8,128)(2,1)S...) custom-call(f32[136,256]{1,0:T(8,128)S(1)} %add.95.a_ref.half_ref, ...), custom_call_target="tpu_custom_call" | custom-call | flops 1006632960 | bytes 524288 | tf_op jit(solution)/shard_map/prepare/pallas_call | solution.py:346
  96.8 3.0 %last.1 = (f32[1024,256]{1,0:T(8,128)}, f32[1024,256]{1,0:T(8,128)}) custom-call(f32[64,256]{1,0:T(8,128)S(1)} %add.93.refs_0_, f32[64,256]{1,0:T(8,128)S(1)} %collective-permute-done.43.refs_1_, f32[192,256]{1,0:T(8,128)S(1)} %add.94.refs_2_, f32[192,256]{1,0:T(8,128)S(1)} %collective-permute-done.45.refs_3_, ...), custom_call_target="tpu_custom_call" | custom-call | tf_op jit(solution)/shard_map/last/pallas_call | solution.py:346
  (91 shorter events, 11.1 us)
Async XLA Ops:
  3.2 1.6 %collective-permute-start = (f32[192,256]{1,0:T(8,128)S(1)}, f32[192,256]{1,0:T(8,128)S(1)}, u32[]{:S(2)}, u32[]{:S(2)}) collective-permute-start(f32[192,256]{1,0:T(8,128)S(1)} %get-tuple-element.46), channel_id=1, source_target_pairs={{0,1},{1,0},{2,3},{3,2},{4,5},{5,4},{6,7},{7,6},{8,9},{9,8},{10,11... | collective-permute-start | bytes 589832 | tf_op jit(solution)/shard_map/ppermute | solution.py:44
  3.7 4.6 %collective-permute-start.6 = (f32[192,256]{1,0:T(8,128)S(1)}, f32[192,256]{1,0:T(8,128)S(1)}, u32[]{:S(2)}, u32[]{:S(2)}) collective-permute-start(f32[192,256]{1,0:T(8,128)S(1)} %get-tuple-element.48), channel_id=1, source_target_pairs={{0,1},{1,0},{2,3},{3,2},{4,5},{5,4},{6,7},{7,6},{8,9},{9,8},{10,11... | collective-permute-start | bytes 589832 | tf_op jit(solution)/shard_map/ppermute | solution.py:44
  3.8 4.0 %collective-permute-start.12 = (f32[128,256]{1,0:T(8,128)S(1)}, f32[128,256]{1,0:T(8,128)S(1)}, u32[]{:S(2)}, u32[]{:S(2)}) collective-permute-start(f32[128,256]{1,0:T(8,128)S(1)} %get-tuple-element.50), channel_id=1, source_target_pairs={{0,1},{1,0},{2,3},{3,2},{4,5},{5,4},{6,7},{7,6},{8,9},{9,8},{10,11... | collective-permute-start | bytes 393224 | tf_op jit(solution)/shard_map/ppermute | solution.py:44
  4.8 6.6 %collective-permute-start.1 = (f32[96,256]{1,0:T(8,128)S(1)}, f32[96,256]{1,0:T(8,128)S(1)}, u32[]{:S(2)}, u32[]{:S(2)}) collective-permute-start(f32[96,256]{1,0:T(8,128)S(1)} %slice.49), channel_id=1, source_target_pairs={{0,2},{1,3},{2,0},{3,1},{4,6},{5,7},{6,4},{7,5},{8,10},{9,11},{10,... | collective-permute-start | bytes 294920 | tf_op jit(solution)/shard_map/ppermute | solution.py:44
  7.9 10.2 %collective-permute-start.13 = (f32[64,256]{1,0:T(8,128)S(1)}, f32[64,256]{1,0:T(8,128)S(1)}, u32[]{:S(2)}, u32[]{:S(2)}) collective-permute-start(f32[64,256]{1,0:T(8,128)S(1)} %slice.53), channel_id=1, source_target_pairs={{0,2},{1,3},{2,0},{3,1},{4,6},{5,7},{6,4},{7,5},{8,10},{9,11},{10,... | collective-permute-start | bytes 196616 | tf_op jit(solution)/shard_map/ppermute | solution.py:44
  8.3 7.2 %collective-permute-start.7 = (f32[96,256]{1,0:T(8,128)S(1)}, f32[96,256]{1,0:T(8,128)S(1)}, u32[]{:S(2)}, u32[]{:S(2)}) collective-permute-start(f32[96,256]{1,0:T(8,128)S(1)} %slice.51), channel_id=1, source_target_pairs={{0,2},{1,3},{2,0},{3,1},{4,6},{5,7},{6,4},{7,5},{8,10},{9,11},{10,... | collective-permute-start | bytes 294920 | tf_op jit(solution)/shard_map/ppermute | solution.py:44
  11.4 9.1 %collective-permute-start.2 = (f32[96,256]{1,0:T(8,128)S(1)}, f32[96,256]{1,0:T(8,128)S(1)}, u32[]{:S(2)}, u32[]{:S(2)}) collective-permute-start(f32[96,256]{1,0:T(8,128)S(1)} %slice_add_fusion.3), channel_id=1, source_target_pairs={{0,4},{1,5},{2,6},{3,7},{4,0},{5,1},{6,2},{7,3},{8,12},{9,13},{10,... | collective-permute-start | bytes 294920 | tf_op jit(solution)/shard_map/ppermute | solution.py:44
  15.5 9.5 %collective-permute-start.8 = (f32[96,256]{1,0:T(8,128)S(1)}, f32[96,256]{1,0:T(8,128)S(1)}, u32[]{:S(2)}, u32[]{:S(2)}) collective-permute-start(f32[96,256]{1,0:T(8,128)S(1)} %slice_add_fusion.2), channel_id=1, source_target_pairs={{0,4},{1,5},{2,6},{3,7},{4,0},{5,1},{6,2},{7,3},{8,12},{9,13},{10,... | collective-permute-start | bytes 294920 | tf_op jit(solution)/shard_map/ppermute | solution.py:44
  18.0 8.2 %collective-permute-start.14 = (f32[64,256]{1,0:T(8,128)S(1)}, f32[64,256]{1,0:T(8,128)S(1)}, u32[]{:S(2)}, u32[]{:S(2)}) collective-permute-start(f32[64,256]{1,0:T(8,128)S(1)} %slice_add_fusion.5), channel_id=1, source_target_pairs={{0,4},{1,5},{2,6},{3,7},{4,0},{5,1},{6,2},{7,3},{8,12},{9,13},{10,... | collective-permute-start | bytes 196616 | tf_op jit(solution)/shard_map/ppermute | solution.py:44
  20.5 7.2 %collective-permute-start.3 = (f32[96,256]{1,0:T(8,128)S(1)}, f32[96,256]{1,0:T(8,128)S(1)}, u32[]{:S(2)}, u32[]{:S(2)}) collective-permute-start(f32[96,256]{1,0:T(8,128)S(1)} %add.74.more_0_), channel_id=1, source_target_pairs={{0,2},{1,3},{2,0},{3,1},{4,6},{5,7},{6,4},{7,5},{8,10},{9,11},{10,... | collective-permute-start | bytes 294920 | tf_op jit(solution)/shard_map/ppermute | solution.py:44
  25.0 4.9 %collective-permute-start.9 = (f32[96,256]{1,0:T(8,128)S(1)}, f32[96,256]{1,0:T(8,128)S(1)}, u32[]{:S(2)}, u32[]{:S(2)}) collective-permute-start(f32[96,256]{1,0:T(8,128)S(1)} %add.77.more_4_), channel_id=1, source_target_pairs={{0,2},{1,3},{2,0},{3,1},{4,6},{5,7},{6,4},{7,5},{8,10},{9,11},{10,... | collective-permute-start | bytes 294920 | tf_op jit(solution)/shard_map/ppermute | solution.py:44
  26.2 1.3 %collective-permute-start.16 = (f32[64,256]{1,0:T(8,128)S(1)}, f32[64,256]{1,0:T(8,128)S(1)}, u32[]{:S(2)}, u32[]{:S(2)}) collective-permute-start(f32[64,256]{1,0:T(8,128)S(1)} %add.80.more_8_), channel_id=1, source_target_pairs={{0,1},{1,0},{2,3},{3,2},{4,5},{5,4},{6,7},{7,6},{8,9},{9,8},{10,11... | collective-permute-start | bytes 196616 | tf_op jit(solution)/shard_map/ppermute | solution.py:44
  26.3 4.7 %collective-permute-start.15 = (f32[64,256]{1,0:T(8,128)S(1)}, f32[64,256]{1,0:T(8,128)S(1)}, u32[]{:S(2)}, u32[]{:S(2)}) collective-permute-start(f32[64,256]{1,0:T(8,128)S(1)} %add.80.more_8_), channel_id=1, source_target_pairs={{0,2},{1,3},{2,0},{3,1},{4,6},{5,7},{6,4},{7,5},{8,10},{9,11},{10,... | collective-permute-start | bytes 196616 | tf_op jit(solution)/shard_map/ppermute | solution.py:44
  27.2 5.1 %collective-permute-start.4 = (f32[96,256]{1,0:T(8,128)S(1)}, f32[96,256]{1,0:T(8,128)S(1)}, u32[]{:S(2)}, u32[]{:S(2)}) collective-permute-start(f32[96,256]{1,0:T(8,128)S(1)} %add.74.more_0_), channel_id=1, source_target_pairs={{0,1},{1,0},{2,3},{3,2},{4,5},{5,4},{6,7},{7,6},{8,9},{9,8},{10,11... | collective-permute-start | bytes 294920 | tf_op jit(solution)/shard_map/ppermute | solution.py:44
  27.6 4.8 %collective-permute-start.10 = (f32[96,256]{1,0:T(8,128)S(1)}, f32[96,256]{1,0:T(8,128)S(1)}, u32[]{:S(2)}, u32[]{:S(2)}) collective-permute-start(f32[96,256]{1,0:T(8,128)S(1)} %add.77.more_4_), channel_id=1, source_target_pairs={{0,1},{1,0},{2,3},{3,2},{4,5},{5,4},{6,7},{7,6},{8,9},{9,8},{10,11... | collective-permute-start | bytes 294920 | tf_op jit(solution)/shard_map/ppermute | solution.py:44
  27.8 4.6 %collective-permute-start.5 = (f32[96,256]{1,0:T(8,128)S(1)}, f32[96,256]{1,0:T(8,128)S(1)}, u32[]{:S(2)}, u32[]{:S(2)}) collective-permute-start(f32[96,256]{1,0:T(8,128)S(1)} %collective-permute-done.3.more_1_), channel_id=1, source_target_pairs={{0,1},{1,0},{2,3},{3,2},{4,5},{5,4},{6,7},{7,6},{8,9},{9,8},{10,11... | collective-permute-start | bytes 294920 | tf_op jit(solution)/shard_map/ppermute | solution.py:44
  29.9 2.4 %collective-permute-start.11 = (f32[96,256]{1,0:T(8,128)S(1)}, f32[96,256]{1,0:T(8,128)S(1)}, u32[]{:S(2)}, u32[]{:S(2)}) collective-permute-start(f32[96,256]{1,0:T(8,128)S(1)} %collective-permute-done.9.more_5_), channel_id=1, source_target_pairs={{0,1},{1,0},{2,3},{3,2},{4,5},{5,4},{6,7},{7,6},{8,9},{9,8},{10,11... | collective-permute-start | bytes 294920 | tf_op jit(solution)/shard_map/ppermute | solution.py:44
  31.1 1.3 %collective-permute-start.17 = (f32[64,256]{1,0:T(8,128)S(1)}, f32[64,256]{1,0:T(8,128)S(1)}, u32[]{:S(2)}, u32[]{:S(2)}) collective-permute-start(f32[64,256]{1,0:T(8,128)S(1)} %collective-permute-done.15.more_9_), channel_id=1, source_target_pairs={{0,1},{1,0},{2,3},{3,2},{4,5},{5,4},{6,7},{7,6},{8,9},{9,8},{10,11... | collective-permute-start | bytes 196616 | tf_op jit(solution)/shard_map/ppermute | solution.py:44
  33.7 10.3 %collective-permute-start.20 = (f32[192,256]{1,0:T(8,128)S(1)}, f32[192,256]{1,0:T(8,128)S(1)}, u32[]{:S(2)}, u32[]{:S(2)}) collective-permute-start(f32[192,256]{1,0:T(8,128)S(1)} %get-tuple-element.56), channel_id=1, source_target_pairs={{0,16},{8,24},{16,0},{24,8},{1,17},{9,25},{17,1},{25,9},{2,18},{10... | collective-permute-start | bytes 589832 | tf_op jit(solution)/shard_map/ppermute | solution.py:44
  35.6 6.2 %collective-permute-start.22 = (f32[136,256]{1,0:T(8,128)S(1)}, f32[136,256]{1,0:T(8,128)S(1)}, u32[]{:S(2)}, u32[]{:S(2)}) collective-permute-start(f32[136,256]{1,0:T(8,128)S(1)} %get-tuple-element.57), channel_id=1, source_target_pairs={{0,8},{8,0},{16,24},{24,16},{1,9},{9,1},{17,25},{25,17},{2,10},{10... | collective-permute-start | bytes 417800 | tf_op jit(solution)/shard_map/ppermute | solution.py:44
  37.1 5.4 %collective-permute-start.18 = (f32[64,256]{1,0:T(8,128)S(1)}, f32[64,256]{1,0:T(8,128)S(1)}, u32[]{:S(2)}, u32[]{:S(2)}) collective-permute-start(f32[64,256]{1,0:T(8,128)S(1)} %get-tuple-element.55), channel_id=1, source_target_pairs={{0,8},{8,0},{16,24},{24,16},{1,9},{9,1},{17,25},{25,17},{2,10},{10... | collective-permute-start | bytes 196616 | tf_op jit(solution)/shard_map/ppermute | solution.py:44
  41.8 6.1 %collective-permute-start.23 = (f32[136,256]{1,0:T(8,128)S(1)}, f32[136,256]{1,0:T(8,128)S(1)}, u32[]{:S(2)}, u32[]{:S(2)}) collective-permute-start(f32[136,256]{1,0:T(8,128)S(1)} %add.83.a_ref.half_ref), channel_id=1, source_target_pairs={{0,16},{8,24},{16,0},{24,8},{1,17},{9,25},{17,1},{25,9},{2,18},{10... | collective-permute-start | bytes 417800 | tf_op jit(solution)/shard_map/ppermute | solution.py:44
  42.5 7.4 %collective-permute-start.19 = (f32[64,256]{1,0:T(8,128)S(1)}, f32[64,256]{1,0:T(8,128)S(1)}, u32[]{:S(2)}, u32[]{:S(2)}) collective-permute-start(f32[64,256]{1,0:T(8,128)S(1)} %add.81.refs_0_), channel_id=1, source_target_pairs={{0,16},{8,24},{16,0},{24,8},{1,17},{9,25},{17,1},{25,9},{2,18},{10... | collective-permute-start | bytes 196616 | tf_op jit(solution)/shard_map/ppermute | solution.py:44
  44.0 5.8 %collective-permute-start.21 = (f32[192,256]{1,0:T(8,128)S(1)}, f32[192,256]{1,0:T(8,128)S(1)}, u32[]{:S(2)}, u32[]{:S(2)}) collective-permute-start(f32[192,256]{1,0:T(8,128)S(1)} %add.82.refs_2_), channel_id=1, source_target_pairs={{0,8},{8,0},{16,24},{24,16},{1,9},{9,1},{17,25},{25,17},{2,10},{10... | collective-permute-start | bytes 589832 | tf_op jit(solution)/shard_map/ppermute | solution.py:44
  52.6 1.5 %collective-permute-start.24 = (f32[192,256]{1,0:T(8,128)S(1)}, f32[192,256]{1,0:T(8,128)S(1)}, u32[]{:S(2)}, u32[]{:S(2)}) collective-permute-start(f32[192,256]{1,0:T(8,128)S(1)} %get-tuple-element.68), channel_id=1, source_target_pairs={{0,1},{1,0},{2,3},{3,2},{4,5},{5,4},{6,7},{7,6},{8,9},{9,8},{10,11... | collective-permute-start | bytes 589832 | tf_op jit(solution)/shard_map/ppermute | solution.py:44
  52.7 3.7 %collective-permute-start.30 = (f32[192,256]{1,0:T(8,128)S(1)}, f32[192,256]{1,0:T(8,128)S(1)}, u32[]{:S(2)}, u32[]{:S(2)}) collective-permute-start(f32[192,256]{1,0:T(8,128)S(1)} %get-tuple-element.70), channel_id=1, source_target_pairs={{0,1},{1,0},{2,3},{3,2},{4,5},{5,4},{6,7},{7,6},{8,9},{9,8},{10,11... | collective-permute-start | bytes 589832 | tf_op jit(solution)/shard_map/ppermute | solution.py:44
  53.2 1.7 %collective-permute-start.36 = (f32[128,256]{1,0:T(8,128)S(1)}, f32[128,256]{1,0:T(8,128)S(1)}, u32[]{:S(2)}, u32[]{:S(2)}) collective-permute-start(f32[128,256]{1,0:T(8,128)S(1)} %get-tuple-element.72), channel_id=1, source_target_pairs={{0,1},{1,0},{2,3},{3,2},{4,5},{5,4},{6,7},{7,6},{8,9},{9,8},{10,11... | collective-permute-start | bytes 393224 | tf_op jit(solution)/shard_map/ppermute | solution.py:44
  54.2 5.7 %collective-permute-start.25 = (f32[96,256]{1,0:T(8,128)S(1)}, f32[96,256]{1,0:T(8,128)S(1)}, u32[]{:S(2)}, u32[]{:S(2)}) collective-permute-start(f32[96,256]{1,0:T(8,128)S(1)} %slice.55), channel_id=1, source_target_pairs={{0,2},{1,3},{2,0},{3,1},{4,6},{5,7},{6,4},{7,5},{8,10},{9,11},{10,... | collective-permute-start | bytes 294920 | tf_op jit(solution)/shard_map/ppermute | solution.py:44
  54.9 10.7 %collective-permute-start.37 = (f32[64,256]{1,0:T(8,128)S(1)}, f32[64,256]{1,0:T(8,128)S(1)}, u32[]{:S(2)}, u32[]{:S(2)}) collective-permute-start(f32[64,256]{1,0:T(8,128)S(1)} %slice.59), channel_id=1, source_target_pairs={{0,2},{1,3},{2,0},{3,1},{4,6},{5,7},{6,4},{7,5},{8,10},{9,11},{10,... | collective-permute-start | bytes 196616 | tf_op jit(solution)/shard_map/ppermute | solution.py:44
  56.4 7.2 %collective-permute-start.31 = (f32[96,256]{1,0:T(8,128)S(1)}, f32[96,256]{1,0:T(8,128)S(1)}, u32[]{:S(2)}, u32[]{:S(2)}) collective-permute-start(f32[96,256]{1,0:T(8,128)S(1)} %slice.57), channel_id=1, source_target_pairs={{0,2},{1,3},{2,0},{3,1},{4,6},{5,7},{6,4},{7,5},{8,10},{9,11},{10,... | collective-permute-start | bytes 294920 | tf_op jit(solution)/shard_map/ppermute | solution.py:44
  59.9 11.3 %collective-permute-start.26 = (f32[96,256]{1,0:T(8,128)S(1)}, f32[96,256]{1,0:T(8,128)S(1)}, u32[]{:S(2)}, u32[]{:S(2)}) collective-permute-start(f32[96,256]{1,0:T(8,128)S(1)} %slice_add_fusion.1), channel_id=1, source_target_pairs={{0,4},{1,5},{2,6},{3,7},{4,0},{5,1},{6,2},{7,3},{8,12},{9,13},{10,... | collective-permute-start | bytes 294920 | tf_op jit(solution)/shard_map/ppermute | solution.py:44
  63.6 9.7 %collective-permute-start.32 = (f32[96,256]{1,0:T(8,128)S(1)}, f32[96,256]{1,0:T(8,128)S(1)}, u32[]{:S(2)}, u32[]{:S(2)}) collective-permute-start(f32[96,256]{1,0:T(8,128)S(1)} %slice_add_fusion), channel_id=1, source_target_pairs={{0,4},{1,5},{2,6},{3,7},{4,0},{5,1},{6,2},{7,3},{8,12},{9,13},{10,... | collective-permute-start | bytes 294920 | tf_op jit(solution)/shard_map/ppermute | solution.py:44
  65.6 8.5 %collective-permute-start.38 = (f32[64,256]{1,0:T(8,128)S(1)}, f32[64,256]{1,0:T(8,128)S(1)}, u32[]{:S(2)}, u32[]{:S(2)}) collective-permute-start(f32[64,256]{1,0:T(8,128)S(1)} %slice_add_fusion.4), channel_id=1, source_target_pairs={{0,4},{1,5},{2,6},{3,7},{4,0},{5,1},{6,2},{7,3},{8,12},{9,13},{10,... | collective-permute-start | bytes 196616 | tf_op jit(solution)/shard_map/ppermute | solution.py:44
  71.2 5.6 %collective-permute-start.27 = (f32[96,256]{1,0:T(8,128)S(1)}, f32[96,256]{1,0:T(8,128)S(1)}, u32[]{:S(2)}, u32[]{:S(2)}) collective-permute-start(f32[96,256]{1,0:T(8,128)S(1)} %add.86.more_0_), channel_id=1, source_target_pairs={{0,2},{1,3},{2,0},{3,1},{4,6},{5,7},{6,4},{7,5},{8,10},{9,11},{10,... | collective-permute-start | bytes 294920 | tf_op jit(solution)/shard_map/ppermute | solution.py:44
  73.3 5.4 %collective-permute-start.33 = (f32[96,256]{1,0:T(8,128)S(1)}, f32[96,256]{1,0:T(8,128)S(1)}, u32[]{:S(2)}, u32[]{:S(2)}) collective-permute-start(f32[96,256]{1,0:T(8,128)S(1)} %add.89.more_4_), channel_id=1, source_target_pairs={{0,2},{1,3},{2,0},{3,1},{4,6},{5,7},{6,4},{7,5},{8,10},{9,11},{10,... | collective-permute-start | bytes 294920 | tf_op jit(solution)/shard_map/ppermute | solution.py:44
  74.1 1.7 %collective-permute-start.40 = (f32[64,256]{1,0:T(8,128)S(1)}, f32[64,256]{1,0:T(8,128)S(1)}, u32[]{:S(2)}, u32[]{:S(2)}) collective-permute-start(f32[64,256]{1,0:T(8,128)S(1)} %add.92.more_8_), channel_id=1, source_target_pairs={{0,1},{1,0},{2,3},{3,2},{4,5},{5,4},{6,7},{7,6},{8,9},{9,8},{10,11... | collective-permute-start | bytes 196616 | tf_op jit(solution)/shard_map/ppermute | solution.py:44
  74.1 5.3 %collective-permute-start.39 = (f32[64,256]{1,0:T(8,128)S(1)}, f32[64,256]{1,0:T(8,128)S(1)}, u32[]{:S(2)}, u32[]{:S(2)}) collective-permute-start(f32[64,256]{1,0:T(8,128)S(1)} %add.92.more_8_), channel_id=1, source_target_pairs={{0,2},{1,3},{2,0},{3,1},{4,6},{5,7},{6,4},{7,5},{8,10},{9,11},{10,... | collective-permute-start | bytes 196616 | tf_op jit(solution)/shard_map/ppermute | solution.py:44
  75.6 5.1 %collective-permute-start.28 = (f32[96,256]{1,0:T(8,128)S(1)}, f32[96,256]{1,0:T(8,128)S(1)}, u32[]{:S(2)}, u32[]{:S(2)}) collective-permute-start(f32[96,256]{1,0:T(8,128)S(1)} %add.86.more_0_), channel_id=1, source_target_pairs={{0,1},{1,0},{2,3},{3,2},{4,5},{5,4},{6,7},{7,6},{8,9},{9,8},{10,11... | collective-permute-start | bytes 294920 | tf_op jit(solution)/shard_map/ppermute | solution.py:44
  75.8 4.9 %collective-permute-start.34 = (f32[96,256]{1,0:T(8,128)S(1)}, f32[96,256]{1,0:T(8,128)S(1)}, u32[]{:S(2)}, u32[]{:S(2)}) collective-permute-start(f32[96,256]{1,0:T(8,128)S(1)} %add.89.more_4_), channel_id=1, source_target_pairs={{0,1},{1,0},{2,3},{3,2},{4,5},{5,4},{6,7},{7,6},{8,9},{9,8},{10,11... | collective-permute-start | bytes 294920 | tf_op jit(solution)/shard_map/ppermute | solution.py:44
  76.9 3.8 %collective-permute-start.29 = (f32[96,256]{1,0:T(8,128)S(1)}, f32[96,256]{1,0:T(8,128)S(1)}, u32[]{:S(2)}, u32[]{:S(2)}) collective-permute-start(f32[96,256]{1,0:T(8,128)S(1)} %collective-permute-done.27.more_1_), channel_id=1, source_target_pairs={{0,1},{1,0},{2,3},{3,2},{4,5},{5,4},{6,7},{7,6},{8,9},{9,8},{10,11... | collective-permute-start | bytes 294920 | tf_op jit(solution)/shard_map/ppermute | solution.py:44
  78.7 2.0 %collective-permute-start.35 = (f32[96,256]{1,0:T(8,128)S(1)}, f32[96,256]{1,0:T(8,128)S(1)}, u32[]{:S(2)}, u32[]{:S(2)}) collective-permute-start(f32[96,256]{1,0:T(8,128)S(1)} %collective-permute-done.33.more_5_), channel_id=1, source_target_pairs={{0,1},{1,0},{2,3},{3,2},{4,5},{5,4},{6,7},{7,6},{8,9},{9,8},{10,11... | collective-permute-start | bytes 294920 | tf_op jit(solution)/shard_map/ppermute | solution.py:44
  79.4 1.3 %collective-permute-start.41 = (f32[64,256]{1,0:T(8,128)S(1)}, f32[64,256]{1,0:T(8,128)S(1)}, u32[]{:S(2)}, u32[]{:S(2)}) collective-permute-start(f32[64,256]{1,0:T(8,128)S(1)} %collective-permute-done.39.more_9_), channel_id=1, source_target_pairs={{0,1},{1,0},{2,3},{3,2},{4,5},{5,4},{6,7},{7,6},{8,9},{9,8},{10,11... | collective-permute-start | bytes 196616 | tf_op jit(solution)/shard_map/ppermute | solution.py:44
  82.0 9.0 %collective-permute-start.44 = (f32[192,256]{1,0:T(8,128)S(1)}, f32[192,256]{1,0:T(8,128)S(1)}, u32[]{:S(2)}, u32[]{:S(2)}) collective-permute-start(f32[192,256]{1,0:T(8,128)S(1)} %get-tuple-element.78), channel_id=1, source_target_pairs={{0,16},{8,24},{16,0},{24,8},{1,17},{9,25},{17,1},{25,9},{2,18},{10... | collective-permute-start | bytes 589832 | tf_op jit(solution)/shard_map/ppermute | solution.py:44
  82.7 6.2 %collective-permute-start.46 = (f32[136,256]{1,0:T(8,128)S(1)}, f32[136,256]{1,0:T(8,128)S(1)}, u32[]{:S(2)}, u32[]{:S(2)}) collective-permute-start(f32[136,256]{1,0:T(8,128)S(1)} %get-tuple-element.79), channel_id=1, source_target_pairs={{0,8},{8,0},{16,24},{24,16},{1,9},{9,1},{17,25},{25,17},{2,10},{10... | collective-permute-start | bytes 417800 | tf_op jit(solution)/shard_map/ppermute | solution.py:44
  84.1 6.3 %collective-permute-start.42 = (f32[64,256]{1,0:T(8,128)S(1)}, f32[64,256]{1,0:T(8,128)S(1)}, u32[]{:S(2)}, u32[]{:S(2)}) collective-permute-start(f32[64,256]{1,0:T(8,128)S(1)} %get-tuple-element.77), channel_id=1, source_target_pairs={{0,8},{8,0},{16,24},{24,16},{1,9},{9,1},{17,25},{25,17},{2,10},{10... | collective-permute-start | bytes 196616 | tf_op jit(solution)/shard_map/ppermute | solution.py:44
  88.9 6.0 %collective-permute-start.47 = (f32[136,256]{1,0:T(8,128)S(1)}, f32[136,256]{1,0:T(8,128)S(1)}, u32[]{:S(2)}, u32[]{:S(2)}) collective-permute-start(f32[136,256]{1,0:T(8,128)S(1)} %add.95.a_ref.half_ref), channel_id=1, source_target_pairs={{0,16},{8,24},{16,0},{24,8},{1,17},{9,25},{17,1},{25,9},{2,18},{10... | collective-permute-start | bytes 417800 | tf_op jit(solution)/shard_map/ppermute | solution.py:44
  90.4 6.4 %collective-permute-start.43 = (f32[64,256]{1,0:T(8,128)S(1)}, f32[64,256]{1,0:T(8,128)S(1)}, u32[]{:S(2)}, u32[]{:S(2)}) collective-permute-start(f32[64,256]{1,0:T(8,128)S(1)} %add.93.refs_0_), channel_id=1, source_target_pairs={{0,16},{8,24},{16,0},{24,8},{1,17},{9,25},{17,1},{25,9},{2,18},{10... | collective-permute-start | bytes 196616 | tf_op jit(solution)/shard_map/ppermute | solution.py:44
  91.1 5.7 %collective-permute-start.45 = (f32[192,256]{1,0:T(8,128)S(1)}, f32[192,256]{1,0:T(8,128)S(1)}, u32[]{:S(2)}, u32[]{:S(2)}) collective-permute-start(f32[192,256]{1,0:T(8,128)S(1)} %add.94.refs_2_), channel_id=1, source_target_pairs={{0,8},{8,0},{16,24},{24,16},{1,9},{9,1},{17,25},{25,17},{2,10},{10... | collective-permute-start | bytes 589832 | tf_op jit(solution)/shard_map/ppermute | solution.py:44
  (1 other events, 1.6 us)

commit v7 on v6

--- a/solution.py
+++ b/solution.py
@@ -129,8 +129,8 @@
     write_left(left, left_refs, blocks)
 
 
-def gram_kernel(blocks, counts, *more):
-    left_refs, (gram_ref, left_top_ref, left_rest_ref) = more[:-3], more[-3:]
+def product_kernel(blocks, counts, top_ref, rest_ref, *more):
+    left_refs, (first_ref, second_ref, left_top_ref, left_rest_ref) = more[:-4], more[-4:]
     rows, rank = left_top_ref.shape
     tall = rows // blocks
     taken = 0
@@ -144,14 +144,13 @@
                 p += 1
         taken += counts[c]
     left = left_top_ref[...], left_rest_ref[...]
+    right = dot3(left, (top_ref[...], rest_ref[...]), TN)
+    head = rank // 2 + SUBLANES
+    taken = first_ref.shape[0] - head
+    first_ref[head:, :], second_ref[...] = right[:taken], right[taken:]
     cross = dot(left[0], left[1], TN)
     gram = dot(left[0], left[0], TN) + (cross + cross.T + dot(left[1], left[1], TN))
-    pack(gram, gram_ref)
-
-
-def right_kernel(left_top_ref, left_rest_ref, top_ref, rest_ref, a_ref, b_ref):
-    right = dot3((left_top_ref[...], left_rest_ref[...]), (top_ref[...], rest_ref[...]), TN)
-    a_ref[...], b_ref[...] = right[: a_ref.shape[0]], right[a_ref.shape[0] :]
+    pack(gram, first_ref)
 
 
 def pack(gram, out_ref):
@@ -159,7 +158,7 @@
     out_ref[:half, :half] = jnp.where(below(half), gram[:half, :half], gram[half:, half:])
     out_ref[:half, half:] = gram[half:, :half]
     diagonal = jnp.sum(jnp.where(identity(half), gram[half:, half:], 0.0), 0, keepdims=True)
-    out_ref[half:, :] = jnp.broadcast_to(jnp.concatenate([diagonal, diagonal], 1), (SUBLANES, 2 * half))
+    out_ref[half : half + SUBLANES, :] = jnp.broadcast_to(jnp.concatenate([diagonal, diagonal], 1), (SUBLANES, 2 * half))
 
 
 def unpack_gram(a):
@@ -278,9 +277,10 @@
 
 
 def weights_of(refs):
-    a_ref, other_a_ref, b_ref, other_b_ref, top_ref, rest_ref, *exact_refs, down_ref = refs
+    first_ref, other_first_ref, second_ref, other_second_ref, top_ref, rest_ref, *exact_refs, down_ref = refs
+    head = first_ref.shape[1] // 2 + SUBLANES
     down = down_ref[:, :1]
-    right = jnp.concatenate([a_ref[...] + other_a_ref[...], b_ref[...] + other_b_ref[...]], 0) * down
+    right = jnp.concatenate([first_ref[head:, :] + other_first_ref[head:, :], second_ref[...] + other_second_ref[...]], 0) * down
     factors, exact = (top_ref[...], rest_ref[...]), [ref[...] for ref in exact_refs]
     scale = jnp.sum(right * right)
     sides = split(right, 2)
@@ -360,6 +360,7 @@
     rank = right_basis.shape[1]
     blocks = n_tm // 2
     whole = [((rows, cols), bf16)] * 2
+    first_rows = rank // 2 + SUBLANES + rank // 8
     lefts = [((share * blocks // 2, rank), f32) for _, share in chunks_of(rows // blocks) for _ in range(2)]
     data, top, rest, *left = call(
         functools.partial(head_kernel, blocks),
@@ -376,29 +377,23 @@
     level = threshold[None, :]
     for iteration in range(ITERS):
         pieces = sum_tm(list(zip(left[::2], left[1::2])), n_tm)
-        gram, left_top, left_rest = call(
-            functools.partial(gram_kernel, blocks, [len(x) for x in pieces]),
-            [x for parts in pieces for x in parts],
-            [((rank // 2 + SUBLANES, rank), f32)] + [((rows, rank), bf16)] * 2,
-            name="gram",
+        first, second, left_top, left_rest = call(
+            functools.partial(product_kernel, blocks, [len(x) for x in pieces]),
+            (top, rest, *[x for parts in pieces for x in parts]),
+            [((first_rows, cols), f32), ((rank // 2 * 3 + SUBLANES - first_rows, cols), f32)] + [((rows, rank), bf16)] * 2,
+            name="products",
         )
-        a, b = call(
-            right_kernel,
-            (left_top, left_rest, top, rest),
-            [((rank // 4, cols), f32), ((rank - rank // 4, cols), f32)],
-            name="right",
-        )
-        gram, other_gram, *sums = sum_rows((gram, a, b), (0, 0, 1), n_rows)
+        sums = sum_rows((first, second), (0, 1), n_rows)
         start, level = call(
             inverse_kernel,
-            (gram, level),
+            (sums[0], level),
             [((rank, rank), f32), (level.shape, f32)],
             cost=pl.CostEstimate(flops=80 * rank**3, bytes_accessed=rank * rank * 8, transcendentals=0),
             name="inverse",
         )
         prepared = call(
             prepare_kernel,
-            (gram, other_gram, start),
+            (*sums[:2], start),
             [((rank, rank), bf16)] * 5 + [((rank, 128), f32)],
             cost=pl.CostEstimate(flops=60 * rank**3, bytes_accessed=rank * rank * 8, transcendentals=0),
             name="prepare",

time: 100 us -> 98.9 us (0.989)
  starting transfers between devices: 42.3 us -> 39.3 us
  waiting for transfers between devices: 36.8 us -> 39 us
    ppermute x48 -> x44, starting transfers between devices: 42.3 us -> 39.3 us  [swap(): return lax.ppermute(x, axis, [(i, i ^ bit) for i in range(size)])]
    ppermute x48 -> x44, waiting for transfers between devices: 36.8 us -> 39 us  [swap(): return lax.ppermute(x, axis, [(i, i ^ bit) for i in range(size)])]
    pallas_call x11 -> x9, Pallas kernels: 19.4 us -> 19 us  [call(): pl.pallas_call(body, out_shape=[jax.ShapeDtypeStruct(shape, dtype) for sh...]
  transfers between devices with their start and end apart: 48 -> 44, of which waited for: 23 -> 24; matrix products, arithmetic and copies ran while one was open for 0% -> 0% of each run, Pallas kernels for 8% -> 9%
where the time goes in v7:
time: 98.9 us; the launch traced here: 98.8 us
  starting transfers between devices  39.3 us (40%)
  waiting for transfers between devices  39 us (39%)
  Pallas kernels  19 us (19%)
  between operations  1.07 us (1%)
    ppermute x44, starting transfers between devices, swap(): return lax.ppermute(x, axis, [(i, i ^ bit) for i in range(size)])  39.3 us
    ppermute x44, waiting for transfers between devices, swap(): return lax.ppermute(x, axis, [(i, i ^ bit) for i in range(size)])  39 us
    pallas_call x9, Pallas kernels, call(): pl.pallas_call(body, out_shape=[jax.ShapeDtypeStruct(shape, dtype) for sh...  19 us
  transfers between devices with their start and end apart: 44, of which 24 were waited for; matrix products, arithmetic and copies ran while one was open for 0% of the time, Pallas kernels for 9%

profile of v7, /device:TPU:0, one launch (start us, length us, event | category | flops | bytes accessed | tf_op | source)
XLA Modules:
  0.0 98.8 jit_solution(2504284193890597424)
XLA Ops:
  0.6 2.5 %head.1 = (f32[1024,256]{1,0:T(8,128)S(1)}, bf16[1024,256]{1,0:T(8,128)(2,1)S(1)}, bf16[1024,256]{1,0:T(8,128)(2,1)S(1)}, f32[192,256]{1,0:T(8,128)S(1)}, f32[19...) custom-call(f32[1024,256]{1,0:T(8,128)} %snap_ref.1, ...), custom_call_target="tpu_custom_call" | custom-call | tf_op jit(solution)/shard_map/head/pallas_call | solution.py:346
  4.8 3.0 %collective-permute-start.1 = (f32[96,256]{1,0:T(8,128)S(1)}, f32[96,256]{1,0:T(8,128)S(1)}, u32[]{:S(2)}, u32[]{:S(2)}) collective-permute-start(f32[96,256]{1,0:T(8,128)S(1)} %slice.49), channel_id=1, source_target_pairs={{0,2},{1,3},{2,0},{3,1},{4,6},{5,7},{6,4},{7,5},{8,10},{9,11},{10,... | collective-permute-start | bytes 294920 | tf_op jit(solution)/shard_map/ppermute | solution.py:44
  8.3 1.7 %collective-permute-start.7 = (f32[96,256]{1,0:T(8,128)S(1)}, f32[96,256]{1,0:T(8,128)S(1)}, u32[]{:S(2)}, u32[]{:S(2)}) collective-permute-start(f32[96,256]{1,0:T(8,128)S(1)} %slice.51), channel_id=1, source_target_pairs={{0,2},{1,3},{2,0},{3,1},{4,6},{5,7},{6,4},{7,5},{8,10},{9,11},{10,... | collective-permute-start | bytes 294920 | tf_op jit(solution)/shard_map/ppermute | solution.py:44
  10.1 1.3 %collective-permute-done.1 = f32[96,256]{1,0:T(8,128)S(1)} collective-permute-done((f32[96,256]{1,0:T(8,128)S(1)}, f32[96,256]{1,0:T(8,128)S(1)}, u32[]{:S(2)}, u32[]{:S(2)}) %collective-permute-start.1) | collective-permute-done | bytes 98336 | tf_op jit(solution)/shard_map/ppermute | solution.py:44
  11.4 3.1 %collective-permute-start.2 = (f32[96,256]{1,0:T(8,128)S(1)}, f32[96,256]{1,0:T(8,128)S(1)}, u32[]{:S(2)}, u32[]{:S(2)}) collective-permute-start(f32[96,256]{1,0:T(8,128)S(1)} %slice_add_fusion.3), channel_id=1, source_target_pairs={{0,4},{1,5},{2,6},{3,7},{4,0},{5,1},{6,2},{7,3},{8,12},{9,13},{10,... | collective-permute-start | bytes 294920 | tf_op jit(solution)/shard_map/ppermute | solution.py:44
  14.5 1.0 collective-permute-done.7
  15.5 2.5 %collective-permute-start.8 = (f32[96,256]{1,0:T(8,128)S(1)}, f32[96,256]{1,0:T(8,128)S(1)}, u32[]{:S(2)}, u32[]{:S(2)}) collective-permute-start(f32[96,256]{1,0:T(8,128)S(1)} %slice_add_fusion.2), channel_id=1, source_target_pairs={{0,4},{1,5},{2,6},{3,7},{4,0},{5,1},{6,2},{7,3},{8,12},{9,13},{10,... | collective-permute-start | bytes 294920 | tf_op jit(solution)/shard_map/ppermute | solution.py:44
  18.6 1.9 %collective-permute-done.2 = f32[96,256]{1,0:T(8,128)S(1)} collective-permute-done((f32[96,256]{1,0:T(8,128)S(1)}, f32[96,256]{1,0:T(8,128)S(1)}, u32[]{:S(2)}, u32[]{:S(2)}) %collective-permute-start.2) | collective-permute-done | bytes 98336 | tf_op jit(solution)/shard_map/ppermute | solution.py:44
  20.5 3.0 %collective-permute-start.3 = (f32[96,256]{1,0:T(8,128)S(1)}, f32[96,256]{1,0:T(8,128)S(1)}, u32[]{:S(2)}, u32[]{:S(2)}) collective-permute-start(f32[96,256]{1,0:T(8,128)S(1)} %add.68.more_0_), channel_id=1, source_target_pairs={{0,2},{1,3},{2,0},{3,1},{4,6},{5,7},{6,4},{7,5},{8,10},{9,11},{10,... | collective-permute-start | bytes 294920 | tf_op jit(solution)/shard_map/ppermute | solution.py:44
  23.6 1.4 %collective-permute-done.8 = f32[96,256]{1,0:T(8,128)S(1)} collective-permute-done((f32[96,256]{1,0:T(8,128)S(1)}, f32[96,256]{1,0:T(8,128)S(1)}, u32[]{:S(2)}, u32[]{:S(2)}) %collective-permute-start.8) | collective-permute-done | bytes 98336 | tf_op jit(solution)/shard_map/ppermute | solution.py:44
  26.3 0.9 collective-permute-start.15
  28.1 1.8 %collective-permute-done.9.more_5_ = f32[96,256]{1,0:T(8,128)S(1)} collective-permute-done((f32[96,256]{1,0:T(8,128)S(1)}, f32[96,256]{1,0:T(8,128)S(1)}, u32[]{:S(2)}, u32[]{:S(2)}) %collective-permute-start.9) | collective-permute-done | bytes 98336 | tf_op jit(solution)/shard_map/ppermute | solution.py:44
  29.9 1.1 %collective-permute-done.15.more_9_ = f32[64,256]{1,0:T(8,128)S(1)} collective-permute-done((f32[64,256]{1,0:T(8,128)S(1)}, f32[64,256]{1,0:T(8,128)S(1)}, u32[]{:S(2)}, u32[]{:S(2)}) %collective-permute-start.15) | collective-permute-done | bytes 65568 | tf_op jit(solution)/shard_map/ppermute | solution.py:44
  31.1 1.3 %collective-permute-done.17.more_11_ = f32[64,256]{1,0:T(8,128)S(1)} collective-permute-done((f32[64,256]{1,0:T(8,128)S(1)}, f32[64,256]{1,0:T(8,128)S(1)}, u32[]{:S(2)}, u32[]{:S(2)}) %collective-permute-start.17) | collective-permute-done | bytes 65568 | tf_op jit(solution)/shard_map/ppermute | solution.py:44
  32.3 1.1 %products.2 = (f32[168,256]{1,0:T(8,128)S(1)}, f32[224,256]{1,0:T(8,128)S(1)}, bf16[1024,256]{1,0:T(8,128)(2,1)S(1)}, bf16[1024,256]{1,0:T(8,128)(2,1)S(1)}) custom-call(bf16[1024,256]{1,0:T(8,128)(2,1)S(1)} %get-tuple-element.43.top_ref, bf16[1024,256]{1,0:T(8,128)(2,1)S(1)} %get-tuple-element.44.rest_ref, f32[96,256]{1,0:T(8,128)S(1)} %add.68.more_0_, ...), custom_call_target="tpu_custom_call" | custom-call | tf_op jit(solution)/shard_map/products/pallas_call | solution.py:346
  33.4 1.9 %collective-permute-start.20 = (f32[224,256]{1,0:T(8,128)S(1)}, f32[224,256]{1,0:T(8,128)S(1)}, u32[]{:S(2)}, u32[]{:S(2)}) collective-permute-start(f32[224,256]{1,0:T(8,128)S(1)} %get-tuple-element.52), channel_id=1, source_target_pairs={{0,16},{8,24},{16,0},{24,8},{1,17},{9,25},{17,1},{25,9},{2,18},{10... | collective-permute-start | bytes 688136 | tf_op jit(solution)/shard_map/ppermute | solution.py:44
  35.4 1.5 %collective-permute-start.18 = (f32[168,256]{1,0:T(8,128)S(1)}, f32[168,256]{1,0:T(8,128)S(1)}, u32[]{:S(2)}, u32[]{:S(2)}) collective-permute-start(f32[168,256]{1,0:T(8,128)S(1)} %get-tuple-element.51), channel_id=1, source_target_pairs={{0,8},{8,0},{16,24},{24,16},{1,9},{9,1},{17,25},{25,17},{2,10},{10... | collective-permute-start | bytes 516104 | tf_op jit(solution)/shard_map/ppermute | solution.py:44
  36.9 4.7 %collective-permute-done.18 = f32[168,256]{1,0:T(8,128)S(1)} collective-permute-done((f32[168,256]{1,0:T(8,128)S(1)}, f32[168,256]{1,0:T(8,128)S(1)}, u32[]{:S(2)}, u32[]{:S(2)}) %collective-permute-start.18) | collective-permute-done | bytes 172064 | tf_op jit(solution)/shard_map/ppermute | solution.py:44
  42.0 1.7 %collective-permute-start.21 = (f32[224,256]{1,0:T(8,128)S(1)}, f32[224,256]{1,0:T(8,128)S(1)}, u32[]{:S(2)}, u32[]{:S(2)}) collective-permute-start(f32[224,256]{1,0:T(8,128)S(1)} %add.76.refs_2_), channel_id=1, source_target_pairs={{0,8},{8,0},{16,24},{24,16},{1,9},{9,1},{17,25},{25,17},{2,10},{10... | collective-permute-start | bytes 688136 | tf_op jit(solution)/shard_map/ppermute | solution.py:44
  43.7 2.3 %inverse.2 = (f32[256,256]{1,0:T(8,128)S(1)}, f32[1,256]{1,0:T(1,128)S(1)}) custom-call(f32[168,256]{1,0:T(8,128)S(1)} %add.75.a_ref.half_ref.refs_0_, f32[1,256]{1,0:T(1,128)S(1)} %bitcast.1), custom_call_target="tpu_custom_call" | custom-call | flops 1342177280 | bytes 524288 | tf_op jit(solution)/shard_map/inverse/pallas_call | solution.py:346
  46.1 1.0 collective-permute-done.19.other_ref.refs_1_
  47.0 1.9 %prepare.2 = (bf16[256,256]{1,0:T(8,128)(2,1)S(1)}, bf16[256,256]{1,0:T(8,128)(2,1)S(1)}, bf16[256,256]{1,0:T(8,128)(2,1)S(1)}, bf16[256,256]{1,0:T(8,128)(2,1)S...) custom-call(f32[168,256]{1,0:T(8,128)S(1)} %add.75.a_ref.half_ref.refs_0_, ...), custom_call_target="tpu_custom_call" | custom-call | flops 1006632960 | bytes 524288 | tf_op jit(solution)/shard_map/prepare/pallas_call | solution.py:346
  49.0 2.8 %middle.1 = (bf16[1024,256]{1,0:T(8,128)(2,1)S(1)}, bf16[1024,256]{1,0:T(8,128)(2,1)S(1)}, f32[192,256]{1,0:T(8,128)S(1)}, f32[192,256]{1,0:T(8,128)S(1)}, f32[1...) custom-call(f32[168,256]{1,0:T(8,128)S(1)} %add.75.a_ref.half_ref.refs_0_, ...), custom_call_target="tpu_custom_call" | custom-call | tf_op jit(solution)/shard_map/middle/pallas_call | solution.py:346
  52.4 0.9 collective-permute-done.22
  53.3 0.7 collective-permute-start.23
  54.0 1.5 %collective-permute-start.35 = (f32[64,256]{1,0:T(8,128)S(1)}, f32[64,256]{1,0:T(8,128)S(1)}, u32[]{:S(2)}, u32[]{:S(2)}) collective-permute-start(f32[64,256]{1,0:T(8,128)S(1)} %slice.59), channel_id=1, source_target_pairs={{0,2},{1,3},{2,0},{3,1},{4,6},{5,7},{6,4},{7,5},{8,10},{9,11},{10,... | collective-permute-start | bytes 196616 | tf_op jit(solution)/shard_map/ppermute | solution.py:44
  55.5 0.7 collective-permute-start.29
  56.2 2.8 %collective-permute-done.23 = f32[96,256]{1,0:T(8,128)S(1)} collective-permute-done((f32[96,256]{1,0:T(8,128)S(1)}, f32[96,256]{1,0:T(8,128)S(1)}, u32[]{:S(2)}, u32[]{:S(2)}) %collective-permute-start.23) | collective-permute-done | bytes 98336 | tf_op jit(solution)/shard_map/ppermute | solution.py:44
  59.0 2.2 %collective-permute-start.24 = (f32[96,256]{1,0:T(8,128)S(1)}, f32[96,256]{1,0:T(8,128)S(1)}, u32[]{:S(2)}, u32[]{:S(2)}) collective-permute-start(f32[96,256]{1,0:T(8,128)S(1)} %slice_add_fusion.1), channel_id=1, source_target_pairs={{0,4},{1,5},{2,6},{3,7},{4,0},{5,1},{6,2},{7,3},{8,12},{9,13},{10,... | collective-permute-start | bytes 294920 | tf_op jit(solution)/shard_map/ppermute | solution.py:44
  61.2 1.6 %collective-permute-done.29 = f32[96,256]{1,0:T(8,128)S(1)} collective-permute-done((f32[96,256]{1,0:T(8,128)S(1)}, f32[96,256]{1,0:T(8,128)S(1)}, u32[]{:S(2)}, u32[]{:S(2)}) %collective-permute-start.29) | collective-permute-done | bytes 98336 | tf_op jit(solution)/shard_map/ppermute | solution.py:44
  62.8 1.9 %collective-permute-start.30 = (f32[96,256]{1,0:T(8,128)S(1)}, f32[96,256]{1,0:T(8,128)S(1)}, u32[]{:S(2)}, u32[]{:S(2)}) collective-permute-start(f32[96,256]{1,0:T(8,128)S(1)} %slice_add_fusion), channel_id=1, source_target_pairs={{0,4},{1,5},{2,6},{3,7},{4,0},{5,1},{6,2},{7,3},{8,12},{9,13},{10,... | collective-permute-start | bytes 294920 | tf_op jit(solution)/shard_map/ppermute | solution.py:44
  64.7 1.1 %collective-permute-start.36 = (f32[64,256]{1,0:T(8,128)S(1)}, f32[64,256]{1,0:T(8,128)S(1)}, u32[]{:S(2)}, u32[]{:S(2)}) collective-permute-start(f32[64,256]{1,0:T(8,128)S(1)} %slice_add_fusion.4), channel_id=1, source_target_pairs={{0,4},{1,5},{2,6},{3,7},{4,0},{5,1},{6,2},{7,3},{8,12},{9,13},{10,... | collective-permute-start | bytes 196616 | tf_op jit(solution)/shard_map/ppermute | solution.py:44
  65.8 4.5 %collective-permute-done.24 = f32[96,256]{1,0:T(8,128)S(1)} collective-permute-done((f32[96,256]{1,0:T(8,128)S(1)}, f32[96,256]{1,0:T(8,128)S(1)}, u32[]{:S(2)}, u32[]{:S(2)}) %collective-permute-start.24) | collective-permute-done | bytes 98336 | tf_op jit(solution)/shard_map/ppermute | solution.py:44
  70.4 2.0 %collective-permute-done.30 = f32[96,256]{1,0:T(8,128)S(1)} collective-permute-done((f32[96,256]{1,0:T(8,128)S(1)}, f32[96,256]{1,0:T(8,128)S(1)}, u32[]{:S(2)}, u32[]{:S(2)}) %collective-permute-start.30) | collective-permute-done | bytes 98336 | tf_op jit(solution)/shard_map/ppermute | solution.py:44
  73.2 1.5 %collective-permute-start.37 = (f32[64,256]{1,0:T(8,128)S(1)}, f32[64,256]{1,0:T(8,128)S(1)}, u32[]{:S(2)}, u32[]{:S(2)}) collective-permute-start(f32[64,256]{1,0:T(8,128)S(1)} %add.85.more_8_), channel_id=1, source_target_pairs={{0,2},{1,3},{2,0},{3,1},{4,6},{5,7},{6,4},{7,5},{8,10},{9,11},{10,... | collective-permute-start | bytes 196616 | tf_op jit(solution)/shard_map/ppermute | solution.py:44
  75.2 0.7 collective-permute-done.25.more_1_
  76.0 1.9 %collective-permute-done.31.more_5_ = f32[96,256]{1,0:T(8,128)S(1)} collective-permute-done((f32[96,256]{1,0:T(8,128)S(1)}, f32[96,256]{1,0:T(8,128)S(1)}, u32[]{:S(2)}, u32[]{:S(2)}) %collective-permute-start.31) | collective-permute-done | bytes 98336 | tf_op jit(solution)/shard_map/ppermute | solution.py:44
  77.8 0.7 collective-permute-done.37.more_9_
  78.5 1.3 %collective-permute-done.39.more_11_ = f32[64,256]{1,0:T(8,128)S(1)} collective-permute-done((f32[64,256]{1,0:T(8,128)S(1)}, f32[64,256]{1,0:T(8,128)S(1)}, u32[]{:S(2)}, u32[]{:S(2)}) %collective-permute-start.39) | collective-permute-done | bytes 65568 | tf_op jit(solution)/shard_map/ppermute | solution.py:44
  79.8 1.1 %products.3 = (f32[168,256]{1,0:T(8,128)S(1)}, f32[224,256]{1,0:T(8,128)S(1)}, bf16[1024,256]{1,0:T(8,128)(2,1)S(1)}, bf16[1024,256]{1,0:T(8,128)(2,1)S(1)}) custom-call(bf16[1024,256]{1,0:T(8,128)(2,1)S(1)} %get-tuple-element.64.top_ref, bf16[1024,256]{1,0:T(8,128)(2,1)S(1)} %get-tuple-element.65.rest_ref, f32[96,256]{1,0:T(8,128)S(1)} %add.79.more_0_, ...), custom_call_target="tpu_custom_call" | custom-call | tf_op jit(solution)/shard_map/products/pallas_call | solution.py:346
  80.9 1.1 %collective-permute-start.42 = (f32[224,256]{1,0:T(8,128)S(1)}, f32[224,256]{1,0:T(8,128)S(1)}, u32[]{:S(2)}, u32[]{:S(2)}) collective-permute-start(f32[224,256]{1,0:T(8,128)S(1)} %get-tuple-element.73), channel_id=1, source_target_pairs={{0,16},{8,24},{16,0},{24,8},{1,17},{9,25},{17,1},{25,9},{2,18},{10... | collective-permute-start | bytes 688136 | tf_op jit(solution)/shard_map/ppermute | solution.py:44
  82.0 1.5 %collective-permute-start.40 = (f32[168,256]{1,0:T(8,128)S(1)}, f32[168,256]{1,0:T(8,128)S(1)}, u32[]{:S(2)}, u32[]{:S(2)}) collective-permute-start(f32[168,256]{1,0:T(8,128)S(1)} %get-tuple-element.72), channel_id=1, source_target_pairs={{0,8},{8,0},{16,24},{24,16},{1,9},{9,1},{17,25},{25,17},{2,10},{10... | collective-permute-start | bytes 516104 | tf_op jit(solution)/shard_map/ppermute | solution.py:44
  83.5 4.7 %collective-permute-done.40 = f32[168,256]{1,0:T(8,128)S(1)} collective-permute-done((f32[168,256]{1,0:T(8,128)S(1)}, f32[168,256]{1,0:T(8,128)S(1)}, u32[]{:S(2)}, u32[]{:S(2)}) %collective-permute-start.40) | collective-permute-done | bytes 172064 | tf_op jit(solution)/shard_map/ppermute | solution.py:44
  88.2 1.1 %collective-permute-start.41 = (f32[168,256]{1,0:T(8,128)S(1)}, f32[168,256]{1,0:T(8,128)S(1)}, u32[]{:S(2)}, u32[]{:S(2)}) collective-permute-start(f32[168,256]{1,0:T(8,128)S(1)} %add.86.a_ref.half_ref.refs_0_), channel_id=1, source_target_pairs={{0,16},{8,24},{16,0},{24,8},{1,17},{9,25},{17,1},{25,9},{2,18},{10... | collective-permute-start | bytes 516104 | tf_op jit(solution)/shard_map/ppermute | solution.py:44
  89.3 1.6 %collective-permute-start.43 = (f32[224,256]{1,0:T(8,128)S(1)}, f32[224,256]{1,0:T(8,128)S(1)}, u32[]{:S(2)}, u32[]{:S(2)}) collective-permute-start(f32[224,256]{1,0:T(8,128)S(1)} %add.87.refs_2_), channel_id=1, source_target_pairs={{0,8},{8,0},{16,24},{24,16},{1,9},{9,1},{17,25},{25,17},{2,10},{10... | collective-permute-start | bytes 688136 | tf_op jit(solution)/shard_map/ppermute | solution.py:44
  90.8 2.3 %inverse.3 = (f32[256,256]{1,0:T(8,128)S(1)}, f32[1,256]{1,0:T(1,128)S(1)}) custom-call(f32[168,256]{1,0:T(8,128)S(1)} %add.86.a_ref.half_ref.refs_0_, f32[1,256]{1,0:T(1,128)S(1)} %get-tuple-element.63.refs_13_.level_ref), custom_call_target="tpu_custom_call" | custom-call | flops 1342177280 | bytes 524288 | tf_op jit(solution)/shard_map/inverse/pallas_call | solution.py:346
  93.6 1.9 %prepare.3 = (bf16[256,256]{1,0:T(8,128)(2,1)S(1)}, bf16[256,256]{1,0:T(8,128)(2,1)S(1)}, bf16[256,256]{1,0:T(8,128)(2,1)S(1)}, bf16[256,256]{1,0:T(8,128)(2,1)S...) custom-call(f32[168,256]{1,0:T(8,128)S(1)} %add.86.a_ref.half_ref.refs_0_, ...), custom_call_target="tpu_custom_call" | custom-call | flops 1006632960 | bytes 524288 | tf_op jit(solution)/shard_map/prepare/pallas_call | solution.py:346
  95.6 3.0 %last.1 = (f32[1024,256]{1,0:T(8,128)}, f32[1024,256]{1,0:T(8,128)}) custom-call(f32[168,256]{1,0:T(8,128)S(1)} %add.86.a_ref.half_ref.refs_0_, f32[168,256]{1,0:T(8,128)S(1)} %collective-permute-done.41.other_ref.refs_1_, f32[224,256]{1,0:T(8,128)S(1)} %add.87.refs_2_, f32[224,256]{1,0:T(8,128)S(1)} %collective-permute-done.43.refs_3_, ...), custom_call_target="tpu_custom_call" | custom-call | tf_op jit(solution)/shard_map/last/pallas_call | solution.py:346
  (79 shorter events, 8.1 us)
Async XLA Ops:
  3.2 1.6 %collective-permute-start = (f32[192,256]{1,0:T(8,128)S(1)}, f32[192,256]{1,0:T(8,128)S(1)}, u32[]{:S(2)}, u32[]{:S(2)}) collective-permute-start(f32[192,256]{1,0:T(8,128)S(1)} %get-tuple-element.46), channel_id=1, source_target_pairs={{0,1},{1,0},{2,3},{3,2},{4,5},{5,4},{6,7},{7,6},{8,9},{9,8},{10,11... | collective-permute-start | bytes 589832 | tf_op jit(solution)/shard_map/ppermute | solution.py:44
  3.7 4.6 %collective-permute-start.6 = (f32[192,256]{1,0:T(8,128)S(1)}, f32[192,256]{1,0:T(8,128)S(1)}, u32[]{:S(2)}, u32[]{:S(2)}) collective-permute-start(f32[192,256]{1,0:T(8,128)S(1)} %get-tuple-element.48), channel_id=1, source_target_pairs={{0,1},{1,0},{2,3},{3,2},{4,5},{5,4},{6,7},{7,6},{8,9},{9,8},{10,11... | collective-permute-start | bytes 589832 | tf_op jit(solution)/shard_map/ppermute | solution.py:44
  3.8 4.0 %collective-permute-start.12 = (f32[128,256]{1,0:T(8,128)S(1)}, f32[128,256]{1,0:T(8,128)S(1)}, u32[]{:S(2)}, u32[]{:S(2)}) collective-permute-start(f32[128,256]{1,0:T(8,128)S(1)} %get-tuple-element.50), channel_id=1, source_target_pairs={{0,1},{1,0},{2,3},{3,2},{4,5},{5,4},{6,7},{7,6},{8,9},{9,8},{10,11... | collective-permute-start | bytes 393224 | tf_op jit(solution)/shard_map/ppermute | solution.py:44
  4.8 6.6 %collective-permute-start.1 = (f32[96,256]{1,0:T(8,128)S(1)}, f32[96,256]{1,0:T(8,128)S(1)}, u32[]{:S(2)}, u32[]{:S(2)}) collective-permute-start(f32[96,256]{1,0:T(8,128)S(1)} %slice.49), channel_id=1, source_target_pairs={{0,2},{1,3},{2,0},{3,1},{4,6},{5,7},{6,4},{7,5},{8,10},{9,11},{10,... | collective-permute-start | bytes 294920 | tf_op jit(solution)/shard_map/ppermute | solution.py:44
  7.9 10.2 %collective-permute-start.13 = (f32[64,256]{1,0:T(8,128)S(1)}, f32[64,256]{1,0:T(8,128)S(1)}, u32[]{:S(2)}, u32[]{:S(2)}) collective-permute-start(f32[64,256]{1,0:T(8,128)S(1)} %slice.53), channel_id=1, source_target_pairs={{0,2},{1,3},{2,0},{3,1},{4,6},{5,7},{6,4},{7,5},{8,10},{9,11},{10,... | collective-permute-start | bytes 196616 | tf_op jit(solution)/shard_map/ppermute | solution.py:44
  8.3 7.2 %collective-permute-start.7 = (f32[96,256]{1,0:T(8,128)S(1)}, f32[96,256]{1,0:T(8,128)S(1)}, u32[]{:S(2)}, u32[]{:S(2)}) collective-permute-start(f32[96,256]{1,0:T(8,128)S(1)} %slice.51), channel_id=1, source_target_pairs={{0,2},{1,3},{2,0},{3,1},{4,6},{5,7},{6,4},{7,5},{8,10},{9,11},{10,... | collective-permute-start | bytes 294920 | tf_op jit(solution)/shard_map/ppermute | solution.py:44
  11.4 9.1 %collective-permute-start.2 = (f32[96,256]{1,0:T(8,128)S(1)}, f32[96,256]{1,0:T(8,128)S(1)}, u32[]{:S(2)}, u32[]{:S(2)}) collective-permute-start(f32[96,256]{1,0:T(8,128)S(1)} %slice_add_fusion.3), channel_id=1, source_target_pairs={{0,4},{1,5},{2,6},{3,7},{4,0},{5,1},{6,2},{7,3},{8,12},{9,13},{10,... | collective-permute-start | bytes 294920 | tf_op jit(solution)/shard_map/ppermute | solution.py:44
  15.5 9.5 %collective-permute-start.8 = (f32[96,256]{1,0:T(8,128)S(1)}, f32[96,256]{1,0:T(8,128)S(1)}, u32[]{:S(2)}, u32[]{:S(2)}) collective-permute-start(f32[96,256]{1,0:T(8,128)S(1)} %slice_add_fusion.2), channel_id=1, source_target_pairs={{0,4},{1,5},{2,6},{3,7},{4,0},{5,1},{6,2},{7,3},{8,12},{9,13},{10,... | collective-permute-start | bytes 294920 | tf_op jit(solution)/shard_map/ppermute | solution.py:44
  18.0 8.2 %collective-permute-start.14 = (f32[64,256]{1,0:T(8,128)S(1)}, f32[64,256]{1,0:T(8,128)S(1)}, u32[]{:S(2)}, u32[]{:S(2)}) collective-permute-start(f32[64,256]{1,0:T(8,128)S(1)} %slice_add_fusion.5), channel_id=1, source_target_pairs={{0,4},{1,5},{2,6},{3,7},{4,0},{5,1},{6,2},{7,3},{8,12},{9,13},{10,... | collective-permute-start | bytes 196616 | tf_op jit(solution)/shard_map/ppermute | solution.py:44
  20.5 7.2 %collective-permute-start.3 = (f32[96,256]{1,0:T(8,128)S(1)}, f32[96,256]{1,0:T(8,128)S(1)}, u32[]{:S(2)}, u32[]{:S(2)}) collective-permute-start(f32[96,256]{1,0:T(8,128)S(1)} %add.68.more_0_), channel_id=1, source_target_pairs={{0,2},{1,3},{2,0},{3,1},{4,6},{5,7},{6,4},{7,5},{8,10},{9,11},{10,... | collective-permute-start | bytes 294920 | tf_op jit(solution)/shard_map/ppermute | solution.py:44
  25.0 4.9 %collective-permute-start.9 = (f32[96,256]{1,0:T(8,128)S(1)}, f32[96,256]{1,0:T(8,128)S(1)}, u32[]{:S(2)}, u32[]{:S(2)}) collective-permute-start(f32[96,256]{1,0:T(8,128)S(1)} %add.71.more_4_), channel_id=1, source_target_pairs={{0,2},{1,3},{2,0},{3,1},{4,6},{5,7},{6,4},{7,5},{8,10},{9,11},{10,... | collective-permute-start | bytes 294920 | tf_op jit(solution)/shard_map/ppermute | solution.py:44
  26.2 1.3 %collective-permute-start.16 = (f32[64,256]{1,0:T(8,128)S(1)}, f32[64,256]{1,0:T(8,128)S(1)}, u32[]{:S(2)}, u32[]{:S(2)}) collective-permute-start(f32[64,256]{1,0:T(8,128)S(1)} %add.74.more_8_), channel_id=1, source_target_pairs={{0,1},{1,0},{2,3},{3,2},{4,5},{5,4},{6,7},{7,6},{8,9},{9,8},{10,11... | collective-permute-start | bytes 196616 | tf_op jit(solution)/shard_map/ppermute | solution.py:44
  26.3 4.7 %collective-permute-start.15 = (f32[64,256]{1,0:T(8,128)S(1)}, f32[64,256]{1,0:T(8,128)S(1)}, u32[]{:S(2)}, u32[]{:S(2)}) collective-permute-start(f32[64,256]{1,0:T(8,128)S(1)} %add.74.more_8_), channel_id=1, source_target_pairs={{0,2},{1,3},{2,0},{3,1},{4,6},{5,7},{6,4},{7,5},{8,10},{9,11},{10,... | collective-permute-start | bytes 196616 | tf_op jit(solution)/shard_map/ppermute | solution.py:44
  27.2 5.1 %collective-permute-start.4 = (f32[96,256]{1,0:T(8,128)S(1)}, f32[96,256]{1,0:T(8,128)S(1)}, u32[]{:S(2)}, u32[]{:S(2)}) collective-permute-start(f32[96,256]{1,0:T(8,128)S(1)} %add.68.more_0_), channel_id=1, source_target_pairs={{0,1},{1,0},{2,3},{3,2},{4,5},{5,4},{6,7},{7,6},{8,9},{9,8},{10,11... | collective-permute-start | bytes 294920 | tf_op jit(solution)/shard_map/ppermute | solution.py:44
  27.6 4.8 %collective-permute-start.10 = (f32[96,256]{1,0:T(8,128)S(1)}, f32[96,256]{1,0:T(8,128)S(1)}, u32[]{:S(2)}, u32[]{:S(2)}) collective-permute-start(f32[96,256]{1,0:T(8,128)S(1)} %add.71.more_4_), channel_id=1, source_target_pairs={{0,1},{1,0},{2,3},{3,2},{4,5},{5,4},{6,7},{7,6},{8,9},{9,8},{10,11... | collective-permute-start | bytes 294920 | tf_op jit(solution)/shard_map/ppermute | solution.py:44
  27.8 4.6 %collective-permute-start.5 = (f32[96,256]{1,0:T(8,128)S(1)}, f32[96,256]{1,0:T(8,128)S(1)}, u32[]{:S(2)}, u32[]{:S(2)}) collective-permute-start(f32[96,256]{1,0:T(8,128)S(1)} %collective-permute-done.3.more_1_), channel_id=1, source_target_pairs={{0,1},{1,0},{2,3},{3,2},{4,5},{5,4},{6,7},{7,6},{8,9},{9,8},{10,11... | collective-permute-start | bytes 294920 | tf_op jit(solution)/shard_map/ppermute | solution.py:44
  29.9 2.4 %collective-permute-start.11 = (f32[96,256]{1,0:T(8,128)S(1)}, f32[96,256]{1,0:T(8,128)S(1)}, u32[]{:S(2)}, u32[]{:S(2)}) collective-permute-start(f32[96,256]{1,0:T(8,128)S(1)} %collective-permute-done.9.more_5_), channel_id=1, source_target_pairs={{0,1},{1,0},{2,3},{3,2},{4,5},{5,4},{6,7},{7,6},{8,9},{9,8},{10,11... | collective-permute-start | bytes 294920 | tf_op jit(solution)/shard_map/ppermute | solution.py:44
  31.1 1.3 %collective-permute-start.17 = (f32[64,256]{1,0:T(8,128)S(1)}, f32[64,256]{1,0:T(8,128)S(1)}, u32[]{:S(2)}, u32[]{:S(2)}) collective-permute-start(f32[64,256]{1,0:T(8,128)S(1)} %collective-permute-done.15.more_9_), channel_id=1, source_target_pairs={{0,1},{1,0},{2,3},{3,2},{4,5},{5,4},{6,7},{7,6},{8,9},{9,8},{10,11... | collective-permute-start | bytes 196616 | tf_op jit(solution)/shard_map/ppermute | solution.py:44
  33.4 8.6 %collective-permute-start.20 = (f32[224,256]{1,0:T(8,128)S(1)}, f32[224,256]{1,0:T(8,128)S(1)}, u32[]{:S(2)}, u32[]{:S(2)}) collective-permute-start(f32[224,256]{1,0:T(8,128)S(1)} %get-tuple-element.52), channel_id=1, source_target_pairs={{0,16},{8,24},{16,0},{24,8},{1,17},{9,25},{17,1},{25,9},{2,18},{10... | collective-permute-start | bytes 688136 | tf_op jit(solution)/shard_map/ppermute | solution.py:44
  35.4 6.2 %collective-permute-start.18 = (f32[168,256]{1,0:T(8,128)S(1)}, f32[168,256]{1,0:T(8,128)S(1)}, u32[]{:S(2)}, u32[]{:S(2)}) collective-permute-start(f32[168,256]{1,0:T(8,128)S(1)} %get-tuple-element.51), channel_id=1, source_target_pairs={{0,8},{8,0},{16,24},{24,16},{1,9},{9,1},{17,25},{25,17},{2,10},{10... | collective-permute-start | bytes 516104 | tf_op jit(solution)/shard_map/ppermute | solution.py:44
  41.6 5.5 %collective-permute-start.19 = (f32[168,256]{1,0:T(8,128)S(1)}, f32[168,256]{1,0:T(8,128)S(1)}, u32[]{:S(2)}, u32[]{:S(2)}) collective-permute-start(f32[168,256]{1,0:T(8,128)S(1)} %add.75.a_ref.half_ref.refs_0_), channel_id=1, source_target_pairs={{0,16},{8,24},{16,0},{24,8},{1,17},{9,25},{17,1},{25,9},{2,18},{10... | collective-permute-start | bytes 516104 | tf_op jit(solution)/shard_map/ppermute | solution.py:44
  42.0 1.7 %copy-start = (f32[256]{0:T(256)S(1)}, f32[256]{0:T(256)}, u32[]{:S(2)}) copy-start(f32[256]{0:T(256)} %param.5) | copy-start | bytes 3076
  42.0 6.9 %collective-permute-start.21 = (f32[224,256]{1,0:T(8,128)S(1)}, f32[224,256]{1,0:T(8,128)S(1)}, u32[]{:S(2)}, u32[]{:S(2)}) collective-permute-start(f32[224,256]{1,0:T(8,128)S(1)} %add.76.refs_2_), channel_id=1, source_target_pairs={{0,8},{8,0},{16,24},{24,16},{1,9},{9,1},{17,25},{25,17},{2,10},{10... | collective-permute-start | bytes 688136 | tf_op jit(solution)/shard_map/ppermute | solution.py:44
  51.7 1.5 %collective-permute-start.22 = (f32[192,256]{1,0:T(8,128)S(1)}, f32[192,256]{1,0:T(8,128)S(1)}, u32[]{:S(2)}, u32[]{:S(2)}) collective-permute-start(f32[192,256]{1,0:T(8,128)S(1)} %get-tuple-element.67), channel_id=1, source_target_pairs={{0,1},{1,0},{2,3},{3,2},{4,5},{5,4},{6,7},{7,6},{8,9},{9,8},{10,11... | collective-permute-start | bytes 589832 | tf_op jit(solution)/shard_map/ppermute | solution.py:44
  51.8 3.7 %collective-permute-start.28 = (f32[192,256]{1,0:T(8,128)S(1)}, f32[192,256]{1,0:T(8,128)S(1)}, u32[]{:S(2)}, u32[]{:S(2)}) collective-permute-start(f32[192,256]{1,0:T(8,128)S(1)} %get-tuple-element.69), channel_id=1, source_target_pairs={{0,1},{1,0},{2,3},{3,2},{4,5},{5,4},{6,7},{7,6},{8,9},{9,8},{10,11... | collective-permute-start | bytes 589832 | tf_op jit(solution)/shard_map/ppermute | solution.py:44
  52.3 1.7 %collective-permute-start.34 = (f32[128,256]{1,0:T(8,128)S(1)}, f32[128,256]{1,0:T(8,128)S(1)}, u32[]{:S(2)}, u32[]{:S(2)}) collective-permute-start(f32[128,256]{1,0:T(8,128)S(1)} %get-tuple-element.71), channel_id=1, source_target_pairs={{0,1},{1,0},{2,3},{3,2},{4,5},{5,4},{6,7},{7,6},{8,9},{9,8},{10,11... | collective-permute-start | bytes 393224 | tf_op jit(solution)/shard_map/ppermute | solution.py:44
  53.3 5.7 %collective-permute-start.23 = (f32[96,256]{1,0:T(8,128)S(1)}, f32[96,256]{1,0:T(8,128)S(1)}, u32[]{:S(2)}, u32[]{:S(2)}) collective-permute-start(f32[96,256]{1,0:T(8,128)S(1)} %slice.55), channel_id=1, source_target_pairs={{0,2},{1,3},{2,0},{3,1},{4,6},{5,7},{6,4},{7,5},{8,10},{9,11},{10,... | collective-permute-start | bytes 294920 | tf_op jit(solution)/shard_map/ppermute | solution.py:44
  54.0 10.7 %collective-permute-start.35 = (f32[64,256]{1,0:T(8,128)S(1)}, f32[64,256]{1,0:T(8,128)S(1)}, u32[]{:S(2)}, u32[]{:S(2)}) collective-permute-start(f32[64,256]{1,0:T(8,128)S(1)} %slice.59), channel_id=1, source_target_pairs={{0,2},{1,3},{2,0},{3,1},{4,6},{5,7},{6,4},{7,5},{8,10},{9,11},{10,... | collective-permute-start | bytes 196616 | tf_op jit(solution)/shard_map/ppermute | solution.py:44
  55.5 7.2 %collective-permute-start.29 = (f32[96,256]{1,0:T(8,128)S(1)}, f32[96,256]{1,0:T(8,128)S(1)}, u32[]{:S(2)}, u32[]{:S(2)}) collective-permute-start(f32[96,256]{1,0:T(8,128)S(1)} %slice.57), channel_id=1, source_target_pairs={{0,2},{1,3},{2,0},{3,1},{4,6},{5,7},{6,4},{7,5},{8,10},{9,11},{10,... | collective-permute-start | bytes 294920 | tf_op jit(solution)/shard_map/ppermute | solution.py:44
  59.0 11.3 %collective-permute-start.24 = (f32[96,256]{1,0:T(8,128)S(1)}, f32[96,256]{1,0:T(8,128)S(1)}, u32[]{:S(2)}, u32[]{:S(2)}) collective-permute-start(f32[96,256]{1,0:T(8,128)S(1)} %slice_add_fusion.1), channel_id=1, source_target_pairs={{0,4},{1,5},{2,6},{3,7},{4,0},{5,1},{6,2},{7,3},{8,12},{9,13},{10,... | collective-permute-start | bytes 294920 | tf_op jit(solution)/shard_map/ppermute | solution.py:44
  62.8 9.7 %collective-permute-start.30 = (f32[96,256]{1,0:T(8,128)S(1)}, f32[96,256]{1,0:T(8,128)S(1)}, u32[]{:S(2)}, u32[]{:S(2)}) collective-permute-start(f32[96,256]{1,0:T(8,128)S(1)} %slice_add_fusion), channel_id=1, source_target_pairs={{0,4},{1,5},{2,6},{3,7},{4,0},{5,1},{6,2},{7,3},{8,12},{9,13},{10,... | collective-permute-start | bytes 294920 | tf_op jit(solution)/shard_map/ppermute | solution.py:44
  64.7 8.5 %collective-permute-start.36 = (f32[64,256]{1,0:T(8,128)S(1)}, f32[64,256]{1,0:T(8,128)S(1)}, u32[]{:S(2)}, u32[]{:S(2)}) collective-permute-start(f32[64,256]{1,0:T(8,128)S(1)} %slice_add_fusion.4), channel_id=1, source_target_pairs={{0,4},{1,5},{2,6},{3,7},{4,0},{5,1},{6,2},{7,3},{8,12},{9,13},{10,... | collective-permute-start | bytes 196616 | tf_op jit(solution)/shard_map/ppermute | solution.py:44
  70.3 5.6 %collective-permute-start.25 = (f32[96,256]{1,0:T(8,128)S(1)}, f32[96,256]{1,0:T(8,128)S(1)}, u32[]{:S(2)}, u32[]{:S(2)}) collective-permute-start(f32[96,256]{1,0:T(8,128)S(1)} %add.79.more_0_), channel_id=1, source_target_pairs={{0,2},{1,3},{2,0},{3,1},{4,6},{5,7},{6,4},{7,5},{8,10},{9,11},{10,... | collective-permute-start | bytes 294920 | tf_op jit(solution)/shard_map/ppermute | solution.py:44
  72.5 5.4 %collective-permute-start.31 = (f32[96,256]{1,0:T(8,128)S(1)}, f32[96,256]{1,0:T(8,128)S(1)}, u32[]{:S(2)}, u32[]{:S(2)}) collective-permute-start(f32[96,256]{1,0:T(8,128)S(1)} %add.82.more_4_), channel_id=1, source_target_pairs={{0,2},{1,3},{2,0},{3,1},{4,6},{5,7},{6,4},{7,5},{8,10},{9,11},{10,... | collective-permute-start | bytes 294920 | tf_op jit(solution)/shard_map/ppermute | solution.py:44
  73.2 1.7 %collective-permute-start.38 = (f32[64,256]{1,0:T(8,128)S(1)}, f32[64,256]{1,0:T(8,128)S(1)}, u32[]{:S(2)}, u32[]{:S(2)}) collective-permute-start(f32[64,256]{1,0:T(8,128)S(1)} %add.85.more_8_), channel_id=1, source_target_pairs={{0,1},{1,0},{2,3},{3,2},{4,5},{5,4},{6,7},{7,6},{8,9},{9,8},{10,11... | collective-permute-start | bytes 196616 | tf_op jit(solution)/shard_map/ppermute | solution.py:44
  73.2 5.3 %collective-permute-start.37 = (f32[64,256]{1,0:T(8,128)S(1)}, f32[64,256]{1,0:T(8,128)S(1)}, u32[]{:S(2)}, u32[]{:S(2)}) collective-permute-start(f32[64,256]{1,0:T(8,128)S(1)} %add.85.more_8_), channel_id=1, source_target_pairs={{0,2},{1,3},{2,0},{3,1},{4,6},{5,7},{6,4},{7,5},{8,10},{9,11},{10,... | collective-permute-start | bytes 196616 | tf_op jit(solution)/shard_map/ppermute | solution.py:44
  74.7 5.1 %collective-permute-start.26 = (f32[96,256]{1,0:T(8,128)S(1)}, f32[96,256]{1,0:T(8,128)S(1)}, u32[]{:S(2)}, u32[]{:S(2)}) collective-permute-start(f32[96,256]{1,0:T(8,128)S(1)} %add.79.more_0_), channel_id=1, source_target_pairs={{0,1},{1,0},{2,3},{3,2},{4,5},{5,4},{6,7},{7,6},{8,9},{9,8},{10,11... | collective-permute-start | bytes 294920 | tf_op jit(solution)/shard_map/ppermute | solution.py:44
  74.9 4.9 %collective-permute-start.32 = (f32[96,256]{1,0:T(8,128)S(1)}, f32[96,256]{1,0:T(8,128)S(1)}, u32[]{:S(2)}, u32[]{:S(2)}) collective-permute-start(f32[96,256]{1,0:T(8,128)S(1)} %add.82.more_4_), channel_id=1, source_target_pairs={{0,1},{1,0},{2,3},{3,2},{4,5},{5,4},{6,7},{7,6},{8,9},{9,8},{10,11... | collective-permute-start | bytes 294920 | tf_op jit(solution)/shard_map/ppermute | solution.py:44
  75.9 3.9 %collective-permute-start.27 = (f32[96,256]{1,0:T(8,128)S(1)}, f32[96,256]{1,0:T(8,128)S(1)}, u32[]{:S(2)}, u32[]{:S(2)}) collective-permute-start(f32[96,256]{1,0:T(8,128)S(1)} %collective-permute-done.25.more_1_), channel_id=1, source_target_pairs={{0,1},{1,0},{2,3},{3,2},{4,5},{5,4},{6,7},{7,6},{8,9},{9,8},{10,11... | collective-permute-start | bytes 294920 | tf_op jit(solution)/shard_map/ppermute | solution.py:44
  77.8 2.0 %collective-permute-start.33 = (f32[96,256]{1,0:T(8,128)S(1)}, f32[96,256]{1,0:T(8,128)S(1)}, u32[]{:S(2)}, u32[]{:S(2)}) collective-permute-start(f32[96,256]{1,0:T(8,128)S(1)} %collective-permute-done.31.more_5_), channel_id=1, source_target_pairs={{0,1},{1,0},{2,3},{3,2},{4,5},{5,4},{6,7},{7,6},{8,9},{9,8},{10,11... | collective-permute-start | bytes 294920 | tf_op jit(solution)/shard_map/ppermute | solution.py:44
  78.5 1.3 %collective-permute-start.39 = (f32[64,256]{1,0:T(8,128)S(1)}, f32[64,256]{1,0:T(8,128)S(1)}, u32[]{:S(2)}, u32[]{:S(2)}) collective-permute-start(f32[64,256]{1,0:T(8,128)S(1)} %collective-permute-done.37.more_9_), channel_id=1, source_target_pairs={{0,1},{1,0},{2,3},{3,2},{4,5},{5,4},{6,7},{7,6},{8,9},{9,8},{10,11... | collective-permute-start | bytes 196616 | tf_op jit(solution)/shard_map/ppermute | solution.py:44
  80.9 8.3 %collective-permute-start.42 = (f32[224,256]{1,0:T(8,128)S(1)}, f32[224,256]{1,0:T(8,128)S(1)}, u32[]{:S(2)}, u32[]{:S(2)}) collective-permute-start(f32[224,256]{1,0:T(8,128)S(1)} %get-tuple-element.73), channel_id=1, source_target_pairs={{0,16},{8,24},{16,0},{24,8},{1,17},{9,25},{17,1},{25,9},{2,18},{10... | collective-permute-start | bytes 688136 | tf_op jit(solution)/shard_map/ppermute | solution.py:44
  82.0 6.2 %collective-permute-start.40 = (f32[168,256]{1,0:T(8,128)S(1)}, f32[168,256]{1,0:T(8,128)S(1)}, u32[]{:S(2)}, u32[]{:S(2)}) collective-permute-start(f32[168,256]{1,0:T(8,128)S(1)} %get-tuple-element.72), channel_id=1, source_target_pairs={{0,8},{8,0},{16,24},{24,16},{1,9},{9,1},{17,25},{25,17},{2,10},{10... | collective-permute-start | bytes 516104 | tf_op jit(solution)/shard_map/ppermute | solution.py:44
  88.2 5.5 %collective-permute-start.41 = (f32[168,256]{1,0:T(8,128)S(1)}, f32[168,256]{1,0:T(8,128)S(1)}, u32[]{:S(2)}, u32[]{:S(2)}) collective-permute-start(f32[168,256]{1,0:T(8,128)S(1)} %add.86.a_ref.half_ref.refs_0_), channel_id=1, source_target_pairs={{0,16},{8,24},{16,0},{24,8},{1,17},{9,25},{17,1},{25,9},{2,18},{10... | collective-permute-start | bytes 516104 | tf_op jit(solution)/shard_map/ppermute | solution.py:44
  89.3 6.3 %collective-permute-start.43 = (f32[224,256]{1,0:T(8,128)S(1)}, f32[224,256]{1,0:T(8,128)S(1)}, u32[]{:S(2)}, u32[]{:S(2)}) collective-permute-start(f32[224,256]{1,0:T(8,128)S(1)} %add.87.refs_2_), channel_id=1, source_target_pairs={{0,8},{8,0},{16,24},{24,16},{1,9},{9,1},{17,25},{25,17},{2,10},{10... | collective-permute-start | bytes 688136 | tf_op jit(solution)/shard_map/ppermute | solution.py:44
